TPU v7x, 32 devices: a whole 2x2x4 slice. The times are simulated.
32 devices in a mesh: parts: 2 (over y), band: 4 (over z), feat: 4 (over x, core).
Axes of the slice: x: 2, y: 2, z: 4, core: 2. Of those that a mesh axis runs over, the one named last changes fastest.
Arguments:
- x_grid: bfloat16 [4096, 474], P(('parts', 'band')), parts along dimension 0, may hold values from -6 to 6
- mesh_pos: float32 [3, 2048], P(None, 'band'), may hold values from -4 to 4
- pos_weight: float32 [3, 512], replicated, may hold values from -3.5 to 3.5
- embed_in: bfloat16 [474, 512], P(None, 'feat'), may hold values from -0.25 to 0.25
- pair_in: bfloat16 [8, 1024, 512], P(None, None, 'feat'), may hold values from -0.1875 to 0.1875
- pair_out: bfloat16 [9, 512, 512], P(None, 'feat'), may hold values from -0.25 to 0.25
- hidden_bias: float32 [9, 512], P(None, 'feat'), may hold values from -1 to 1
- norm_gain: float32 [9, 512], replicated, may hold values from 0.1 to 1.9
- norm_shift: float32 [9, 512], replicated, may hold values from -3 to 3
- head: bfloat16 [512, 227], replicated, may hold values from -0.25 to 0.25
- g2m_take: int32 [4, 4, 256], P('band'), may hold values from 0 to 511, as said below
- g2m_from: int32 [4096], P('band'), may hold values from 0 to 1023, as said below
- g2m_to: int32 [4096], P('band'), may hold values from 0 to 511, as said below
- m2m_take: int32 [4, 4, 512], P('band'), may hold values from 0 to 511, as said below
- m2m_from: int32 [8192], P('band'), may hold values from 0 to 2047, as said below
- m2m_to: int32 [8192], P('band'), may hold values from 0 to 511, as said below
- m2g_take: int32 [4, 4, 384], P('band'), may hold values from 0 to 511, as said below
- m2g_from: int32 [6144], P('band'), may hold values from 0 to 1535, as said below
Outputs:
- forecast: float32 [4096, 227], P(('parts', 'band', 'feat')), parts along dimension 0
There are 2 independent parts, one for each index of `parts`. A program takes and returns all parts, laid end to end along the dimension named above; an argument that names none is the same for every part. Nothing has to cross between parts.
Inputs may be any that keep to these rules, and one draw needn't show every extreme that they name: `g2m_take`: every value names a row of the sending device; a slot may repeat a row. `m2m_take`: every value names a node of the sending partition; a slot may repeat a node. `m2g_take`: every value names a node of the sending partition; a slot may repeat a node. `g2m_from`: A slot index on the receiving device, source device major (256 slots per source). From each source the device's edges name exactly the slots below a count for that pair, which lies between half of 256 (rounded up) and 256; one receiving device has the full count from every source. The remaining slots are unused, though their take entries are valid rows. `m2m_from`: as for g2m_from, with 512 slots per source. `m2g_from`: as for g2m_from, with 384 slots per source. `g2m_to`: on each device, edges k * 128 * 2 to (k + 1) * 128 * 2 - 1 go to nodes of receiver block k (nodes k * 128 to (k + 1) * 128 - 1), in non-decreasing order; every node receives at least one edge. `m2m_to`: on each device, edges k * 128 * 4 to (k + 1) * 128 * 4 - 1 go to nodes of receiver block k, in non-decreasing order; every node receives at least one edge.
All inputs are finite; a program needn't handle non-finite values.
Results may differ from a plain program's by a relative error of at most 0.017.
Values may be sent and summed in bfloat16 or wider, within the bound.
No kernel may reach another device: no remote copies, remote signals or barrier semaphores. Data moves between devices by JAX's collectives and lax.ppermute only.
A program may use at most 64 MiB of HBM per device.

v0:
```python
import jax
import jax.numpy as jnp
from jax import lax
from jax.sharding import PartitionSpec as P

LAYERS = 2
NODE_BLK = 128


EPSILON = 1e-05


def layer_norm(values, gain_row, shift_row):
    average = jnp.mean(values, axis=-1, keepdims=True)
    centered = values - average
    variance = jnp.mean(centered * centered, axis=-1, keepdims=True)
    return centered * lax.rsqrt(variance + EPSILON) * gain_row + shift_row


def block_sum(messages, receivers, node_rows):
    latent = messages.shape[1]
    blocks = node_rows // NODE_BLK
    grouped = messages.reshape(blocks, -1, latent)
    position = (receivers % NODE_BLK).reshape(blocks, -1)
    onehot = (position[:, None, :] == jnp.arange(NODE_BLK, dtype=jnp.int32)[None, :, None]).astype(
        jnp.bfloat16
    )
    summed = jnp.einsum("bne,bel->bnl", onehot, grouped, preferred_element_type=jnp.float32)
    return summed.reshape(node_rows, latent)


def local(
    x_grid,
    mesh_pos,
    pos_weight,
    embed_in,
    pair_in,
    pair_out,
    hidden_bias,
    norm_gain,
    norm_shift,
    head,
    g2m_take,
    g2m_from,
    g2m_to,
    m2m_take,
    m2m_from,
    m2m_to,
    m2g_take,
    m2g_from,
):
    quarters = lax.axis_size("feat")
    feat_index = lax.axis_index("feat")
    latent = norm_gain.shape[1]
    embed_id = pair_out.shape[0] - 1
    embed_w, in_w, out_w, bias_w = (embed_in, pair_in, pair_out, hidden_bias)

    def own_rows(full):
        row_count = full.shape[0] // quarters
        return lax.dynamic_slice_in_dim(full, feat_index * row_count, row_count, 0)

    def spread(rows):
        return lax.all_gather(rows, "feat", axis=0, tiled=True)

    def finish(hidden, section_id):
        partial_value = jnp.dot(hidden, out_w[section_id], preferred_element_type=jnp.float32)
        summed = lax.psum_scatter(
            partial_value.astype(jnp.bfloat16), "feat", scatter_dimension=0, tiled=True
        ).astype(jnp.float32)
        return layer_norm(summed, norm_gain[section_id], norm_shift[section_id])

    def sender_terms(source_latent, take_rows, send_weight, senders):
        projected = jnp.dot(source_latent, send_weight, preferred_element_type=jnp.float32)
        picked = jnp.take(projected, take_rows[0], axis=0)
        arrived = lax.all_to_all(
            picked.astype(jnp.bfloat16), "band", split_axis=0, concat_axis=0, tiled=True
        ).astype(picked.dtype)
        arrived = arrived.reshape(-1, arrived.shape[-1])
        return jnp.take(arrived, senders, axis=0)

    def edge_messages(section_id, send_part, receive_part):
        preact = send_part + receive_part + bias_w[section_id]
        hidden = jax.nn.silu(preact).astype(jnp.bfloat16)
        return finish(hidden, section_id).astype(jnp.bfloat16)

    def node_update(section_id, node_latent, aggregate):
        weights = in_w[section_id]
        preact = (
            jnp.dot(node_latent, weights[:latent], preferred_element_type=jnp.float32)
            + jnp.dot(aggregate, weights[latent:], preferred_element_type=jnp.float32)
            + bias_w[section_id]
        )
        hidden = jax.nn.silu(preact).astype(jnp.bfloat16)
        base = own_rows(node_latent)
        return base.astype(jnp.float32) + finish(hidden, section_id)

    def mesh_section(
        section_id, source_latent, take_rows, senders_all, receivers_all, mesh_latent, node_rows
    ):
        weights = in_w[section_id]
        receive_part = jnp.take(
            jnp.dot(mesh_latent, weights[latent:], preferred_element_type=jnp.float32),
            receivers_all,
            axis=0,
        )
        send_part = sender_terms(source_latent, take_rows, weights[:latent], senders_all)
        messages = edge_messages(section_id, send_part, receive_part)
        aggregate = block_sum(messages, own_rows(receivers_all), node_rows).astype(jnp.bfloat16)
        updated = node_update(section_id + 1, mesh_latent, spread(aggregate))
        return spread(updated.astype(jnp.bfloat16))

    preact = jnp.dot(x_grid, embed_w, preferred_element_type=jnp.float32) + bias_w[embed_id]
    grid_own = finish(jax.nn.silu(preact).astype(jnp.bfloat16), embed_id).astype(jnp.bfloat16)
    grid_latent = spread(grid_own)
    mesh_latent = (
        mesh_pos[0][:, None] * pos_weight[0][None, :]
        + mesh_pos[1][:, None] * pos_weight[1][None, :]
    )
    mesh_latent = (mesh_latent + mesh_pos[2][:, None] * pos_weight[2][None, :]).astype(jnp.bfloat16)
    node_rows = mesh_latent.shape[0] // quarters
    mesh_latent = mesh_section(0, grid_latent, g2m_take, g2m_from, g2m_to, mesh_latent, node_rows)
    for layer_id in range(LAYERS):
        section_id = 2 + 2 * layer_id
        mesh_latent = mesh_section(
            section_id, mesh_latent, m2m_take, m2m_from, m2m_to, mesh_latent, node_rows
        )
    section_id = 2 * LAYERS + 2
    weights = in_w[section_id]
    senders = m2g_from
    receive_part = jnp.repeat(
        jnp.dot(grid_latent, weights[latent:], preferred_element_type=jnp.float32), 3, axis=0
    )
    send_part = sender_terms(mesh_latent, m2g_take, weights[:latent], senders)
    messages = edge_messages(section_id, send_part, receive_part)
    grid_sum = messages.astype(jnp.float32).reshape(-1, 3, latent).sum(axis=1).astype(jnp.bfloat16)
    final_latent = node_update(section_id + 1, grid_latent, spread(grid_sum)).astype(jnp.bfloat16)
    return jnp.dot(final_latent, head, preferred_element_type=jnp.float32)


def solution(mesh):
    return jax.shard_map(
        local,
        mesh=mesh,
        in_specs=(
            P(("parts", "band"), None),
            P(None, "band"),
            P(),
            P(None, "feat"),
            P(None, None, "feat"),
            P(None, "feat", None),
            P(None, "feat"),
            P(),
            P(),
            P(),
            P("band", None, None),
            P("band"),
            P("band"),
            P("band", None, None),
            P("band"),
            P("band"),
            P("band", None, None),
            P("band"),
        ),
        out_specs=P(("parts", "band", "feat"), None),
        check_vma=False,
    )
```

profile of v0, /device:TPU:0, one launch (start us, length us, event | category | flops | bytes accessed | tf_op | source)
XLA Modules:
  0.0 468.8 jit_solution(8747287858276124016)
XLA Ops:
  14.3 20.2 %reduce-scatter.10.cloned.1.call-done = bf16[128,512]{1,0:T(8,128)(2,1)} async-done(((bf16[512,512]{1,0:T(8,128)(2,1)}), bf16[128,512]{1,0:T(8,128)(2,1)}) %reduce-scatter.10.cloned.1.call-update) | async-done | bytes 131088 | tf_op jit(solution)/shard_map/reduce_scatter | solution.py:67
  37.6 6.8 %all_gather.24 = bf16[512,512]{1,0:T(8,128)(2,1)S(1)} all-gather(bf16[128,512]{1,0:T(8,128)(2,1)S(1)} %fusion.84), channel_id=1, replica_groups=mesh['parts'=2,'band'=4,'feat'=4] {'feat'}, dimensions={0}, use_global_device_ids=true | all-gather | bytes 655360 | tf_op jit(solution)/shard_map/all_gather | solution.py:63
  54.3 9.3 %all-to-all-done = bf16[4,256,128]{2,1,0:T(8,128)(2,1)S(1)} async-done(((bf16[4,256,128]{2,1,0:T(8,128)(2,1)}), bf16[4,256,128]{2,1,0:T(8,128)(2,1)S(1)}, u32[]{:S(2)}, u32[]{:S(2)}) %all-to-all-start) | async-done | bytes 262176 | tf_op jit(solution)/shard_map/all_to_all | solution.py:75
  70.8 22.1 %reduce-scatter.12.cloned.1.call-done = bf16[256,512]{1,0:T(8,128)(2,1)} async-done(((bf16[1024,512]{1,0:T(8,128)(2,1)}), bf16[256,512]{1,0:T(8,128)(2,1)}) %reduce-scatter.12.cloned.1.call-update) | async-done | bytes 262160 | tf_op jit(solution)/shard_map/reduce_scatter | solution.py:67
  96.5 6.8 %all_gather.25 = bf16[512,512]{1,0:T(8,128)(2,1)S(1)} all-gather(bf16[128,512]{1,0:T(8,128)(2,1)S(1)} %convolution_convert_fusion.11), channel_id=1, replica_groups=mesh['parts'=2,'band'=4,'feat'=4] {'feat'}, dimensions={0}, use_global_device_ids=true | all-gather | bytes 655360 | tf_op jit(solution)/shard_map/all_gather | solution.py:63
  105.8 21.8 %reduce-scatter.14.cloned.1.call-done = bf16[128,512]{1,0:T(8,128)(2,1)} async-done(((bf16[512,512]{1,0:T(8,128)(2,1)}), bf16[128,512]{1,0:T(8,128)(2,1)}) %reduce-scatter.14.cloned.1.call-update) | async-done | bytes 131088 | tf_op jit(solution)/shard_map/reduce_scatter | solution.py:67
  130.8 6.8 %all_gather.26 = bf16[512,512]{1,0:T(8,128)(2,1)S(1)} all-gather(bf16[128,512]{1,0:T(8,128)(2,1)S(1)} %fusion.80), channel_id=1, replica_groups=mesh['parts'=2,'band'=4,'feat'=4] {'feat'}, dimensions={0}, use_global_device_ids=true | all-gather | bytes 655360 | tf_op jit(solution)/shard_map/all_gather | solution.py:63
  152.0 7.6 %gather_fusion.7 = f32[2048,128]{1,0:T(8,128)} fusion(f32[512,128]{1,0:T(8,128)S(1)} %fusion.119, s32[2048]{0:T(1024)S(1)} %fusion.186), kind=kCustom, calls=%fused_computation.2.clone | custom fusion | bytes 2105344 | tf_op jit(solution)/shard_map/jit(_take)/gather | solution.py:101
  165.9 7.5 %gather_fusion.6 = f32[2048,128]{1,0:T(8,128)} fusion(f32[2048,128]{1,0:T(8,128)S(1)} %bitcast_convert_fusion.1, s32[2048]{0:T(1024)S(1)} %fusion.185), kind=kCustom, calls=%fused_computation.1.clone | custom fusion | bytes 2105344 | tf_op jit(solution)/shard_map/jit(_take)/gather | solution.py:79
  178.1 28.7 %reduce-scatter.16.cloned.1.call-done = bf16[512,512]{1,0:T(8,128)(2,1)} async-done(((bf16[2048,512]{1,0:T(8,128)(2,1)}), bf16[512,512]{1,0:T(8,128)(2,1)}) %reduce-scatter.16.cloned.1.call-update) | async-done | bytes 524304 | tf_op jit(solution)/shard_map/reduce_scatter | solution.py:67
  210.8 6.8 %all_gather.27 = bf16[512,512]{1,0:T(8,128)(2,1)S(1)} all-gather(bf16[128,512]{1,0:T(8,128)(2,1)S(1)} %convolution_convert_fusion.10), channel_id=1, replica_groups=mesh['parts'=2,'band'=4,'feat'=4] {'feat'}, dimensions={0}, use_global_device_ids=true | all-gather | bytes 655360 | tf_op jit(solution)/shard_map/all_gather | solution.py:63
  219.8 22.2 %reduce-scatter.18.cloned.1.call-done = bf16[128,512]{1,0:T(8,128)(2,1)} async-done(((bf16[512,512]{1,0:T(8,128)(2,1)}), bf16[128,512]{1,0:T(8,128)(2,1)}) %reduce-scatter.18.cloned.1.call-update) | async-done | bytes 131088 | tf_op jit(solution)/shard_map/reduce_scatter | solution.py:67
  245.2 6.8 %all_gather.28 = bf16[512,512]{1,0:T(8,128)(2,1)S(1)} all-gather(bf16[128,512]{1,0:T(8,128)(2,1)S(1)} %fusion.75), channel_id=1, replica_groups=mesh['parts'=2,'band'=4,'feat'=4] {'feat'}, dimensions={0}, use_global_device_ids=true | all-gather | bytes 655360 | tf_op jit(solution)/shard_map/all_gather | solution.py:63
  266.3 7.6 %gather_fusion.10 = f32[2048,128]{1,0:T(8,128)} fusion(f32[512,128]{1,0:T(8,128)S(1)} %fusion.109, s32[2048]{0:T(1024)S(1)} %fusion.186), kind=kCustom, calls=%fused_computation.5.clone | custom fusion | bytes 2105344 | tf_op jit(solution)/shard_map/jit(_take)/gather | solution.py:101
  273.9 6.2 %all-to-all-done.2 = bf16[4,512,128]{2,1,0:T(8,128)(2,1)S(1)} async-done(((bf16[4,512,128]{2,1,0:T(8,128)(2,1)}), bf16[4,512,128]{2,1,0:T(8,128)(2,1)S(1)}, u32[]{:S(2)}, u32[]{:S(2)}) %all-to-all-start.2) | async-done | bytes 524320 | tf_op jit(solution)/shard_map/all_to_all | solution.py:75
  280.2 7.5 %gather_fusion.9 = f32[2048,128]{1,0:T(8,128)} fusion(f32[2048,128]{1,0:T(8,128)S(1)} %bitcast_convert_fusion, s32[2048]{0:T(1024)S(1)} %fusion.185), kind=kCustom, calls=%fused_computation.4.clone | custom fusion | bytes 2105344 | tf_op jit(solution)/shard_map/jit(_take)/gather | solution.py:79
  292.6 28.6 %reduce-scatter.20.cloned.1.call-done = bf16[512,512]{1,0:T(8,128)(2,1)} async-done(((bf16[2048,512]{1,0:T(8,128)(2,1)}), bf16[512,512]{1,0:T(8,128)(2,1)}) %reduce-scatter.20.cloned.1.call-update) | async-done | bytes 524304 | tf_op jit(solution)/shard_map/reduce_scatter | solution.py:67
  325.2 6.8 %all_gather.29 = bf16[512,512]{1,0:T(8,128)(2,1)S(1)} all-gather(bf16[128,512]{1,0:T(8,128)(2,1)S(1)} %convolution_convert_fusion.9), channel_id=1, replica_groups=mesh['parts'=2,'band'=4,'feat'=4] {'feat'}, dimensions={0}, use_global_device_ids=true | all-gather | bytes 655360 | tf_op jit(solution)/shard_map/all_gather | solution.py:63
  334.3 22.1 %reduce-scatter.22.cloned.1.call-done = bf16[128,512]{1,0:T(8,128)(2,1)} async-done(((bf16[512,512]{1,0:T(8,128)(2,1)}), bf16[128,512]{1,0:T(8,128)(2,1)}) %reduce-scatter.22.cloned.1.call-update) | async-done | bytes 131088 | tf_op jit(solution)/shard_map/reduce_scatter | solution.py:67
  359.6 6.8 %all_gather.30 = bf16[512,512]{1,0:T(8,128)(2,1)S(1)} all-gather(bf16[128,512]{1,0:T(8,128)(2,1)S(1)} %fusion.70), channel_id=1, replica_groups=mesh['parts'=2,'band'=4,'feat'=4] {'feat'}, dimensions={0}, use_global_device_ids=true | all-gather | bytes 655360 | tf_op jit(solution)/shard_map/all_gather | solution.py:63
  377.9 10.7 %all-to-all-done.3 = bf16[4,384,128]{2,1,0:T(8,128)(2,1)S(1)} async-done(((bf16[4,384,128]{2,1,0:T(8,128)(2,1)}), bf16[4,384,128]{2,1,0:T(8,128)(2,1)S(1)}, u32[]{:S(2)}, u32[]{:S(2)}) %all-to-all-start.3) | async-done | bytes 393248 | tf_op jit(solution)/shard_map/all_to_all | solution.py:75
  396.9 25.5 %reduce-scatter.24.cloned.1.call-done = bf16[384,512]{1,0:T(8,128)(2,1)} async-done(((bf16[1536,512]{1,0:T(8,128)(2,1)}), bf16[384,512]{1,0:T(8,128)(2,1)}) %reduce-scatter.24.cloned.1.call-update) | async-done | bytes 393232 | tf_op jit(solution)/shard_map/reduce_scatter | solution.py:67
  427.0 6.8 %all_gather.31 = bf16[512,512]{1,0:T(8,128)(2,1)S(1)} all-gather(bf16[128,512]{1,0:T(8,128)(2,1)S(1)} %reduce), channel_id=1, replica_groups=mesh['parts'=2,'band'=4,'feat'=4] {'feat'}, dimensions={0}, use_global_device_ids=true | all-gather | bytes 655360 | tf_op jit(solution)/shard_map/all_gather | solution.py:63
  436.0 22.2 %reduce-scatter.26.cloned.1.call-done = bf16[128,512]{1,0:T(8,128)(2,1)} async-done(((bf16[512,512]{1,0:T(8,128)(2,1)}), bf16[128,512]{1,0:T(8,128)(2,1)}) %reduce-scatter.26.cloned.1.call-update) | async-done | bytes 131088 | tf_op jit(solution)/shard_map/reduce_scatter | solution.py:67
  (167 shorter events, 130.5 us)
Async XLA Ops:
  6.5 3.4 copy-start.7
  6.5 3.4 copy-start.11
  6.5 3.4 copy-start.12
  6.5 27.9 %reduce-scatter.10.cloned.1.call-start = ((), (), s32[]{:S(2)}) async-start(), calls=%async_computation.13 | async-start | bytes 655360 | tf_op jit(solution)/shard_map/reduce_scatter | solution.py:67
  7.6 3.7 copy-start.6
  44.4 10.0 %copy-start.8 = (s32[1024]{0:T(1024)S(1)}, s32[1024]{0:T(1024)}, u32[]{:S(2)}) copy-start(s32[1024]{0:T(1024)} %param.35) | copy-start | bytes 12292
  49.7 14.0 %all-to-all-start = ((bf16[4,256,128]{2,1,0:T(8,128)(2,1)}), bf16[4,256,128]{2,1,0:T(8,128)(2,1)S(1)}, u32[]{:S(2)}, u32[]{:S(2)}) async-start(bf16[4,256,128]{2,1,0:T(8,128)(2,1)} %select_convert_fusion.3), calls=%async_computation.1 | async-start | bytes 524288 | tf_op jit(solution)/shard_map/all_to_all | solution.py:75
  54.3 38.6 %reduce-scatter.12.cloned.1.call-start = ((), (), s32[]{:S(2)}) async-start(), calls=%async_computation.14 | async-start | bytes 1310720 | tf_op jit(solution)/shard_map/reduce_scatter | solution.py:67
  69.3 58.3 %reduce-scatter.14.cloned.1.call-start = ((), (), s32[]{:S(2)}) async-start(), calls=%async_computation.15 | async-start | bytes 655360 | tf_op jit(solution)/shard_map/reduce_scatter | solution.py:67
  95.2 10.3 %copy-start.2 = (s32[1,4,512]{2,1,0:T(4,128)S(1)}, s32[1,4,512]{2,1,0:T(4,128)}, u32[]{:S(2)}) copy-start(s32[1,4,512]{2,1,0:T(4,128)} %param.37) | copy-start | bytes 24580
  145.0 5.7 %copy-start.4 = (s32[2048]{0:T(1024)S(1)}, s32[2048]{0:T(1024)}, u32[]{:S(2)}) copy-start(s32[2048]{0:T(1024)} %param.38) | copy-start | bytes 24580
  145.0 5.7 %copy-start.1 = (s32[2048]{0:T(1024)S(1)}, s32[2048]{0:T(1024)}, u32[]{:S(2)}) copy-start(s32[2048]{0:T(1024)} %param.39) | copy-start | bytes 24580
  146.2 19.6 %all-to-all-start.1 = ((bf16[4,512,128]{2,1,0:T(8,128)(2,1)}), bf16[4,512,128]{2,1,0:T(8,128)(2,1)S(1)}, u32[]{:S(2)}, u32[]{:S(2)}) async-start(bf16[4,512,128]{2,1,0:T(8,128)(2,1)} %select_convert_fusion.1), calls=%async_computation.4 | async-start | bytes 1048576 | tf_op jit(solution)/shard_map/all_to_all | solution.py:75
  150.8 56.1 %reduce-scatter.16.cloned.1.call-start = ((), (), s32[]{:S(2)}) async-start(), calls=%async_computation.16 | async-start | bytes 2621440 | tf_op jit(solution)/shard_map/reduce_scatter | solution.py:67
  176.7 65.3 %reduce-scatter.18.cloned.1.call-start = ((), (), s32[]{:S(2)}) async-start(), calls=%async_computation.17 | async-start | bytes 655360 | tf_op jit(solution)/shard_map/reduce_scatter | solution.py:67
  260.5 19.6 %all-to-all-start.2 = ((bf16[4,512,128]{2,1,0:T(8,128)(2,1)}), bf16[4,512,128]{2,1,0:T(8,128)(2,1)S(1)}, u32[]{:S(2)}, u32[]{:S(2)}) async-start(bf16[4,512,128]{2,1,0:T(8,128)(2,1)} %select_convert_fusion), calls=%async_computation.7 | async-start | bytes 1048576 | tf_op jit(solution)/shard_map/all_to_all | solution.py:75
  265.1 56.0 %reduce-scatter.20.cloned.1.call-start = ((), (), s32[]{:S(2)}) async-start(), calls=%async_computation.18 | async-start | bytes 2621440 | tf_op jit(solution)/shard_map/reduce_scatter | solution.py:67
  291.1 65.3 %reduce-scatter.22.cloned.1.call-start = ((), (), s32[]{:S(2)}) async-start(), calls=%async_computation.19 | async-start | bytes 655360 | tf_op jit(solution)/shard_map/reduce_scatter | solution.py:67
  323.7 10.5 %copy-start.5 = (s32[1,4,384]{2,1,0:T(4,128)S(1)}, s32[1,4,384]{2,1,0:T(4,128)}, u32[]{:S(2)}) copy-start(s32[1,4,384]{2,1,0:T(4,128)} %param.40) | copy-start | bytes 18436
  367.6 8.8 %copy-start.3 = (s32[1536]{0:T(1024)S(1)}, s32[1536]{0:T(1024)}, u32[]{:S(2)}) copy-start(s32[1536]{0:T(1024)} %param.41) | copy-start | bytes 18436
  371.8 16.8 %all-to-all-start.3 = ((bf16[4,384,128]{2,1,0:T(8,128)(2,1)}), bf16[4,384,128]{2,1,0:T(8,128)(2,1)S(1)}, u32[]{:S(2)}, u32[]{:S(2)}) async-start(bf16[4,384,128]{2,1,0:T(8,128)(2,1)} %select_convert_fusion.2), calls=%async_computation.10 | async-start | bytes 786432 | tf_op jit(solution)/shard_map/all_to_all | solution.py:75
  376.4 46.0 %reduce-scatter.24.cloned.1.call-start = ((), (), s32[]{:S(2)}) async-start(), calls=%async_computation.20 | async-start | bytes 1966080 | tf_op jit(solution)/shard_map/reduce_scatter | solution.py:67
  395.7 62.5 %reduce-scatter.26.cloned.1.call-start = ((), (), s32[]{:S(2)}) async-start(), calls=%async_computation.21 | async-start | bytes 655360 | tf_op jit(solution)/shard_map/reduce_scatter | solution.py:67
  426.3 34.0 %copy-start.13 = (bf16[512,227]{0,1:T(8,128)(2,1)S(1)}, bf16[512,227]{0,1:T(8,128)(2,1)}, u32[]{:S(2)}) copy-start(bf16[512,227]{0,1:T(8,128)(2,1)} %param.33) | copy-start | bytes 697348
  (3 other events, 6.9 us)
Sparse Core Ops, SparseCore 0:
  10.0 24.3 reduce-scatter.9
  69.5 23.4 reduce-scatter.11
  105.6 22.0 reduce-scatter.13
  176.9 29.9 reduce-scatter.15
  220.0 22.0 reduce-scatter.17
  291.3 29.8 reduce-scatter.19
  334.3 22.0 reduce-scatter.21
  395.8 26.6 reduce-scatter.23
  436.1 22.0 reduce-scatter.25
where the time goes:
time: 470 us; the launch traced here: 469 us
  waiting for transfers between devices  246 us (52%)
  local copies, waits for them, and re-layouts  59.5 us (13%)
  blocking collectives  54.2 us (12%)
  matrix products  43.7 us (9%)
  other arithmetic  32.4 us (7%)
  starting transfers between devices  18.8 us (4%)
  between operations  14 us (3%)
    reduce_scatter x9, waiting for transfers between devices, finish(): lax.psum_scatter(partial_value.astype(jnp.bfloat16), 'feat', scatter_dime...  214 us
    all_gather x8, blocking collectives, spread(): return lax.all_gather(rows, 'feat', axis=0, tiled=True)  54.2 us
    all_to_all x4, waiting for transfers between devices, sender_terms(): lax.all_to_all(picked.astype(jnp.bfloat16), 'band', split_axis=0, concat_...  32.4 us
    dot_general x9, matrix products, finish(): jnp.dot(hidden, out_w[section_id], preferred_element_type=jnp.float32)  23 us
    gather x5, local copies, waits for them, and re-layouts, sender_terms(): return jnp.take(arrived, senders, axis=0)  20.8 us
    gather x4, local copies, waits for them, and re-layouts, sender_terms(): picked = jnp.take(projected, take_rows[0], axis=0)  18.8 us
    all_to_all x4, starting transfers between devices, sender_terms(): lax.all_to_all(picked.astype(jnp.bfloat16), 'band', split_axis=0, concat_...  18.4 us
    gather x3, local copies, waits for them, and re-layouts, mesh_section(): jnp.take(jnp.dot(mesh_latent, weights[latent:], preferred_element_type=jn...  17.9 us
  transfers between devices with their start and end apart: 13, of which 13 were waited for; matrix products, arithmetic and copies ran while one was open for 6% of the time, Pallas kernels for 0%

commit v1 on v0

v1 whole, which is shorter than its diff:
```python
import jax
import jax.numpy as jnp
from jax import lax
from jax.sharding import PartitionSpec as P

LAYERS = 2
EPSILON = 1e-05


def layer_norm(values, gain_row, shift_row):
    average = jnp.mean(values, axis=-1, keepdims=True)
    centered = values - average
    variance = jnp.mean(centered * centered, axis=-1, keepdims=True)
    return centered * lax.rsqrt(variance + EPSILON) * gain_row + shift_row


def local(
    x_grid,
    mesh_pos,
    pos_weight,
    embed_in,
    pair_in,
    pair_out,
    hidden_bias,
    norm_gain,
    norm_shift,
    head,
    g2m_take,
    g2m_from,
    g2m_to,
    m2m_take,
    m2m_from,
    m2m_to,
    m2g_take,
    m2g_from,
):
    quarters = lax.axis_size("feat")
    bands = lax.axis_size("band")
    feat_index = lax.axis_index("feat")
    band_index = lax.axis_index("band")
    latent = norm_gain.shape[1]
    embed_id = pair_out.shape[0] - 1
    band_mesh = mesh_pos.shape[1]
    band_grid = x_grid.shape[0]
    mesh_rows = band_mesh // quarters
    grid_rows = band_grid // quarters

    def own(full, axis=0):
        count = full.shape[axis] // quarters
        return lax.dynamic_slice_in_dim(full, feat_index * count, count, axis)

    bias = lax.all_gather(hidden_bias, "feat", axis=1, tiled=True)
    embed_w = lax.all_gather(embed_in, "feat", axis=0, tiled=False)
    out_w = {}
    in_w = {}
    out_w[embed_id] = lax.all_gather(pair_out[embed_id], "feat", axis=0, tiled=True)
    for s in range(embed_id):
        in_w[s] = lax.all_gather(pair_in[s], "feat", axis=0, tiled=False)
        out_w[s] = lax.all_gather(pair_out[s], "feat", axis=0, tiled=True)

    def sender_ids(take, senders, source_rows):
        cap = take.shape[2]
        table = lax.all_to_all(take[0], "band", split_axis=0, concat_axis=0, tiled=True)
        rows = table + (jnp.arange(bands, dtype=jnp.int32) * source_rows)[:, None]
        return jnp.take(rows.reshape(-1), own(senders), axis=0)

    g2m_ids = sender_ids(g2m_take, g2m_from, band_grid)
    m2m_ids = sender_ids(m2m_take, m2m_from, band_mesh)
    m2g_ids = sender_ids(m2g_take, m2g_from, band_mesh)

    def first(rows, weights):
        return jnp.concatenate(
            [jnp.dot(rows, weights[f], preferred_element_type=jnp.float32) for f in range(quarters)],
            axis=1,
        )

    def finish(preact, section_id):
        hidden = jax.nn.silu(preact + bias[section_id]).astype(jnp.bfloat16)
        summed = jnp.dot(hidden, out_w[section_id], preferred_element_type=jnp.float32)
        return layer_norm(summed, norm_gain[section_id], norm_shift[section_id])

    def everyone(rows):
        return lax.all_gather(rows, ("band", "feat"), axis=0, tiled=True)

    def edges(section_id, table, ids, receiver_latent, spread_receiver):
        send_part = first(jnp.take(table, ids, axis=0), in_w[section_id][:, :latent])
        recv_part = spread_receiver(first(receiver_latent, in_w[section_id][:, latent:]))
        return finish(send_part + recv_part, section_id).astype(jnp.bfloat16)

    def node_update(section_id, own_latent, aggregate):
        preact = first(own_latent, in_w[section_id][:, :latent]) + first(
            aggregate, in_w[section_id][:, latent:]
        )
        return (own_latent.astype(jnp.float32) + finish(preact, section_id)).astype(jnp.bfloat16)

    def mesh_section(section_id, table, ids, receivers_all, own_latent):
        receivers = own(receivers_all) - feat_index * mesh_rows
        messages = edges(
            section_id, table, ids, own_latent, lambda part: jnp.take(part, receivers, axis=0)
        )
        onehot = (
            receivers[None, :] == jnp.arange(mesh_rows, dtype=jnp.int32)[:, None]
        ).astype(jnp.bfloat16)
        aggregate = jnp.dot(onehot, messages, preferred_element_type=jnp.float32)
        return node_update(section_id + 1, own_latent, aggregate.astype(jnp.bfloat16))

    own_grid = finish(first(own(x_grid), embed_w), embed_id).astype(jnp.bfloat16)
    own_pos = own(mesh_pos, 1)
    mesh = own_pos[0][:, None] * pos_weight[0][None, :] + own_pos[1][:, None] * pos_weight[1][None, :]
    mesh = (mesh + own_pos[2][:, None] * pos_weight[2][None, :]).astype(jnp.bfloat16)
    mesh = mesh_section(0, everyone(own_grid), g2m_ids, g2m_to, mesh)
    for layer_id in range(LAYERS):
        mesh = mesh_section(2 + 2 * layer_id, everyone(mesh), m2m_ids, m2m_to, mesh)
    section_id = 2 * LAYERS + 2
    messages = edges(
        section_id, everyone(mesh), m2g_ids, own_grid, lambda part: jnp.repeat(part, 3, axis=0)
    )
    grid_sum = messages.astype(jnp.float32).reshape(-1, 3, latent).sum(axis=1).astype(jnp.bfloat16)
    final_latent = node_update(section_id + 1, own_grid, grid_sum)
    return jnp.dot(final_latent, head, preferred_element_type=jnp.float32)


def solution(mesh):
    return jax.shard_map(
        local,
        mesh=mesh,
        in_specs=(
            P(("parts", "band"), None),
            P(None, "band"),
            P(),
            P(None, "feat"),
            P(None, None, "feat"),
            P(None, "feat", None),
            P(None, "feat"),
            P(),
            P(),
            P(),
            P("band", None, None),
            P("band"),
            P("band"),
            P("band", None, None),
            P("band"),
            P("band"),
            P("band", None, None),
            P("band"),
        ),
        out_specs=P(("parts", "band", "feat"), None),
        check_vma=False,
    )
```

time: 470 us -> 355 us (0.76)
  waiting for transfers between devices: 246 us -> 117 us
  blocking collectives: 54.2 us -> 89.2 us
  matrix products: 43.7 us -> 73.5 us
  other arithmetic: 32.4 us -> 9.25 us
  local copies, waits for them, and re-layouts: 59.5 us -> 38.1 us
  starting transfers between devices: 18.8 us -> 12 us
    reduce_scatter x9 -> x0, waiting for transfers between devices: 214 us -> none  [finish(): lax.psum_scatter(partial_value.astype(jnp.bfloat16), 'feat', scatter_dime...]
    all_gather x0 -> x12, waiting for transfers between devices: none -> 112 us  [the longest x4 112 us: everyone(): return lax.all_gather(rows, ('band', 'feat'), axis=0, tiled=True)]
    dot_general x15 -> x71, matrix products: 18.8 us -> 67.5 us  [the longest x68 66.2 us: first(): jnp.dot(rows, weights[f], preferred_element_type=jnp.float32)]
    all_gather x8 -> x11, blocking collectives: 54.2 us -> 89.2 us  [the longest x8 68.2 us: local(): out_w[s] = lax.all_gather(pair_out[s], 'feat', axis=0, tiled=True)]
    all_to_all x4 -> x3, waiting for transfers between devices: 32.4 us -> 0.01 us  [sender_ids(): lax.all_to_all(take[0], 'band', split_axis=0, concat_axis=0, tiled=True)]
    gather x12 -> x13, local copies, waits for them, and re-layouts: 57.6 us -> 27.6 us  [the longest x4 14.7 us: edges(): jnp.take(table, ids, axis=0)]
    dot_general x9, matrix products: 23 us -> 5.03 us  [finish(): jnp.dot(hidden, out_w[section_id], preferred_element_type=jnp.float32)]
    reduce_sum x9 -> x0, other arithmetic: 9.62 us -> none  [layer_norm(): average = jnp.mean(values, axis=-1, keepdims=True)]
  transfers between devices with their start and end apart: 13 -> 15, of which waited for: 13 -> 4; matrix products, arithmetic and copies ran while one was open for 6% -> 29% of each run, Pallas kernels for 0% -> 0%
where the time goes in v1:
time: 355 us; the launch traced here: 354 us
  waiting for transfers between devices  117 us (33%)
  blocking collectives  89.2 us (25%)
  matrix products  73.5 us (21%)
  local copies, waits for them, and re-layouts  38.1 us (11%)
  between operations  15.3 us (4%)
  starting transfers between devices  12 us (3%)
  other arithmetic  9.25 us (3%)
    all_gather x4, waiting for transfers between devices, everyone(): return lax.all_gather(rows, ('band', 'feat'), axis=0, tiled=True)  112 us
    all_gather x8, blocking collectives, local(): out_w[s] = lax.all_gather(pair_out[s], 'feat', axis=0, tiled=True)  68.2 us
    dot_general x68, matrix products, first(): jnp.dot(rows, weights[f], preferred_element_type=jnp.float32)  66.2 us
    gather x4, local copies, waits for them, and re-layouts, edges(): jnp.take(table, ids, axis=0)  14.7 us
    all_to_all x3, starting transfers between devices, sender_ids(): lax.all_to_all(take[0], 'band', split_axis=0, concat_axis=0, tiled=True)  11.6 us
    all_gather x1, blocking collectives, local(): embed_w = lax.all_gather(embed_in, 'feat', axis=0, tiled=False)  8.44 us
    all_gather x1, blocking collectives, local(): lax.all_gather(pair_out[embed_id], 'feat', axis=0, tiled=True)  7.25 us
  transfers between devices with their start and end apart: 15, of which 4 were waited for; matrix products, arithmetic and copies ran while one was open for 29% of the time, Pallas kernels for 0%

profile of v1, /device:TPU:0, one launch (start us, length us, event | category | flops | bytes accessed | tf_op | source)
XLA Modules:
  0.0 353.9 jit_solution(12531827846279519351)
XLA Ops:
  6.5 3.0 fusion.159
  10.4 8.4 %all-gather.10 = bf16[4,474,128]{2,1,0:T(8,128)(2,1)S(1)} all-gather(bf16[1,474,128]{2,1,0:T(8,128)(2,1)S(1)} %bitcast.335), channel_id=2, replica_groups=mesh['parts'=2,'band'=4,'feat'=4] {'feat'}, dimensions={0}, use_global_device_ids=true | all-gather | bytes 606720 | tf_op jit(solution)/shard_map/all_gather | solution.py:53
  20.0 5.3 %all_gather.74 = f32[9,512]{1,0:T(8,128)S(1)} all-gather(f32[9,128]{1,0:T(8,128)S(1)} %copy-done.26), channel_id=1, replica_groups=mesh['parts'=2,'band'=4,'feat'=4] {'feat'}, dimensions={1}, use_global_device_ids=true | all-gather | bytes 23040 | tf_op jit(solution)/shard_map/all_gather | solution.py:52
  25.9 7.2 %all-gather.1 = bf16[1,512,512]{2,1,0:T(8,128)(2,1)S(1)} all-gather(bf16[1,128,512]{2,1,0:T(8,128)(2,1)S(1)} %get-tuple-element.31), channel_id=3, replica_groups=mesh['parts'=2,'band'=4,'feat'=4] {'feat'}, dimensions={1}, use_global_device_ids=true | all-gather | bytes 655360 | tf_op jit(solution)/shard_map/all_gather | solution.py:56
  37.0 4.9 %all-to-all-start.1 = ((s32[4,1,256]{2,1,0:T(1,128)}), s32[4,1,256]{2,1,0:T(1,128)S(1)}, u32[]{:S(2)}, u32[]{:S(2)}) async-start(s32[4,1,256]{2,1,0:T(1,128)} %all_to_all.27), calls=%async_computation.1 | async-start | bytes 8192 | tf_op jit(solution)/shard_map/all_to_all | solution.py:63
  44.2 7.0 %all-gather.2 = bf16[1,512,512]{2,1,0:T(8,128)(2,1)S(1)} all-gather(bf16[1,128,512]{2,1,0:T(8,128)(2,1)S(1)} %get-tuple-element.30), channel_id=4, replica_groups=mesh['parts'=2,'band'=4,'feat'=4] {'feat'}, dimensions={1}, use_global_device_ids=true | all-gather | bytes 655360 | tf_op jit(solution)/shard_map/all_gather | solution.py:59
  51.2 7.3 %all-gather.3 = bf16[1,512,512]{2,1,0:T(8,128)(2,1)S(1)} all-gather(bf16[1,128,512]{2,1,0:T(8,128)(2,1)S(1)} %get-tuple-element.29), channel_id=5, replica_groups=mesh['parts'=2,'band'=4,'feat'=4] {'feat'}, dimensions={1}, use_global_device_ids=true | all-gather | bytes 655360 | tf_op jit(solution)/shard_map/all_gather | solution.py:59
  73.6 17.6 %all-gather.28.cloned.1.call-done = bf16[2048,512]{1,0:T(8,128)(2,1)} async-done(((bf16[128,512]{1,0:T(8,128)(2,1)}), bf16[2048,512]{1,0:T(8,128)(2,1)}) %all-gather.28.cloned.1.call-update) | async-done | bytes 2097168 | tf_op jit(solution)/shard_map/all_gather | solution.py:83
  91.2 3.1 gather_fusion.2
  104.3 3.4 all-to-all-start.2
  110.0 7.5 %all-gather.4 = bf16[1,512,512]{2,1,0:T(8,128)(2,1)} all-gather(bf16[1,128,512]{2,1,0:T(8,128)(2,1)S(1)} %get-tuple-element.28), channel_id=6, replica_groups=mesh['parts'=2,'band'=4,'feat'=4] {'feat'}, dimensions={1}, use_global_device_ids=true | all-gather | bytes 655360 | tf_op jit(solution)/shard_map/all_gather | solution.py:59
  117.5 11.1 %all-gather.5 = bf16[1,512,512]{2,1,0:T(8,128)(2,1)} all-gather(bf16[1,128,512]{2,1,0:T(8,128)(2,1)S(1)} %get-tuple-element.27), channel_id=7, replica_groups=mesh['parts'=2,'band'=4,'feat'=4] {'feat'}, dimensions={1}, use_global_device_ids=true | all-gather | bytes 655360 | tf_op jit(solution)/shard_map/all_gather | solution.py:59
  128.7 3.1 gather_fusion.4
  146.2 26.5 %all-gather.34.cloned.1.call-done = bf16[2048,512]{1,0:T(8,128)(2,1)} async-done(((bf16[128,512]{1,0:T(8,128)(2,1)}), bf16[2048,512]{1,0:T(8,128)(2,1)}) %all-gather.34.cloned.1.call-update) | async-done | bytes 2097168 | tf_op jit(solution)/shard_map/all_gather | solution.py:83
  172.6 3.8 %gather_fusion.6 = bf16[512,512]{1,0:T(8,128)(2,1)S(1)} fusion(bf16[2048,512]{1,0:T(8,128)(2,1)} %all-gather.34.cloned.1.call-done, s32[1024]{0:T(1024)S(1)} %pad_clamp_fusion.2), kind=kCustom, calls=%fused_computation.clone | custom fusion | bytes 1050624 | tf_op jit(solution)/shard_map/jit(_take)/gather | solution.py:86
  187.9 7.7 %all-gather.6 = bf16[1,512,512]{2,1,0:T(8,128)(2,1)} all-gather(bf16[1,128,512]{2,1,0:T(8,128)(2,1)S(1)} %get-tuple-element.25), channel_id=8, replica_groups=mesh['parts'=2,'band'=4,'feat'=4] {'feat'}, dimensions={1}, use_global_device_ids=true | all-gather | bytes 655360 | tf_op jit(solution)/shard_map/all_gather | solution.py:59
  195.5 9.7 %all-gather.7 = bf16[1,512,512]{2,1,0:T(8,128)(2,1)} all-gather(bf16[1,128,512]{2,1,0:T(8,128)(2,1)S(1)} %get-tuple-element.26), channel_id=9, replica_groups=mesh['parts'=2,'band'=4,'feat'=4] {'feat'}, dimensions={1}, use_global_device_ids=true | all-gather | bytes 655360 | tf_op jit(solution)/shard_map/all_gather | solution.py:59
  216.6 35.1 %all-gather.40.cloned.1.call-done = bf16[2048,512]{1,0:T(8,128)(2,1)} async-done(((bf16[128,512]{1,0:T(8,128)(2,1)}), bf16[2048,512]{1,0:T(8,128)(2,1)}) %all-gather.40.cloned.1.call-update) | async-done | bytes 2097168 | tf_op jit(solution)/shard_map/all_gather | solution.py:83
  251.7 3.8 %gather_fusion.8 = bf16[512,512]{1,0:T(8,128)(2,1)S(1)} fusion(bf16[2048,512]{1,0:T(8,128)(2,1)} %all-gather.40.cloned.1.call-done, s32[1024]{0:T(1024)S(1)} %pad_clamp_fusion.2), kind=kCustom, calls=%fused_computation.2.clone | custom fusion | bytes 1050624 | tf_op jit(solution)/shard_map/jit(_take)/gather | solution.py:86
  266.0 3.4 all-to-all-start
  269.4 7.1 %all-gather.8 = bf16[1,512,512]{2,1,0:T(8,128)(2,1)S(1)} all-gather(bf16[1,128,512]{2,1,0:T(8,128)(2,1)S(1)} %get-tuple-element.33), channel_id=10, replica_groups=mesh['parts'=2,'band'=4,'feat'=4] {'feat'}, dimensions={1}, use_global_device_ids=true | all-gather | bytes 655360 | tf_op jit(solution)/shard_map/all_gather | solution.py:59
  276.6 10.8 %all-gather.9 = bf16[1,512,512]{2,1,0:T(8,128)(2,1)} all-gather(bf16[1,128,512]{2,1,0:T(8,128)(2,1)S(1)} %get-tuple-element.32), channel_id=11, replica_groups=mesh['parts'=2,'band'=4,'feat'=4] {'feat'}, dimensions={1}, use_global_device_ids=true | all-gather | bytes 655360 | tf_op jit(solution)/shard_map/all_gather | solution.py:59
  300.4 32.8 %all-gather.44.cloned.1.call-done = bf16[2048,512]{1,0:T(8,128)(2,1)} async-done(((bf16[128,512]{1,0:T(8,128)(2,1)}), bf16[2048,512]{1,0:T(8,128)(2,1)}) %all-gather.44.cloned.1.call-update) | async-done | bytes 2097168 | tf_op jit(solution)/shard_map/all_gather | solution.py:83
  333.2 3.9 %gather_fusion.5 = bf16[384,512]{1,0:T(8,128)(2,1)S(1)} fusion(bf16[2048,512]{1,0:T(8,128)(2,1)} %all-gather.44.cloned.1.call-done, s32[1024]{0:T(1024)S(1)} %pad_clamp_fusion), kind=kCustom, calls=%fused_computation.9 | custom fusion | bytes 787968 | tf_op jit(solution)/shard_map/jit(_take)/gather | solution.py:86
  (341 shorter events, 105.0 us)
Async XLA Ops:
  6.5 53.5 %all-gather.30.cloned.1.call-start = ((), (), s32[]{:S(2)}) async-start(), calls=%async_computation.6 | async-start | bytes 1310720 | tf_op jit(solution)/shard_map/all_gather | solution.py:58
  9.5 57.4 %all-gather.26.cloned.1.call-start = ((), (), s32[]{:S(2)}) async-start(), calls=%async_computation.4 | async-start | bytes 1310720 | tf_op jit(solution)/shard_map/all_gather | solution.py:58
  10.3 81.0 %all-gather.28.cloned.1.call-start = ((), (), s32[]{:S(2)}) async-start(), calls=%async_computation.5 | async-start | bytes 2228224 | tf_op jit(solution)/shard_map/all_gather | solution.py:83
  35.8 96.6 %all-gather.36.cloned.1.call-start = ((), (), s32[]{:S(2)}) async-start(), calls=%async_computation.9 | async-start | bytes 1310720 | tf_op jit(solution)/shard_map/all_gather | solution.py:58
  37.0 21.5 %all-to-all-start.1 = ((s32[4,1,256]{2,1,0:T(1,128)}), s32[4,1,256]{2,1,0:T(1,128)S(1)}, u32[]{:S(2)}, u32[]{:S(2)}) async-start(s32[4,1,256]{2,1,0:T(1,128)} %all_to_all.27), calls=%async_computation.1 | async-start | bytes 8192 | tf_op jit(solution)/shard_map/all_to_all | solution.py:63
  41.9 97.3 %all-gather.32.cloned.1.call-start = ((), (), s32[]{:S(2)}) async-start(), calls=%async_computation.7 | async-start | bytes 1310720 | tf_op jit(solution)/shard_map/all_gather | solution.py:58
  42.5 130.2 %all-gather.34.cloned.1.call-start = ((), (), s32[]{:S(2)}) async-start(), calls=%async_computation.8 | async-start | bytes 2228224 | tf_op jit(solution)/shard_map/all_gather | solution.py:83
  42.5 66.0 %copy-start.41 = (s32[4]{0:T(128)}, s32[4]{0:T(128)S(1)}, u32[]{:S(2)}) copy-start(s32[4]{0:T(128)S(1)} %iota_multiply_fusion) | copy-start | bytes 52
  43.2 58.8 %copy-start.34 = (f32[128]{0:T(128)}, f32[128]{0:T(128)S(1)}, u32[]{:S(2)}) copy-start(f32[128]{0:T(128)S(1)} %get-tuple-element.64) | copy-start | bytes 1540
  43.2 58.8 %copy-start.36 = (f32[128]{0:T(128)}, f32[128]{0:T(128)S(1)}, u32[]{:S(2)}) copy-start(f32[128]{0:T(128)S(1)} %get-tuple-element.65) | copy-start | bytes 1540
  43.2 58.8 %copy-start.38 = (f32[128]{0:T(128)}, f32[128]{0:T(128)S(1)}, u32[]{:S(2)}) copy-start(f32[128]{0:T(128)S(1)} %get-tuple-element.66) | copy-start | bytes 1540
  102.1 29.8 %copy-start.44 = (f32[128]{0:T(128)}, f32[128]{0:T(128)S(1)}, u32[]{:S(2)}) copy-start(f32[128]{0:T(128)S(1)} %add_rsqrt_fusion.7) | copy-start | bytes 1540
  102.9 29.5 %copy-start.3 = (bf16[128,512]{1,0:T(8,128)(2,1)S(1)}, bf16[128,512]{1,0:T(8,128)(2,1)}, u32[]{:S(2)}) copy-start(bf16[128,512]{1,0:T(8,128)(2,1)} %add_convert_fusion.10) | copy-start | bytes 393220
  102.9 102.3 %all-gather.42.cloned.1.call-start = ((), (), s32[]{:S(2)}) async-start(), calls=%async_computation.12 | async-start | bytes 1310720 | tf_op jit(solution)/shard_map/all_gather | solution.py:58
  104.3 24.3 %all-to-all-start.2 = ((s32[4,1,512]{2,1,0:T(1,128)}), s32[4,1,512]{2,1,0:T(1,128)S(1)}, u32[]{:S(2)}, u32[]{:S(2)}) async-start(s32[4,1,512]{2,1,0:T(1,128)} %all_to_all.30), calls=%async_computation.2 | async-start | bytes 16384 | tf_op jit(solution)/shard_map/all_to_all | solution.py:63
  107.7 104.3 %all-gather.38.cloned.1.call-start = ((), (), s32[]{:S(2)}) async-start(), calls=%async_computation.10 | async-start | bytes 1310720 | tf_op jit(solution)/shard_map/all_gather | solution.py:58
  108.4 143.3 %all-gather.40.cloned.1.call-start = ((), (), s32[]{:S(2)}) async-start(), calls=%async_computation.11 | async-start | bytes 2228224 | tf_op jit(solution)/shard_map/all_gather | solution.py:83
  146.2 30.3 %copy-start.59 = (pred[512]{0:T(512)(128)(4,1)S(1)}, pred[512]{0:T(512)(128)(4,1)}, u32[]{:S(2)}) copy-start(pred[512]{0:T(512)(128)(4,1)} %get-tuple-element.11) | copy-start | bytes 1540
  186.5 103.7 %all-gather.46.cloned.1.call-start = ((), (), s32[]{:S(2)}) async-start(), calls=%async_computation.14 | async-start | bytes 1310720 | tf_op jit(solution)/shard_map/all_gather | solution.py:58
  187.1 108.7 %all-gather.24.cloned.1.call-start = ((), (), s32[]{:S(2)}) async-start(), calls=%async_computation.3 | async-start | bytes 1310720 | tf_op jit(solution)/shard_map/all_gather | solution.py:58
  187.8 145.3 %all-gather.44.cloned.1.call-start = ((), (), s32[]{:S(2)}) async-start(), calls=%async_computation.13 | async-start | bytes 2228224 | tf_op jit(solution)/shard_map/all_gather | solution.py:83
  216.6 38.9 %copy-start.60 = (pred[512]{0:T(512)(128)(4,1)S(1)}, pred[512]{0:T(512)(128)(4,1)}, u32[]{:S(2)}) copy-start(pred[512]{0:T(512)(128)(4,1)} %get-tuple-element.11) | copy-start | bytes 1540
  264.6 25.6 %copy-start.1 = (bf16[128,512]{1,0:T(8,128)(2,1)S(1)}, bf16[128,512]{1,0:T(8,128)(2,1)}, u32[]{:S(2)}) copy-start(bf16[128,512]{1,0:T(8,128)(2,1)} %add_convert_fusion.12) | copy-start | bytes 393220
  266.0 21.5 %all-to-all-start = ((s32[4,1,384]{2,1,0:T(1,128)}), s32[4,1,384]{2,1,0:T(1,128)S(1)}, u32[]{:S(2)}, u32[]{:S(2)}) async-start(s32[4,1,384]{2,1,0:T(1,128)} %all_to_all.24), calls=%async_computation | async-start | bytes 12288 | tf_op jit(solution)/shard_map/all_to_all | solution.py:63
  (57 other events, 304.9 us)
Sparse Core Ops, SparseCore 0:
  9.6 19.6 all-gather.29
  30.9 16.7 all-gather.25
  49.8 41.3 all-gather.27
  92.7 15.4 all-gather.35
  109.6 19.6 all-gather.31
  131.3 41.3 all-gather.33
  174.2 15.5 all-gather.41
  191.3 17.8 all-gather.37
  211.4 40.2 all-gather.39
  253.1 15.4 all-gather.45
  270.2 19.5 all-gather.23
  291.9 41.2 all-gather.43

commit v2 on v1

--- a/solution.py
+++ b/solution.py
@@ -49,24 +49,50 @@
         count = full.shape[axis] // quarters
         return lax.dynamic_slice_in_dim(full, feat_index * count, count, axis)
 
-    bias = lax.all_gather(hidden_bias, "feat", axis=1, tiled=True)
-    embed_w = lax.all_gather(embed_in, "feat", axis=0, tiled=False)
-    out_w = {}
+    bits = [1 << b for b in reversed(range(quarters.bit_length() - 1))]
+
+    def swap(value, bit):
+        return lax.ppermute(value, "feat", [(f, f ^ bit) for f in range(quarters)])
+
+    def pieces(value):
+        parts = [value]
+        for bit in bits:
+            parts = parts + [swap(part, bit) for part in parts]
+        return parts
+
+    order = [0]
+    for bit in bits:
+        order = order + [other ^ bit for other in order]
+    slot_of = jnp.array([order.index(f) for f in range(quarters)], jnp.int32)
+
+    bias = jnp.concatenate(pieces(hidden_bias), axis=1)
+    embed_w = pieces(embed_in)
+    out_w = {embed_id: jnp.concatenate(pieces(pair_out[embed_id]), axis=0)}
     in_w = {}
-    out_w[embed_id] = lax.all_gather(pair_out[embed_id], "feat", axis=0, tiled=True)
-    for s in range(embed_id):
-        in_w[s] = lax.all_gather(pair_in[s], "feat", axis=0, tiled=False)
-        out_w[s] = lax.all_gather(pair_out[s], "feat", axis=0, tiled=True)
+    for s in range(0, embed_id, 2):
+        in_parts = pieces(pair_in[s : s + 2])
+        out_parts = pieces(pair_out[s : s + 2])
+        for t in range(2):
+            in_w[s + t] = [part[t] for part in in_parts]
+            out_w[s + t] = jnp.concatenate([part[t] for part in out_parts], axis=0)
 
-    def sender_ids(take, senders, source_rows):
+    tables = lax.all_to_all(
+        jnp.concatenate([g2m_take[0], m2m_take[0], m2g_take[0]], axis=1),
+        "band", split_axis=0, concat_axis=0, tiled=True,
+    )
+
+    def sender_ids(begin, take, senders, source_rows):
         cap = take.shape[2]
-        table = lax.all_to_all(take[0], "band", split_axis=0, concat_axis=0, tiled=True)
-        rows = table + (jnp.arange(bands, dtype=jnp.int32) * source_rows)[:, None]
+        count = source_rows // quarters
+        rows = tables[:, begin : begin + cap]
+        slot = jnp.take(slot_of, (rows // count) ^ feat_index, axis=0)
+        source = jnp.arange(bands, dtype=jnp.int32)[:, None]
+        rows = slot * (bands * count) + source * count + rows % count
         return jnp.take(rows.reshape(-1), own(senders), axis=0)
 
-    g2m_ids = sender_ids(g2m_take, g2m_from, band_grid)
-    m2m_ids = sender_ids(m2m_take, m2m_from, band_mesh)
-    m2g_ids = sender_ids(m2g_take, m2g_from, band_mesh)
+    g2m_ids = sender_ids(0, g2m_take, g2m_from, band_grid)
+    m2m_ids = sender_ids(g2m_take.shape[2], m2m_take, m2m_from, band_mesh)
+    m2g_ids = sender_ids(g2m_take.shape[2] + m2m_take.shape[2], m2g_take, m2g_from, band_mesh)
 
     def first(rows, weights):
         return jnp.concatenate(
@@ -80,16 +106,21 @@
         return layer_norm(summed, norm_gain[section_id], norm_shift[section_id])
 
     def everyone(rows):
-        return lax.all_gather(rows, ("band", "feat"), axis=0, tiled=True)
+        parts = [rows]
+        for bit in bits[:-1]:
+            parts = parts + [swap(part, bit) for part in parts]
+        parts = [lax.all_gather(part, "band", axis=0, tiled=True) for part in parts]
+        parts = parts + [swap(part, bits[-1]) for part in parts]
+        return jnp.concatenate(parts, axis=0)
 
     def edges(section_id, table, ids, receiver_latent, spread_receiver):
-        send_part = first(jnp.take(table, ids, axis=0), in_w[section_id][:, :latent])
-        recv_part = spread_receiver(first(receiver_latent, in_w[section_id][:, latent:]))
+        send_part = first(jnp.take(table, ids, axis=0), [w[:latent] for w in in_w[section_id]])
+        recv_part = spread_receiver(first(receiver_latent, [w[latent:] for w in in_w[section_id]]))
         return finish(send_part + recv_part, section_id).astype(jnp.bfloat16)
 
     def node_update(section_id, own_latent, aggregate):
-        preact = first(own_latent, in_w[section_id][:, :latent]) + first(
-            aggregate, in_w[section_id][:, latent:]
+        preact = first(own_latent, [w[:latent] for w in in_w[section_id]]) + first(
+            aggregate, [w[latent:] for w in in_w[section_id]]
         )
         return (own_latent.astype(jnp.float32) + finish(preact, section_id)).astype(jnp.bfloat16)
 

time: 355 us -> 372 us (1.048)
  waiting for transfers between devices: 117 us -> 29.6 us
  blocking collectives: 89.2 us -> 131 us
  local copies, waits for them, and re-layouts: 38.1 us -> 71.6 us
  matrix products: 73.5 us -> 90 us
  starting transfers between devices: 12 us -> 28.1 us
  between operations: 15.3 us -> 2.6 us
  other arithmetic: 9.25 us -> 18 us
    all_gather x12 -> x0, waiting for transfers between devices: 112 us -> none  [the longest x4 112 us: everyone(): return lax.all_gather(rows, ('band', 'feat'), axis=0, tiled=True)]
    all_gather x11 -> x8, blocking collectives: 89.2 us -> 131 us  [everyone(): parts = [lax.all_gather(part, 'band', axis=0, tiled=True) for part in parts]]
    ppermute x0 -> x45, waiting for transfers between devices: none -> 29.6 us  [swap(): return lax.ppermute(value, 'feat', [(f, f ^ bit) for f in range(quarters)])]
    gather x0 -> x6, local copies, waits for them, and re-layouts: none -> 28.2 us  [sender_ids(): slot = jnp.take(slot_of, rows // count ^ feat_index, axis=0)]
    ppermute x0 -> x45, starting transfers between devices: none -> 23.2 us  [swap(): return lax.ppermute(value, 'feat', [(f, f ^ bit) for f in range(quarters)])]
    dot_general x68, matrix products: 66.2 us -> 80.7 us  [first(): jnp.dot(rows, weights[f], preferred_element_type=jnp.float32)]
    squeeze x0 -> x13, local copies, waits for them, and re-layouts: none -> 10.4 us  [local(): out_w[s + t] = jnp.concatenate([part[t] for part in out_parts], axis=0)]
    gather x4, local copies, waits for them, and re-layouts: 14.7 us -> 7.16 us  [edges(): jnp.take(table, ids, axis=0)]
  transfers between devices with their start and end apart: 15 -> 46, of which waited for: 4 -> 7; matrix products, arithmetic and copies ran while one was open for 29% -> 44% of each run, Pallas kernels for 0% -> 0%
where the time goes in v2:
time: 372 us; the launch traced here: 371 us
  blocking collectives  131 us (35%)
  matrix products  90 us (24%)
  local copies, waits for them, and re-layouts  71.6 us (19%)
  waiting for transfers between devices  29.6 us (8%)
  starting transfers between devices  28.1 us (8%)
  other arithmetic  18 us (5%)
    all_gather x8, blocking collectives, everyone(): parts = [lax.all_gather(part, 'band', axis=0, tiled=True) for part in parts]  131 us
    dot_general x68, matrix products, first(): jnp.dot(rows, weights[f], preferred_element_type=jnp.float32)  80.7 us
    ppermute x45, waiting for transfers between devices, swap(): return lax.ppermute(value, 'feat', [(f, f ^ bit) for f in range(quarters)])  29.6 us
    gather x6, local copies, waits for them, and re-layouts, sender_ids(): slot = jnp.take(slot_of, rows // count ^ feat_index, axis=0)  28.2 us
    ppermute x45, starting transfers between devices, swap(): return lax.ppermute(value, 'feat', [(f, f ^ bit) for f in range(quarters)])  23.2 us
    squeeze x13, local copies, waits for them, and re-layouts, local(): out_w[s + t] = jnp.concatenate([part[t] for part in out_parts], axis=0)  10.4 us
  transfers between devices with their start and end apart: 46, of which 7 were waited for; matrix products, arithmetic and copies ran while one was open for 44% of the time, Pallas kernels for 0%

profile of v2, /device:TPU:0, one launch (start us, length us, event | category | flops | bytes accessed | tf_op | source)
XLA Modules:
  0.0 370.5 jit_solution(17319790641574496189)
XLA Ops:
  0.0 3.0 collective-permute-start
  3.0 2.4 slice_bitcast_fusion.123
  8.3 4.9 %all-to-all-start = ((s32[4,1,1152]{2,1,0:T(1,128)}), s32[4,1,1152]{2,1,0:T(1,128)S(1)}, u32[]{:S(2)}, u32[]{:S(2)}) async-start(s32[4,1,1152]{2,1,0:T(1,128)} %all_to_all.8), calls=%async_computation | async-start | bytes 36864 | tf_op jit(solution)/shard_map/all_to_all | solution.py:79
  13.2 2.2 fusion.268
  32.3 6.6 %gather_fusion.2 = s32[1024]{0:T(1024)S(1)} fusion(s32[4]{0:T(128)S(1)} %copy-done.1, s32[1024]{0:T(1024)S(1)} %get-tuple-element.122), kind=kCustom, calls=%fused_computation.6 | custom fusion | bytes 12288 | tf_op jit(solution)/shard_map/jit(_take)/gather | solution.py:88
  41.7 12.6 %gather_fusion.6 = s32[2048]{0:T(1024)S(1)} fusion(s32[4]{0:T(128)S(1)} %copy-done.1, s32[2048]{0:T(1024)S(1)} %get-tuple-element.116), kind=kCustom, calls=%fused_computation.10 | custom fusion | bytes 24576 | tf_op jit(solution)/shard_map/jit(_take)/gather | solution.py:88
  54.4 3.1 gather_fusion.7
  58.9 9.0 %gather_fusion = s32[1536]{0:T(1024)S(1)} fusion(s32[4]{0:T(128)S(1)} %copy-done.1, s32[2048]{0:T(1024)S(1)} %get-tuple-element.115), kind=kCustom, calls=%fused_computation.4 | custom fusion | bytes 18432 | tf_op jit(solution)/shard_map/jit(_take)/gather | solution.py:88
  68.0 2.5 gather_fusion.1
  79.4 15.4 %collective-permute-done.27 = bf16[2,128,512]{2,1,0:T(8,128)(2,1)S(1)} collective-permute-done((bf16[2,128,512]{2,1,0:T(8,128)(2,1)}, bf16[2,128,512]{2,1,0:T(8,128)(2,1)S(1)}, u32[]{:S(2)}, u32[]{:S(2)}) %collective-permute-start.27) | collective-permute-done | bytes 262176 | tf_op jit(solution)/shard_map/ppermute | solution.py:55
  100.6 4.1 %collective-permute-done.36 = bf16[2,128,512]{2,1,0:T(8,128)(2,1)S(1)} collective-permute-done((bf16[2,128,512]{2,1,0:T(8,128)(2,1)S(1)}, bf16[2,128,512]{2,1,0:T(8,128)(2,1)S(1)}, u32[]{:S(2)}, u32[]{:S(2)}) %collective-permute-start.36) | collective-permute-done | bytes 262176 | tf_op jit(solution)/shard_map/ppermute | solution.py:55
  114.1 16.5 %all_gather.24 = bf16[512,512]{1,0:T(8,128)(2,1)S(1)} all-gather(bf16[128,512]{1,0:T(8,128)(2,1)S(1)} %add_convert_fusion.12), channel_id=1, replica_groups=mesh['parts'=2,'band'=4,'feat'=4] {'band'}, dimensions={0}, use_global_device_ids=true | all-gather | bytes 655360 | tf_op jit(solution)/shard_map/all_gather | solution.py:112
  131.1 16.0 %all_gather.25 = bf16[512,512]{1,0:T(8,128)(2,1)S(1)} all-gather(bf16[128,512]{1,0:T(8,128)(2,1)S(1)} %collective-permute-done.15), channel_id=1, replica_groups=mesh['parts'=2,'band'=4,'feat'=4] {'band'}, dimensions={0}, use_global_device_ids=true | all-gather | bytes 655360 | tf_op jit(solution)/shard_map/all_gather | solution.py:112
  166.3 1.9 fusion.139
  170.2 4.8 %collective-permute-done.30 = bf16[2,1024,128]{2,1,0:T(8,128)(2,1)} collective-permute-done((bf16[2,1024,128]{2,1,0:T(8,128)(2,1)}, bf16[2,1024,128]{2,1,0:T(8,128)(2,1)}, u32[]{:S(2)}, u32[]{:S(2)}) %collective-permute-start.30) | collective-permute-done | bytes 524320 | tf_op jit(solution)/shard_map/ppermute | solution.py:55
  192.7 15.3 %all_gather.26 = bf16[512,512]{1,0:T(8,128)(2,1)S(1)} all-gather(bf16[128,512]{1,0:T(8,128)(2,1)S(1)} %add_convert_fusion.10), channel_id=1, replica_groups=mesh['parts'=2,'band'=4,'feat'=4] {'band'}, dimensions={0}, use_global_device_ids=true | all-gather | bytes 655360 | tf_op jit(solution)/shard_map/all_gather | solution.py:112
  213.0 15.9 %all_gather.27 = bf16[512,512]{1,0:T(8,128)(2,1)S(1)} all-gather(bf16[128,512]{1,0:T(8,128)(2,1)S(1)} %collective-permute-done.24), channel_id=1, replica_groups=mesh['parts'=2,'band'=4,'feat'=4] {'band'}, dimensions={0}, use_global_device_ids=true | all-gather | bytes 655360 | tf_op jit(solution)/shard_map/all_gather | solution.py:112
  237.0 2.0 gather_fusion.9
  251.8 16.9 %all_gather.28 = bf16[512,512]{1,0:T(8,128)(2,1)S(1)} all-gather(bf16[128,512]{1,0:T(8,128)(2,1)S(1)} %add_convert_fusion.9), channel_id=1, replica_groups=mesh['parts'=2,'band'=4,'feat'=4] {'band'}, dimensions={0}, use_global_device_ids=true | all-gather | bytes 655360 | tf_op jit(solution)/shard_map/all_gather | solution.py:112
  274.4 16.6 %all_gather.29 = bf16[512,512]{1,0:T(8,128)(2,1)S(1)} all-gather(bf16[128,512]{1,0:T(8,128)(2,1)S(1)} %collective-permute-done.33), channel_id=1, replica_groups=mesh['parts'=2,'band'=4,'feat'=4] {'band'}, dimensions={0}, use_global_device_ids=true | all-gather | bytes 655360 | tf_op jit(solution)/shard_map/all_gather | solution.py:112
  299.2 2.0 gather_fusion.11
  315.1 16.4 %all_gather.30 = bf16[512,512]{1,0:T(8,128)(2,1)S(1)} all-gather(bf16[128,512]{1,0:T(8,128)(2,1)S(1)} %add_convert_fusion.8), channel_id=1, replica_groups=mesh['parts'=2,'band'=4,'feat'=4] {'band'}, dimensions={0}, use_global_device_ids=true | all-gather | bytes 655360 | tf_op jit(solution)/shard_map/all_gather | solution.py:112
  331.4 17.1 %all_gather.31 = bf16[512,512]{1,0:T(8,128)(2,1)} all-gather(bf16[128,512]{1,0:T(8,128)(2,1)S(1)} %collective-permute-done.39), channel_id=1, replica_groups=mesh['parts'=2,'band'=4,'feat'=4] {'band'}, dimensions={0}, use_global_device_ids=true | all-gather | bytes 655360 | tf_op jit(solution)/shard_map/all_gather | solution.py:112
  354.3 2.1 gather_fusion.8
  (525 shorter events, 158.6 us)
Async XLA Ops:
  0.0 72.0 %collective-permute-start = (bf16[474,128]{1,0:T(8,128)(2,1)}, bf16[474,128]{1,0:T(8,128)(2,1)}, u32[]{:S(2)}, u32[]{:S(2)}) collective-permute-start(bf16[474,128]{1,0:T(8,128)(2,1)} %param.26), channel_id=1, source_target_pairs={{0,2},{1,3},{2,0},{3,1},{4,6},{5,7},{6,4},{7,5},{8,10},{9,11},{10,... | collective-permute-start | bytes 364040 | tf_op jit(solution)/shard_map/ppermute | solution.py:55
  3.0 70.2 %collective-permute-start.1 = (bf16[474,128]{1,0:T(8,128)(2,1)}, bf16[474,128]{1,0:T(8,128)(2,1)}, u32[]{:S(2)}, u32[]{:S(2)}) collective-permute-start(bf16[474,128]{1,0:T(8,128)(2,1)} %param.26), channel_id=1, source_target_pairs={{0,1},{1,0},{2,3},{3,2},{4,5},{5,4},{6,7},{7,6},{8,9},{9,8},{10,11... | collective-permute-start | bytes 364040 | tf_op jit(solution)/shard_map/ppermute | solution.py:55
  5.4 73.4 %collective-permute-start.6 = (bf16[128,512]{1,0:T(8,128)(2,1)}, bf16[128,512]{1,0:T(8,128)(2,1)}, u32[]{:S(2)}, u32[]{:S(2)}) collective-permute-start(bf16[128,512]{1,0:T(8,128)(2,1)} %get-tuple-element.34), channel_id=1, source_target_pairs={{0,2},{1,3},{2,0},{3,1},{4,6},{5,7},{6,4},{7,5},{8,10},{9,11},{10,... | collective-permute-start | bytes 393224 | tf_op jit(solution)/shard_map/ppermute | solution.py:55
  5.7 89.9 %collective-permute-start.7 = (bf16[128,512]{1,0:T(8,128)(2,1)}, bf16[128,512]{1,0:T(8,128)(2,1)}, u32[]{:S(2)}, u32[]{:S(2)}) collective-permute-start(bf16[128,512]{1,0:T(8,128)(2,1)} %get-tuple-element.34), channel_id=1, source_target_pairs={{0,1},{1,0},{2,3},{3,2},{4,5},{5,4},{6,7},{7,6},{8,9},{9,8},{10,11... | collective-permute-start | bytes 393224 | tf_op jit(solution)/shard_map/ppermute | solution.py:55
  6.0 20.9 %collective-permute-start.3 = (f32[9,128]{1,0:T(8,128)S(1)}, f32[9,128]{1,0:T(8,128)S(1)}, u32[]{:S(2)}, u32[]{:S(2)}) collective-permute-start(f32[9,128]{1,0:T(8,128)S(1)} %copy-done.75), channel_id=1, source_target_pairs={{0,2},{1,3},{2,0},{3,1},{4,6},{5,7},{6,4},{7,5},{8,10},{9,11},{10,... | collective-permute-start | bytes 13832 | tf_op jit(solution)/shard_map/ppermute | solution.py:55
  8.3 23.8 %all-to-all-start = ((s32[4,1,1152]{2,1,0:T(1,128)}), s32[4,1,1152]{2,1,0:T(1,128)S(1)}, u32[]{:S(2)}, u32[]{:S(2)}) async-start(s32[4,1,1152]{2,1,0:T(1,128)} %all_to_all.8), calls=%async_computation | async-start | bytes 36864 | tf_op jit(solution)/shard_map/all_to_all | solution.py:79
  29.4 47.4 %collective-permute-start.18 = (bf16[2,128,512]{2,1,0:T(8,128)(2,1)}, bf16[2,128,512]{2,1,0:T(8,128)(2,1)S(1)}, u32[]{:S(2)}, u32[]{:S(2)}) collective-permute-start(bf16[2,128,512]{2,1,0:T(8,128)(2,1)} %get-tuple-element.38), channel_id=1, source_target_pairs={{0,2},{1,3},{2,0},{3,1},{4,6},{5,7},{6,4},{7,5},{8,10},{9,11},{10,... | collective-permute-start | bytes 786440 | tf_op jit(solution)/shard_map/ppermute | solution.py:55
  75.0 77.8 %collective-permute-start.12 = (bf16[2,1024,128]{2,1,0:T(8,128)(2,1)S(1)}, bf16[2,1024,128]{2,1,0:T(8,128)(2,1)}, u32[]{:S(2)}, u32[]{:S(2)}) collective-permute-start(bf16[2,1024,128]{2,1,0:T(8,128)(2,1)S(1)} %get-tuple-element.25), channel_id=1, source_target_pairs={{0,2},{1,3},{2,0},{3,1},{4,6},{5,7},{6,4},{7,5},{8,10},{9,11},{10,... | collective-permute-start | bytes 1572872 | tf_op jit(solution)/shard_map/ppermute | solution.py:55
  76.8 18.0 %collective-permute-start.27 = (bf16[2,128,512]{2,1,0:T(8,128)(2,1)}, bf16[2,128,512]{2,1,0:T(8,128)(2,1)S(1)}, u32[]{:S(2)}, u32[]{:S(2)}) collective-permute-start(bf16[2,128,512]{2,1,0:T(8,128)(2,1)} %get-tuple-element.37), channel_id=1, source_target_pairs={{0,2},{1,3},{2,0},{3,1},{4,6},{5,7},{6,4},{7,5},{8,10},{9,11},{10,... | collective-permute-start | bytes 786440 | tf_op jit(solution)/shard_map/ppermute | solution.py:55
  78.2 79.7 %collective-permute-start.13 = (bf16[2,1024,128]{2,1,0:T(8,128)(2,1)S(1)}, bf16[2,1024,128]{2,1,0:T(8,128)(2,1)S(1)}, u32[]{:S(2)}, u32[]{:S(2)}) collective-permute-start(bf16[2,1024,128]{2,1,0:T(8,128)(2,1)S(1)} %get-tuple-element.25), channel_id=1, source_target_pairs={{0,1},{1,0},{2,3},{3,2},{4,5},{5,4},{6,7},{7,6},{8,9},{9,8},{10,11... | collective-permute-start | bytes 1572872 | tf_op jit(solution)/shard_map/ppermute | solution.py:55
  78.9 20.2 %collective-permute-start.28 = (bf16[2,128,512]{2,1,0:T(8,128)(2,1)}, bf16[2,128,512]{2,1,0:T(8,128)(2,1)S(1)}, u32[]{:S(2)}, u32[]{:S(2)}) collective-permute-start(bf16[2,128,512]{2,1,0:T(8,128)(2,1)} %get-tuple-element.37), channel_id=1, source_target_pairs={{0,1},{1,0},{2,3},{3,2},{4,5},{5,4},{6,7},{7,6},{8,9},{9,8},{10,11... | collective-permute-start | bytes 786440 | tf_op jit(solution)/shard_map/ppermute | solution.py:55
  105.6 43.3 %collective-permute-start.9 = (bf16[2,1024,128]{2,1,0:T(8,128)(2,1)S(1)}, bf16[2,1024,128]{2,1,0:T(8,128)(2,1)}, u32[]{:S(2)}, u32[]{:S(2)}) collective-permute-start(bf16[2,1024,128]{2,1,0:T(8,128)(2,1)S(1)} %copy-done.8), channel_id=1, source_target_pairs={{0,2},{1,3},{2,0},{3,1},{4,6},{5,7},{6,4},{7,5},{8,10},{9,11},{10,... | collective-permute-start | bytes 1572872 | tf_op jit(solution)/shard_map/ppermute | solution.py:55
  110.3 36.8 %collective-permute-start.10 = (bf16[2,1024,128]{2,1,0:T(8,128)(2,1)S(1)}, bf16[2,1024,128]{2,1,0:T(8,128)(2,1)S(1)}, u32[]{:S(2)}, u32[]{:S(2)}) collective-permute-start(bf16[2,1024,128]{2,1,0:T(8,128)(2,1)S(1)} %copy-done.8), channel_id=1, source_target_pairs={{0,1},{1,0},{2,3},{3,2},{4,5},{5,4},{6,7},{7,6},{8,9},{9,8},{10,11... | collective-permute-start | bytes 1572872 | tf_op jit(solution)/shard_map/ppermute | solution.py:55
  111.1 19.5 %collective-permute-start.15 = (bf16[128,512]{1,0:T(8,128)(2,1)S(1)}, bf16[128,512]{1,0:T(8,128)(2,1)S(1)}, u32[]{:S(2)}, u32[]{:S(2)}) collective-permute-start(bf16[128,512]{1,0:T(8,128)(2,1)S(1)} %add_convert_fusion.12), channel_id=1, source_target_pairs={{0,2},{1,3},{2,0},{3,1},{4,6},{5,7},{6,4},{7,5},{8,10},{9,11},{10,... | collective-permute-start | bytes 393224 | tf_op jit(solution)/shard_map/ppermute | solution.py:55
  130.5 39.4 %collective-permute-start.21 = (bf16[2,1024,128]{2,1,0:T(8,128)(2,1)}, bf16[2,1024,128]{2,1,0:T(8,128)(2,1)}, u32[]{:S(2)}, u32[]{:S(2)}) collective-permute-start(bf16[2,1024,128]{2,1,0:T(8,128)(2,1)} %get-tuple-element.24), channel_id=1, source_target_pairs={{0,2},{1,3},{2,0},{3,1},{4,6},{5,7},{6,4},{7,5},{8,10},{9,11},{10,... | collective-permute-start | bytes 1572872 | tf_op jit(solution)/shard_map/ppermute | solution.py:55
  159.6 50.9 %collective-permute-start.22 = (bf16[2,1024,128]{2,1,0:T(8,128)(2,1)}, bf16[2,1024,128]{2,1,0:T(8,128)(2,1)}, u32[]{:S(2)}, u32[]{:S(2)}) collective-permute-start(bf16[2,1024,128]{2,1,0:T(8,128)(2,1)} %get-tuple-element.24), channel_id=1, source_target_pairs={{0,1},{1,0},{2,3},{3,2},{4,5},{5,4},{6,7},{7,6},{8,9},{9,8},{10,11... | collective-permute-start | bytes 1572872 | tf_op jit(solution)/shard_map/ppermute | solution.py:55
  162.5 110.7 %collective-permute-start.31 = (bf16[2,1024,128]{2,1,0:T(8,128)(2,1)}, bf16[2,1024,128]{2,1,0:T(8,128)(2,1)}, u32[]{:S(2)}, u32[]{:S(2)}) collective-permute-start(bf16[2,1024,128]{2,1,0:T(8,128)(2,1)} %get-tuple-element.23), channel_id=1, source_target_pairs={{0,1},{1,0},{2,3},{3,2},{4,5},{5,4},{6,7},{7,6},{8,9},{9,8},{10,11... | collective-permute-start | bytes 1572872 | tf_op jit(solution)/shard_map/ppermute | solution.py:55
  170.0 178.6 %collective-permute-start.11 = (bf16[2,1024,128]{2,1,0:T(8,128)(2,1)}, bf16[2,1024,128]{2,1,0:T(8,128)(2,1)}, u32[]{:S(2)}, u32[]{:S(2)}) collective-permute-start(bf16[2,1024,128]{2,1,0:T(8,128)(2,1)} %collective-permute-done.9), channel_id=1, source_target_pairs={{0,1},{1,0},{2,3},{3,2},{4,5},{5,4},{6,7},{7,6},{8,9},{9,8},{10,11... | collective-permute-start | bytes 1572872 | tf_op jit(solution)/shard_map/ppermute | solution.py:55
  175.0 33.0 %collective-permute-start.23 = (bf16[2,1024,128]{2,1,0:T(8,128)(2,1)}, bf16[2,1024,128]{2,1,0:T(8,128)(2,1)S(1)}, u32[]{:S(2)}, u32[]{:S(2)}) collective-permute-start(bf16[2,1024,128]{2,1,0:T(8,128)(2,1)} %collective-permute-done.21), channel_id=1, source_target_pairs={{0,1},{1,0},{2,3},{3,2},{4,5},{5,4},{6,7},{7,6},{8,9},{9,8},{10,11... | collective-permute-start | bytes 1572872 | tf_op jit(solution)/shard_map/ppermute | solution.py:55
  175.0 95.9 %collective-permute-start.32 = (bf16[2,1024,128]{2,1,0:T(8,128)(2,1)}, bf16[2,1024,128]{2,1,0:T(8,128)(2,1)}, u32[]{:S(2)}, u32[]{:S(2)}) collective-permute-start(bf16[2,1024,128]{2,1,0:T(8,128)(2,1)} %collective-permute-done.30), channel_id=1, source_target_pairs={{0,1},{1,0},{2,3},{3,2},{4,5},{5,4},{6,7},{7,6},{8,9},{9,8},{10,11... | collective-permute-start | bytes 1572872 | tf_op jit(solution)/shard_map/ppermute | solution.py:55
  210.5 25.0 %collective-permute-start.25 = (bf16[512,512]{1,0:T(8,128)(2,1)S(1)}, bf16[512,512]{1,0:T(8,128)(2,1)}, u32[]{:S(2)}, u32[]{:S(2)}) collective-permute-start(bf16[512,512]{1,0:T(8,128)(2,1)S(1)} %all_gather.26), channel_id=1, source_target_pairs={{0,1},{1,0},{2,3},{3,2},{4,5},{5,4},{6,7},{7,6},{8,9},{9,8},{10,11... | collective-permute-start | bytes 1572872 | tf_op jit(solution)/shard_map/ppermute | solution.py:55
  249.9 24.5 %collective-permute-start.33 = (bf16[128,512]{1,0:T(8,128)(2,1)S(1)}, bf16[128,512]{1,0:T(8,128)(2,1)S(1)}, u32[]{:S(2)}, u32[]{:S(2)}) collective-permute-start(bf16[128,512]{1,0:T(8,128)(2,1)S(1)} %add_convert_fusion.9), channel_id=1, source_target_pairs={{0,2},{1,3},{2,0},{3,1},{4,6},{5,7},{6,4},{7,5},{8,10},{9,11},{10,... | collective-permute-start | bytes 393224 | tf_op jit(solution)/shard_map/ppermute | solution.py:55
  268.7 29.0 %collective-permute-start.34 = (bf16[512,512]{1,0:T(8,128)(2,1)S(1)}, bf16[512,512]{1,0:T(8,128)(2,1)}, u32[]{:S(2)}, u32[]{:S(2)}) collective-permute-start(bf16[512,512]{1,0:T(8,128)(2,1)S(1)} %all_gather.28), channel_id=1, source_target_pairs={{0,1},{1,0},{2,3},{3,2},{4,5},{5,4},{6,7},{7,6},{8,9},{9,8},{10,11... | collective-permute-start | bytes 1572872 | tf_op jit(solution)/shard_map/ppermute | solution.py:55
  331.4 21.4 %collective-permute-start.40 = (bf16[512,512]{1,0:T(8,128)(2,1)S(1)}, bf16[512,512]{1,0:T(8,128)(2,1)}, u32[]{:S(2)}, u32[]{:S(2)}) collective-permute-start(bf16[512,512]{1,0:T(8,128)(2,1)S(1)} %all_gather.30), channel_id=1, source_target_pairs={{0,1},{1,0},{2,3},{3,2},{4,5},{5,4},{6,7},{7,6},{8,9},{9,8},{10,11... | collective-permute-start | bytes 1572872 | tf_op jit(solution)/shard_map/ppermute | solution.py:55
  (143 other events, 1036.3 us)

commit v3 on v2

v3 whole, which is shorter than its diff:
```python
import functools

import jax
import jax.numpy as jnp
from jax import lax
from jax.experimental import pallas as pl
from jax.experimental.pallas import tpu as pltpu
from jax.sharding import PartitionSpec as P

LAYERS = 2
EPSILON = 1e-05
CHUNK = 2048
F32 = jnp.float32
BF16 = jnp.bfloat16


def layer_norm(values, gain_row, shift_row):
    average = jnp.mean(values, axis=-1, keepdims=True)
    centered = values - average
    variance = jnp.mean(centered * centered, axis=-1, keepdims=True)
    return centered * lax.rsqrt(variance + EPSILON) * gain_row + shift_row


def silu(values):
    return 0.5 * values * (1.0 + jnp.tanh(0.5 * values))


def dot(a, b):
    return jnp.dot(a, b, preferred_element_type=F32)


def kernel_call(body, out_shape, operands, spaces, scratch=(), flops=0, vmem=24 << 20):
    return pl.pallas_call(
        body,
        out_shape=out_shape,
        in_specs=[pl.BlockSpec(memory_space=space) for space in spaces],
        out_specs=jax.tree.map(lambda _: pl.BlockSpec(memory_space=pltpu.VMEM), out_shape),
        scratch_shapes=list(scratch),
        compiler_params=pltpu.CompilerParams(vmem_limit_bytes=vmem),
        cost_estimate=pl.CostEstimate(flops=flops, bytes_accessed=4 << 20, transcendentals=0),
    )(*operands)


def embed_hidden(order, index_ref, x_ref, w_ref, bias_ref, *outs):
    me = index_ref[0]
    rows = outs[0].shape[0]
    for other, out in zip(order, outs):
        begin = pl.multiple_of((me ^ other) * rows, rows)
        out[...] = silu(dot(x_ref[pl.ds(begin, rows), :], w_ref[...]) + bias_ref[...]).astype(BF16)


def embed_finish(section_id, count, *refs):
    hidden = jnp.concatenate([r[...] for r in refs[:count]], axis=1)
    weights = jnp.concatenate([r[...] for r in refs[count : 2 * count]], axis=0)
    gain, shift, out = refs[2 * count :]
    row = slice(section_id, section_id + 1)
    out[...] = layer_norm(dot(hidden, weights), gain[row, :], shift[row, :]).astype(BF16)


def unpack(pieces, t, latent):
    w_in = jnp.concatenate([w[t, : 2 * latent, :] for w in pieces], axis=1)
    width = pieces[0].shape[2]
    w_out = jnp.concatenate(
        [
            jnp.concatenate(
                [w[t, 2 * latent + b : 2 * latent + b + width, :] for b in range(0, latent, width)],
                axis=1,
            )
            for w in pieces
        ],
        axis=0,
    )
    return w_in, w_out


def phase(section_id, tables, count, mesh_like, *refs):
    table_refs = refs[:tables]
    pieces = refs[tables : tables + count]
    bias, gain, shift, ids, own_ref = refs[tables + count : tables + count + 5]
    rest = refs[tables + count + 5 :]
    if mesh_like:
        recv_col, recv_row, out, table, sem = rest
    else:
        head, out, table, sem = rest
    copies = []
    begin = 0
    for i, ref in enumerate(table_refs):
        copies.append(pltpu.make_async_copy(ref, table.at[pl.ds(begin, ref.shape[0])], sem.at[i]))
        begin += ref.shape[0]
    for copy in copies:
        copy.start()
    own = own_ref[...]
    rows, latent = own.shape
    edges = ids.shape[0]
    w_in, w_out = unpack(pieces, 0, latent)
    if mesh_like:
        spread = recv_col[...] == lax.broadcasted_iota(jnp.int32, (edges, rows), 1)
        received = dot(spread.astype(BF16), own).astype(BF16)
        preact = dot(received, w_in[latent:]) + bias[section_id : section_id + 1, :]
    else:
        preact = dot(own, w_in[latent:]) + bias[section_id : section_id + 1, :]
        preact = jnp.concatenate([preact] * (edges // rows), axis=0)
    for copy in copies:
        copy.wait()
    sent = None
    for start in range(0, begin, CHUNK):
        size = min(CHUNK, begin - start)
        hot = ids[...] == lax.broadcasted_iota(jnp.int32, (edges, size), 1) + start
        part = dot(hot.astype(BF16), table[pl.ds(start, size), :])
        sent = part if sent is None else sent + part
    preact = preact + dot(sent.astype(BF16), w_in[:latent])
    row = slice(section_id, section_id + 1)
    messages = layer_norm(dot(silu(preact).astype(BF16), w_out), gain[row, :], shift[row, :])
    messages = messages.astype(BF16)
    if mesh_like:
        collect = lax.broadcasted_iota(jnp.int32, (rows, edges), 0) == recv_row[...]
        aggregate = dot(collect.astype(BF16), messages).astype(BF16)
    else:
        total = messages[:rows].astype(F32)
        for begin in range(rows, edges, rows):
            total = total + messages[begin : begin + rows].astype(F32)
        aggregate = total.astype(BF16)
    w_in, w_out = unpack(pieces, 1, latent)
    row = slice(section_id + 1, section_id + 2)
    preact = dot(own, w_in[:latent]) + dot(aggregate, w_in[latent:]) + bias[row, :]
    update = layer_norm(dot(silu(preact).astype(BF16), w_out), gain[row, :], shift[row, :])
    updated = (own.astype(F32) + update).astype(BF16)
    if mesh_like:
        out[...] = updated
    else:
        out[...] = dot(updated, head[...])


def local(
    x_grid,
    mesh_pos,
    pos_weight,
    embed_in,
    pair_in,
    pair_out,
    hidden_bias,
    norm_gain,
    norm_shift,
    head,
    g2m_take,
    g2m_from,
    g2m_to,
    m2m_take,
    m2m_from,
    m2m_to,
    m2g_take,
    m2g_from,
):
    quarters = lax.axis_size("feat")
    bands = lax.axis_size("band")
    feat_index = lax.axis_index("feat")
    band_index = lax.axis_index("band")
    latent = norm_gain.shape[1]
    width = hidden_bias.shape[1]
    embed_id = pair_out.shape[0] - 1
    band_mesh = mesh_pos.shape[1]
    band_grid = x_grid.shape[0]
    mesh_rows = band_mesh // quarters
    grid_rows = band_grid // quarters
    direct = bands <= 4
    vmem, anywhere, scalar = pltpu.VMEM, pl.ANY, pltpu.SMEM

    bits = [1 << b for b in reversed(range(quarters.bit_length() - 1))]
    order = [0]
    for bit in bits:
        order = order + [other ^ bit for other in order]

    def own(full, axis=0):
        count = full.shape[axis] // quarters
        return lax.dynamic_slice_in_dim(full, feat_index * count, count, axis)

    def swap(value, bit):
        return lax.ppermute(value, "feat", [(f, f ^ bit) for f in range(quarters)])

    def pieces(value):
        parts = [value]
        for bit in bits:
            parts = parts + [swap(part, bit) for part in parts]
        return parts

    def everyone(rows):
        if direct:
            parts = [rows] + [
                lax.ppermute(rows, "band", [(b, (b + step) % bands) for b in range(bands)])
                for step in range(1, bands)
            ]
            for bit in bits:
                parts = parts + [swap(part, bit) for part in parts]
            return parts
        parts = [rows]
        for bit in bits[:-1]:
            parts = parts + [swap(part, bit) for part in parts]
        parts = [lax.all_gather(part, "band", axis=0, tiled=True) for part in parts]
        return parts + [swap(part, bits[-1]) for part in parts]

    tables = lax.all_to_all(
        jnp.concatenate([g2m_take[0], m2m_take[0], m2g_take[0]], axis=1),
        "band",
        split_axis=0,
        concat_axis=0,
        tiled=True,
    )

    def sender_ids(begin, take, senders, source_rows):
        cap = take.shape[2]
        count = source_rows // quarters
        rows = tables[:, begin : begin + cap]
        other = (rows // count) ^ feat_index
        slot = jnp.zeros_like(other)
        for i, bit in enumerate(bits):
            slot = slot + jnp.where(other & bit != 0, 1 << i, 0)
        source = jnp.arange(bands, dtype=jnp.int32)[:, None]
        if direct:
            source = (band_index - source) % bands
        rows = (slot * bands + source) * count + rows % count
        return rows.reshape(-1).at[senders].get(mode="promise_in_bounds")

    grid_edges = own(m2g_from).reshape(grid_rows, -1).T.reshape(-1)
    g2m_ids = sender_ids(0, g2m_take, own(g2m_from), band_grid)[:, None]
    m2m_ids = sender_ids(g2m_take.shape[2], m2m_take, own(m2m_from), band_mesh)[:, None]
    m2g_ids = sender_ids(g2m_take.shape[2] + m2m_take.shape[2], m2g_take, grid_edges, band_mesh)[:, None]
    g2m_recv = own(g2m_to) - feat_index * mesh_rows
    m2m_recv = own(m2m_to) - feat_index * mesh_rows

    hidden = kernel_call(
        functools.partial(embed_hidden, order),
        [jax.ShapeDtypeStruct((grid_rows, width), BF16)] * quarters,
        (feat_index.astype(jnp.int32)[None], x_grid, embed_in, hidden_bias[embed_id:]),
        (scalar, vmem, vmem, vmem),
    )
    hidden = [hidden[0]] + [swap(h, other) for h, other in zip(hidden[1:], order[1:])]
    out_pieces = pieces(pair_out[embed_id])
    grid = kernel_call(
        functools.partial(embed_finish, embed_id, quarters),
        jax.ShapeDtypeStruct((grid_rows, latent), BF16),
        (*hidden, *out_pieces, norm_gain, norm_shift),
        (vmem,) * (2 * quarters + 2),
    )

    bias = jnp.concatenate(pieces(hidden_bias), axis=1)

    def packed(first_id):
        turned = pair_out[first_id : first_id + 2].reshape(2, width, latent // width, width)
        turned = turned.transpose(0, 2, 1, 3).reshape(2, latent, width)
        return jnp.concatenate([pair_in[first_id : first_id + 2], turned], axis=1)

    groups = [pieces(packed(s)) for s in range(0, embed_id, 2)]

    def run(section_id, table, ids, own_latent, extra, out_shape, mesh_like):
        rows = sum(part.shape[0] for part in table)
        edges = ids.shape[0]
        return kernel_call(
            functools.partial(phase, section_id, len(table), quarters, mesh_like),
            out_shape,
            (*table, *groups[section_id // 2], bias, norm_gain, norm_shift, ids, own_latent, *extra),
            (anywhere,) * len(table) + (vmem,) * (quarters + 5 + len(extra)),
            scratch=(
                pltpu.VMEM((rows, latent), BF16),
                pltpu.SemaphoreType.DMA((len(table),)),
            ),
            flops=2 * edges * latent * (rows + 3 * latent),
            vmem=(20 << 20) + 2 * rows * latent * 2,
        )

    own_pos = own(mesh_pos, 1)
    mesh = own_pos[0][:, None] * pos_weight[0][None, :] + own_pos[1][:, None] * pos_weight[1][None, :]
    mesh = (mesh + own_pos[2][:, None] * pos_weight[2][None, :]).astype(BF16)
    shape = jax.ShapeDtypeStruct((mesh_rows, latent), BF16)
    mesh = run(0, everyone(grid), g2m_ids, mesh, (g2m_recv[:, None], g2m_recv[None, :]), shape, True)
    for layer_id in range(LAYERS):
        mesh = run(
            2 + 2 * layer_id,
            everyone(mesh),
            m2m_ids,
            mesh,
            (m2m_recv[:, None], m2m_recv[None, :]),
            shape,
            True,
        )
    return run(
        2 * LAYERS + 2,
        everyone(mesh),
        m2g_ids,
        grid,
        (head,),
        jax.ShapeDtypeStruct((grid_rows, head.shape[1]), F32),
        False,
    )


def solution(mesh):
    return jax.shard_map(
        local,
        mesh=mesh,
        in_specs=(
            P(("parts", "band"), None),
            P(None, "band"),
            P(),
            P(None, "feat"),
            P(None, None, "feat"),
            P(None, "feat", None),
            P(None, "feat"),
            P(),
            P(),
            P(),
            P("band", None, None),
            P("band"),
            P("band"),
            P("band", None, None),
            P("band"),
            P("band"),
            P("band", None, None),
            P("band"),
        ),
        out_specs=P(("parts", "band", "feat"), None),
        check_vma=False,
    )
```

time: 372 us -> 246 us (0.66)
  blocking collectives: 131 us -> 0 us
  matrix products: 90 us -> 0 us
  waiting for transfers between devices: 29.6 us -> 77.3 us
  starting transfers between devices: 28.1 us -> 62.3 us
  Pallas kernels: 0 us -> 28.1 us
  other arithmetic: 18 us -> 7.73 us
    all_gather x8 -> x0, blocking collectives: 131 us -> none  [everyone(): parts = [lax.all_gather(part, 'band', axis=0, tiled=True) for part in parts]]
    dot_general x81 -> x0, matrix products: 90 us -> none  [the longest x68 80.7 us: first(): jnp.dot(rows, weights[f], preferred_element_type=jnp.float32)]
    unnamed x250 -> x159, local copies, waits for them, and re-layouts: 0.81 us -> 46 us
    gather x19 -> x3, local copies, waits for them, and re-layouts: 49.8 us -> 8.86 us  [sender_ids(): return rows.reshape(-1).at[senders].get(mode='promise_in_bounds')]
    pallas_call x0 -> x6, Pallas kernels: none -> 28.1 us  [kernel_call(): pl.pallas_call(body, out_shape=out_shape, in_specs=[pl.BlockSpec(memory_s...]
    ppermute x45 -> x69, waiting for transfers between devices: 29.6 us -> 55.4 us  [swap(): return lax.ppermute(value, 'feat', [(f, f ^ bit) for f in range(quarters)])]
    ppermute x0 -> x12, starting transfers between devices: none -> 22 us  [everyone(): lax.ppermute(rows, 'band', [(b, (b + step) % bands) for b in range(bands)])]
    ppermute x0 -> x12, waiting for transfers between devices: none -> 21.9 us  [everyone(): lax.ppermute(rows, 'band', [(b, (b + step) % bands) for b in range(bands)])]
  transfers between devices with their start and end apart: 46 -> 82, of which waited for: 7 -> 22; matrix products, arithmetic and copies ran while one was open for 44% -> 14% of each run, Pallas kernels for 0% -> 9%
where the time goes in v3:
time: 246 us; the launch traced here: 244 us
  waiting for transfers between devices  77.3 us (31%)
  local copies, waits for them, and re-layouts  67.9 us (28%)
  starting transfers between devices  62.3 us (25%)
  Pallas kernels  28.1 us (11%)
  other arithmetic  7.73 us (3%)
    ppermute x69, waiting for transfers between devices, swap(): return lax.ppermute(value, 'feat', [(f, f ^ bit) for f in range(quarters)])  55.4 us
    unnamed x159, local copies, waits for them, and re-layouts  46 us
    ppermute x69, starting transfers between devices, swap(): return lax.ppermute(value, 'feat', [(f, f ^ bit) for f in range(quarters)])  35.4 us
    pallas_call x6, Pallas kernels, kernel_call(): pl.pallas_call(body, out_shape=out_shape, in_specs=[pl.BlockSpec(memory_s...  28.1 us
    ppermute x12, starting transfers between devices, everyone(): lax.ppermute(rows, 'band', [(b, (b + step) % bands) for b in range(bands)])  22 us
    ppermute x12, waiting for transfers between devices, everyone(): lax.ppermute(rows, 'band', [(b, (b + step) % bands) for b in range(bands)])  21.9 us
    gather x3, local copies, waits for them, and re-layouts, sender_ids(): return rows.reshape(-1).at[senders].get(mode='promise_in_bounds')  8.86 us
  transfers between devices with their start and end apart: 82, of which 22 were waited for; matrix products, arithmetic and copies ran while one was open for 14% of the time, Pallas kernels for 9%

profile of v3, /device:TPU:0, one launch (start us, length us, event | category | flops | bytes accessed | tf_op | source)
XLA Modules:
  0.0 244.0 jit_solution(10758851803236695544)
XLA Ops:
  1.0 3.0 %collective-permute-start.3 = (bf16[128,512]{1,0:T(8,128)(2,1)S(1)}, bf16[128,512]{1,0:T(8,128)(2,1)S(1)}, u32[]{:S(2)}, u32[]{:S(2)}) collective-permute-start(bf16[128,512]{1,0:T(8,128)(2,1)S(1)} %slice_bitcast_fusion.4.refs_4_), channel_id=1, source_target_pairs={{0,2},{1,3},{2,0},{3,1},{4,6},{5,7},{6,4},{7,5},{8,10},{9,11},{10,... | collective-permute-start | bytes 393224 | tf_op jit(solution)/shard_map/ppermute | solution.py:178
  10.0 4.9 %all-to-all-start = ((s32[4,1,1152]{2,1,0:T(1,128)}), s32[4,1,1152]{2,1,0:T(1,128)}, u32[]{:S(2)}, u32[]{:S(2)}) async-start(s32[4,1,1152]{2,1,0:T(1,128)} %all_to_all.8), calls=%async_computation | async-start | bytes 36864 | tf_op jit(solution)/shard_map/all_to_all | solution.py:201
  14.9 2.4 %fusion.16 = (bf16[2,1024,128]{2,1,0:T(8,128)(2,1)}, bf16[2,1024,128]{2,1,0:T(8,128)(2,1)S(1)}, bf16[2,1024,128]{2,1,0:T(8,128)(2,1)S(1)}, bf16[2,1024,128]{2,1,0:T(8,128)(2,1)S(1)}) fusion(bf16[8,1024,128]{2,1,0:T(8,128)(2,1)} %param.22), kind=kLoop, calls=%fused_computation.78 | loop fusion | bytes 4194304 | tf_op jit(solution)/shard_map/slice | solution.py:250
  25.6 2.4 collective-permute-start.7
  31.6 4.4 %collective-permute-done.7.refs_2_ = bf16[128,512]{1,0:T(8,128)(2,1)S(1)} collective-permute-done((bf16[128,512]{1,0:T(8,128)(2,1)S(1)}, bf16[128,512]{1,0:T(8,128)(2,1)S(1)}, u32[]{:S(2)}, u32[]{:S(2)}) %collective-permute-start.7) | collective-permute-done | bytes 131104 | tf_op jit(solution)/shard_map/ppermute | solution.py:189
  41.4 34.6 %collective-permute-done.11.refs_6_ = bf16[128,512]{1,0:T(8,128)(2,1)S(1)} collective-permute-done((bf16[128,512]{1,0:T(8,128)(2,1)S(1)}, bf16[128,512]{1,0:T(8,128)(2,1)S(1)}, u32[]{:S(2)}, u32[]{:S(2)}) %collective-permute-start.11) | collective-permute-done | bytes 131104 | tf_op jit(solution)/shard_map/ppermute | solution.py:178
  115.3 6.2 %shard_map.174.refs_0_.refs_24_ = bf16[128,512]{1,0:T(8,128)(2,1)} custom-call(bf16[128,512]{1,0:T(8,128)(2,1)S(1)} %shard_map.173.refs_0_.refs_24_, bf16[128,512]{1,0:T(8,128)(2,1)S(1)} %copy-done.18, bf16[128,512]{1,0:T(8,128)(2,1)S(1)} %copy-done.20, bf16[128,512]{1,0:T(8,128)(2,1)S(1)} %copy-done.22, bf16[128,512]{1,0:T(8,128)(2,1)S(1)} %copy-done.24, ...), custom_call_target="tpu_custom_call" | custom-call | flops 939524096 | bytes 4194304 | tf_op jit(solution)/shard_map/pallas_call | solution.py:33
  123.6 2.4 collective-permute-start.28
  127.6 2.5 %collective-permute-done.27.refs_1_ = bf16[128,512]{1,0:T(8,128)(2,1)S(1)} collective-permute-done((bf16[128,512]{1,0:T(8,128)(2,1)}, bf16[128,512]{1,0:T(8,128)(2,1)S(1)}, u32[]{:S(2)}, u32[]{:S(2)}) %collective-permute-start.27) | collective-permute-done | bytes 131104 | tf_op jit(solution)/shard_map/ppermute | solution.py:189
  131.6 3.9 %collective-permute-done.28.refs_2_ = bf16[128,512]{1,0:T(8,128)(2,1)S(1)} collective-permute-done((bf16[128,512]{1,0:T(8,128)(2,1)}, bf16[128,512]{1,0:T(8,128)(2,1)S(1)}, u32[]{:S(2)}, u32[]{:S(2)}) %collective-permute-start.28) | collective-permute-done | bytes 131104 | tf_op jit(solution)/shard_map/ppermute | solution.py:189
  141.9 2.7 %collective-permute-done.33.refs_7_ = bf16[128,512]{1,0:T(8,128)(2,1)S(1)} collective-permute-done((bf16[128,512]{1,0:T(8,128)(2,1)S(1)}, bf16[128,512]{1,0:T(8,128)(2,1)S(1)}, u32[]{:S(2)}, u32[]{:S(2)}) %collective-permute-start.33) | collective-permute-done | bytes 131104 | tf_op jit(solution)/shard_map/ppermute | solution.py:178
  152.7 4.3 %gather_fusion.1 = s32[512]{0:T(512)} fusion(s32[2048]{0:T(1024)S(1)} %bitcast.69, s32[1024]{0:T(1024)S(1)} %get-tuple-element.32), kind=kCustom, calls=%fused_computation.1 | custom fusion | bytes 6144 | tf_op jit(solution)/shard_map/gather | solution.py:221
  162.4 7.8 %shard_map.175.refs_0_.refs_24_ = bf16[128,512]{1,0:T(8,128)(2,1)S(1)} custom-call(bf16[128,512]{1,0:T(8,128)(2,1)} %shard_map.174.refs_0_.refs_24_, bf16[128,512]{1,0:T(8,128)(2,1)S(1)} %collective-permute-done.27.refs_1_, bf16[128,512]{1,0:T(8,128)(2,1)S(1)} %collective-permute-done.28.refs_2_, bf16[128,512]{1,0:T(8,128)(2,1)S(1)} %collective-permute-done.29.refs_3_, ...), custom_call_target="tpu_custom_call" | custom-call | flops 1879048192 | bytes 4194304 | tf_op jit(solution)/shard_map/pallas_call | solution.py:33
  170.2 3.4 %collective-permute-start.45 = (bf16[128,512]{1,0:T(8,128)(2,1)S(1)}, bf16[128,512]{1,0:T(8,128)(2,1)S(1)}, u32[]{:S(2)}, u32[]{:S(2)}) collective-permute-start(bf16[128,512]{1,0:T(8,128)(2,1)S(1)} %shard_map.175.refs_0_.refs_24_), channel_id=1, source_target_pairs={{0,4},{4,8},{8,12},{12,0},{1,5},{5,9},{9,13},{13,1},{2,6},{6,10},{... | collective-permute-start | bytes 393224 | tf_op jit(solution)/shard_map/ppermute | solution.py:189
  180.0 3.3 %collective-permute-done.46.refs_2_ = bf16[128,512]{1,0:T(8,128)(2,1)S(1)} collective-permute-done((bf16[128,512]{1,0:T(8,128)(2,1)S(1)}, bf16[128,512]{1,0:T(8,128)(2,1)S(1)}, u32[]{:S(2)}, u32[]{:S(2)}) %collective-permute-start.46) | collective-permute-done | bytes 131104 | tf_op jit(solution)/shard_map/ppermute | solution.py:189
  186.9 2.8 %collective-permute-done.49.refs_5_ = bf16[128,512]{1,0:T(8,128)(2,1)S(1)} collective-permute-done((bf16[128,512]{1,0:T(8,128)(2,1)S(1)}, bf16[128,512]{1,0:T(8,128)(2,1)S(1)}, u32[]{:S(2)}, u32[]{:S(2)}) %collective-permute-start.49) | collective-permute-done | bytes 131104 | tf_op jit(solution)/shard_map/ppermute | solution.py:178
  189.6 2.8 %collective-permute-done.50.refs_6_ = bf16[128,512]{1,0:T(8,128)(2,1)S(1)} collective-permute-done((bf16[128,512]{1,0:T(8,128)(2,1)S(1)}, bf16[128,512]{1,0:T(8,128)(2,1)S(1)}, u32[]{:S(2)}, u32[]{:S(2)}) %collective-permute-start.50) | collective-permute-done | bytes 131104 | tf_op jit(solution)/shard_map/ppermute | solution.py:178
  192.4 2.4 collective-permute-done.51.refs_7_
  199.7 8.3 %shard_map.176.refs_0_ = bf16[128,512]{1,0:T(8,128)(2,1)S(1)} custom-call(bf16[128,512]{1,0:T(8,128)(2,1)S(1)} %shard_map.175.refs_0_.refs_24_, bf16[128,512]{1,0:T(8,128)(2,1)S(1)} %collective-permute-done.45.refs_1_, bf16[128,512]{1,0:T(8,128)(2,1)S(1)} %collective-permute-done.46.refs_2_, bf16[128,512]{1,0:T(8,128)(2,1)S(1)} %collective-permute-done.47.refs_3_, ...), custom_call_target="tpu_custom_call" | custom-call | flops 1879048192 | bytes 4194304 | tf_op jit(solution)/shard_map/pallas_call | solution.py:33
  208.0 2.8 %collective-permute-start.63 = (bf16[128,512]{1,0:T(8,128)(2,1)S(1)}, bf16[128,512]{1,0:T(8,128)(2,1)S(1)}, u32[]{:S(2)}, u32[]{:S(2)}) collective-permute-start(bf16[128,512]{1,0:T(8,128)(2,1)S(1)} %shard_map.176.refs_0_), channel_id=1, source_target_pairs={{0,4},{4,8},{8,12},{12,0},{1,5},{5,9},{9,13},{13,1},{2,6},{6,10},{... | collective-permute-start | bytes 393224 | tf_op jit(solution)/shard_map/ppermute | solution.py:189
  210.8 2.7 %collective-permute-start.64 = (bf16[128,512]{1,0:T(8,128)(2,1)S(1)}, bf16[128,512]{1,0:T(8,128)(2,1)S(1)}, u32[]{:S(2)}, u32[]{:S(2)}) collective-permute-start(bf16[128,512]{1,0:T(8,128)(2,1)S(1)} %shard_map.176.refs_0_), channel_id=1, source_target_pairs={{0,8},{4,12},{8,0},{12,4},{1,9},{5,13},{9,1},{13,5},{2,10},{6,14},... | collective-permute-start | bytes 393224 | tf_op jit(solution)/shard_map/ppermute | solution.py:189
  218.8 3.8 %collective-permute-done.64.refs_2_ = bf16[128,512]{1,0:T(8,128)(2,1)S(1)} collective-permute-done((bf16[128,512]{1,0:T(8,128)(2,1)S(1)}, bf16[128,512]{1,0:T(8,128)(2,1)S(1)}, u32[]{:S(2)}, u32[]{:S(2)}) %collective-permute-start.64) | collective-permute-done | bytes 131104 | tf_op jit(solution)/shard_map/ppermute | solution.py:189
  231.6 2.5 %gather_fusion.2 = s32[384]{0:T(512)S(1)} fusion(s32[1536]{0:T(1024)S(1)} %reshape.104, s32[1024]{0:T(1024)S(1)} %get-tuple-element.31), kind=kCustom, calls=%fused_computation.2 | custom fusion | bytes 4608 | tf_op jit(solution)/shard_map/gather | solution.py:221
  238.2 5.1 %shard_map.177 = f32[128,227]{1,0:T(8,128)S(1)} custom-call(bf16[128,512]{1,0:T(8,128)(2,1)S(1)} %shard_map.176.refs_0_, bf16[128,512]{1,0:T(8,128)(2,1)S(1)} %collective-permute-done.63.refs_1_, bf16[128,512]{1,0:T(8,128)(2,1)S(1)} %copy-done.40, bf16[128,512]{1,0:T(8,128)(2,1)S(1)} %copy-done.42, bf16[128,512]{1,0:T(8,128)(2,1)} %collective-permute-done.66.refs_4_, ...), custom_call_target="tpu_custom_call" | custom-call | flops 1409286144 | bytes 4194304 | tf_op jit(solution)/shard_map/pallas_call | solution.py:33
  (345 shorter events, 121.8 us)
Async XLA Ops:
  1.0 17.8 %collective-permute-start.3 = (bf16[128,512]{1,0:T(8,128)(2,1)S(1)}, bf16[128,512]{1,0:T(8,128)(2,1)S(1)}, u32[]{:S(2)}, u32[]{:S(2)}) collective-permute-start(bf16[128,512]{1,0:T(8,128)(2,1)S(1)} %slice_bitcast_fusion.4.refs_4_), channel_id=1, source_target_pairs={{0,2},{1,3},{2,0},{3,1},{4,6},{5,7},{6,4},{7,5},{8,10},{9,11},{10,... | collective-permute-start | bytes 393224 | tf_op jit(solution)/shard_map/ppermute | solution.py:178
  4.0 17.8 %collective-permute-start.4 = (bf16[128,512]{1,0:T(8,128)(2,1)S(1)}, bf16[128,512]{1,0:T(8,128)(2,1)S(1)}, u32[]{:S(2)}, u32[]{:S(2)}) collective-permute-start(bf16[128,512]{1,0:T(8,128)(2,1)S(1)} %slice_bitcast_fusion.4.refs_4_), channel_id=1, source_target_pairs={{0,1},{1,0},{2,3},{3,2},{4,5},{5,4},{6,7},{7,6},{8,9},{9,8},{10,11... | collective-permute-start | bytes 393224 | tf_op jit(solution)/shard_map/ppermute | solution.py:178
  4.0 14.5 %collective-permute-start.24 = (f32[9,128]{1,0:T(8,128)}, f32[9,128]{1,0:T(8,128)S(1)}, u32[]{:S(2)}, u32[]{:S(2)}) collective-permute-start(f32[9,128]{1,0:T(8,128)} %param.24), channel_id=1, source_target_pairs={{0,2},{1,3},{2,0},{3,1},{4,6},{5,7},{6,4},{7,5},{8,10},{9,11},{10,... | collective-permute-start | bytes 13832 | tf_op jit(solution)/shard_map/ppermute | solution.py:178
  7.4 12.6 %collective-permute-start = (bf16[128,128]{1,0:T(8,128)(2,1)S(1)}, bf16[128,128]{1,0:T(8,128)(2,1)S(1)}, u32[]{:S(2)}, u32[]{:S(2)}) collective-permute-start(bf16[128,128]{1,0:T(8,128)(2,1)S(1)} %get-tuple-element.10), channel_id=1, source_target_pairs={{0,2},{1,3},{2,0},{3,1},{4,6},{5,7},{6,4},{7,5},{8,10},{9,11},{10,... | collective-permute-start | bytes 98312 | tf_op jit(solution)/shard_map/ppermute | solution.py:178
  10.0 84.5 %all-to-all-start = ((s32[4,1,1152]{2,1,0:T(1,128)}), s32[4,1,1152]{2,1,0:T(1,128)}, u32[]{:S(2)}, u32[]{:S(2)}) async-start(s32[4,1,1152]{2,1,0:T(1,128)} %all_to_all.8), calls=%async_computation | async-start | bytes 36864 | tf_op jit(solution)/shard_map/all_to_all | solution.py:201
  35.9 50.8 %collective-permute-start.21 = (bf16[2,1536,128]{2,1,0:T(8,128)(2,1)S(1)}, bf16[2,1536,128]{2,1,0:T(8,128)(2,1)S(1)}, u32[]{:S(2)}, u32[]{:S(2)}) collective-permute-start(bf16[2,1536,128]{2,1,0:T(8,128)(2,1)S(1)} %pad_maximum_fusion.refs_16_), channel_id=1, source_target_pairs={{0,2},{1,3},{2,0},{3,1},{4,6},{5,7},{6,4},{7,5},{8,10},{9,11},{10,... | collective-permute-start | bytes 2359304 | tf_op jit(solution)/shard_map/ppermute | solution.py:178
  36.5 54.0 %collective-permute-start.42 = (bf16[2,1536,128]{2,1,0:T(8,128)(2,1)}, bf16[2,1536,128]{2,1,0:T(8,128)(2,1)}, u32[]{:S(2)}, u32[]{:S(2)}) collective-permute-start(bf16[2,1536,128]{2,1,0:T(8,128)(2,1)} %pad_maximum_fusion.1.refs_16_), channel_id=1, source_target_pairs={{0,2},{1,3},{2,0},{3,1},{4,6},{5,7},{6,4},{7,5},{8,10},{9,11},{10,... | collective-permute-start | bytes 2359304 | tf_op jit(solution)/shard_map/ppermute | solution.py:178
  38.0 40.5 %collective-permute-start.14 = (bf16[128,512]{1,0:T(8,128)(2,1)S(1)}, bf16[128,512]{1,0:T(8,128)(2,1)S(1)}, u32[]{:S(2)}, u32[]{:S(2)}) collective-permute-start(bf16[128,512]{1,0:T(8,128)(2,1)S(1)} %collective-permute-done.6.refs_1_), channel_id=1, source_target_pairs={{0,1},{1,0},{2,3},{3,2},{4,5},{5,4},{6,7},{7,6},{8,9},{9,8},{10,11... | collective-permute-start | bytes 393224 | tf_op jit(solution)/shard_map/ppermute | solution.py:178
  39.3 36.6 %collective-permute-start.11 = (bf16[128,512]{1,0:T(8,128)(2,1)S(1)}, bf16[128,512]{1,0:T(8,128)(2,1)S(1)}, u32[]{:S(2)}, u32[]{:S(2)}) collective-permute-start(bf16[128,512]{1,0:T(8,128)(2,1)S(1)} %collective-permute-done.7.refs_2_), channel_id=1, source_target_pairs={{0,2},{1,3},{2,0},{3,1},{4,6},{5,7},{6,4},{7,5},{8,10},{9,11},{10,... | collective-permute-start | bytes 393224 | tf_op jit(solution)/shard_map/ppermute | solution.py:178
  39.9 38.0 %collective-permute-start.12 = (bf16[128,512]{1,0:T(8,128)(2,1)S(1)}, bf16[128,512]{1,0:T(8,128)(2,1)}, u32[]{:S(2)}, u32[]{:S(2)}) collective-permute-start(bf16[128,512]{1,0:T(8,128)(2,1)S(1)} %collective-permute-done.8.refs_3_), channel_id=1, source_target_pairs={{0,2},{1,3},{2,0},{3,1},{4,6},{5,7},{6,4},{7,5},{8,10},{9,11},{10,... | collective-permute-start | bytes 393224 | tf_op jit(solution)/shard_map/ppermute | solution.py:178
  86.2 13.2 %collective-permute-start.22 = (bf16[2,1536,128]{2,1,0:T(8,128)(2,1)S(1)}, bf16[2,1536,128]{2,1,0:T(8,128)(2,1)S(1)}, u32[]{:S(2)}, u32[]{:S(2)}) collective-permute-start(bf16[2,1536,128]{2,1,0:T(8,128)(2,1)S(1)} %pad_maximum_fusion.refs_16_), channel_id=1, source_target_pairs={{0,1},{1,0},{2,3},{3,2},{4,5},{5,4},{6,7},{7,6},{8,9},{9,8},{10,11... | collective-permute-start | bytes 2359304 | tf_op jit(solution)/shard_map/ppermute | solution.py:178
  86.8 12.7 %collective-permute-start.23 = (bf16[2,1536,128]{2,1,0:T(8,128)(2,1)S(1)}, bf16[2,1536,128]{2,1,0:T(8,128)(2,1)S(1)}, u32[]{:S(2)}, u32[]{:S(2)}) collective-permute-start(bf16[2,1536,128]{2,1,0:T(8,128)(2,1)S(1)} %collective-permute-done.21.refs_17_), channel_id=1, source_target_pairs={{0,1},{1,0},{2,3},{3,2},{4,5},{5,4},{6,7},{7,6},{8,9},{9,8},{10,11... | collective-permute-start | bytes 2359304 | tf_op jit(solution)/shard_map/ppermute | solution.py:178
  88.0 38.0 %collective-permute-start.43 = (bf16[2,1536,128]{2,1,0:T(8,128)(2,1)}, bf16[2,1536,128]{2,1,0:T(8,128)(2,1)}, u32[]{:S(2)}, u32[]{:S(2)}) collective-permute-start(bf16[2,1536,128]{2,1,0:T(8,128)(2,1)} %pad_maximum_fusion.1.refs_16_), channel_id=1, source_target_pairs={{0,1},{1,0},{2,3},{3,2},{4,5},{5,4},{6,7},{7,6},{8,9},{9,8},{10,11... | collective-permute-start | bytes 2359304 | tf_op jit(solution)/shard_map/ppermute | solution.py:178
  89.1 36.9 %collective-permute-start.60 = (bf16[2,1536,128]{2,1,0:T(8,128)(2,1)}, bf16[2,1536,128]{2,1,0:T(8,128)(2,1)}, u32[]{:S(2)}, u32[]{:S(2)}) collective-permute-start(bf16[2,1536,128]{2,1,0:T(8,128)(2,1)} %pad_maximum_fusion.2.refs_16_), channel_id=1, source_target_pairs={{0,2},{1,3},{2,0},{3,1},{4,6},{5,7},{6,4},{7,5},{8,10},{9,11},{10,... | collective-permute-start | bytes 2359304 | tf_op jit(solution)/shard_map/ppermute | solution.py:178
  90.5 37.1 %collective-permute-start.44 = (bf16[2,1536,128]{2,1,0:T(8,128)(2,1)}, bf16[2,1536,128]{2,1,0:T(8,128)(2,1)}, u32[]{:S(2)}, u32[]{:S(2)}) collective-permute-start(bf16[2,1536,128]{2,1,0:T(8,128)(2,1)} %collective-permute-done.42.refs_17_), channel_id=1, source_target_pairs={{0,1},{1,0},{2,3},{3,2},{4,5},{5,4},{6,7},{7,6},{8,9},{9,8},{10,11... | collective-permute-start | bytes 2359304 | tf_op jit(solution)/shard_map/ppermute | solution.py:178
  123.6 11.9 %collective-permute-start.28 = (bf16[128,512]{1,0:T(8,128)(2,1)}, bf16[128,512]{1,0:T(8,128)(2,1)S(1)}, u32[]{:S(2)}, u32[]{:S(2)}) collective-permute-start(bf16[128,512]{1,0:T(8,128)(2,1)} %shard_map.174.refs_0_.refs_24_), channel_id=1, source_target_pairs={{0,8},{4,12},{8,0},{12,4},{1,9},{5,13},{9,1},{13,5},{2,10},{6,14},... | collective-permute-start | bytes 393224 | tf_op jit(solution)/shard_map/ppermute | solution.py:189
  127.6 11.2 %collective-permute-start.34 = (bf16[128,512]{1,0:T(8,128)(2,1)}, bf16[128,512]{1,0:T(8,128)(2,1)S(1)}, u32[]{:S(2)}, u32[]{:S(2)}) collective-permute-start(bf16[128,512]{1,0:T(8,128)(2,1)} %shard_map.174.refs_0_.refs_24_), channel_id=1, source_target_pairs={{0,1},{1,0},{2,3},{3,2},{4,5},{5,4},{6,7},{7,6},{8,9},{9,8},{10,11... | collective-permute-start | bytes 393224 | tf_op jit(solution)/shard_map/ppermute | solution.py:178
  138.8 35.3 %collective-permute-start.61 = (bf16[2,1536,128]{2,1,0:T(8,128)(2,1)S(1)}, bf16[2,1536,128]{2,1,0:T(8,128)(2,1)}, u32[]{:S(2)}, u32[]{:S(2)}) collective-permute-start(bf16[2,1536,128]{2,1,0:T(8,128)(2,1)S(1)} %copy-done.1), channel_id=1, source_target_pairs={{0,1},{1,0},{2,3},{3,2},{4,5},{5,4},{6,7},{7,6},{8,9},{9,8},{10,11... | collective-permute-start | bytes 2359304 | tf_op jit(solution)/shard_map/ppermute | solution.py:178
  138.8 37.2 %collective-permute-start.78 = (bf16[2,1536,128]{2,1,0:T(8,128)(2,1)S(1)}, bf16[2,1536,128]{2,1,0:T(8,128)(2,1)S(1)}, u32[]{:S(2)}, u32[]{:S(2)}) collective-permute-start(bf16[2,1536,128]{2,1,0:T(8,128)(2,1)S(1)} %pad_maximum_fusion.3.refs_16_), channel_id=1, source_target_pairs={{0,2},{1,3},{2,0},{3,1},{4,6},{5,7},{6,4},{7,5},{8,10},{9,11},{10,... | collective-permute-start | bytes 2359304 | tf_op jit(solution)/shard_map/ppermute | solution.py:178
  141.9 34.2 %collective-permute-start.62 = (bf16[2,1536,128]{2,1,0:T(8,128)(2,1)}, bf16[2,1536,128]{2,1,0:T(8,128)(2,1)}, u32[]{:S(2)}, u32[]{:S(2)}) collective-permute-start(bf16[2,1536,128]{2,1,0:T(8,128)(2,1)} %collective-permute-done.60.refs_17_), channel_id=1, source_target_pairs={{0,1},{1,0},{2,3},{3,2},{4,5},{5,4},{6,7},{7,6},{8,9},{9,8},{10,11... | collective-permute-start | bytes 2359304 | tf_op jit(solution)/shard_map/ppermute | solution.py:178
  176.1 37.4 %collective-permute-start.79 = (bf16[2,1536,128]{2,1,0:T(8,128)(2,1)S(1)}, bf16[2,1536,128]{2,1,0:T(8,128)(2,1)S(1)}, u32[]{:S(2)}, u32[]{:S(2)}) collective-permute-start(bf16[2,1536,128]{2,1,0:T(8,128)(2,1)S(1)} %pad_maximum_fusion.3.refs_16_), channel_id=1, source_target_pairs={{0,1},{1,0},{2,3},{3,2},{4,5},{5,4},{6,7},{7,6},{8,9},{9,8},{10,11... | collective-permute-start | bytes 2359304 | tf_op jit(solution)/shard_map/ppermute | solution.py:178
  176.1 38.9 %collective-permute-start.80 = (bf16[2,1536,128]{2,1,0:T(8,128)(2,1)S(1)}, bf16[2,1536,128]{2,1,0:T(8,128)(2,1)S(1)}, u32[]{:S(2)}, u32[]{:S(2)}) collective-permute-start(bf16[2,1536,128]{2,1,0:T(8,128)(2,1)S(1)} %collective-permute-done.78.refs_17_), channel_id=1, source_target_pairs={{0,1},{1,0},{2,3},{3,2},{4,5},{5,4},{6,7},{7,6},{8,9},{9,8},{10,11... | collective-permute-start | bytes 2359304 | tf_op jit(solution)/shard_map/ppermute | solution.py:178
  210.8 11.8 %collective-permute-start.64 = (bf16[128,512]{1,0:T(8,128)(2,1)S(1)}, bf16[128,512]{1,0:T(8,128)(2,1)S(1)}, u32[]{:S(2)}, u32[]{:S(2)}) collective-permute-start(bf16[128,512]{1,0:T(8,128)(2,1)S(1)} %shard_map.176.refs_0_), channel_id=1, source_target_pairs={{0,8},{4,12},{8,0},{12,4},{1,9},{5,13},{9,1},{13,5},{2,10},{6,14},... | collective-permute-start | bytes 393224 | tf_op jit(solution)/shard_map/ppermute | solution.py:189
  213.5 11.2 %collective-permute-start.66 = (bf16[128,512]{1,0:T(8,128)(2,1)S(1)}, bf16[128,512]{1,0:T(8,128)(2,1)}, u32[]{:S(2)}, u32[]{:S(2)}) collective-permute-start(bf16[128,512]{1,0:T(8,128)(2,1)S(1)} %shard_map.176.refs_0_), channel_id=1, source_target_pairs={{0,2},{1,3},{2,0},{3,1},{4,6},{5,7},{6,4},{7,5},{8,10},{9,11},{10,... | collective-permute-start | bytes 393224 | tf_op jit(solution)/shard_map/ppermute | solution.py:178
  (133 other events, 882.0 us)

commit v4 on v3

--- a/solution.py
+++ b/solution.py
@@ -41,12 +41,13 @@
     )(*operands)
 
 
-def embed_hidden(order, index_ref, x_ref, w_ref, bias_ref, *outs):
+def embed_hidden(order, section_id, index_ref, x_ref, w_ref, bias_ref, *outs):
     me = index_ref[0]
+    bias = bias_ref[section_id : section_id + 1, :]
     rows = outs[0].shape[0]
     for other, out in zip(order, outs):
         begin = pl.multiple_of((me ^ other) * rows, rows)
-        out[...] = silu(dot(x_ref[pl.ds(begin, rows), :], w_ref[...]) + bias_ref[...]).astype(BF16)
+        out[...] = silu(dot(x_ref[pl.ds(begin, rows), :], w_ref[...]) + bias).astype(BF16)
 
 
 def embed_finish(section_id, count, *refs):
@@ -57,60 +58,72 @@
     out[...] = layer_norm(dot(hidden, weights), gain[row, :], shift[row, :]).astype(BF16)
 
 
-def unpack(pieces, t, latent):
-    w_in = jnp.concatenate([w[t, : 2 * latent, :] for w in pieces], axis=1)
-    width = pieces[0].shape[2]
-    w_out = jnp.concatenate(
-        [
-            jnp.concatenate(
-                [w[t, 2 * latent + b : 2 * latent + b + width, :] for b in range(0, latent, width)],
-                axis=1,
+def phase(section_id, tables, places, mesh_like, *refs):
+    part_ref = refs[0]
+    table_refs = refs[1 : 1 + tables]
+    refs = refs[1 + tables :]
+    pieces = refs[: len(places)]
+    refs = refs[len(places) :]
+    w_count = count = max(slot for _, slot in places) + 1
+    biases = refs[:count]
+    gain, shift, ids, own_ref = refs[count : count + 4]
+    rest = refs[count + 4 :]
+    if mesh_like:
+        recv_col, recv_row, out, table, w_in, w_out, table_sem, w_sem = rest
+    else:
+        head, out, table, w_in, w_out, table_sem, w_sem = rest
+    own = own_ref[...]
+    rows, latent = own.shape
+    width = latent // w_count
+    edges = ids.shape[0]
+    part = part_ref[0]
+    w_copies = []
+    for (kind, slot), ref in zip(places, pieces):
+        if kind is None:
+            src, dst_in, dst_out = (ref, w_in, w_out)
+            lead = (slice(None),)
+        else:
+            t = part if kind == 0 else 1 - part
+            src, dst_in, dst_out = (ref, w_in.at[t], w_out.at[t])
+            lead = ()
+        columns = pl.ds(slot * width, width)
+        w_copies.append((src.at[(*lead, pl.ds(0, 2 * latent))], dst_in.at[(*lead, slice(None), columns)]))
+        for b in range(0, latent, width):
+            w_copies.append(
+                (src.at[(*lead, pl.ds(2 * latent + b, width))], dst_out.at[(*lead, columns, pl.ds(b, width))])
             )
-            for w in pieces
-        ],
-        axis=0,
-    )
-    return w_in, w_out
-
-
-def phase(section_id, tables, count, mesh_like, *refs):
-    table_refs = refs[:tables]
-    pieces = refs[tables : tables + count]
-    bias, gain, shift, ids, own_ref = refs[tables + count : tables + count + 5]
-    rest = refs[tables + count + 5 :]
-    if mesh_like:
-        recv_col, recv_row, out, table, sem = rest
-    else:
-        head, out, table, sem = rest
+    w_copies = [pltpu.make_async_copy(src, dst, w_sem.at[i]) for i, (src, dst) in enumerate(w_copies)]
     copies = []
     begin = 0
     for i, ref in enumerate(table_refs):
-        copies.append(pltpu.make_async_copy(ref, table.at[pl.ds(begin, ref.shape[0])], sem.at[i]))
+        copies.append(pltpu.make_async_copy(ref, table.at[pl.ds(begin, ref.shape[0])], table_sem.at[i]))
         begin += ref.shape[0]
-    for copy in copies:
+    for copy in copies + w_copies:
         copy.start()
-    own = own_ref[...]
-    rows, latent = own.shape
-    edges = ids.shape[0]
-    w_in, w_out = unpack(pieces, 0, latent)
+    def bias(t):
+        return jnp.concatenate([b[section_id + t : section_id + t + 1, :] for b in biases], axis=1)
+
     if mesh_like:
         spread = recv_col[...] == lax.broadcasted_iota(jnp.int32, (edges, rows), 1)
         received = dot(spread.astype(BF16), own).astype(BF16)
-        preact = dot(received, w_in[latent:]) + bias[section_id : section_id + 1, :]
-    else:
-        preact = dot(own, w_in[latent:]) + bias[section_id : section_id + 1, :]
-        preact = jnp.concatenate([preact] * (edges // rows), axis=0)
     for copy in copies:
         copy.wait()
     sent = None
     for start in range(0, begin, CHUNK):
         size = min(CHUNK, begin - start)
         hot = ids[...] == lax.broadcasted_iota(jnp.int32, (edges, size), 1) + start
-        part = dot(hot.astype(BF16), table[pl.ds(start, size), :])
-        sent = part if sent is None else sent + part
-    preact = preact + dot(sent.astype(BF16), w_in[:latent])
+        term = dot(hot.astype(BF16), table[pl.ds(start, size), :])
+        sent = term if sent is None else sent + term
+    for copy in w_copies:
+        copy.wait()
+    if mesh_like:
+        preact = dot(received, w_in[0, latent:, :])
+    else:
+        preact = dot(own, w_in[0, latent:, :])
+        preact = jnp.concatenate([preact] * (edges // rows), axis=0)
+    preact = preact + dot(sent.astype(BF16), w_in[0, :latent, :]) + bias(0)
     row = slice(section_id, section_id + 1)
-    messages = layer_norm(dot(silu(preact).astype(BF16), w_out), gain[row, :], shift[row, :])
+    messages = layer_norm(dot(silu(preact).astype(BF16), w_out[0]), gain[row, :], shift[row, :])
     messages = messages.astype(BF16)
     if mesh_like:
         collect = lax.broadcasted_iota(jnp.int32, (rows, edges), 0) == recv_row[...]
@@ -120,10 +133,9 @@
         for begin in range(rows, edges, rows):
             total = total + messages[begin : begin + rows].astype(F32)
         aggregate = total.astype(BF16)
-    w_in, w_out = unpack(pieces, 1, latent)
     row = slice(section_id + 1, section_id + 2)
-    preact = dot(own, w_in[:latent]) + dot(aggregate, w_in[latent:]) + bias[row, :]
-    update = layer_norm(dot(silu(preact).astype(BF16), w_out), gain[row, :], shift[row, :])
+    preact = dot(own, w_in[1, :latent, :]) + dot(aggregate, w_in[1, latent:, :]) + bias(1)
+    update = layer_norm(dot(silu(preact).astype(BF16), w_out[1]), gain[row, :], shift[row, :])
     updated = (own.astype(F32) + update).astype(BF16)
     if mesh_like:
         out[...] = updated
@@ -163,7 +175,10 @@
     mesh_rows = band_mesh // quarters
     grid_rows = band_grid // quarters
     direct = bands <= 4
-    vmem, anywhere, scalar = pltpu.VMEM, pl.ANY, pltpu.SMEM
+    parts = lax.axis_size("parts")
+    part_index = lax.axis_index("parts")
+    halves = parts == 2
+    vmem, hbm, scalar = pltpu.VMEM, pltpu.HBM, pltpu.SMEM
 
     bits = [1 << b for b in reversed(range(quarters.bit_length() - 1))]
     order = [0]
@@ -228,9 +243,9 @@
     m2m_recv = own(m2m_to) - feat_index * mesh_rows
 
     hidden = kernel_call(
-        functools.partial(embed_hidden, order),
+        functools.partial(embed_hidden, order, embed_id),
         [jax.ShapeDtypeStruct((grid_rows, width), BF16)] * quarters,
-        (feat_index.astype(jnp.int32)[None], x_grid, embed_in, hidden_bias[embed_id:]),
+        (feat_index.astype(jnp.int32)[None], x_grid, embed_in, hidden_bias),
         (scalar, vmem, vmem, vmem),
     )
     hidden = [hidden[0]] + [swap(h, other) for h, other in zip(hidden[1:], order[1:])]
@@ -241,27 +256,52 @@
         (*hidden, *out_pieces, norm_gain, norm_shift),
         (vmem,) * (2 * quarters + 2),
     )
-
-    bias = jnp.concatenate(pieces(hidden_bias), axis=1)
-
-    def packed(first_id):
-        turned = pair_out[first_id : first_id + 2].reshape(2, width, latent // width, width)
-        turned = turned.transpose(0, 2, 1, 3).reshape(2, latent, width)
-        return jnp.concatenate([pair_in[first_id : first_id + 2], turned], axis=1)
-
-    groups = [pieces(packed(s)) for s in range(0, embed_id, 2)]
-
-    def run(section_id, table, ids, own_latent, extra, out_shape, mesh_like):
+    grid, ids = lax.optimization_barrier(
+        (grid, (g2m_ids, m2m_ids, m2g_ids, g2m_recv[:, None], m2m_recv[:, None]))
+    )
+    g2m_ids, m2m_ids, m2g_ids, g2m_column, m2m_column = ids
+    biases = pieces(hidden_bias)
+
+    def packed(section_id):
+        turned = lax.dynamic_index_in_dim(pair_out, section_id, 0, False)
+        turned = turned.reshape(width, latent // width, width)
+        turned = turned.transpose(1, 0, 2).reshape(latent, width)
+        return jnp.concatenate([lax.dynamic_index_in_dim(pair_in, section_id, 0, False), turned], axis=0)
+
+    def group(section_id, after):
+        if not halves:
+            mine = jnp.stack([packed(section_id), packed(section_id + 1)])
+            if after is not None:
+                mine, _ = lax.optimization_barrier((mine, after))
+            return [((None, slot), piece) for slot, piece in enumerate(pieces(mine))]
+        first = packed(section_id + part_index)
+        second = packed(section_id + 1 - part_index)
+        if after is not None:
+            first, second, _ = lax.optimization_barrier((first, second, after))
+        across = swap(first, bits[0])
+        over = lax.ppermute(across, "parts", [(0, 1), (1, 0)])
+        found = [((0, 0), first), ((1, 0), second), ((0, 1), across), ((1, 1), over)]
+        for i, bit in enumerate(bits[1:]):
+            found = found + [((kind, slot + (2 << i)), swap(piece, bit)) for (kind, slot), piece in found]
+        return found
+
+    def run(section_id, table, after, ids, own_latent, extra, out_shape, mesh_like):
         rows = sum(part.shape[0] for part in table)
         edges = ids.shape[0]
+        weights = group(section_id, after)
+        places = [place for place, _ in weights]
+        weights = [piece for _, piece in weights]
         return kernel_call(
-            functools.partial(phase, section_id, len(table), quarters, mesh_like),
+            functools.partial(phase, section_id, len(table), places, mesh_like),
             out_shape,
-            (*table, *groups[section_id // 2], bias, norm_gain, norm_shift, ids, own_latent, *extra),
-            (anywhere,) * len(table) + (vmem,) * (quarters + 5 + len(extra)),
+            (part_index.astype(jnp.int32)[None], *table, *weights, *biases, norm_gain, norm_shift, ids, own_latent, *extra),
+            (scalar,) + (hbm,) * (len(table) + len(weights)) + (vmem,) * (quarters + 4 + len(extra)),
             scratch=(
                 pltpu.VMEM((rows, latent), BF16),
+                pltpu.VMEM((2, 2 * latent, latent), BF16),
+                pltpu.VMEM((2, latent, latent), BF16),
                 pltpu.SemaphoreType.DMA((len(table),)),
+                pltpu.SemaphoreType.DMA((len(weights) * (1 + quarters),)),
             ),
             flops=2 * edges * latent * (rows + 3 * latent),
             vmem=(20 << 20) + 2 * rows * latent * 2,
@@ -271,20 +311,19 @@
     mesh = own_pos[0][:, None] * pos_weight[0][None, :] + own_pos[1][:, None] * pos_weight[1][None, :]
     mesh = (mesh + own_pos[2][:, None] * pos_weight[2][None, :]).astype(BF16)
     shape = jax.ShapeDtypeStruct((mesh_rows, latent), BF16)
-    mesh = run(0, everyone(grid), g2m_ids, mesh, (g2m_recv[:, None], g2m_recv[None, :]), shape, True)
+    table = everyone(grid)
+    mesh = run(0, table, None, g2m_ids, mesh, (g2m_column, g2m_recv[None, :]), shape, True)
     for layer_id in range(LAYERS):
+        after = table[2 * bands - 1] if direct else None
+        table = everyone(mesh)
         mesh = run(
-            2 + 2 * layer_id,
-            everyone(mesh),
-            m2m_ids,
-            mesh,
-            (m2m_recv[:, None], m2m_recv[None, :]),
-            shape,
-            True,
+            2 + 2 * layer_id, table, after, m2m_ids, mesh, (m2m_column, m2m_recv[None, :]), shape, True
         )
+    after = table[2 * bands - 1] if direct else None
     return run(
         2 * LAYERS + 2,
         everyone(mesh),
+        after,
         m2g_ids,
         grid,
         (head,),

time: 246 us -> 255 us (1.037)
  local copies, waits for them, and re-layouts: 67.9 us -> 76.5 us
    ppermute x69 -> x77, waiting for transfers between devices: 55.4 us -> 44.6 us  [swap(): return lax.ppermute(value, 'feat', [(f, f ^ bit) for f in range(quarters)])]
    unnamed x159 -> x211, local copies, waits for them, and re-layouts: 46 us -> 56.7 us
    ppermute x12, waiting for transfers between devices: 21.9 us -> 31.9 us  [everyone(): lax.ppermute(rows, 'band', [(b, (b + step) % bands) for b in range(bands)])]
    ppermute x0 -> x4, starting transfers between devices: none -> 4.06 us  [group(): over = lax.ppermute(across, 'parts', [(0, 1), (1, 0)])]
    slice x2 -> x0, local copies, waits for them, and re-layouts: 3.16 us -> none  [the longest x1 2.44 us: packed(): return jnp.concatenate([pair_in[first_id:first_id + 2], turned], axis=1)]
    transpose x0 -> x8, local copies, waits for them, and re-layouts: none -> 2.99 us  [packed(): turned = turned.transpose(1, 0, 2).reshape(latent, width)]
    broadcast_in_dim x4 -> x0, local copies, waits for them, and re-layouts: 2.57 us -> none  [the longest x1 1.47 us: local(): g2m_ids = sender_ids(0, g2m_take, own(g2m_from), band_grid)[:, None]]
    ppermute x69 -> x77, starting transfers between devices: 35.4 us -> 33.6 us  [swap(): return lax.ppermute(value, 'feat', [(f, f ^ bit) for f in range(quarters)])]
  transfers between devices with their start and end apart: 82 -> 94, of which waited for: 22 -> 27; matrix products, arithmetic and copies ran while one was open for 14% -> 12% of each run, Pallas kernels for 9% -> 8%
where the time goes in v4:
time: 255 us; the launch traced here: 253 us
  waiting for transfers between devices  76.8 us (30%)
  local copies, waits for them, and re-layouts  76.5 us (30%)
  starting transfers between devices  63.9 us (25%)
  Pallas kernels  27.5 us (11%)
  other arithmetic  7.66 us (3%)
    unnamed x211, local copies, waits for them, and re-layouts  56.7 us
    ppermute x77, waiting for transfers between devices, swap(): return lax.ppermute(value, 'feat', [(f, f ^ bit) for f in range(quarters)])  44.6 us
    ppermute x77, starting transfers between devices, swap(): return lax.ppermute(value, 'feat', [(f, f ^ bit) for f in range(quarters)])  33.6 us
    ppermute x12, waiting for transfers between devices, everyone(): lax.ppermute(rows, 'band', [(b, (b + step) % bands) for b in range(bands)])  31.9 us
    pallas_call x6, Pallas kernels, kernel_call(): pl.pallas_call(body, out_shape=out_shape, in_specs=[pl.BlockSpec(memory_s...  27.5 us
    ppermute x12, starting transfers between devices, everyone(): lax.ppermute(rows, 'band', [(b, (b + step) % bands) for b in range(bands)])  21.4 us
    gather x3, local copies, waits for them, and re-layouts, sender_ids(): return rows.reshape(-1).at[senders].get(mode='promise_in_bounds')  8.76 us
  transfers between devices with their start and end apart: 94, of which 27 were waited for; matrix products, arithmetic and copies ran while one was open for 12% of the time, Pallas kernels for 8%

profile of v4, /device:TPU:0, one launch (start us, length us, event | category | flops | bytes accessed | tf_op | source)
XLA Modules:
  0.0 253.3 jit_solution(2520500075500076630)
XLA Ops:
  2.5 2.9 %collective-permute-start.3 = (bf16[128,512]{1,0:T(8,128)(2,1)S(1)}, bf16[128,512]{1,0:T(8,128)(2,1)S(1)}, u32[]{:S(2)}, u32[]{:S(2)}) collective-permute-start(bf16[128,512]{1,0:T(8,128)(2,1)S(1)} %get-tuple-element.53.refs_4_), channel_id=1, source_target_pairs={{0,2},{1,3},{2,0},{3,1},{4,6},{5,7},{6,4},{7,5},{8,10},{9,11},{10,... | collective-permute-start | bytes 393224 | tf_op jit(solution)/shard_map/ppermute | solution.py:193
  9.9 4.9 %all-to-all-start = ((s32[4,1,1152]{2,1,0:T(1,128)}), s32[4,1,1152]{2,1,0:T(1,128)S(1)}, u32[]{:S(2)}, u32[]{:S(2)}) async-start(s32[4,1,1152]{2,1,0:T(1,128)} %all_to_all.8), calls=%async_computation | async-start | bytes 36864 | tf_op jit(solution)/shard_map/all_to_all | solution.py:216
  27.7 4.3 %gather_fusion.1 = s32[512]{0:T(512)} fusion(s32[2048]{0:T(1024)S(1)} %bitcast.90, s32[1024]{0:T(1024)S(1)} %pad_clamp_fusion.1), kind=kCustom, calls=%fused_computation.1 | custom fusion | bytes 6144 | tf_op jit(solution)/shard_map/gather | solution.py:236
  37.0 6.7 %collective-permute-done.27.refs_26_ = f32[9,128]{1,0:T(8,128)S(1)} collective-permute-done((f32[9,128]{1,0:T(8,128)S(1)}, f32[9,128]{1,0:T(8,128)S(1)}, u32[]{:S(2)}, u32[]{:S(2)}) %collective-permute-start.27) | collective-permute-done | bytes 4640 | tf_op jit(solution)/shard_map/ppermute | solution.py:193
  46.0 2.9 %collective-permute-start.7 = (bf16[128,512]{1,0:T(8,128)(2,1)S(1)}, bf16[128,512]{1,0:T(8,128)(2,1)S(1)}, u32[]{:S(2)}, u32[]{:S(2)}) collective-permute-start(bf16[128,512]{1,0:T(8,128)(2,1)S(1)} %shard_map.173.refs_1_.refs_32_), channel_id=1, source_target_pairs={{0,8},{4,12},{8,0},{12,4},{1,9},{5,13},{9,1},{13,5},{2,10},{6,14},... | collective-permute-start | bytes 393224 | tf_op jit(solution)/shard_map/ppermute | solution.py:204
  50.4 5.6 %collective-permute-done.7.refs_3_ = bf16[128,512]{1,0:T(8,128)(2,1)S(1)} collective-permute-done((bf16[128,512]{1,0:T(8,128)(2,1)S(1)}, bf16[128,512]{1,0:T(8,128)(2,1)S(1)}, u32[]{:S(2)}, u32[]{:S(2)}) %collective-permute-start.7) | collective-permute-done | bytes 131104 | tf_op jit(solution)/shard_map/ppermute | solution.py:204
  58.4 2.6 %collective-permute-done.9.refs_5_ = bf16[128,512]{1,0:T(8,128)(2,1)S(1)} collective-permute-done((bf16[128,512]{1,0:T(8,128)(2,1)S(1)}, bf16[128,512]{1,0:T(8,128)(2,1)S(1)}, u32[]{:S(2)}, u32[]{:S(2)}) %collective-permute-start.9) | collective-permute-done | bytes 131104 | tf_op jit(solution)/shard_map/ppermute | solution.py:193
  78.5 7.0 %collective-permute-done.45.refs_19_ = bf16[1536,128]{1,0:T(8,128)(2,1)} collective-permute-done((bf16[1536,128]{1,0:T(8,128)(2,1)}, bf16[1536,128]{1,0:T(8,128)(2,1)}, u32[]{:S(2)}, u32[]{:S(2)}) %collective-permute-start.45) | collective-permute-done | bytes 393248 | tf_op jit(solution)/shard_map/ppermute | solution.py:193
  94.2 5.5 %shard_map.174.refs_1_.refs_32_ = bf16[128,512]{1,0:T(8,128)(2,1)S(1)} custom-call(s32[1]{0:T(128)} %bitcast.refs_0_, bf16[128,512]{1,0:T(8,128)(2,1)S(1)} %shard_map.173.refs_1_.refs_32_, bf16[128,512]{1,0:T(8,128)(2,1)S(1)} %collective-permute-done.6.refs_2_, bf16[128,512]{1,0:T(8,128)(2,1)S(1)} %copy-done.10, bf16[128,512]{1,0:T(8,128)(2,1)S(1)} %copy-done.12, ...), custom_call_target="tpu_custom_call" | custom-call | flops 939524096 | bytes 4194304 | tf_op jit(solution)/shard_map/pallas_call | solution.py:33
  99.7 3.6 %collective-permute-start.30 = (bf16[128,512]{1,0:T(8,128)(2,1)S(1)}, bf16[128,512]{1,0:T(8,128)(2,1)S(1)}, u32[]{:S(2)}, u32[]{:S(2)}) collective-permute-start(bf16[128,512]{1,0:T(8,128)(2,1)S(1)} %shard_map.174.refs_1_.refs_32_), channel_id=1, source_target_pairs={{0,4},{4,8},{8,12},{12,0},{1,5},{5,9},{9,13},{13,1},{2,6},{6,10},{... | collective-permute-start | bytes 393224 | tf_op jit(solution)/shard_map/ppermute | solution.py:204
  103.4 3.4 %collective-permute-start.31 = (bf16[128,512]{1,0:T(8,128)(2,1)S(1)}, bf16[128,512]{1,0:T(8,128)(2,1)S(1)}, u32[]{:S(2)}, u32[]{:S(2)}) collective-permute-start(bf16[128,512]{1,0:T(8,128)(2,1)S(1)} %shard_map.174.refs_1_.refs_32_), channel_id=1, source_target_pairs={{0,8},{4,12},{8,0},{12,4},{1,9},{5,13},{9,1},{13,5},{2,10},{6,14},... | collective-permute-start | bytes 393224 | tf_op jit(solution)/shard_map/ppermute | solution.py:204
  106.7 3.9 %collective-permute-done.30.refs_2_ = bf16[128,512]{1,0:T(8,128)(2,1)S(1)} collective-permute-done((bf16[128,512]{1,0:T(8,128)(2,1)S(1)}, bf16[128,512]{1,0:T(8,128)(2,1)S(1)}, u32[]{:S(2)}, u32[]{:S(2)}) %collective-permute-start.30) | collective-permute-done | bytes 131104 | tf_op jit(solution)/shard_map/ppermute | solution.py:204
  111.4 4.5 %collective-permute-done.31.refs_3_ = bf16[128,512]{1,0:T(8,128)(2,1)S(1)} collective-permute-done((bf16[128,512]{1,0:T(8,128)(2,1)S(1)}, bf16[128,512]{1,0:T(8,128)(2,1)S(1)}, u32[]{:S(2)}, u32[]{:S(2)}) %collective-permute-start.31) | collective-permute-done | bytes 131104 | tf_op jit(solution)/shard_map/ppermute | solution.py:204
  123.0 2.8 %collective-permute-done.35.refs_7_ = bf16[128,512]{1,0:T(8,128)(2,1)S(1)} collective-permute-done((bf16[128,512]{1,0:T(8,128)(2,1)S(1)}, bf16[128,512]{1,0:T(8,128)(2,1)S(1)}, u32[]{:S(2)}, u32[]{:S(2)}) %collective-permute-start.35) | collective-permute-done | bytes 131104 | tf_op jit(solution)/shard_map/ppermute | solution.py:193
  136.3 7.7 %shard_map.175.refs_1_.refs_32_ = bf16[128,512]{1,0:T(8,128)(2,1)S(1)} custom-call(s32[1]{0:T(128)} %bitcast.refs_0_, bf16[128,512]{1,0:T(8,128)(2,1)S(1)} %copy-done.18, bf16[128,512]{1,0:T(8,128)(2,1)S(1)} %collective-permute-done.30.refs_2_, bf16[128,512]{1,0:T(8,128)(2,1)S(1)} %collective-permute-done.31.refs_3_, ...), custom_call_target="tpu_custom_call" | custom-call | flops 1879048192 | bytes 4194304 | tf_op jit(solution)/shard_map/pallas_call | solution.py:33
  144.1 2.8 %collective-permute-start.51 = (bf16[128,512]{1,0:T(8,128)(2,1)S(1)}, bf16[128,512]{1,0:T(8,128)(2,1)S(1)}, u32[]{:S(2)}, u32[]{:S(2)}) collective-permute-start(bf16[128,512]{1,0:T(8,128)(2,1)S(1)} %shard_map.175.refs_1_.refs_32_), channel_id=1, source_target_pairs={{0,4},{4,8},{8,12},{12,0},{1,5},{5,9},{9,13},{13,1},{2,6},{6,10},{... | collective-permute-start | bytes 393224 | tf_op jit(solution)/shard_map/ppermute | solution.py:204
  148.0 4.4 %collective-permute-done.51.refs_2_ = bf16[128,512]{1,0:T(8,128)(2,1)S(1)} collective-permute-done((bf16[128,512]{1,0:T(8,128)(2,1)S(1)}, bf16[128,512]{1,0:T(8,128)(2,1)S(1)}, u32[]{:S(2)}, u32[]{:S(2)}) %collective-permute-start.51) | collective-permute-done | bytes 131104 | tf_op jit(solution)/shard_map/ppermute | solution.py:204
  152.4 4.9 %collective-permute-done.52.refs_3_ = bf16[128,512]{1,0:T(8,128)(2,1)S(1)} collective-permute-done((bf16[128,512]{1,0:T(8,128)(2,1)S(1)}, bf16[128,512]{1,0:T(8,128)(2,1)S(1)}, u32[]{:S(2)}, u32[]{:S(2)}) %collective-permute-start.52) | collective-permute-done | bytes 131104 | tf_op jit(solution)/shard_map/ppermute | solution.py:204
  179.6 5.5 %collective-permute-done.87.refs_19_ = bf16[1536,128]{1,0:T(8,128)(2,1)S(1)} collective-permute-done((bf16[1536,128]{1,0:T(8,128)(2,1)S(1)}, bf16[1536,128]{1,0:T(8,128)(2,1)S(1)}, u32[]{:S(2)}, u32[]{:S(2)}) %collective-permute-start.87) | collective-permute-done | bytes 393248 | tf_op jit(solution)/shard_map/ppermute | solution.py:193
  197.8 7.5 %shard_map.176.refs_1_ = bf16[128,512]{1,0:T(8,128)(2,1)S(1)} custom-call(s32[1]{0:T(128)} %bitcast.refs_0_, bf16[128,512]{1,0:T(8,128)(2,1)S(1)} %copy-done.65, bf16[128,512]{1,0:T(8,128)(2,1)S(1)} %copy-done.67, bf16[128,512]{1,0:T(8,128)(2,1)S(1)} %copy-done.69, bf16[128,512]{1,0:T(8,128)(2,1)S(1)} %copy-done.71, bf16[128,512]{1,0:T(8,128)(2,1)S(1)} %copy-done.73, ...), custom_call_target="tpu_custom_call" | custom-call | flops 1879048192 | bytes 4194304 | tf_op jit(solution)/shard_map/pallas_call | solution.py:33
  206.5 3.4 %collective-permute-start.73 = (bf16[128,512]{1,0:T(8,128)(2,1)S(1)}, bf16[128,512]{1,0:T(8,128)(2,1)S(1)}, u32[]{:S(2)}, u32[]{:S(2)}) collective-permute-start(bf16[128,512]{1,0:T(8,128)(2,1)S(1)} %shard_map.176.refs_1_), channel_id=1, source_target_pairs={{0,8},{4,12},{8,0},{12,4},{1,9},{5,13},{9,1},{13,5},{2,10},{6,14},... | collective-permute-start | bytes 393224 | tf_op jit(solution)/shard_map/ppermute | solution.py:204
  209.9 3.9 %collective-permute-done.72.refs_2_ = bf16[128,512]{1,0:T(8,128)(2,1)S(1)} collective-permute-done((bf16[128,512]{1,0:T(8,128)(2,1)S(1)}, bf16[128,512]{1,0:T(8,128)(2,1)S(1)}, u32[]{:S(2)}, u32[]{:S(2)}) %collective-permute-start.72) | collective-permute-done | bytes 131104 | tf_op jit(solution)/shard_map/ppermute | solution.py:204
  215.0 4.2 %collective-permute-done.73.refs_3_ = bf16[128,512]{1,0:T(8,128)(2,1)S(1)} collective-permute-done((bf16[128,512]{1,0:T(8,128)(2,1)S(1)}, bf16[128,512]{1,0:T(8,128)(2,1)S(1)}, u32[]{:S(2)}, u32[]{:S(2)}) %collective-permute-start.73) | collective-permute-done | bytes 131104 | tf_op jit(solution)/shard_map/ppermute | solution.py:204
  246.5 6.0 %shard_map.177 = f32[128,227]{1,0:T(8,128)S(1)} custom-call(s32[1]{0:T(128)} %bitcast.refs_0_, bf16[128,512]{1,0:T(8,128)(2,1)S(1)} %copy-done.22, bf16[128,512]{1,0:T(8,128)(2,1)S(1)} %copy-done.24, bf16[128,512]{1,0:T(8,128)(2,1)S(1)} %copy-done.28, bf16[128,512]{1,0:T(8,128)(2,1)S(1)} %copy-done.30, bf16[128,512]{1,0:T(8,128)(2,1)} %collective-permute-done.75.refs_5_, ...), custom_call_target="tpu_custom_call" | custom-call | flops 1409286144 | bytes 4194304 | tf_op jit(solution)/shard_map/pallas_call | solution.py:33
  (428 shorter events, 141.5 us)
Async XLA Ops:
  2.5 20.0 %collective-permute-start.3 = (bf16[128,512]{1,0:T(8,128)(2,1)S(1)}, bf16[128,512]{1,0:T(8,128)(2,1)S(1)}, u32[]{:S(2)}, u32[]{:S(2)}) collective-permute-start(bf16[128,512]{1,0:T(8,128)(2,1)S(1)} %get-tuple-element.53.refs_4_), channel_id=1, source_target_pairs={{0,2},{1,3},{2,0},{3,1},{4,6},{5,7},{6,4},{7,5},{8,10},{9,11},{10,... | collective-permute-start | bytes 393224 | tf_op jit(solution)/shard_map/ppermute | solution.py:193
  5.5 27.3 %collective-permute-start.4 = (bf16[128,512]{1,0:T(8,128)(2,1)S(1)}, bf16[128,512]{1,0:T(8,128)(2,1)S(1)}, u32[]{:S(2)}, u32[]{:S(2)}) collective-permute-start(bf16[128,512]{1,0:T(8,128)(2,1)S(1)} %get-tuple-element.53.refs_4_), channel_id=1, source_target_pairs={{0,1},{1,0},{2,3},{3,2},{4,5},{5,4},{6,7},{7,6},{8,9},{9,8},{10,11... | collective-permute-start | bytes 393224 | tf_op jit(solution)/shard_map/ppermute | solution.py:193
  7.0 25.0 %collective-permute-start = (bf16[128,128]{1,0:T(8,128)(2,1)S(1)}, bf16[128,128]{1,0:T(8,128)(2,1)S(1)}, u32[]{:S(2)}, u32[]{:S(2)}) collective-permute-start(bf16[128,128]{1,0:T(8,128)(2,1)S(1)} %get-tuple-element.22), channel_id=1, source_target_pairs={{0,2},{1,3},{2,0},{3,1},{4,6},{5,7},{6,4},{7,5},{8,10},{9,11},{10,... | collective-permute-start | bytes 98312 | tf_op jit(solution)/shard_map/ppermute | solution.py:193
  7.2 25.4 %collective-permute-start.1 = (bf16[128,128]{1,0:T(8,128)(2,1)S(1)}, bf16[128,128]{1,0:T(8,128)(2,1)S(1)}, u32[]{:S(2)}, u32[]{:S(2)}) collective-permute-start(bf16[128,128]{1,0:T(8,128)(2,1)S(1)} %get-tuple-element.23), channel_id=1, source_target_pairs={{0,1},{1,0},{2,3},{3,2},{4,5},{5,4},{6,7},{7,6},{8,9},{9,8},{10,11... | collective-permute-start | bytes 98312 | tf_op jit(solution)/shard_map/ppermute | solution.py:193
  7.7 25.1 %collective-permute-start.2 = (bf16[128,128]{1,0:T(8,128)(2,1)S(1)}, bf16[128,128]{1,0:T(8,128)(2,1)S(1)}, u32[]{:S(2)}, u32[]{:S(2)}) collective-permute-start(bf16[128,128]{1,0:T(8,128)(2,1)S(1)} %get-tuple-element.24), channel_id=1, source_target_pairs={{0,3},{1,2},{2,1},{3,0},{4,7},{5,6},{6,5},{7,4},{8,11},{9,10},{10,... | collective-permute-start | bytes 98312 | tf_op jit(solution)/shard_map/ppermute | solution.py:193
  32.0 30.2 %collective-permute-start.21 = (bf16[1536,128]{1,0:T(8,128)(2,1)S(1)}, bf16[1536,128]{1,0:T(8,128)(2,1)S(1)}, u32[]{:S(2)}, u32[]{:S(2)}) collective-permute-start(bf16[1536,128]{1,0:T(8,128)(2,1)S(1)} %pad_maximum_fusion.refs_17_), channel_id=1, source_target_pairs={{0,2},{1,3},{2,0},{3,1},{4,6},{5,7},{6,4},{7,5},{8,10},{9,11},{10,... | collective-permute-start | bytes 1179656 | tf_op jit(solution)/shard_map/ppermute | solution.py:193
  32.5 31.2 %collective-permute-start.23 = (bf16[1536,128]{1,0:T(8,128)(2,1)S(1)}, bf16[1536,128]{1,0:T(8,128)(2,1)S(1)}, u32[]{:S(2)}, u32[]{:S(2)}) collective-permute-start(bf16[1536,128]{1,0:T(8,128)(2,1)S(1)} %pad_maximum_fusion.refs_17_), channel_id=1, source_target_pairs={{0,1},{1,0},{2,3},{3,2},{4,5},{5,4},{6,7},{7,6},{8,9},{9,8},{10,11... | collective-permute-start | bytes 1179656 | tf_op jit(solution)/shard_map/ppermute | solution.py:193
  33.2 15.7 %collective-permute-start.6 = (bf16[128,512]{1,0:T(8,128)(2,1)S(1)}, bf16[128,512]{1,0:T(8,128)(2,1)S(1)}, u32[]{:S(2)}, u32[]{:S(2)}) collective-permute-start(bf16[128,512]{1,0:T(8,128)(2,1)S(1)} %shard_map.173.refs_1_.refs_32_), channel_id=1, source_target_pairs={{0,4},{4,8},{8,12},{12,0},{1,5},{5,9},{9,13},{13,1},{2,6},{6,10},{... | collective-permute-start | bytes 393224 | tf_op jit(solution)/shard_map/ppermute | solution.py:204
  35.3 28.9 %collective-permute-start.24 = (bf16[1536,128]{1,0:T(8,128)(2,1)S(1)}, bf16[1536,128]{1,0:T(8,128)(2,1)S(1)}, u32[]{:S(2)}, u32[]{:S(2)}) collective-permute-start(bf16[1536,128]{1,0:T(8,128)(2,1)S(1)} %pad_maximum_fusion.1.refs_18_), channel_id=1, source_target_pairs={{0,1},{1,0},{2,3},{3,2},{4,5},{5,4},{6,7},{7,6},{8,9},{9,8},{10,11... | collective-permute-start | bytes 1179656 | tf_op jit(solution)/shard_map/ppermute | solution.py:193
  73.6 13.4 %collective-permute-start.25 = (bf16[1536,128]{1,0:T(8,128)(2,1)S(1)}, bf16[1536,128]{1,0:T(8,128)(2,1)S(1)}, u32[]{:S(2)}, u32[]{:S(2)}) collective-permute-start(bf16[1536,128]{1,0:T(8,128)(2,1)S(1)} %collective-permute-done.21.refs_19_), channel_id=1, source_target_pairs={{0,1},{1,0},{2,3},{3,2},{4,5},{5,4},{6,7},{7,6},{8,9},{9,8},{10,11... | collective-permute-start | bytes 1179656 | tf_op jit(solution)/shard_map/ppermute | solution.py:193
  76.9 26.5 %collective-permute-start.47 = (bf16[1536,128]{1,0:T(8,128)(2,1)}, bf16[1536,128]{1,0:T(8,128)(2,1)}, u32[]{:S(2)}, u32[]{:S(2)}) collective-permute-start(bf16[1536,128]{1,0:T(8,128)(2,1)} %get-tuple-element.28.refs_17_), channel_id=1, source_target_pairs={{0,1},{1,0},{2,3},{3,2},{4,5},{5,4},{6,7},{7,6},{8,9},{9,8},{10,11... | collective-permute-start | bytes 1179656 | tf_op jit(solution)/shard_map/ppermute | solution.py:193
  77.8 28.9 %collective-permute-start.48 = (bf16[1536,128]{1,0:T(8,128)(2,1)}, bf16[1536,128]{1,0:T(8,128)(2,1)}, u32[]{:S(2)}, u32[]{:S(2)}) collective-permute-start(bf16[1536,128]{1,0:T(8,128)(2,1)} %get-tuple-element.29.refs_18_), channel_id=1, source_target_pairs={{0,1},{1,0},{2,3},{3,2},{4,5},{5,4},{6,7},{7,6},{8,9},{9,8},{10,11... | collective-permute-start | bytes 1179656 | tf_op jit(solution)/shard_map/ppermute | solution.py:193
  85.4 33.3 %collective-permute-start.46 = (bf16[1536,128]{1,0:T(8,128)(2,1)}, bf16[1536,128]{1,0:T(8,128)(2,1)}, u32[]{:S(2)}, u32[]{:S(2)}) collective-permute-start(bf16[1536,128]{1,0:T(8,128)(2,1)} %collective-permute-done.45.refs_19_), channel_id=1, source_target_pairs={{0,16},{16,0},{1,17},{17,1},{2,18},{18,2},{3,19},{19,3},{4,20},{20... | collective-permute-start | bytes 1179656 | tf_op jit(solution)/shard_map/ppermute | solution.py:282
  87.0 32.7 %collective-permute-start.49 = (bf16[1536,128]{1,0:T(8,128)(2,1)}, bf16[1536,128]{1,0:T(8,128)(2,1)S(1)}, u32[]{:S(2)}, u32[]{:S(2)}) collective-permute-start(bf16[1536,128]{1,0:T(8,128)(2,1)} %collective-permute-done.45.refs_19_), channel_id=1, source_target_pairs={{0,1},{1,0},{2,3},{3,2},{4,5},{5,4},{6,7},{7,6},{8,9},{9,8},{10,11... | collective-permute-start | bytes 1179656 | tf_op jit(solution)/shard_map/ppermute | solution.py:193
  118.7 14.8 %collective-permute-start.50 = (bf16[1536,128]{1,0:T(8,128)(2,1)}, bf16[1536,128]{1,0:T(8,128)(2,1)S(1)}, u32[]{:S(2)}, u32[]{:S(2)}) collective-permute-start(bf16[1536,128]{1,0:T(8,128)(2,1)} %collective-permute-done.46.refs_20_), channel_id=1, source_target_pairs={{0,1},{1,0},{2,3},{3,2},{4,5},{5,4},{6,7},{7,6},{8,9},{9,8},{10,11... | collective-permute-start | bytes 1179656 | tf_op jit(solution)/shard_map/ppermute | solution.py:193
  132.6 27.1 %collective-permute-start.66 = (bf16[1536,128]{1,0:T(8,128)(2,1)S(1)}, bf16[1536,128]{1,0:T(8,128)(2,1)}, u32[]{:S(2)}, u32[]{:S(2)}) collective-permute-start(bf16[1536,128]{1,0:T(8,128)(2,1)S(1)} %get-tuple-element.32.refs_17_), channel_id=1, source_target_pairs={{0,2},{1,3},{2,0},{3,1},{4,6},{5,7},{6,4},{7,5},{8,10},{9,11},{10,... | collective-permute-start | bytes 1179656 | tf_op jit(solution)/shard_map/ppermute | solution.py:193
  146.9 20.2 %collective-permute-start.68 = (bf16[1536,128]{1,0:T(8,128)(2,1)S(1)}, bf16[1536,128]{1,0:T(8,128)(2,1)S(1)}, u32[]{:S(2)}, u32[]{:S(2)}) collective-permute-start(bf16[1536,128]{1,0:T(8,128)(2,1)S(1)} %get-tuple-element.32.refs_17_), channel_id=1, source_target_pairs={{0,1},{1,0},{2,3},{3,2},{4,5},{5,4},{6,7},{7,6},{8,9},{9,8},{10,11... | collective-permute-start | bytes 1179656 | tf_op jit(solution)/shard_map/ppermute | solution.py:193
  146.9 21.5 %collective-permute-start.69 = (bf16[1536,128]{1,0:T(8,128)(2,1)S(1)}, bf16[1536,128]{1,0:T(8,128)(2,1)S(1)}, u32[]{:S(2)}, u32[]{:S(2)}) collective-permute-start(bf16[1536,128]{1,0:T(8,128)(2,1)S(1)} %get-tuple-element.33.refs_18_), channel_id=1, source_target_pairs={{0,1},{1,0},{2,3},{3,2},{4,5},{5,4},{6,7},{7,6},{8,9},{9,8},{10,11... | collective-permute-start | bytes 1179656 | tf_op jit(solution)/shard_map/ppermute | solution.py:193
  159.7 15.8 %collective-permute-start.67 = (bf16[1536,128]{1,0:T(8,128)(2,1)}, bf16[1536,128]{1,0:T(8,128)(2,1)}, u32[]{:S(2)}, u32[]{:S(2)}) collective-permute-start(bf16[1536,128]{1,0:T(8,128)(2,1)} %collective-permute-done.66.refs_19_), channel_id=1, source_target_pairs={{0,16},{16,0},{1,17},{17,1},{2,18},{18,2},{3,19},{19,3},{4,20},{20... | collective-permute-start | bytes 1179656 | tf_op jit(solution)/shard_map/ppermute | solution.py:282
  179.0 27.5 %collective-permute-start.89 = (bf16[1536,128]{1,0:T(8,128)(2,1)S(1)}, bf16[1536,128]{1,0:T(8,128)(2,1)S(1)}, u32[]{:S(2)}, u32[]{:S(2)}) collective-permute-start(bf16[1536,128]{1,0:T(8,128)(2,1)S(1)} %get-tuple-element.34.refs_17_), channel_id=1, source_target_pairs={{0,1},{1,0},{2,3},{3,2},{4,5},{5,4},{6,7},{7,6},{8,9},{9,8},{10,11... | collective-permute-start | bytes 1179656 | tf_op jit(solution)/shard_map/ppermute | solution.py:193
  179.4 30.5 %collective-permute-start.90 = (bf16[1536,128]{1,0:T(8,128)(2,1)S(1)}, bf16[1536,128]{1,0:T(8,128)(2,1)S(1)}, u32[]{:S(2)}, u32[]{:S(2)}) collective-permute-start(bf16[1536,128]{1,0:T(8,128)(2,1)S(1)} %get-tuple-element.35.refs_18_), channel_id=1, source_target_pairs={{0,1},{1,0},{2,3},{3,2},{4,5},{5,4},{6,7},{7,6},{8,9},{9,8},{10,11... | collective-permute-start | bytes 1179656 | tf_op jit(solution)/shard_map/ppermute | solution.py:193
  185.1 36.8 %collective-permute-start.88 = (bf16[1536,128]{1,0:T(8,128)(2,1)S(1)}, bf16[1536,128]{1,0:T(8,128)(2,1)S(1)}, u32[]{:S(2)}, u32[]{:S(2)}) collective-permute-start(bf16[1536,128]{1,0:T(8,128)(2,1)S(1)} %collective-permute-done.87.refs_19_), channel_id=1, source_target_pairs={{0,16},{16,0},{1,17},{17,1},{2,18},{18,2},{3,19},{19,3},{4,20},{20... | collective-permute-start | bytes 1179656 | tf_op jit(solution)/shard_map/ppermute | solution.py:282
  185.6 38.1 %collective-permute-start.91 = (bf16[1536,128]{1,0:T(8,128)(2,1)S(1)}, bf16[1536,128]{1,0:T(8,128)(2,1)S(1)}, u32[]{:S(2)}, u32[]{:S(2)}) collective-permute-start(bf16[1536,128]{1,0:T(8,128)(2,1)S(1)} %collective-permute-done.87.refs_19_), channel_id=1, source_target_pairs={{0,1},{1,0},{2,3},{3,2},{4,5},{5,4},{6,7},{7,6},{8,9},{9,8},{10,11... | collective-permute-start | bytes 1179656 | tf_op jit(solution)/shard_map/ppermute | solution.py:193
  221.9 14.4 %collective-permute-start.92 = (bf16[1536,128]{1,0:T(8,128)(2,1)S(1)}, bf16[1536,128]{1,0:T(8,128)(2,1)}, u32[]{:S(2)}, u32[]{:S(2)}) collective-permute-start(bf16[1536,128]{1,0:T(8,128)(2,1)S(1)} %collective-permute-done.88.refs_20_), channel_id=1, source_target_pairs={{0,1},{1,0},{2,3},{3,2},{4,5},{5,4},{6,7},{7,6},{8,9},{9,8},{10,11... | collective-permute-start | bytes 1179656 | tf_op jit(solution)/shard_map/ppermute | solution.py:193
  (169 other events, 1585.3 us)

commit v5 on v4

v5 whole, which is shorter than its diff:
```python
import functools

import jax
import jax.numpy as jnp
from jax import lax
from jax.experimental import pallas as pl
from jax.experimental.pallas import tpu as pltpu
from jax.sharding import PartitionSpec as P

LAYERS = 2
EPSILON = 1e-05
CHUNK = 2048
BIAS_ROWS = 16
F32 = jnp.float32
BF16 = jnp.bfloat16


def layer_norm(values, gain_row, shift_row):
    average = jnp.mean(values, axis=-1, keepdims=True)
    centered = values - average
    variance = jnp.mean(centered * centered, axis=-1, keepdims=True)
    return centered * lax.rsqrt(variance + EPSILON) * gain_row + shift_row


def silu(values):
    return 0.5 * values * (1.0 + jnp.tanh(0.5 * values))


def dot(a, b):
    return jnp.dot(a, b, preferred_element_type=F32)


def kernel_call(body, out_shape, operands, spaces, scratch=(), outs=None, flops=0, vmem=24 << 20):
    if outs is None:
        outs = jax.tree.map(lambda _: pltpu.VMEM, out_shape)
    return pl.pallas_call(
        body,
        out_shape=out_shape,
        in_specs=[pl.BlockSpec(memory_space=space) for space in spaces],
        out_specs=jax.tree.map(lambda space: pl.BlockSpec(memory_space=space), outs),
        scratch_shapes=list(scratch),
        compiler_params=pltpu.CompilerParams(vmem_limit_bytes=vmem),
        cost_estimate=pl.CostEstimate(flops=flops, bytes_accessed=4 << 20, transcendentals=0),
    )(*operands)


def started(pairs, sem):
    copies = [pltpu.make_async_copy(src, dst, sem.at[i]) for i, (src, dst) in enumerate(pairs)]
    for copy in copies:
        copy.start()
    return copies


def wait_all(copies):
    for copy in copies:
        copy.wait()


def embed_hidden(order, section_id, place_ref, x_hbm, w_hbm, out_hbm, bias_ref, *refs):
    out_w = refs[0]
    outs = refs[1 : 1 + len(order)]
    x_ref, w_ref, sem = refs[1 + len(order) :]
    copies = started([(x_hbm, x_ref), (w_hbm, w_ref), (out_hbm.at[section_id], out_w)], sem)
    wait_all(copies)
    me = place_ref[0]
    bias = bias_ref[section_id : section_id + 1, :]
    rows = outs[0].shape[0]
    for other, out in zip(order, outs):
        begin = pl.multiple_of((me ^ other) * rows, rows)
        out[...] = silu(dot(x_ref[pl.ds(begin, rows), :], w_ref[...]) + bias).astype(BF16)


def embed_finish(section_id, count, *refs):
    hidden = jnp.concatenate([r[...] for r in refs[:count]], axis=1)
    weights = jnp.concatenate([r[...] for r in refs[count : 2 * count]], axis=0)
    gain, shift, out = refs[2 * count :]
    row = slice(section_id, section_id + 1)
    out[...] = layer_norm(dot(hidden, weights), gain[row, :], shift[row, :]).astype(BF16)


def pack(first_id, place_ref, in_hbm, out_hbm, bias_ref, *refs):
    outs = refs[:-2]
    terms, sem = refs[-2:]
    part = place_ref[2]
    inner, width = in_hbm.shape[1:]
    latent = out_hbm.shape[2]
    pairs = []
    for i, out in enumerate(outs):
        section_id = first_id + (i - i % 2) + (part if i % 2 == 0 else 1 - part)
        pairs.append((in_hbm.at[section_id], out.at[pl.ds(0, inner)]))
        for b in range(0, latent, width):
            pairs.append((out_hbm.at[section_id, :, pl.ds(b, width)], out.at[pl.ds(inner + b, width)]))
        rest = bias_ref[pl.ds(section_id, 1), :]
        index = lax.broadcasted_iota(jnp.int32, (BIAS_ROWS, width), 0)
        value = jnp.zeros((BIAS_ROWS, width), F32)
        for term in range(3):
            head = rest.astype(BF16).astype(F32)
            value = jnp.where(index == term, head, value)
            rest = rest - head
        terms[i] = value.astype(BF16)
        pairs.append((terms.at[i], out.at[pl.ds(inner + latent, BIAS_ROWS)]))
    wait_all(started(pairs, sem))


def route(bits, direct, caps, counts, edges, place_ref, tables, from_g, from_m, from_d, to_g, to_m, pos, pos_w, *outs):
    ids_g, ids_m, ids_d, col_g, col_m, row_g, row_m, mesh_out = outs
    me, band = place_ref[0], place_ref[1]
    bands = tables.shape[0]

    def column(row):
        return jnp.broadcast_to(row, (8, row.shape[1])).T[:, :1].astype(jnp.int32)

    begin = 0
    for cap, count, size, senders, out in zip(caps, counts, edges, (from_g, from_m, from_d), (ids_g, ids_m, ids_d)):
        padded = -(-cap // 128) * 128
        names = senders[:, pl.ds(pl.multiple_of(me * size, size), size)]
        total = jnp.zeros((16, size), F32)
        for s in range(bands):
            value = tables[s : s + 1, begin : begin + padded]
            other = (value >> (count.bit_length() - 1)) ^ me
            slot = jnp.zeros_like(other)
            for i, bit in enumerate(bits):
                slot = slot + jnp.where((other & bit) != 0, 1 << i, 0)
            source = s
            if direct:
                source = jnp.where(band >= s, band - s, band - s + bands)
            value = (slot * bands + source) * count + (value & (count - 1))
            index = lax.broadcasted_iota(jnp.int32, (16, padded), 0)
            high = jnp.broadcast_to((value >> 7).astype(F32), index.shape)
            low = jnp.broadcast_to((value & 127).astype(F32), index.shape)
            digits = jnp.where(index == 0, high, jnp.where(index == 1, low, 0.0)).astype(BF16)
            slots = lax.broadcasted_iota(jnp.int32, (padded, size), 0)
            hot = jnp.where((slots + s * cap == names) & (slots < cap), 1.0, 0.0).astype(BF16)
            total = total + dot(digits, hot)
        out[...] = column(total[0:1] * 128.0 + total[1:2])
        begin += padded
    for size, rows, to, col, row in ((edges[0], mesh_out.shape[0], to_g, col_g, row_g), (edges[1], mesh_out.shape[0], to_m, col_m, row_m)):
        mine = to[:, pl.ds(pl.multiple_of(me * size, size), size)] - me * rows
        row[...] = mine
        col[...] = column(mine.astype(F32))
    rows = mesh_out.shape[0]
    mine = pos[:, pl.ds(pl.multiple_of(me * rows, rows), rows)]
    index = lax.broadcasted_iota(jnp.int32, (8, rows), 0)
    stacked = jnp.zeros((8, rows), F32)
    for t in range(3):
        stacked = jnp.where(index == t, mine[t : t + 1, :], stacked)
    turned = stacked.T
    mesh = turned[:, 0:1] * pos_w[0:1, :] + turned[:, 1:2] * pos_w[1:2, :]
    mesh_out[...] = (mesh + turned[:, 2:3] * pos_w[2:3, :]).astype(BF16)


def phase(section_id, tables, places, last, *refs):
    place_ref = refs[0]
    table_refs = refs[1 : 1 + tables]
    refs = refs[1 + tables :]
    pieces = refs[: len(places)]
    gain, shift, ids, own_ref, *rest = refs[len(places) :]
    if last:
        head_hbm, out_hbm, table, w_in, w_out, w_bias, table_sem, w_sem, head, out, head_sem = rest
    else:
        recv_col, recv_row, out, table, w_in, w_out, w_bias, table_sem, w_sem = rest
    own = own_ref[...]
    rows, latent = own.shape
    width = pieces[0].shape[1]
    edges = ids.shape[0]
    part = place_ref[2]
    pairs = []
    begin = 0
    for ref in table_refs:
        pairs.append((ref, table.at[pl.ds(begin, ref.shape[0])]))
        begin += ref.shape[0]
    t_copies = started(pairs, table_sem)
    pairs = []
    for (kind, slot), ref in zip(places, pieces):
        t = part if kind == 0 else 1 - part
        columns = pl.ds(slot * width, width)
        pairs.append((ref.at[pl.ds(0, 2 * latent)], w_in.at[t, :, columns]))
        for b in range(0, latent, width):
            pairs.append((ref.at[pl.ds(2 * latent + b, width)], w_out.at[t, columns, pl.ds(b, width)]))
        pairs.append((ref.at[pl.ds(3 * latent, BIAS_ROWS)], w_bias.at[t, :, columns]))
    w_copies = started(pairs, w_sem)
    if last:
        h_copies = started([(head_hbm, head)], head_sem)
        degree = edges // rows
        edge = lax.broadcasted_iota(jnp.int32, (edges, rows), 0)
        node = lax.broadcasted_iota(jnp.int32, (edges, rows), 1) * degree
        spread = (edge >= node) & (edge < node + degree)
        edge = lax.broadcasted_iota(jnp.int32, (rows, edges), 1)
        node = lax.broadcasted_iota(jnp.int32, (rows, edges), 0) * degree
        collect = (edge >= node) & (edge < node + degree)
    else:
        spread = recv_col[...] == lax.broadcasted_iota(jnp.int32, (edges, rows), 1)
        collect = lax.broadcasted_iota(jnp.int32, (rows, edges), 0) == recv_row[...]
    received = dot(spread.astype(BF16), own).astype(BF16)
    wait_all(t_copies)
    sent = None
    for start in range(0, begin, CHUNK):
        size = min(CHUNK, begin - start)
        hot = ids[...] == lax.broadcasted_iota(jnp.int32, (edges, size), 1) + start
        term = dot(hot.astype(BF16), table[pl.ds(start, size), :])
        sent = term if sent is None else sent + term
    wait_all(w_copies)

    def mlp(t, first, second):
        terms = w_bias[t].astype(F32)
        bias = (terms[0:1] + terms[1:2]) + terms[2:3]
        preact = dot(first, w_in[t, :latent, :]) + dot(second, w_in[t, latent:, :]) + bias
        row = slice(section_id + t, section_id + t + 1)
        return layer_norm(dot(silu(preact).astype(BF16), w_out[t]), gain[row, :], shift[row, :])

    messages = mlp(0, sent.astype(BF16), received).astype(BF16)
    aggregate = dot(collect.astype(BF16), messages).astype(BF16)
    updated = (own.astype(F32) + mlp(1, own, aggregate)).astype(BF16)
    if last:
        wait_all(h_copies)
        out[...] = dot(updated, head[...])
        wait_all(started([(out, out_hbm)], head_sem))
    else:
        out[...] = updated


def local(
    x_grid,
    mesh_pos,
    pos_weight,
    embed_in,
    pair_in,
    pair_out,
    hidden_bias,
    norm_gain,
    norm_shift,
    head,
    g2m_take,
    g2m_from,
    g2m_to,
    m2m_take,
    m2m_from,
    m2m_to,
    m2g_take,
    m2g_from,
):
    quarters = lax.axis_size("feat")
    bands = lax.axis_size("band")
    feat_index = lax.axis_index("feat")
    band_index = lax.axis_index("band")
    latent = norm_gain.shape[1]
    width = hidden_bias.shape[1]
    embed_id = pair_out.shape[0] - 1
    band_mesh = mesh_pos.shape[1]
    band_grid = x_grid.shape[0]
    mesh_rows = band_mesh // quarters
    grid_rows = band_grid // quarters
    direct = bands <= 4
    part_index = lax.axis_index("parts")
    vmem, hbm, scalar = pltpu.VMEM, pltpu.HBM, pltpu.SMEM
    place = jnp.stack([feat_index, band_index, part_index]).astype(jnp.int32)

    bits = [1 << b for b in reversed(range(quarters.bit_length() - 1))]
    order = [0]
    for bit in bits:
        order = order + [other ^ bit for other in order]

    def swap(value, bit):
        return lax.ppermute(value, "feat", [(f, f ^ bit) for f in range(quarters)])

    def pieces(value):
        parts = [value]
        for bit in bits:
            parts = parts + [swap(part, bit) for part in parts]
        return parts

    def everyone(rows):
        if direct:
            parts = [rows] + [
                lax.ppermute(rows, "band", [(b, (b + step) % bands) for b in range(bands)])
                for step in range(1, bands)
            ]
            for bit in bits:
                parts = parts + [swap(part, bit) for part in parts]
            return parts
        parts = [rows]
        for bit in bits[:-1]:
            parts = parts + [swap(part, bit) for part in parts]
        parts = [lax.all_gather(part, "band", axis=0, tiled=True) for part in parts]
        return parts + [swap(part, bits[-1]) for part in parts]

    hidden = kernel_call(
        functools.partial(embed_hidden, order, embed_id),
        [jax.ShapeDtypeStruct((width, latent), BF16)]
        + [jax.ShapeDtypeStruct((grid_rows, width), BF16)] * quarters,
        (place, x_grid, embed_in, pair_out, hidden_bias),
        (scalar, hbm, hbm, hbm, vmem),
        scratch=(
            pltpu.VMEM(x_grid.shape, BF16),
            pltpu.VMEM(embed_in.shape, BF16),
            pltpu.SemaphoreType.DMA((3,)),
        ),
    )
    out_pieces = pieces(hidden[0])
    hidden = [hidden[1]] + [swap(h, other) for h, other in zip(hidden[2:], order[1:])]

    def packs(first_id, sections):
        shape = jax.ShapeDtypeStruct((3 * latent + BIAS_ROWS, width), BF16)
        return kernel_call(
            functools.partial(pack, first_id),
            [shape] * sections,
            (place, pair_in, pair_out, hidden_bias),
            (scalar, hbm, hbm, vmem),
            scratch=(
                pltpu.VMEM((sections, BIAS_ROWS, width), BF16),
                pltpu.SemaphoreType.DMA((sections * (2 + latent // width),)),
            ),
            outs=[hbm] * sections,
        )

    packed = packs(0, 2)
    later = packs(2, embed_id - 2)

    takes = [take[0] for take in (g2m_take, m2m_take, m2g_take)]
    caps = [take.shape[1] for take in takes]
    takes = [jnp.pad(take, ((0, 0), (0, -take.shape[1] % 128))) for take in takes]
    tables = lax.all_to_all(
        jnp.concatenate(takes, axis=1), "band", split_axis=0, concat_axis=0, tiled=True
    )
    edges = [names.shape[0] // quarters for names in (g2m_from, m2m_from, m2g_from)]
    columns = [jax.ShapeDtypeStruct((n, 1), jnp.int32) for n in edges + edges[:2]]
    lines = [jax.ShapeDtypeStruct((1, n), jnp.int32) for n in edges[:2]]
    shape = jax.ShapeDtypeStruct((mesh_rows, latent), BF16)
    routed = kernel_call(
        functools.partial(route, bits, direct, caps, (grid_rows, mesh_rows, mesh_rows), edges),
        [*columns, *lines, shape],
        (place, tables, *[v[None, :] for v in (g2m_from, m2m_from, m2g_from, g2m_to, m2m_to)], mesh_pos, pos_weight),
        (scalar,) + (vmem,) * 8,
    )
    hidden, out_pieces, routed, later = lax.optimization_barrier((hidden, out_pieces, routed, later))
    ids_g, ids_m, ids_d, col_g, col_m, row_g, row_m, mesh = routed
    packed = packed + later
    grid = kernel_call(
        functools.partial(embed_finish, embed_id, quarters),
        jax.ShapeDtypeStruct((grid_rows, latent), BF16),
        (*hidden, *out_pieces, norm_gain, norm_shift),
        (vmem,) * (2 * quarters + 2),
    )

    def group(section_id, after):
        first, second = packed[section_id : section_id + 2]
        if after is not None:
            first, second, _ = lax.optimization_barrier((first, second, after))
        across = swap(first, bits[0])
        over = lax.ppermute(across, "parts", [(0, 1), (1, 0)])
        found = [((0, 0), first), ((1, 0), second), ((0, 1), across), ((1, 1), over)]
        for i, bit in enumerate(bits[1:]):
            found = found + [((kind, slot + (2 << i)), swap(piece, bit)) for (kind, slot), piece in found]
        return found

    def run(section_id, table, after, ids, own_latent, extra, last=False):
        rows = sum(part.shape[0] for part in table)
        weights = group(section_id, after)
        places = [p for p, _ in weights]
        weights = [piece for _, piece in weights]
        scratch = [
            pltpu.VMEM((rows, latent), BF16),
            pltpu.VMEM((2, 2 * latent, latent), BF16),
            pltpu.VMEM((2, latent, latent), BF16),
            pltpu.VMEM((2, BIAS_ROWS, latent), BF16),
            pltpu.SemaphoreType.DMA((len(table),)),
            pltpu.SemaphoreType.DMA((len(weights) * (2 + quarters),)),
        ]
        out_shape = jax.ShapeDtypeStruct(own_latent.shape, BF16)
        if last:
            out_shape = jax.ShapeDtypeStruct((own_latent.shape[0], head.shape[1]), F32)
            scratch += [
                pltpu.VMEM(head.shape, BF16),
                pltpu.VMEM(out_shape.shape, F32),
                pltpu.SemaphoreType.DMA((1,)),
            ]
        return kernel_call(
            functools.partial(phase, section_id, len(table), places, last),
            out_shape,
            (place, *table, *weights, norm_gain, norm_shift, ids, own_latent, *extra),
            (scalar,) + (hbm,) * (len(table) + len(weights)) + (vmem,) * 4 + ((hbm,) if last else (vmem, vmem)),
            scratch=scratch,
            outs=hbm if last else vmem,
            flops=2 * ids.shape[0] * latent * (rows + 3 * latent),
            vmem=(20 << 20) + 2 * rows * latent * 2,
        )

    def held(table):
        return table[2 * bands - 1] if direct else None

    table = everyone(grid)
    mesh = run(0, table, None, ids_g, mesh, (col_g, row_g))
    for layer_id in range(LAYERS):
        after = held(table)
        table = everyone(mesh)
        mesh = run(2 + 2 * layer_id, table, after, ids_m, mesh, (col_m, row_m))
    return run(2 * LAYERS + 2, everyone(mesh), held(table), ids_d, grid, (head,), True)


def solution(mesh):
    return jax.shard_map(
        local,
        mesh=mesh,
        in_specs=(
            P(("parts", "band"), None),
            P(None, "band"),
            P(),
            P(None, "feat"),
            P(None, None, "feat"),
            P(None, "feat", None),
            P(None, "feat"),
            P(),
            P(),
            P(),
            P("band", None, None),
            P("band"),
            P("band"),
            P("band", None, None),
            P("band"),
            P("band"),
            P("band", None, None),
            P("band"),
        ),
        out_specs=P(("parts", "band", "feat"), None),
        check_vma=False,
    )
```

time: 255 us -> 214 us (0.84)
  local copies, waits for them, and re-layouts: 76.5 us -> 34.8 us
  Pallas kernels: 27.5 us -> 38 us
  other arithmetic: 7.66 us -> 0.08 us
  starting transfers between devices: 63.9 us -> 58.8 us
  waiting for transfers between devices: 76.8 us -> 81.2 us
    unnamed x211 -> x111, local copies, waits for them, and re-layouts: 56.7 us -> 32.8 us
    pallas_call x6 -> x9, Pallas kernels: 27.5 us -> 38 us  [kernel_call(): pl.pallas_call(body, out_shape=out_shape, in_specs=[pl.BlockSpec(memory_s...]
    gather x3 -> x0, local copies, waits for them, and re-layouts: 8.76 us -> none  [sender_ids(): return rows.reshape(-1).at[senders].get(mode='promise_in_bounds')]
    ppermute x77 -> x74, waiting for transfers between devices: 44.6 us -> 49.1 us  [swap(): return lax.ppermute(value, 'feat', [(f, f ^ bit) for f in range(quarters)])]
    concatenate x6 -> x1, other arithmetic: 4.19 us -> 0.01 us  [local(): jnp.concatenate(takes, axis=1)]
    dynamic_slice x3 -> x0, local copies, waits for them, and re-layouts: 3.24 us -> none  [the longest x1 2.46 us: packed(): turned = lax.dynamic_index_in_dim(pair_out, section_id, 0, False)]
    transpose x9 -> x0, local copies, waits for them, and re-layouts: 3.05 us -> none  [the longest x8 2.99 us: packed(): turned = turned.transpose(1, 0, 2).reshape(latent, width)]
    ppermute x12, starting transfers between devices: 21.4 us -> 18.5 us  [everyone(): lax.ppermute(rows, 'band', [(b, (b + step) % bands) for b in range(bands)])]
  transfers between devices with their start and end apart: 94 -> 91, of which waited for: 27 -> 33; matrix products, arithmetic and copies ran while one was open for 12% -> 1% of each run, Pallas kernels for 8% -> 13%
where the time goes in v5:
time: 214 us; the launch traced here: 213 us
  waiting for transfers between devices  81.2 us (38%)
  starting transfers between devices  58.8 us (27%)
  Pallas kernels  38 us (18%)
  local copies, waits for them, and re-layouts  34.8 us (16%)
    ppermute x74, waiting for transfers between devices, swap(): return lax.ppermute(value, 'feat', [(f, f ^ bit) for f in range(quarters)])  49.1 us
    pallas_call x9, Pallas kernels, kernel_call(): pl.pallas_call(body, out_shape=out_shape, in_specs=[pl.BlockSpec(memory_s...  38 us
    unnamed x111, local copies, waits for them, and re-layouts  32.8 us
    ppermute x12, waiting for transfers between devices, everyone(): lax.ppermute(rows, 'band', [(b, (b + step) % bands) for b in range(bands)])  32.1 us
    ppermute x74, starting transfers between devices, swap(): return lax.ppermute(value, 'feat', [(f, f ^ bit) for f in range(quarters)])  30.9 us
    ppermute x12, starting transfers between devices, everyone(): lax.ppermute(rows, 'band', [(b, (b + step) % bands) for b in range(bands)])  18.5 us
    all_to_all x1, starting transfers between devices, local(): lax.all_to_all(jnp.concatenate(takes, axis=1), 'band', split_axis=0, conc...  5.41 us
  transfers between devices with their start and end apart: 91, of which 33 were waited for; matrix products, arithmetic and copies ran while one was open for 1% of the time, Pallas kernels for 13%

profile of v5, /device:TPU:0, one launch (start us, length us, event | category | flops | bytes accessed | tf_op | source)
XLA Modules:
  0.0 213.3 jit_solution(7704988014668426398)
XLA Ops:
  6.2 3.0 %collective-permute-start.3 = (bf16[128,512]{1,0:T(8,128)(2,1)S(1)}, bf16[128,512]{1,0:T(8,128)(2,1)}, u32[]{:S(2)}, u32[]{:S(2)}) collective-permute-start(bf16[128,512]{1,0:T(8,128)(2,1)S(1)} %get-tuple-element.77.refs_4_), channel_id=1, source_target_pairs={{0,2},{1,3},{2,0},{3,1},{4,6},{5,7},{6,4},{7,5},{8,10},{9,11},{10,... | collective-permute-start | bytes 393224 | tf_op jit(solution)/shard_map/ppermute | solution.py:264
  13.5 5.4 %all-to-all-start = ((s32[4,1,1152]{2,1,0:T(1,128)}), s32[4,1,1152]{2,1,0:T(1,128)}, u32[]{:S(2)}, u32[]{:S(2)}) async-start(s32[4,1,1152]{2,1,0:T(1,128)} %all_to_all.7), calls=%async_computation | async-start | bytes 36864 | tf_op jit(solution)/shard_map/all_to_all | solution.py:322
  41.5 2.4 %collective-permute-start.7 = (bf16[128,512]{1,0:T(8,128)(2,1)S(1)}, bf16[128,512]{1,0:T(8,128)(2,1)S(1)}, u32[]{:S(2)}, u32[]{:S(2)}) collective-permute-start(bf16[128,512]{1,0:T(8,128)(2,1)S(1)} %shard_map.175.refs_1_.refs_28_), channel_id=1, source_target_pairs={{0,8},{4,12},{8,0},{12,4},{1,9},{5,13},{9,1},{13,5},{2,10},{6,14},... | collective-permute-start | bytes 393224 | tf_op jit(solution)/shard_map/ppermute | solution.py:275
  45.7 5.8 %collective-permute-done.7.refs_3_ = bf16[128,512]{1,0:T(8,128)(2,1)S(1)} collective-permute-done((bf16[128,512]{1,0:T(8,128)(2,1)S(1)}, bf16[128,512]{1,0:T(8,128)(2,1)S(1)}, u32[]{:S(2)}, u32[]{:S(2)}) %collective-permute-start.7) | collective-permute-done | bytes 131104 | tf_op jit(solution)/shard_map/ppermute | solution.py:275
  52.1 4.8 %collective-permute-done.9.refs_5_ = bf16[128,512]{1,0:T(8,128)(2,1)S(1)} collective-permute-done((bf16[128,512]{1,0:T(8,128)(2,1)S(1)}, bf16[128,512]{1,0:T(8,128)(2,1)S(1)}, u32[]{:S(2)}, u32[]{:S(2)}) %collective-permute-start.9) | collective-permute-done | bytes 131104 | tf_op jit(solution)/shard_map/ppermute | solution.py:264
  69.7 5.5 %collective-permute-done.42.refs_19_ = bf16[1552,128]{1,0:T(8,128)(2,1)S(1)} collective-permute-done((bf16[1552,128]{1,0:T(8,128)(2,1)S(1)}, bf16[1552,128]{1,0:T(8,128)(2,1)S(1)}, u32[]{:S(2)}, u32[]{:S(2)}) %collective-permute-start.42) | collective-permute-done | bytes 397344 | tf_op jit(solution)/shard_map/ppermute | solution.py:264
  76.7 7.3 %shard_map.177.refs_1_.refs_28_ = bf16[128,512]{1,0:T(8,128)(2,1)S(1)} custom-call(s32[3]{0:T(128)S(1)} %pad_add_fusion.1.place_ref.refs_0_, bf16[128,512]{1,0:T(8,128)(2,1)S(1)} %shard_map.175.refs_1_.refs_28_, bf16[128,512]{1,0:T(8,128)(2,1)S(1)} %collective-permute-done.6.refs_2_, bf16[128,512]{1,0:T(8,128)(2,1)S(1)} %collective-permute-done.7.refs_3_, ...), custom_call_target="tpu_custom_call" | custom-call | flops 939524096 | bytes 4194304 | tf_op jit(solution)/shard_map/pallas_call | solution.py:36
  85.0 4.0 %collective-permute-start.28 = (bf16[128,512]{1,0:T(8,128)(2,1)S(1)}, bf16[128,512]{1,0:T(8,128)(2,1)S(1)}, u32[]{:S(2)}, u32[]{:S(2)}) collective-permute-start(bf16[128,512]{1,0:T(8,128)(2,1)S(1)} %shard_map.177.refs_1_.refs_28_), channel_id=1, source_target_pairs={{0,8},{4,12},{8,0},{12,4},{1,9},{5,13},{9,1},{13,5},{2,10},{6,14},... | collective-permute-start | bytes 393224 | tf_op jit(solution)/shard_map/ppermute | solution.py:275
  89.6 3.2 %collective-permute-done.27.refs_2_ = bf16[128,512]{1,0:T(8,128)(2,1)S(1)} collective-permute-done((bf16[128,512]{1,0:T(8,128)(2,1)S(1)}, bf16[128,512]{1,0:T(8,128)(2,1)S(1)}, u32[]{:S(2)}, u32[]{:S(2)}) %collective-permute-start.27) | collective-permute-done | bytes 131104 | tf_op jit(solution)/shard_map/ppermute | solution.py:275
  92.8 5.3 %collective-permute-done.28.refs_3_ = bf16[128,512]{1,0:T(8,128)(2,1)S(1)} collective-permute-done((bf16[128,512]{1,0:T(8,128)(2,1)S(1)}, bf16[128,512]{1,0:T(8,128)(2,1)S(1)}, u32[]{:S(2)}, u32[]{:S(2)}) %collective-permute-start.28) | collective-permute-done | bytes 131104 | tf_op jit(solution)/shard_map/ppermute | solution.py:275
  100.7 3.8 %collective-permute-done.31.refs_6_ = bf16[128,512]{1,0:T(8,128)(2,1)S(1)} collective-permute-done((bf16[128,512]{1,0:T(8,128)(2,1)S(1)}, bf16[128,512]{1,0:T(8,128)(2,1)S(1)}, u32[]{:S(2)}, u32[]{:S(2)}) %collective-permute-start.31) | collective-permute-done | bytes 131104 | tf_op jit(solution)/shard_map/ppermute | solution.py:264
  104.5 2.8 %collective-permute-done.32.refs_7_ = bf16[128,512]{1,0:T(8,128)(2,1)S(1)} collective-permute-done((bf16[128,512]{1,0:T(8,128)(2,1)S(1)}, bf16[128,512]{1,0:T(8,128)(2,1)S(1)}, u32[]{:S(2)}, u32[]{:S(2)}) %collective-permute-start.32) | collective-permute-done | bytes 131104 | tf_op jit(solution)/shard_map/ppermute | solution.py:264
  111.3 8.3 %shard_map.178.refs_1_.refs_28_ = bf16[128,512]{1,0:T(8,128)(2,1)S(1)} custom-call(s32[3]{0:T(128)S(1)} %pad_add_fusion.1.place_ref.refs_0_, bf16[128,512]{1,0:T(8,128)(2,1)S(1)} %shard_map.177.refs_1_.refs_28_, bf16[128,512]{1,0:T(8,128)(2,1)S(1)} %collective-permute-done.27.refs_2_, bf16[128,512]{1,0:T(8,128)(2,1)S(1)} %collective-permute-done.28.refs_3_, ...), custom_call_target="tpu_custom_call" | custom-call | flops 1879048192 | bytes 4194304 | tf_op jit(solution)/shard_map/pallas_call | solution.py:36
  120.7 2.4 %collective-permute-start.49 = (bf16[128,512]{1,0:T(8,128)(2,1)S(1)}, bf16[128,512]{1,0:T(8,128)(2,1)S(1)}, u32[]{:S(2)}, u32[]{:S(2)}) collective-permute-start(bf16[128,512]{1,0:T(8,128)(2,1)S(1)} %shard_map.178.refs_1_.refs_28_), channel_id=1, source_target_pairs={{0,8},{4,12},{8,0},{12,4},{1,9},{5,13},{9,1},{13,5},{2,10},{6,14},... | collective-permute-start | bytes 393224 | tf_op jit(solution)/shard_map/ppermute | solution.py:275
  123.1 4.8 %collective-permute-done.48.refs_2_ = bf16[128,512]{1,0:T(8,128)(2,1)S(1)} collective-permute-done((bf16[128,512]{1,0:T(8,128)(2,1)S(1)}, bf16[128,512]{1,0:T(8,128)(2,1)S(1)}, u32[]{:S(2)}, u32[]{:S(2)}) %collective-permute-start.48) | collective-permute-done | bytes 131104 | tf_op jit(solution)/shard_map/ppermute | solution.py:275
  128.1 4.8 %collective-permute-done.49.refs_3_ = bf16[128,512]{1,0:T(8,128)(2,1)S(1)} collective-permute-done((bf16[128,512]{1,0:T(8,128)(2,1)S(1)}, bf16[128,512]{1,0:T(8,128)(2,1)S(1)}, u32[]{:S(2)}, u32[]{:S(2)}) %collective-permute-start.49) | collective-permute-done | bytes 131104 | tf_op jit(solution)/shard_map/ppermute | solution.py:275
  135.3 2.8 %collective-permute-done.51.refs_5_ = bf16[128,512]{1,0:T(8,128)(2,1)S(1)} collective-permute-done((bf16[128,512]{1,0:T(8,128)(2,1)S(1)}, bf16[128,512]{1,0:T(8,128)(2,1)S(1)}, u32[]{:S(2)}, u32[]{:S(2)}) %collective-permute-start.51) | collective-permute-done | bytes 131104 | tf_op jit(solution)/shard_map/ppermute | solution.py:264
  141.2 3.3 %collective-permute-done.52.refs_6_ = bf16[128,512]{1,0:T(8,128)(2,1)S(1)} collective-permute-done((bf16[128,512]{1,0:T(8,128)(2,1)S(1)}, bf16[128,512]{1,0:T(8,128)(2,1)S(1)}, u32[]{:S(2)}, u32[]{:S(2)}) %collective-permute-start.52) | collective-permute-done | bytes 131104 | tf_op jit(solution)/shard_map/ppermute | solution.py:264
  153.0 5.1 %collective-permute-done.84.refs_19_ = bf16[1552,128]{1,0:T(8,128)(2,1)S(1)} collective-permute-done((bf16[1552,128]{1,0:T(8,128)(2,1)S(1)}, bf16[1552,128]{1,0:T(8,128)(2,1)S(1)}, u32[]{:S(2)}, u32[]{:S(2)}) %collective-permute-start.84) | collective-permute-done | bytes 397344 | tf_op jit(solution)/shard_map/ppermute | solution.py:264
  158.7 8.3 %shard_map.179.refs_1_ = bf16[128,512]{1,0:T(8,128)(2,1)S(1)} custom-call(s32[3]{0:T(128)S(1)} %pad_add_fusion.1.place_ref.refs_0_, bf16[128,512]{1,0:T(8,128)(2,1)S(1)} %shard_map.178.refs_1_.refs_28_, bf16[128,512]{1,0:T(8,128)(2,1)S(1)} %collective-permute-done.48.refs_2_, bf16[128,512]{1,0:T(8,128)(2,1)S(1)} %collective-permute-done.49.refs_3_, ...), custom_call_target="tpu_custom_call" | custom-call | flops 1879048192 | bytes 4194304 | tf_op jit(solution)/shard_map/pallas_call | solution.py:36
  167.9 2.9 %collective-permute-start.70 = (bf16[128,512]{1,0:T(8,128)(2,1)S(1)}, bf16[128,512]{1,0:T(8,128)(2,1)S(1)}, u32[]{:S(2)}, u32[]{:S(2)}) collective-permute-start(bf16[128,512]{1,0:T(8,128)(2,1)S(1)} %shard_map.179.refs_1_), channel_id=1, source_target_pairs={{0,8},{4,12},{8,0},{12,4},{1,9},{5,13},{9,1},{13,5},{2,10},{6,14},... | collective-permute-start | bytes 393224 | tf_op jit(solution)/shard_map/ppermute | solution.py:275
  172.7 2.6 %collective-permute-done.69.refs_2_ = bf16[128,512]{1,0:T(8,128)(2,1)S(1)} collective-permute-done((bf16[128,512]{1,0:T(8,128)(2,1)S(1)}, bf16[128,512]{1,0:T(8,128)(2,1)S(1)}, u32[]{:S(2)}, u32[]{:S(2)}) %collective-permute-start.69) | collective-permute-done | bytes 131104 | tf_op jit(solution)/shard_map/ppermute | solution.py:275
  175.9 4.5 %collective-permute-done.70.refs_3_ = bf16[128,512]{1,0:T(8,128)(2,1)S(1)} collective-permute-done((bf16[128,512]{1,0:T(8,128)(2,1)S(1)}, bf16[128,512]{1,0:T(8,128)(2,1)S(1)}, u32[]{:S(2)}, u32[]{:S(2)}) %collective-permute-start.70) | collective-permute-done | bytes 131104 | tf_op jit(solution)/shard_map/ppermute | solution.py:275
  205.4 7.1 %shard_map.180 = f32[128,227]{1,0:T(8,128)S(1)} custom-call(s32[3]{0:T(128)S(1)} %pad_add_fusion.1.place_ref.refs_0_, bf16[128,512]{1,0:T(8,128)(2,1)S(1)} %copy-done.13, bf16[128,512]{1,0:T(8,128)(2,1)S(1)} %copy-done.15, bf16[128,512]{1,0:T(8,128)(2,1)S(1)} %copy-done.17, bf16[128,512]{1,0:T(8,128)(2,1)S(1)} %copy-done.19, ...), custom_call_target="tpu_custom_call" | custom-call | flops 1409286144 | bytes 4194304 | tf_op jit(solution)/shard_map/pallas_call | solution.py:36
  (283 shorter events, 102.7 us)
Async XLA Ops:
  9.2 24.9 %collective-permute-start.4 = (bf16[128,512]{1,0:T(8,128)(2,1)S(1)}, bf16[128,512]{1,0:T(8,128)(2,1)}, u32[]{:S(2)}, u32[]{:S(2)}) collective-permute-start(bf16[128,512]{1,0:T(8,128)(2,1)S(1)} %get-tuple-element.77.refs_4_), channel_id=1, source_target_pairs={{0,1},{1,0},{2,3},{3,2},{4,5},{5,4},{6,7},{7,6},{8,9},{9,8},{10,11... | collective-permute-start | bytes 393224 | tf_op jit(solution)/shard_map/ppermute | solution.py:264
  9.2 24.8 %collective-permute-start = (bf16[128,128]{1,0:T(8,128)(2,1)}, bf16[128,128]{1,0:T(8,128)(2,1)S(1)}, u32[]{:S(2)}, u32[]{:S(2)}) collective-permute-start(bf16[128,128]{1,0:T(8,128)(2,1)} %get-tuple-element.55), channel_id=1, source_target_pairs={{0,2},{1,3},{2,0},{3,1},{4,6},{5,7},{6,4},{7,5},{8,10},{9,11},{10,... | collective-permute-start | bytes 98312 | tf_op jit(solution)/shard_map/ppermute | solution.py:264
  9.3 24.7 %collective-permute-start.1 = (bf16[128,128]{1,0:T(8,128)(2,1)}, bf16[128,128]{1,0:T(8,128)(2,1)}, u32[]{:S(2)}, u32[]{:S(2)}) collective-permute-start(bf16[128,128]{1,0:T(8,128)(2,1)} %get-tuple-element.56), channel_id=1, source_target_pairs={{0,1},{1,0},{2,3},{3,2},{4,5},{5,4},{6,7},{7,6},{8,9},{9,8},{10,11... | collective-permute-start | bytes 98312 | tf_op jit(solution)/shard_map/ppermute | solution.py:264
  9.7 24.3 %collective-permute-start.2 = (bf16[128,128]{1,0:T(8,128)(2,1)}, bf16[128,128]{1,0:T(8,128)(2,1)}, u32[]{:S(2)}, u32[]{:S(2)}) collective-permute-start(bf16[128,128]{1,0:T(8,128)(2,1)} %get-tuple-element.57), channel_id=1, source_target_pairs={{0,3},{1,2},{2,1},{3,0},{4,7},{5,6},{6,5},{7,4},{8,11},{9,10},{10,... | collective-permute-start | bytes 98312 | tf_op jit(solution)/shard_map/ppermute | solution.py:264
  12.9 21.1 %collective-permute-start.5 = (bf16[128,512]{1,0:T(8,128)(2,1)}, bf16[128,512]{1,0:T(8,128)(2,1)}, u32[]{:S(2)}, u32[]{:S(2)}) collective-permute-start(bf16[128,512]{1,0:T(8,128)(2,1)} %collective-permute-done.3.refs_5_), channel_id=1, source_target_pairs={{0,1},{1,0},{2,3},{3,2},{4,5},{5,4},{6,7},{7,6},{8,9},{9,8},{10,11... | collective-permute-start | bytes 393224 | tf_op jit(solution)/shard_map/ppermute | solution.py:264
  13.5 13.4 %all-to-all-start = ((s32[4,1,1152]{2,1,0:T(1,128)}), s32[4,1,1152]{2,1,0:T(1,128)}, u32[]{:S(2)}, u32[]{:S(2)}) async-start(s32[4,1,1152]{2,1,0:T(1,128)} %all_to_all.7), calls=%async_computation | async-start | bytes 36864 | tf_op jit(solution)/shard_map/all_to_all | solution.py:322
  39.4 19.5 %collective-permute-start.21 = (bf16[1552,128]{1,0:T(8,128)(2,1)S(1)}, bf16[1552,128]{1,0:T(8,128)(2,1)S(1)}, u32[]{:S(2)}, u32[]{:S(2)}) collective-permute-start(bf16[1552,128]{1,0:T(8,128)(2,1)S(1)} %get-tuple-element.81.refs_17_), channel_id=1, source_target_pairs={{0,2},{1,3},{2,0},{3,1},{4,6},{5,7},{6,4},{7,5},{8,10},{9,11},{10,... | collective-permute-start | bytes 1191944 | tf_op jit(solution)/shard_map/ppermute | solution.py:264
  41.0 19.5 %collective-permute-start.23 = (bf16[1552,128]{1,0:T(8,128)(2,1)S(1)}, bf16[1552,128]{1,0:T(8,128)(2,1)S(1)}, u32[]{:S(2)}, u32[]{:S(2)}) collective-permute-start(bf16[1552,128]{1,0:T(8,128)(2,1)S(1)} %get-tuple-element.81.refs_17_), channel_id=1, source_target_pairs={{0,1},{1,0},{2,3},{3,2},{4,5},{5,4},{6,7},{7,6},{8,9},{9,8},{10,11... | collective-permute-start | bytes 1191944 | tf_op jit(solution)/shard_map/ppermute | solution.py:264
  41.0 20.0 %collective-permute-start.24 = (bf16[1552,128]{1,0:T(8,128)(2,1)S(1)}, bf16[1552,128]{1,0:T(8,128)(2,1)S(1)}, u32[]{:S(2)}, u32[]{:S(2)}) collective-permute-start(bf16[1552,128]{1,0:T(8,128)(2,1)S(1)} %get-tuple-element.82.refs_18_), channel_id=1, source_target_pairs={{0,1},{1,0},{2,3},{3,2},{4,5},{5,4},{6,7},{7,6},{8,9},{9,8},{10,11... | collective-permute-start | bytes 1191944 | tf_op jit(solution)/shard_map/ppermute | solution.py:264
  69.2 15.8 %collective-permute-start.44 = (bf16[1552,128]{1,0:T(8,128)(2,1)S(1)}, bf16[1552,128]{1,0:T(8,128)(2,1)S(1)}, u32[]{:S(2)}, u32[]{:S(2)}) collective-permute-start(bf16[1552,128]{1,0:T(8,128)(2,1)S(1)} %copy-done.47), channel_id=1, source_target_pairs={{0,1},{1,0},{2,3},{3,2},{4,5},{5,4},{6,7},{7,6},{8,9},{9,8},{10,11... | collective-permute-start | bytes 1191944 | tf_op jit(solution)/shard_map/ppermute | solution.py:264
  69.4 19.6 %collective-permute-start.45 = (bf16[1552,128]{1,0:T(8,128)(2,1)S(1)}, bf16[1552,128]{1,0:T(8,128)(2,1)S(1)}, u32[]{:S(2)}, u32[]{:S(2)}) collective-permute-start(bf16[1552,128]{1,0:T(8,128)(2,1)S(1)} %copy-done.49), channel_id=1, source_target_pairs={{0,1},{1,0},{2,3},{3,2},{4,5},{5,4},{6,7},{7,6},{8,9},{9,8},{10,11... | collective-permute-start | bytes 1191944 | tf_op jit(solution)/shard_map/ppermute | solution.py:264
  75.2 13.8 %collective-permute-start.43 = (bf16[1552,128]{1,0:T(8,128)(2,1)S(1)}, bf16[1552,128]{1,0:T(8,128)(2,1)S(1)}, u32[]{:S(2)}, u32[]{:S(2)}) collective-permute-start(bf16[1552,128]{1,0:T(8,128)(2,1)S(1)} %collective-permute-done.42.refs_19_), channel_id=1, source_target_pairs={{0,16},{16,0},{1,17},{17,1},{2,18},{18,2},{3,19},{19,3},{4,20},{20... | collective-permute-start | bytes 1191944 | tf_op jit(solution)/shard_map/ppermute | solution.py:350
  85.0 13.2 %collective-permute-start.28 = (bf16[128,512]{1,0:T(8,128)(2,1)S(1)}, bf16[128,512]{1,0:T(8,128)(2,1)S(1)}, u32[]{:S(2)}, u32[]{:S(2)}) collective-permute-start(bf16[128,512]{1,0:T(8,128)(2,1)S(1)} %shard_map.177.refs_1_.refs_28_), channel_id=1, source_target_pairs={{0,8},{4,12},{8,0},{12,4},{1,9},{5,13},{9,1},{13,5},{2,10},{6,14},... | collective-permute-start | bytes 393224 | tf_op jit(solution)/shard_map/ppermute | solution.py:275
  89.0 22.3 %collective-permute-start.47 = (bf16[1552,128]{1,0:T(8,128)(2,1)S(1)}, bf16[1552,128]{1,0:T(8,128)(2,1)S(1)}, u32[]{:S(2)}, u32[]{:S(2)}) collective-permute-start(bf16[1552,128]{1,0:T(8,128)(2,1)S(1)} %collective-permute-done.43.refs_20_), channel_id=1, source_target_pairs={{0,1},{1,0},{2,3},{3,2},{4,5},{5,4},{6,7},{7,6},{8,9},{9,8},{10,11... | collective-permute-start | bytes 1191944 | tf_op jit(solution)/shard_map/ppermute | solution.py:264
  110.5 24.2 %collective-permute-start.63 = (bf16[1552,128]{1,0:T(8,128)(2,1)S(1)}, bf16[1552,128]{1,0:T(8,128)(2,1)S(1)}, u32[]{:S(2)}, u32[]{:S(2)}) collective-permute-start(bf16[1552,128]{1,0:T(8,128)(2,1)S(1)} %copy-done.43), channel_id=1, source_target_pairs={{0,2},{1,3},{2,0},{3,1},{4,6},{5,7},{6,4},{7,5},{8,10},{9,11},{10,... | collective-permute-start | bytes 1191944 | tf_op jit(solution)/shard_map/ppermute | solution.py:264
  120.2 19.9 %collective-permute-start.65 = (bf16[1552,128]{1,0:T(8,128)(2,1)S(1)}, bf16[1552,128]{1,0:T(8,128)(2,1)S(1)}, u32[]{:S(2)}, u32[]{:S(2)}) collective-permute-start(bf16[1552,128]{1,0:T(8,128)(2,1)S(1)} %copy-done.43), channel_id=1, source_target_pairs={{0,1},{1,0},{2,3},{3,2},{4,5},{5,4},{6,7},{7,6},{8,9},{9,8},{10,11... | collective-permute-start | bytes 1191944 | tf_op jit(solution)/shard_map/ppermute | solution.py:264
  120.2 20.9 %collective-permute-start.66 = (bf16[1552,128]{1,0:T(8,128)(2,1)S(1)}, bf16[1552,128]{1,0:T(8,128)(2,1)S(1)}, u32[]{:S(2)}, u32[]{:S(2)}) collective-permute-start(bf16[1552,128]{1,0:T(8,128)(2,1)S(1)} %copy-done.45), channel_id=1, source_target_pairs={{0,1},{1,0},{2,3},{3,2},{4,5},{5,4},{6,7},{7,6},{8,9},{9,8},{10,11... | collective-permute-start | bytes 1191944 | tf_op jit(solution)/shard_map/ppermute | solution.py:264
  134.7 15.1 %collective-permute-start.64 = (bf16[1552,128]{1,0:T(8,128)(2,1)S(1)}, bf16[1552,128]{1,0:T(8,128)(2,1)S(1)}, u32[]{:S(2)}, u32[]{:S(2)}) collective-permute-start(bf16[1552,128]{1,0:T(8,128)(2,1)S(1)} %collective-permute-done.63.refs_19_), channel_id=1, source_target_pairs={{0,16},{16,0},{1,17},{17,1},{2,18},{18,2},{3,19},{19,3},{4,20},{20... | collective-permute-start | bytes 1191944 | tf_op jit(solution)/shard_map/ppermute | solution.py:350
  152.5 15.5 %collective-permute-start.86 = (bf16[1552,128]{1,0:T(8,128)(2,1)S(1)}, bf16[1552,128]{1,0:T(8,128)(2,1)S(1)}, u32[]{:S(2)}, u32[]{:S(2)}) collective-permute-start(bf16[1552,128]{1,0:T(8,128)(2,1)S(1)} %copy-done.5), channel_id=1, source_target_pairs={{0,1},{1,0},{2,3},{3,2},{4,5},{5,4},{6,7},{7,6},{8,9},{9,8},{10,11... | collective-permute-start | bytes 1191944 | tf_op jit(solution)/shard_map/ppermute | solution.py:264
  152.7 18.2 %collective-permute-start.87 = (bf16[1552,128]{1,0:T(8,128)(2,1)S(1)}, bf16[1552,128]{1,0:T(8,128)(2,1)S(1)}, u32[]{:S(2)}, u32[]{:S(2)}) collective-permute-start(bf16[1552,128]{1,0:T(8,128)(2,1)S(1)} %copy-done.7), channel_id=1, source_target_pairs={{0,1},{1,0},{2,3},{3,2},{4,5},{5,4},{6,7},{7,6},{8,9},{9,8},{10,11... | collective-permute-start | bytes 1191944 | tf_op jit(solution)/shard_map/ppermute | solution.py:264
  158.1 13.1 %collective-permute-start.85 = (bf16[1552,128]{1,0:T(8,128)(2,1)S(1)}, bf16[1552,128]{1,0:T(8,128)(2,1)S(1)}, u32[]{:S(2)}, u32[]{:S(2)}) collective-permute-start(bf16[1552,128]{1,0:T(8,128)(2,1)S(1)} %collective-permute-done.84.refs_19_), channel_id=1, source_target_pairs={{0,16},{16,0},{1,17},{17,1},{2,18},{18,2},{3,19},{19,3},{4,20},{20... | collective-permute-start | bytes 1191944 | tf_op jit(solution)/shard_map/ppermute | solution.py:350
  158.7 12.5 %collective-permute-start.88 = (bf16[1552,128]{1,0:T(8,128)(2,1)S(1)}, bf16[1552,128]{1,0:T(8,128)(2,1)S(1)}, u32[]{:S(2)}, u32[]{:S(2)}) collective-permute-start(bf16[1552,128]{1,0:T(8,128)(2,1)S(1)} %collective-permute-done.84.refs_19_), channel_id=1, source_target_pairs={{0,1},{1,0},{2,3},{3,2},{4,5},{5,4},{6,7},{7,6},{8,9},{9,8},{10,11... | collective-permute-start | bytes 1191944 | tf_op jit(solution)/shard_map/ppermute | solution.py:264
  167.9 12.5 %collective-permute-start.70 = (bf16[128,512]{1,0:T(8,128)(2,1)S(1)}, bf16[128,512]{1,0:T(8,128)(2,1)S(1)}, u32[]{:S(2)}, u32[]{:S(2)}) collective-permute-start(bf16[128,512]{1,0:T(8,128)(2,1)S(1)} %shard_map.179.refs_1_), channel_id=1, source_target_pairs={{0,8},{4,12},{8,0},{12,4},{1,9},{5,13},{9,1},{13,5},{2,10},{6,14},... | collective-permute-start | bytes 393224 | tf_op jit(solution)/shard_map/ppermute | solution.py:275
  171.2 25.2 %collective-permute-start.89 = (bf16[1552,128]{1,0:T(8,128)(2,1)S(1)}, bf16[1552,128]{1,0:T(8,128)(2,1)}, u32[]{:S(2)}, u32[]{:S(2)}) collective-permute-start(bf16[1552,128]{1,0:T(8,128)(2,1)S(1)} %collective-permute-done.85.refs_20_), channel_id=1, source_target_pairs={{0,1},{1,0},{2,3},{3,2},{4,5},{5,4},{6,7},{7,6},{8,9},{9,8},{10,11... | collective-permute-start | bytes 1191944 | tf_op jit(solution)/shard_map/ppermute | solution.py:264
  (121 other events, 961.4 us)

commit v6 on v5

--- a/solution.py
+++ b/solution.py
@@ -11,6 +11,7 @@
 EPSILON = 1e-05
 CHUNK = 2048
 BIAS_ROWS = 16
+GRANT = 60 << 20
 F32 = jnp.float32
 BF16 = jnp.bfloat16
 
@@ -67,7 +68,10 @@
     rows = outs[0].shape[0]
     for other, out in zip(order, outs):
         begin = pl.multiple_of((me ^ other) * rows, rows)
-        out[...] = silu(dot(x_ref[pl.ds(begin, rows), :], w_ref[...]) + bias).astype(BF16)
+        product = lax.dot_general(
+            x_ref[:, pl.ds(begin, rows)], w_ref[...], (((0,), (0,)), ((), ())), preferred_element_type=F32
+        )
+        out[...] = silu(product + bias).astype(BF16)
 
 
 def embed_finish(section_id, count, *refs):
@@ -149,72 +153,104 @@
     mesh_out[...] = (mesh + turned[:, 2:3] * pos_w[2:3, :]).astype(BF16)
 
 
-def phase(section_id, tables, places, last, *refs):
+def stage(places, last, *refs):
     place_ref = refs[0]
-    table_refs = refs[1 : 1 + tables]
-    refs = refs[1 + tables :]
-    pieces = refs[: len(places)]
-    gain, shift, ids, own_ref, *rest = refs[len(places) :]
+    pieces = refs[1 : 1 + len(places)]
+    own_ref, *rest = refs[1 + len(places) :]
     if last:
-        head_hbm, out_hbm, table, w_in, w_out, w_bias, table_sem, w_sem, head, out, head_sem = rest
+        w_send, w_out, w_agg, w_out2, recv_pre, node_pre = rest
     else:
-        recv_col, recv_row, out, table, w_in, w_out, w_bias, table_sem, w_sem = rest
+        recv_col, w_send, w_out, w_agg, w_out2, recv_pre, node_pre = rest
     own = own_ref[...]
     rows, latent = own.shape
     width = pieces[0].shape[1]
-    edges = ids.shape[0]
-    part = place_ref[2]
-    pairs = []
-    begin = 0
-    for ref in table_refs:
-        pairs.append((ref, table.at[pl.ds(begin, ref.shape[0])]))
-        begin += ref.shape[0]
-    t_copies = started(pairs, table_sem)
-    pairs = []
-    for (kind, slot), ref in zip(places, pieces):
-        t = part if kind == 0 else 1 - part
-        columns = pl.ds(slot * width, width)
-        pairs.append((ref.at[pl.ds(0, 2 * latent)], w_in.at[t, :, columns]))
-        for b in range(0, latent, width):
-            pairs.append((ref.at[pl.ds(2 * latent + b, width)], w_out.at[t, columns, pl.ds(b, width)]))
-        pairs.append((ref.at[pl.ds(3 * latent, BIAS_ROWS)], w_bias.at[t, :, columns]))
-    w_copies = started(pairs, w_sem)
+    edges = recv_pre.shape[0]
     if last:
-        h_copies = started([(head_hbm, head)], head_sem)
         degree = edges // rows
         edge = lax.broadcasted_iota(jnp.int32, (edges, rows), 0)
         node = lax.broadcasted_iota(jnp.int32, (edges, rows), 1) * degree
         spread = (edge >= node) & (edge < node + degree)
+    else:
+        spread = recv_col[...] == lax.broadcasted_iota(jnp.int32, (edges, rows), 1)
+    received = dot(spread.astype(BF16), own).astype(BF16)
+
+    def bias(refs):
+        terms = [ref[pl.ds(3 * latent, BIAS_ROWS), :].astype(F32) for ref in refs]
+        return jnp.concatenate([(t[0:1] + t[1:2]) + t[2:3] for t in terms], axis=1)
+
+    def fill(target, out, begin, refs):
+        for slot, ref in enumerate(refs):
+            columns = pl.ds(slot * width, width)
+            target[:, columns] = ref[pl.ds(begin, latent), :]
+            for b in range(0, latent, width):
+                out[columns, pl.ds(b, width)] = ref[pl.ds(2 * latent + b, width), :]
+
+    def emit(edge_kind):
+        ordered = [
+            [ref for _, ref in sorted(
+                    ((slot, ref) for (kind, slot), ref in zip(places, pieces) if kind == wanted),
+                    key=lambda pair: pair[0],
+                )]
+            for wanted in (edge_kind, 1 - edge_kind)
+        ]
+        first, second = ordered
+        fill(w_send, w_out, 0, first)
+        fill(w_agg, w_out2, latent, second)
+        weights = jnp.concatenate([ref[pl.ds(latent, latent), :] for ref in first], axis=1)
+        recv_pre[...] = dot(received, weights) + bias(first)
+        weights = jnp.concatenate([ref[pl.ds(0, latent), :] for ref in second], axis=1)
+        node_pre[...] = dot(own, weights) + bias(second)
+
+    part = place_ref[2]
+    pl.when(part == 0)(functools.partial(emit, 0))
+    pl.when(part == 1)(functools.partial(emit, 1))
+
+
+def phase(section_id, tables, last, *refs):
+    table_refs = refs[:tables]
+    ids, own_ref, w_send, w_out, w_agg, w_out2, recv_pre, node_pre, gain, shift, extra, out = refs[tables:]
+    rows, latent = own_ref.shape
+    edges = ids.shape[0]
+    chunks = [[]]
+    held = 0
+    for ref in table_refs:
+        size = min(ref.shape[0], CHUNK)
+        for begin in range(0, ref.shape[0], size):
+            if held + size > CHUNK:
+                chunks.append([])
+                held = 0
+            chunks[-1].append(ref[pl.ds(begin, size), :])
+            held += size
+    preact = recv_pre[...]
+    sent = None
+    start = 0
+    for chunk in chunks:
+        chunk = jnp.concatenate(chunk, axis=0) if len(chunk) > 1 else chunk[0]
+        hot = ids[...] == lax.broadcasted_iota(jnp.int32, (edges, chunk.shape[0]), 1) + start
+        term = dot(hot.astype(BF16), chunk)
+        sent = term if sent is None else sent + term
+        start += chunk.shape[0]
+    preact = preact + dot(sent.astype(BF16), w_send[...])
+
+    def finish(t, preact, weights):
+        row = slice(section_id + t, section_id + t + 1)
+        return layer_norm(dot(silu(preact).astype(BF16), weights[...]), gain[row, :], shift[row, :])
+
+    messages = finish(0, preact, w_out).astype(BF16)
+    if last:
+        degree = edges // rows
         edge = lax.broadcasted_iota(jnp.int32, (rows, edges), 1)
         node = lax.broadcasted_iota(jnp.int32, (rows, edges), 0) * degree
         collect = (edge >= node) & (edge < node + degree)
     else:
-        spread = recv_col[...] == lax.broadcasted_iota(jnp.int32, (edges, rows), 1)
-        collect = lax.broadcasted_iota(jnp.int32, (rows, edges), 0) == recv_row[...]
-    received = dot(spread.astype(BF16), own).astype(BF16)
-    wait_all(t_copies)
-    sent = None
-    for start in range(0, begin, CHUNK):
-        size = min(CHUNK, begin - start)
-        hot = ids[...] == lax.broadcasted_iota(jnp.int32, (edges, size), 1) + start
-        term = dot(hot.astype(BF16), table[pl.ds(start, size), :])
-        sent = term if sent is None else sent + term
-    wait_all(w_copies)
-
-    def mlp(t, first, second):
-        terms = w_bias[t].astype(F32)
-        bias = (terms[0:1] + terms[1:2]) + terms[2:3]
-        preact = dot(first, w_in[t, :latent, :]) + dot(second, w_in[t, latent:, :]) + bias
-        row = slice(section_id + t, section_id + t + 1)
-        return layer_norm(dot(silu(preact).astype(BF16), w_out[t]), gain[row, :], shift[row, :])
-
-    messages = mlp(0, sent.astype(BF16), received).astype(BF16)
+        collect = lax.broadcasted_iota(jnp.int32, (rows, edges), 0) == extra[...]
     aggregate = dot(collect.astype(BF16), messages).astype(BF16)
-    updated = (own.astype(F32) + mlp(1, own, aggregate)).astype(BF16)
+    update = finish(1, node_pre[...] + dot(aggregate, w_agg[...]), w_out2)
+    updated = (own_ref[...].astype(F32) + update).astype(BF16)
     if last:
-        wait_all(h_copies)
-        out[...] = dot(updated, head[...])
-        wait_all(started([(out, out_hbm)], head_sem))
+        out[...] = lax.dot_general(
+            extra[...], updated, (((1,), (1,)), ((), ())), preferred_element_type=F32
+        )
     else:
         out[...] = updated
 
@@ -288,13 +324,14 @@
         functools.partial(embed_hidden, order, embed_id),
         [jax.ShapeDtypeStruct((width, latent), BF16)]
         + [jax.ShapeDtypeStruct((grid_rows, width), BF16)] * quarters,
-        (place, x_grid, embed_in, pair_out, hidden_bias),
+        (place, x_grid.T, embed_in, pair_out, hidden_bias),
         (scalar, hbm, hbm, hbm, vmem),
         scratch=(
-            pltpu.VMEM(x_grid.shape, BF16),
+            pltpu.VMEM(x_grid.shape[::-1], BF16),
             pltpu.VMEM(embed_in.shape, BF16),
             pltpu.SemaphoreType.DMA((3,)),
         ),
+        vmem=GRANT,
     )
     out_pieces = pieces(hidden[0])
     hidden = [hidden[1]] + [swap(h, other) for h, other in zip(hidden[2:], order[1:])]
@@ -311,10 +348,8 @@
                 pltpu.SemaphoreType.DMA((sections * (2 + latent // width),)),
             ),
             outs=[hbm] * sections,
+            vmem=GRANT,
         )
-
-    packed = packs(0, 2)
-    later = packs(2, embed_id - 2)
 
     takes = [take[0] for take in (g2m_take, m2m_take, m2g_take)]
     caps = [take.shape[1] for take in takes]
@@ -331,8 +366,14 @@
         [*columns, *lines, shape],
         (place, tables, *[v[None, :] for v in (g2m_from, m2m_from, m2g_from, g2m_to, m2m_to)], mesh_pos, pos_weight),
         (scalar,) + (vmem,) * 8,
-    )
-    hidden, out_pieces, routed, later = lax.optimization_barrier((hidden, out_pieces, routed, later))
+        vmem=GRANT,
+    )
+    pair_in, pair_out, _ = lax.optimization_barrier((pair_in, pair_out, routed[-1]))
+    packed = packs(0, 2)
+    later = packs(2, embed_id - 2)
+    hidden, out_pieces, routed, packed, later = lax.optimization_barrier(
+        (hidden, out_pieces, routed, packed, later)
+    )
     ids_g, ids_m, ids_d, col_g, col_m, row_g, row_m, mesh = routed
     packed = packed + later
     grid = kernel_call(
@@ -342,59 +383,58 @@
         (vmem,) * (2 * quarters + 2),
     )
 
-    def group(section_id, after):
+    def group(section_id, after, gate):
         first, second = packed[section_id : section_id + 2]
         if after is not None:
             first, second, _ = lax.optimization_barrier((first, second, after))
         across = swap(first, bits[0])
+        if after is not None:
+            across, _ = lax.optimization_barrier((across, gate))
         over = lax.ppermute(across, "parts", [(0, 1), (1, 0)])
         found = [((0, 0), first), ((1, 0), second), ((0, 1), across), ((1, 1), over)]
         for i, bit in enumerate(bits[1:]):
             found = found + [((kind, slot + (2 << i)), swap(piece, bit)) for (kind, slot), piece in found]
         return found
 
-    def run(section_id, table, after, ids, own_latent, extra, last=False):
+    def run(section_id, table, after, ids, own_latent, column, extra, last=False):
         rows = sum(part.shape[0] for part in table)
-        weights = group(section_id, after)
+        edges = ids.shape[0]
+        weights = group(section_id, after, table[1])
         places = [p for p, _ in weights]
         weights = [piece for _, piece in weights]
-        scratch = [
-            pltpu.VMEM((rows, latent), BF16),
-            pltpu.VMEM((2, 2 * latent, latent), BF16),
-            pltpu.VMEM((2, latent, latent), BF16),
-            pltpu.VMEM((2, BIAS_ROWS, latent), BF16),
-            pltpu.SemaphoreType.DMA((len(table),)),
-            pltpu.SemaphoreType.DMA((len(weights) * (2 + quarters),)),
-        ]
+        square = jax.ShapeDtypeStruct((latent, latent), BF16)
+        columns = () if last else (column,)
+        staged = kernel_call(
+            functools.partial(stage, places, last),
+            [square] * 4
+            + [jax.ShapeDtypeStruct((n, latent), F32) for n in (edges, own_latent.shape[0])],
+            (place, *weights, own_latent, *columns),
+            (scalar,) + (vmem,) * (len(weights) + 1 + len(columns)),
+            flops=4 * edges * latent * latent,
+            vmem=20 << 20,
+        )
         out_shape = jax.ShapeDtypeStruct(own_latent.shape, BF16)
         if last:
-            out_shape = jax.ShapeDtypeStruct((own_latent.shape[0], head.shape[1]), F32)
-            scratch += [
-                pltpu.VMEM(head.shape, BF16),
-                pltpu.VMEM(out_shape.shape, F32),
-                pltpu.SemaphoreType.DMA((1,)),
-            ]
+            out_shape = jax.ShapeDtypeStruct((head.shape[1], own_latent.shape[0]), F32)
         return kernel_call(
-            functools.partial(phase, section_id, len(table), places, last),
+            functools.partial(phase, section_id, len(table), last),
             out_shape,
-            (place, *table, *weights, norm_gain, norm_shift, ids, own_latent, *extra),
-            (scalar,) + (hbm,) * (len(table) + len(weights)) + (vmem,) * 4 + ((hbm,) if last else (vmem, vmem)),
-            scratch=scratch,
-            outs=hbm if last else vmem,
-            flops=2 * ids.shape[0] * latent * (rows + 3 * latent),
-            vmem=(20 << 20) + 2 * rows * latent * 2,
+            (*table, ids, own_latent, *staged, norm_gain, norm_shift, extra),
+            (vmem,) * (len(table) + 11),
+            flops=2 * edges * latent * (rows + 3 * latent),
+            vmem=(20 << 20) + rows * latent * 2,
         )
 
     def held(table):
-        return table[2 * bands - 1] if direct else None
+        return table[2 * bands - 1] if direct else table[-1]
 
     table = everyone(grid)
-    mesh = run(0, table, None, ids_g, mesh, (col_g, row_g))
+    mesh = run(0, table, None, ids_g, mesh, col_g, row_g)
     for layer_id in range(LAYERS):
         after = held(table)
         table = everyone(mesh)
-        mesh = run(2 + 2 * layer_id, table, after, ids_m, mesh, (col_m, row_m))
-    return run(2 * LAYERS + 2, everyone(mesh), held(table), ids_d, grid, (head,), True)
+        mesh = run(2 + 2 * layer_id, table, after, ids_m, mesh, col_m, row_m)
+    return run(2 * LAYERS + 2, everyone(mesh), held(table), ids_d, grid, None, head.T, True).T
 
 
 def solution(mesh):

time: 214 us -> 289 us (1.35)
  Pallas kernels: 38 us -> 123 us
  local copies, waits for them, and re-layouts: 34.8 us -> 4.59 us
  waiting for transfers between devices: 81.2 us -> 98.5 us
    pallas_call x9 -> x13, Pallas kernels: 38 us -> 123 us  [kernel_call(): pl.pallas_call(body, out_shape=out_shape, in_specs=[pl.BlockSpec(memory_s...]
    unnamed x111 -> x45, local copies, waits for them, and re-layouts: 32.8 us -> 2.69 us
    ppermute x4, waiting for transfers between devices: 0.01 us -> 12.5 us  [group(): over = lax.ppermute(across, 'parts', [(0, 1), (1, 0)])]
    all_to_all x1, waiting for transfers between devices: 0.01 us -> 4.33 us  [local(): lax.all_to_all(jnp.concatenate(takes, axis=1), 'band', split_axis=0, conc...]
    ppermute x74, waiting for transfers between devices: 49.1 us -> 52.7 us  [swap(): return lax.ppermute(value, 'feat', [(f, f ^ bit) for f in range(quarters)])]
    ppermute x12, waiting for transfers between devices: 32.1 us -> 29 us  [everyone(): lax.ppermute(rows, 'band', [(b, (b + step) % bands) for b in range(bands)])]
  transfers between devices with their start and end apart: 91 -> 91, of which waited for: 33 -> 34; matrix products, arithmetic and copies ran while one was open for 1% -> 1% of each run, Pallas kernels for 13% -> 41%
where the time goes in v6:
time: 289 us; the launch traced here: 288 us
  Pallas kernels  123 us (43%)
  waiting for transfers between devices  98.5 us (34%)
  starting transfers between devices  59.5 us (21%)
  local copies, waits for them, and re-layouts  4.59 us (2%)
    pallas_call x13, Pallas kernels, kernel_call(): pl.pallas_call(body, out_shape=out_shape, in_specs=[pl.BlockSpec(memory_s...  123 us
    ppermute x74, waiting for transfers between devices, swap(): return lax.ppermute(value, 'feat', [(f, f ^ bit) for f in range(quarters)])  52.7 us
    ppermute x74, starting transfers between devices, swap(): return lax.ppermute(value, 'feat', [(f, f ^ bit) for f in range(quarters)])  33.5 us
    ppermute x12, waiting for transfers between devices, everyone(): lax.ppermute(rows, 'band', [(b, (b + step) % bands) for b in range(bands)])  29 us
    ppermute x12, starting transfers between devices, everyone(): lax.ppermute(rows, 'band', [(b, (b + step) % bands) for b in range(bands)])  16.7 us
    ppermute x4, waiting for transfers between devices, group(): over = lax.ppermute(across, 'parts', [(0, 1), (1, 0)])  12.5 us
  transfers between devices with their start and end apart: 91, of which 34 were waited for; matrix products, arithmetic and copies ran while one was open for 1% of the time, Pallas kernels for 41%

profile of v6, /device:TPU:0, one launch (start us, length us, event | category | flops | bytes accessed | tf_op | source)
XLA Modules:
  0.0 287.7 jit_solution(12830178840535242483)
XLA Ops:
  0.6 2.8 shard_map.172
  3.4 3.0 %collective-permute-start.3 = (bf16[128,512]{1,0:T(8,128)(2,1)}, bf16[128,512]{1,0:T(8,128)(2,1)S(1)}, u32[]{:S(2)}, u32[]{:S(2)}) collective-permute-start(bf16[128,512]{1,0:T(8,128)(2,1)} %get-tuple-element.112.refs_4_), channel_id=1, source_target_pairs={{0,2},{1,3},{2,0},{3,1},{4,6},{5,7},{6,4},{7,5},{8,10},{9,11},{10,... | collective-permute-start | bytes 393224 | tf_op jit(solution)/shard_map/ppermute | solution.py:300
  11.7 5.5 %all-to-all-start = ((s32[4,1,1152]{2,1,0:T(1,128)}), s32[4,1,1152]{2,1,0:T(1,128)S(1)}, u32[]{:S(2)}, u32[]{:S(2)}) async-start(s32[4,1,1152]{2,1,0:T(1,128)} %all_to_all.7), calls=%async_computation | async-start | bytes 36864 | tf_op jit(solution)/shard_map/all_to_all | solution.py:357
  18.5 4.3 %all-to-all-done = s32[4,1,1152]{2,1,0:T(1,128)S(1)} async-done(((s32[4,1,1152]{2,1,0:T(1,128)}), s32[4,1,1152]{2,1,0:T(1,128)S(1)}, u32[]{:S(2)}, u32[]{:S(2)}) %all-to-all-start) | async-done | bytes 18464 | tf_op jit(solution)/shard_map/all_to_all | solution.py:357
  26.0 73.6 %shard_map.175 = (bf16[1552,128]{1,0:T(8,128)(2,1)}, bf16[1552,128]{1,0:T(8,128)(2,1)}, bf16[1552,128]{1,0:T(8,128)(2,1)}, bf16[1552,128]{1,0:T(8,128)(2,1)}, bf...) custom-call(s32[3]{0:T(128)} %pad_add_fusion.1.place_ref.refs_0_, bf16[8,1024,128]{2,1,0:T(8,128)(2,1)} %in_hbm.1, ...), custom_call_target="tpu_custom_call" | custom-call | bytes 4194304 | tf_op jit(solution)/shard_map/pallas_call | solution.py:37
  99.7 25.8 %shard_map.174 = (bf16[1552,128]{1,0:T(8,128)(2,1)}, bf16[1552,128]{1,0:T(8,128)(2,1)}) custom-call(s32[3]{0:T(128)} %pad_add_fusion.1.place_ref.refs_0_, bf16[8,1024,128]{2,1,0:T(8,128)(2,1)} %in_hbm.1, bf16[9,128,512]{2,1,0:T(8,128)(2,1)} %out_hbm.3, f32[9,128]{1,0:T(8,128)} %bias_ref.5), custom_call_target="tpu_custom_call" | custom-call | bytes 4194304 | tf_op jit(solution)/shard_map/pallas_call | solution.py:37
  127.2 8.9 %collective-permute-done.21.refs_3_ = bf16[1552,128]{1,0:T(8,128)(2,1)S(1)} collective-permute-done((bf16[1552,128]{1,0:T(8,128)(2,1)}, bf16[1552,128]{1,0:T(8,128)(2,1)S(1)}, u32[]{:S(2)}, u32[]{:S(2)}) %collective-permute-start.21) | collective-permute-done | bytes 397344 | tf_op jit(solution)/shard_map/ppermute | solution.py:300
  142.3 2.8 collective-permute-done.8.refs_3_
  169.6 4.0 %collective-permute-start.27 = (bf16[128,512]{1,0:T(8,128)(2,1)S(1)}, bf16[128,512]{1,0:T(8,128)(2,1)S(1)}, u32[]{:S(2)}, u32[]{:S(2)}) collective-permute-start(bf16[128,512]{1,0:T(8,128)(2,1)S(1)} %shard_map.178.refs_9_.refs_0_.refs_17_), channel_id=1, source_target_pairs={{0,4},{4,8},{8,12},{12,0},{1,5},{5,9},{9,13},{13,1},{2,6},{6,10},{... | collective-permute-start | bytes 393224 | tf_op jit(solution)/shard_map/ppermute | solution.py:311
  182.5 4.6 %collective-permute-done.28.refs_2_ = bf16[128,512]{1,0:T(8,128)(2,1)S(1)} collective-permute-done((bf16[128,512]{1,0:T(8,128)(2,1)S(1)}, bf16[128,512]{1,0:T(8,128)(2,1)S(1)}, u32[]{:S(2)}, u32[]{:S(2)}) %collective-permute-start.28) | collective-permute-done | bytes 131104 | tf_op jit(solution)/shard_map/ppermute | solution.py:311
  190.2 3.8 %collective-permute-done.31.refs_5_ = bf16[128,512]{1,0:T(8,128)(2,1)S(1)} collective-permute-done((bf16[128,512]{1,0:T(8,128)(2,1)S(1)}, bf16[128,512]{1,0:T(8,128)(2,1)S(1)}, u32[]{:S(2)}, u32[]{:S(2)}) %collective-permute-start.31) | collective-permute-done | bytes 131104 | tf_op jit(solution)/shard_map/ppermute | solution.py:300
  193.9 2.8 collective-permute-done.32.refs_6_
  203.2 2.9 shard_map.180.refs_9_.refs_0_.refs_17_
  208.8 3.1 %collective-permute-done.63.refs_3_ = bf16[1552,128]{1,0:T(8,128)(2,1)S(1)} collective-permute-done((bf16[1552,128]{1,0:T(8,128)(2,1)S(1)}, bf16[1552,128]{1,0:T(8,128)(2,1)S(1)}, u32[]{:S(2)}, u32[]{:S(2)}) %collective-permute-start.63) | collective-permute-done | bytes 397344 | tf_op jit(solution)/shard_map/ppermute | solution.py:300
  220.2 3.2 %collective-permute-done.64.refs_4_ = bf16[1552,128]{1,0:T(8,128)(2,1)S(1)} collective-permute-done((bf16[1552,128]{1,0:T(8,128)(2,1)S(1)}, bf16[1552,128]{1,0:T(8,128)(2,1)S(1)}, u32[]{:S(2)}, u32[]{:S(2)}) %collective-permute-start.64) | collective-permute-done | bytes 397344 | tf_op jit(solution)/shard_map/ppermute | solution.py:393
  229.1 3.0 %collective-permute-done.54.refs_7_ = bf16[128,512]{1,0:T(8,128)(2,1)S(1)} collective-permute-done((bf16[128,512]{1,0:T(8,128)(2,1)S(1)}, bf16[128,512]{1,0:T(8,128)(2,1)S(1)}, u32[]{:S(2)}, u32[]{:S(2)}) %collective-permute-start.54) | collective-permute-done | bytes 131104 | tf_op jit(solution)/shard_map/ppermute | solution.py:300
  232.1 2.8 collective-permute-done.52.refs_5_
  241.6 2.9 shard_map.182.refs_0_
  244.6 5.4 %collective-permute-done.84.refs_3_ = bf16[1552,128]{1,0:T(8,128)(2,1)S(1)} collective-permute-done((bf16[1552,128]{1,0:T(8,128)(2,1)S(1)}, bf16[1552,128]{1,0:T(8,128)(2,1)S(1)}, u32[]{:S(2)}, u32[]{:S(2)}) %collective-permute-start.84) | collective-permute-done | bytes 397344 | tf_op jit(solution)/shard_map/ppermute | solution.py:300
  252.5 9.2 %collective-permute-done.85.refs_4_ = bf16[1552,128]{1,0:T(8,128)(2,1)S(1)} collective-permute-done((bf16[1552,128]{1,0:T(8,128)(2,1)S(1)}, bf16[1552,128]{1,0:T(8,128)(2,1)S(1)}, u32[]{:S(2)}, u32[]{:S(2)}) %collective-permute-start.85) | collective-permute-done | bytes 397344 | tf_op jit(solution)/shard_map/ppermute | solution.py:393
  263.8 6.2 %collective-permute-done.70.refs_2_ = bf16[128,512]{1,0:T(8,128)(2,1)S(1)} collective-permute-done((bf16[128,512]{1,0:T(8,128)(2,1)S(1)}, bf16[128,512]{1,0:T(8,128)(2,1)S(1)}, u32[]{:S(2)}, u32[]{:S(2)}) %collective-permute-start.70) | collective-permute-done | bytes 131104 | tf_op jit(solution)/shard_map/ppermute | solution.py:311
  273.4 3.4 %collective-permute-done.73.refs_5_ = bf16[128,512]{1,0:T(8,128)(2,1)S(1)} collective-permute-done((bf16[128,512]{1,0:T(8,128)(2,1)S(1)}, bf16[128,512]{1,0:T(8,128)(2,1)S(1)}, u32[]{:S(2)}, u32[]{:S(2)}) %collective-permute-start.73) | collective-permute-done | bytes 131104 | tf_op jit(solution)/shard_map/ppermute | solution.py:300
  276.8 2.8 collective-permute-done.74.refs_6_
  284.3 3.4 %shard_map.184 = f32[227,128]{1,0:T(8,128)} custom-call(bf16[128,512]{1,0:T(8,128)(2,1)S(1)} %shard_map.182.refs_0_, bf16[128,512]{1,0:T(8,128)(2,1)S(1)} %collective-permute-done.69.refs_1_, bf16[128,512]{1,0:T(8,128)(2,1)S(1)} %collective-permute-done.70.refs_2_, bf16[128,512]{1,0:T(8,128)(2,1)S(1)} %collective-permute-done.71.refs_3_, ...), custom_call_target="tpu_custom_call" | custom-call | flops 1409286144 | bytes 4194304 | tf_op jit(solution)/shard_map/pallas_call | solution.py:37
  (220 shorter events, 97.1 us)
Async XLA Ops:
  6.4 119.2 %collective-permute-start.4 = (bf16[128,512]{1,0:T(8,128)(2,1)}, bf16[128,512]{1,0:T(8,128)(2,1)S(1)}, u32[]{:S(2)}, u32[]{:S(2)}) collective-permute-start(bf16[128,512]{1,0:T(8,128)(2,1)} %get-tuple-element.112.refs_4_), channel_id=1, source_target_pairs={{0,1},{1,0},{2,3},{3,2},{4,5},{5,4},{6,7},{7,6},{8,9},{9,8},{10,11... | collective-permute-start | bytes 393224 | tf_op jit(solution)/shard_map/ppermute | solution.py:300
  6.4 119.2 %collective-permute-start = (bf16[128,128]{1,0:T(8,128)(2,1)}, bf16[128,128]{1,0:T(8,128)(2,1)S(1)}, u32[]{:S(2)}, u32[]{:S(2)}) collective-permute-start(bf16[128,128]{1,0:T(8,128)(2,1)} %get-tuple-element.86), channel_id=1, source_target_pairs={{0,2},{1,3},{2,0},{3,1},{4,6},{5,7},{6,4},{7,5},{8,10},{9,11},{10,... | collective-permute-start | bytes 98312 | tf_op jit(solution)/shard_map/ppermute | solution.py:300
  6.5 119.0 %collective-permute-start.1 = (bf16[128,128]{1,0:T(8,128)(2,1)}, bf16[128,128]{1,0:T(8,128)(2,1)S(1)}, u32[]{:S(2)}, u32[]{:S(2)}) collective-permute-start(bf16[128,128]{1,0:T(8,128)(2,1)} %get-tuple-element.87), channel_id=1, source_target_pairs={{0,1},{1,0},{2,3},{3,2},{4,5},{5,4},{6,7},{7,6},{8,9},{9,8},{10,11... | collective-permute-start | bytes 98312 | tf_op jit(solution)/shard_map/ppermute | solution.py:300
  6.9 118.7 %collective-permute-start.2 = (bf16[128,128]{1,0:T(8,128)(2,1)}, bf16[128,128]{1,0:T(8,128)(2,1)S(1)}, u32[]{:S(2)}, u32[]{:S(2)}) collective-permute-start(bf16[128,128]{1,0:T(8,128)(2,1)} %get-tuple-element.88), channel_id=1, source_target_pairs={{0,3},{1,2},{2,1},{3,0},{4,7},{5,6},{6,5},{7,4},{8,11},{9,10},{10,... | collective-permute-start | bytes 98312 | tf_op jit(solution)/shard_map/ppermute | solution.py:300
  10.4 115.2 %collective-permute-start.5 = (bf16[128,512]{1,0:T(8,128)(2,1)S(1)}, bf16[128,512]{1,0:T(8,128)(2,1)S(1)}, u32[]{:S(2)}, u32[]{:S(2)}) collective-permute-start(bf16[128,512]{1,0:T(8,128)(2,1)S(1)} %collective-permute-done.3.refs_5_), channel_id=1, source_target_pairs={{0,1},{1,0},{2,3},{3,2},{4,5},{5,4},{6,7},{7,6},{8,9},{9,8},{10,11... | collective-permute-start | bytes 393224 | tf_op jit(solution)/shard_map/ppermute | solution.py:300
  11.7 11.1 %all-to-all-start = ((s32[4,1,1152]{2,1,0:T(1,128)}), s32[4,1,1152]{2,1,0:T(1,128)S(1)}, u32[]{:S(2)}, u32[]{:S(2)}) async-start(s32[4,1,1152]{2,1,0:T(1,128)} %all_to_all.7), calls=%async_computation | async-start | bytes 36864 | tf_op jit(solution)/shard_map/all_to_all | solution.py:357
  125.6 10.5 %collective-permute-start.21 = (bf16[1552,128]{1,0:T(8,128)(2,1)}, bf16[1552,128]{1,0:T(8,128)(2,1)S(1)}, u32[]{:S(2)}, u32[]{:S(2)}) collective-permute-start(bf16[1552,128]{1,0:T(8,128)(2,1)} %get-tuple-element.118.refs_1_), channel_id=1, source_target_pairs={{0,2},{1,3},{2,0},{3,1},{4,6},{5,7},{6,4},{7,5},{8,10},{9,11},{10,... | collective-permute-start | bytes 1191944 | tf_op jit(solution)/shard_map/ppermute | solution.py:300
  136.1 21.4 %collective-permute-start.22 = (bf16[1552,128]{1,0:T(8,128)(2,1)S(1)}, bf16[1552,128]{1,0:T(8,128)(2,1)S(1)}, u32[]{:S(2)}, u32[]{:S(2)}) collective-permute-start(bf16[1552,128]{1,0:T(8,128)(2,1)S(1)} %collective-permute-done.21.refs_3_), channel_id=1, source_target_pairs={{0,16},{16,0},{1,17},{17,1},{2,18},{18,2},{3,19},{19,3},{4,20},{20... | collective-permute-start | bytes 1191944 | tf_op jit(solution)/shard_map/ppermute | solution.py:393
  140.1 10.6 %collective-permute-start.7 = (bf16[128,512]{1,0:T(8,128)(2,1)S(1)}, bf16[128,512]{1,0:T(8,128)(2,1)S(1)}, u32[]{:S(2)}, u32[]{:S(2)}) collective-permute-start(bf16[128,512]{1,0:T(8,128)(2,1)S(1)} %shard_map.176.refs_0_.refs_9_.refs_17_), channel_id=1, source_target_pairs={{0,8},{4,12},{8,0},{12,4},{1,9},{5,13},{9,1},{13,5},{2,10},{6,14},... | collective-permute-start | bytes 393224 | tf_op jit(solution)/shard_map/ppermute | solution.py:311
  140.8 11.4 %collective-permute-start.9 = (bf16[128,512]{1,0:T(8,128)(2,1)S(1)}, bf16[128,512]{1,0:T(8,128)(2,1)S(1)}, u32[]{:S(2)}, u32[]{:S(2)}) collective-permute-start(bf16[128,512]{1,0:T(8,128)(2,1)S(1)} %shard_map.176.refs_0_.refs_9_.refs_17_), channel_id=1, source_target_pairs={{0,2},{1,3},{2,0},{3,1},{4,6},{5,7},{6,4},{7,5},{8,10},{9,11},{10,... | collective-permute-start | bytes 393224 | tf_op jit(solution)/shard_map/ppermute | solution.py:300
  161.3 12.8 %collective-permute-start.42 = (bf16[1552,128]{1,0:T(8,128)(2,1)S(1)}, bf16[1552,128]{1,0:T(8,128)(2,1)S(1)}, u32[]{:S(2)}, u32[]{:S(2)}) collective-permute-start(bf16[1552,128]{1,0:T(8,128)(2,1)S(1)} %copy-done.6), channel_id=1, source_target_pairs={{0,2},{1,3},{2,0},{3,1},{4,6},{5,7},{6,4},{7,5},{8,10},{9,11},{10,... | collective-permute-start | bytes 1191944 | tf_op jit(solution)/shard_map/ppermute | solution.py:300
  176.9 10.3 %collective-permute-start.43 = (bf16[1552,128]{1,0:T(8,128)(2,1)S(1)}, bf16[1552,128]{1,0:T(8,128)(2,1)S(1)}, u32[]{:S(2)}, u32[]{:S(2)}) collective-permute-start(bf16[1552,128]{1,0:T(8,128)(2,1)S(1)} %collective-permute-done.42.refs_3_), channel_id=1, source_target_pairs={{0,16},{16,0},{1,17},{17,1},{2,18},{18,2},{3,19},{19,3},{4,20},{20... | collective-permute-start | bytes 1191944 | tf_op jit(solution)/shard_map/ppermute | solution.py:393
  179.3 21.0 %collective-permute-start.46 = (bf16[1552,128]{1,0:T(8,128)(2,1)S(1)}, bf16[1552,128]{1,0:T(8,128)(2,1)S(1)}, u32[]{:S(2)}, u32[]{:S(2)}) collective-permute-start(bf16[1552,128]{1,0:T(8,128)(2,1)S(1)} %collective-permute-done.42.refs_3_), channel_id=1, source_target_pairs={{0,1},{1,0},{2,3},{3,2},{4,5},{5,4},{6,7},{7,6},{8,9},{9,8},{10,11... | collective-permute-start | bytes 1191944 | tf_op jit(solution)/shard_map/ppermute | solution.py:300
  187.3 13.4 %collective-permute-start.47 = (bf16[1552,128]{1,0:T(8,128)(2,1)S(1)}, bf16[1552,128]{1,0:T(8,128)(2,1)S(1)}, u32[]{:S(2)}, u32[]{:S(2)}) collective-permute-start(bf16[1552,128]{1,0:T(8,128)(2,1)S(1)} %collective-permute-done.43.refs_4_), channel_id=1, source_target_pairs={{0,1},{1,0},{2,3},{3,2},{4,5},{5,4},{6,7},{7,6},{8,9},{9,8},{10,11... | collective-permute-start | bytes 1191944 | tf_op jit(solution)/shard_map/ppermute | solution.py:300
  200.7 11.3 %collective-permute-start.63 = (bf16[1552,128]{1,0:T(8,128)(2,1)S(1)}, bf16[1552,128]{1,0:T(8,128)(2,1)S(1)}, u32[]{:S(2)}, u32[]{:S(2)}) collective-permute-start(bf16[1552,128]{1,0:T(8,128)(2,1)S(1)} %copy-done.4), channel_id=1, source_target_pairs={{0,2},{1,3},{2,0},{3,1},{4,6},{5,7},{6,4},{7,5},{8,10},{9,11},{10,... | collective-permute-start | bytes 1191944 | tf_op jit(solution)/shard_map/ppermute | solution.py:300
  213.2 10.1 %collective-permute-start.64 = (bf16[1552,128]{1,0:T(8,128)(2,1)S(1)}, bf16[1552,128]{1,0:T(8,128)(2,1)S(1)}, u32[]{:S(2)}, u32[]{:S(2)}) collective-permute-start(bf16[1552,128]{1,0:T(8,128)(2,1)S(1)} %collective-permute-done.63.refs_3_), channel_id=1, source_target_pairs={{0,16},{16,0},{1,17},{17,1},{2,18},{18,2},{3,19},{19,3},{4,20},{20... | collective-permute-start | bytes 1191944 | tf_op jit(solution)/shard_map/ppermute | solution.py:393
  216.4 21.9 %collective-permute-start.67 = (bf16[1552,128]{1,0:T(8,128)(2,1)S(1)}, bf16[1552,128]{1,0:T(8,128)(2,1)S(1)}, u32[]{:S(2)}, u32[]{:S(2)}) collective-permute-start(bf16[1552,128]{1,0:T(8,128)(2,1)S(1)} %collective-permute-done.63.refs_3_), channel_id=1, source_target_pairs={{0,1},{1,0},{2,3},{3,2},{4,5},{5,4},{6,7},{7,6},{8,9},{9,8},{10,11... | collective-permute-start | bytes 1191944 | tf_op jit(solution)/shard_map/ppermute | solution.py:300
  216.5 10.6 %collective-permute-start.51 = (bf16[128,512]{1,0:T(8,128)(2,1)S(1)}, bf16[128,512]{1,0:T(8,128)(2,1)S(1)}, u32[]{:S(2)}, u32[]{:S(2)}) collective-permute-start(bf16[128,512]{1,0:T(8,128)(2,1)S(1)} %shard_map.180.refs_9_.refs_0_.refs_17_), channel_id=1, source_target_pairs={{0,2},{1,3},{2,0},{3,1},{4,6},{5,7},{6,4},{7,5},{8,10},{9,11},{10,... | collective-permute-start | bytes 393224 | tf_op jit(solution)/shard_map/ppermute | solution.py:300
  223.3 15.4 %collective-permute-start.68 = (bf16[1552,128]{1,0:T(8,128)(2,1)S(1)}, bf16[1552,128]{1,0:T(8,128)(2,1)S(1)}, u32[]{:S(2)}, u32[]{:S(2)}) collective-permute-start(bf16[1552,128]{1,0:T(8,128)(2,1)S(1)} %collective-permute-done.64.refs_4_), channel_id=1, source_target_pairs={{0,1},{1,0},{2,3},{3,2},{4,5},{5,4},{6,7},{7,6},{8,9},{9,8},{10,11... | collective-permute-start | bytes 1191944 | tf_op jit(solution)/shard_map/ppermute | solution.py:300
  238.7 11.3 %collective-permute-start.84 = (bf16[1552,128]{1,0:T(8,128)(2,1)S(1)}, bf16[1552,128]{1,0:T(8,128)(2,1)S(1)}, u32[]{:S(2)}, u32[]{:S(2)}) collective-permute-start(bf16[1552,128]{1,0:T(8,128)(2,1)S(1)} %copy-done.2), channel_id=1, source_target_pairs={{0,2},{1,3},{2,0},{3,1},{4,6},{5,7},{6,4},{7,5},{8,10},{9,11},{10,... | collective-permute-start | bytes 1191944 | tf_op jit(solution)/shard_map/ppermute | solution.py:300
  251.6 10.1 %collective-permute-start.85 = (bf16[1552,128]{1,0:T(8,128)(2,1)S(1)}, bf16[1552,128]{1,0:T(8,128)(2,1)S(1)}, u32[]{:S(2)}, u32[]{:S(2)}) collective-permute-start(bf16[1552,128]{1,0:T(8,128)(2,1)S(1)} %collective-permute-done.84.refs_3_), channel_id=1, source_target_pairs={{0,16},{16,0},{1,17},{17,1},{2,18},{18,2},{3,19},{19,3},{4,20},{20... | collective-permute-start | bytes 1191944 | tf_op jit(solution)/shard_map/ppermute | solution.py:393
  252.0 11.0 %collective-permute-start.87 = (bf16[1552,128]{1,0:T(8,128)(2,1)S(1)}, bf16[1552,128]{1,0:T(8,128)(2,1)S(1)}, u32[]{:S(2)}, u32[]{:S(2)}) collective-permute-start(bf16[1552,128]{1,0:T(8,128)(2,1)S(1)} %copy-done.3), channel_id=1, source_target_pairs={{0,1},{1,0},{2,3},{3,2},{4,5},{5,4},{6,7},{7,6},{8,9},{9,8},{10,11... | collective-permute-start | bytes 1191944 | tf_op jit(solution)/shard_map/ppermute | solution.py:300
  252.5 29.6 %collective-permute-start.88 = (bf16[1552,128]{1,0:T(8,128)(2,1)S(1)}, bf16[1552,128]{1,0:T(8,128)(2,1)S(1)}, u32[]{:S(2)}, u32[]{:S(2)}) collective-permute-start(bf16[1552,128]{1,0:T(8,128)(2,1)S(1)} %collective-permute-done.84.refs_3_), channel_id=1, source_target_pairs={{0,1},{1,0},{2,3},{3,2},{4,5},{5,4},{6,7},{7,6},{8,9},{9,8},{10,11... | collective-permute-start | bytes 1191944 | tf_op jit(solution)/shard_map/ppermute | solution.py:300
  261.7 20.9 %collective-permute-start.89 = (bf16[1552,128]{1,0:T(8,128)(2,1)S(1)}, bf16[1552,128]{1,0:T(8,128)(2,1)S(1)}, u32[]{:S(2)}, u32[]{:S(2)}) collective-permute-start(bf16[1552,128]{1,0:T(8,128)(2,1)S(1)} %collective-permute-done.85.refs_4_), channel_id=1, source_target_pairs={{0,1},{1,0},{2,3},{3,2},{4,5},{5,4},{6,7},{7,6},{8,9},{9,8},{10,11... | collective-permute-start | bytes 1191944 | tf_op jit(solution)/shard_map/ppermute | solution.py:300
  (89 other events, 1138.5 us)

commit v7 on v6

--- a/solution.py
+++ b/solution.py
@@ -57,10 +57,18 @@
         copy.wait()
 
 
-def embed_hidden(order, section_id, place_ref, x_hbm, w_hbm, out_hbm, bias_ref, *refs):
+def embed_hidden(order, section_id, place_ref, x_hbm, w_hbm, out_hbm, bias_ref, take_g, take_m, take_d, *refs):
     out_w = refs[0]
     outs = refs[1 : 1 + len(order)]
-    x_ref, w_ref, sem = refs[1 + len(order) :]
+    x_ref, w_ref, sem = refs[-3:]
+    bands = take_g.shape[1]
+    for step, out in enumerate(refs[1 + len(order) : -3]):
+        target = place_ref[1] + step
+        target = jnp.where(target >= bands, target - bands, target)
+        begin = 0
+        for take in (take_g, take_m, take_d):
+            out[:, begin : begin + take.shape[2]] = take[0, pl.ds(target, 1), :]
+            begin += take.shape[2]
     copies = started([(x_hbm, x_ref), (w_hbm, w_ref), (out_hbm.at[section_id], out_w)], sem)
     wait_all(copies)
     me = place_ref[0]
@@ -106,10 +114,11 @@
     wait_all(started(pairs, sem))
 
 
-def route(bits, direct, caps, counts, edges, place_ref, tables, from_g, from_m, from_d, to_g, to_m, pos, pos_w, *outs):
+def route(bits, direct, bands, caps, counts, edges, place_ref, *refs):
+    tables = refs[: bands if direct else 1]
+    from_g, from_m, from_d, to_g, to_m, pos, pos_w, *outs = refs[len(tables) :]
     ids_g, ids_m, ids_d, col_g, col_m, row_g, row_m, mesh_out = outs
     me, band = place_ref[0], place_ref[1]
-    bands = tables.shape[0]
 
     def column(row):
         return jnp.broadcast_to(row, (8, row.shape[1])).T[:, :1].astype(jnp.int32)
@@ -120,21 +129,23 @@
         names = senders[:, pl.ds(pl.multiple_of(me * size, size), size)]
         total = jnp.zeros((16, size), F32)
         for s in range(bands):
-            value = tables[s : s + 1, begin : begin + padded]
+            if direct:
+                value = tables[s][:, begin : begin + padded]
+                source = jnp.where(band >= s, band - s, band - s + bands)
+            else:
+                value = tables[0][s : s + 1, begin : begin + padded]
+                source = s
             other = (value >> (count.bit_length() - 1)) ^ me
             slot = jnp.zeros_like(other)
             for i, bit in enumerate(bits):
                 slot = slot + jnp.where((other & bit) != 0, 1 << i, 0)
-            source = s
-            if direct:
-                source = jnp.where(band >= s, band - s, band - s + bands)
-            value = (slot * bands + source) * count + (value & (count - 1))
+            value = (slot * bands + s) * count + (value & (count - 1))
             index = lax.broadcasted_iota(jnp.int32, (16, padded), 0)
             high = jnp.broadcast_to((value >> 7).astype(F32), index.shape)
             low = jnp.broadcast_to((value & 127).astype(F32), index.shape)
             digits = jnp.where(index == 0, high, jnp.where(index == 1, low, 0.0)).astype(BF16)
             slots = lax.broadcasted_iota(jnp.int32, (padded, size), 0)
-            hot = jnp.where((slots + s * cap == names) & (slots < cap), 1.0, 0.0).astype(BF16)
+            hot = jnp.where((slots + source * cap == names) & (slots < cap), 1.0, 0.0).astype(BF16)
             total = total + dot(digits, hot)
         out[...] = column(total[0:1] * 128.0 + total[1:2])
         begin += padded
@@ -299,6 +310,9 @@
     def swap(value, bit):
         return lax.ppermute(value, "feat", [(f, f ^ bit) for f in range(quarters)])
 
+    def shift(value, step):
+        return lax.ppermute(value, "band", [(b, (b + step) % bands) for b in range(bands)])
+
     def pieces(value):
         parts = [value]
         for bit in bits:
@@ -307,10 +321,7 @@
 
     def everyone(rows):
         if direct:
-            parts = [rows] + [
-                lax.ppermute(rows, "band", [(b, (b + step) % bands) for b in range(bands)])
-                for step in range(1, bands)
-            ]
+            parts = [rows] + [shift(rows, step) for step in range(1, bands)]
             for bit in bits:
                 parts = parts + [swap(part, bit) for part in parts]
             return parts
@@ -320,12 +331,15 @@
         parts = [lax.all_gather(part, "band", axis=0, tiled=True) for part in parts]
         return parts + [swap(part, bits[-1]) for part in parts]
 
+    caps = [take.shape[2] for take in (g2m_take, m2m_take, m2g_take)]
+    direct = direct and all(cap % 128 == 0 for cap in caps)
     hidden = kernel_call(
         functools.partial(embed_hidden, order, embed_id),
         [jax.ShapeDtypeStruct((width, latent), BF16)]
-        + [jax.ShapeDtypeStruct((grid_rows, width), BF16)] * quarters,
-        (place, x_grid.T, embed_in, pair_out, hidden_bias),
-        (scalar, hbm, hbm, hbm, vmem),
+        + [jax.ShapeDtypeStruct((grid_rows, width), BF16)] * quarters
+        + [jax.ShapeDtypeStruct((1, sum(caps)), jnp.int32)] * (bands if direct else 0),
+        (place, x_grid.T, embed_in, pair_out, hidden_bias, g2m_take, m2m_take, m2g_take),
+        (scalar, hbm, hbm, hbm, vmem, vmem, vmem, vmem),
         scratch=(
             pltpu.VMEM(x_grid.shape[::-1], BF16),
             pltpu.VMEM(embed_in.shape, BF16),
@@ -334,6 +348,7 @@
         vmem=GRANT,
     )
     out_pieces = pieces(hidden[0])
+    rows = hidden[1 + quarters :]
     hidden = [hidden[1]] + [swap(h, other) for h, other in zip(hidden[2:], order[1:])]
 
     def packs(first_id, sections):
@@ -347,35 +362,37 @@
                 pltpu.VMEM((sections, BIAS_ROWS, width), BF16),
                 pltpu.SemaphoreType.DMA((sections * (2 + latent // width),)),
             ),
-            outs=[hbm] * sections,
             vmem=GRANT,
         )
 
-    takes = [take[0] for take in (g2m_take, m2m_take, m2g_take)]
-    caps = [take.shape[1] for take in takes]
-    takes = [jnp.pad(take, ((0, 0), (0, -take.shape[1] % 128))) for take in takes]
-    tables = lax.all_to_all(
-        jnp.concatenate(takes, axis=1), "band", split_axis=0, concat_axis=0, tiled=True
-    )
+    if direct:
+        tables = [rows[0]] + [shift(row, step) for step, row in enumerate(rows[1:], 1)]
+    else:
+        takes = [jnp.pad(t[0], ((0, 0), (0, -t.shape[2] % 128))) for t in (g2m_take, m2m_take, m2g_take)]
+        tables = [
+            lax.all_to_all(
+                jnp.concatenate(takes, axis=1), "band", split_axis=0, concat_axis=0, tiled=True
+            )
+        ]
     edges = [names.shape[0] // quarters for names in (g2m_from, m2m_from, m2g_from)]
     columns = [jax.ShapeDtypeStruct((n, 1), jnp.int32) for n in edges + edges[:2]]
     lines = [jax.ShapeDtypeStruct((1, n), jnp.int32) for n in edges[:2]]
     shape = jax.ShapeDtypeStruct((mesh_rows, latent), BF16)
-    routed = kernel_call(
-        functools.partial(route, bits, direct, caps, (grid_rows, mesh_rows, mesh_rows), edges),
-        [*columns, *lines, shape],
-        (place, tables, *[v[None, :] for v in (g2m_from, m2m_from, m2g_from, g2m_to, m2m_to)], mesh_pos, pos_weight),
-        (scalar,) + (vmem,) * 8,
-        vmem=GRANT,
-    )
-    pair_in, pair_out, _ = lax.optimization_barrier((pair_in, pair_out, routed[-1]))
+    names = [v[None, :] for v in (g2m_from, m2m_from, m2g_from, g2m_to, m2m_to)]
     packed = packs(0, 2)
     later = packs(2, embed_id - 2)
-    hidden, out_pieces, routed, packed, later = lax.optimization_barrier(
-        (hidden, out_pieces, routed, packed, later)
+    hidden, out_pieces, names, packed, later = lax.optimization_barrier(
+        (hidden, out_pieces, names, packed, later)
+    )
+    packed = packed + later
+    routed = kernel_call(
+        functools.partial(route, bits, direct, bands, caps, (grid_rows, mesh_rows, mesh_rows), edges),
+        [*columns, *lines, shape],
+        (place, *tables, *names, mesh_pos, pos_weight),
+        (scalar,) + (vmem,) * (len(tables) + 7),
+        vmem=24 << 20,
     )
     ids_g, ids_m, ids_d, col_g, col_m, row_g, row_m, mesh = routed
-    packed = packed + later
     grid = kernel_call(
         functools.partial(embed_finish, embed_id, quarters),
         jax.ShapeDtypeStruct((grid_rows, latent), BF16),
@@ -383,23 +400,25 @@
         (vmem,) * (2 * quarters + 2),
     )
 
-    def group(section_id, after, gate):
+    def group(section_id, after, table):
         first, second = packed[section_id : section_id + 2]
         if after is not None:
-            first, second, _ = lax.optimization_barrier((first, second, after))
+            first, _ = lax.optimization_barrier((first, after))
         across = swap(first, bits[0])
-        if after is not None:
-            across, _ = lax.optimization_barrier((across, gate))
+        across, _ = lax.optimization_barrier((across, table[1]))
         over = lax.ppermute(across, "parts", [(0, 1), (1, 0)])
         found = [((0, 0), first), ((1, 0), second), ((0, 1), across), ((1, 1), over)]
         for i, bit in enumerate(bits[1:]):
-            found = found + [((kind, slot + (2 << i)), swap(piece, bit)) for (kind, slot), piece in found]
+            other = [((kind, slot + (2 << i)), piece) for (kind, slot), piece in found]
+            for place_of, piece in other:
+                piece, _ = lax.optimization_barrier((piece, table[bands - 1 if direct else 1]))
+                found.append((place_of, swap(piece, bit)))
         return found
 
     def run(section_id, table, after, ids, own_latent, column, extra, last=False):
         rows = sum(part.shape[0] for part in table)
         edges = ids.shape[0]
-        weights = group(section_id, after, table[1])
+        weights = group(section_id, after, table)
         places = [p for p, _ in weights]
         weights = [piece for _, piece in weights]
         square = jax.ShapeDtypeStruct((latent, latent), BF16)

time: 289 us -> 184 us (0.64)
  Pallas kernels: 123 us -> 29.9 us
  waiting for transfers between devices: 98.5 us -> 91.1 us
    pallas_call x13, Pallas kernels: 123 us -> 29.9 us  [kernel_call(): pl.pallas_call(body, out_shape=out_shape, in_specs=[pl.BlockSpec(memory_s...]
    ppermute x4, waiting for transfers between devices: 12.5 us -> 0.01 us  [group(): over = lax.ppermute(across, 'parts', [(0, 1), (1, 0)])]
    ppermute x12 -> x15, waiting for transfers between devices: 29 us -> 41.4 us  [shift(): lax.ppermute(value, 'band', [(b, (b + step) % bands) for b in range(bands)])]
    all_to_all x1 -> x0, starting transfers between devices: 5.46 us -> none  [local(): lax.all_to_all(jnp.concatenate(takes, axis=1), 'band', split_axis=0, conc...]
    all_to_all x1 -> x0, waiting for transfers between devices: 4.33 us -> none  [local(): lax.all_to_all(jnp.concatenate(takes, axis=1), 'band', split_axis=0, conc...]
    ppermute x74, waiting for transfers between devices: 52.7 us -> 49.7 us  [swap(): return lax.ppermute(value, 'feat', [(f, f ^ bit) for f in range(quarters)])]
    ppermute x74, starting transfers between devices: 33.5 us -> 36.4 us  [swap(): return lax.ppermute(value, 'feat', [(f, f ^ bit) for f in range(quarters)])]
    ppermute x12 -> x15, starting transfers between devices: 16.7 us -> 18.7 us  [shift(): lax.ppermute(value, 'band', [(b, (b + step) % bands) for b in range(bands)])]
  transfers between devices with their start and end apart: 91 -> 93, of which waited for: 34 -> 36; matrix products, arithmetic and copies ran while one was open for 1% -> 0% of each run, Pallas kernels for 41% -> 13%
where the time goes in v7:
time: 184 us
  waiting for transfers between devices  91.1 us (50%)
  starting transfers between devices  59.3 us (32%)
  Pallas kernels  29.9 us (16%)
  local copies, waits for them, and re-layouts  2.12 us (1%)
    ppermute x74, waiting for transfers between devices, swap(): return lax.ppermute(value, 'feat', [(f, f ^ bit) for f in range(quarters)])  49.7 us
    ppermute x15, waiting for transfers between devices, shift(): lax.ppermute(value, 'band', [(b, (b + step) % bands) for b in range(bands)])  41.4 us
    ppermute x74, starting transfers between devices, swap(): return lax.ppermute(value, 'feat', [(f, f ^ bit) for f in range(quarters)])  36.4 us
    pallas_call x13, Pallas kernels, kernel_call(): pl.pallas_call(body, out_shape=out_shape, in_specs=[pl.BlockSpec(memory_s...  29.9 us
    ppermute x15, starting transfers between devices, shift(): lax.ppermute(value, 'band', [(b, (b + step) % bands) for b in range(bands)])  18.7 us
    ppermute x4, starting transfers between devices, group(): over = lax.ppermute(across, 'parts', [(0, 1), (1, 0)])  4.29 us
  transfers between devices with their start and end apart: 93, of which 36 were waited for; matrix products, arithmetic and copies ran while one was open for 0% of the time, Pallas kernels for 13%

profile of v7, /device:TPU:0, one launch (start us, length us, event | category | flops | bytes accessed | tf_op | source)
XLA Modules:
  0.0 183.7 jit_solution(1667645228725429190)
XLA Ops:
  0.7 2.9 %shard_map.172 = (bf16[128,512]{1,0:T(8,128)(2,1)}, bf16[128,128]{1,0:T(8,128)(2,1)}, bf16[128,128]{1,0:T(8,128)(2,1)}, bf16[128,128]{1,0:T(8,128)(2,1)}, bf16[1...) custom-call(s32[3]{0:T(128)} %pad_add_fusion.place_ref.refs_0_, ...), custom_call_target="tpu_custom_call" | custom-call | bytes 4194304 | tf_op jit(solution)/shard_map/pallas_call | solution.py:37
  3.6 3.0 %collective-permute-start.3 = (bf16[128,512]{1,0:T(8,128)(2,1)}, bf16[128,512]{1,0:T(8,128)(2,1)S(1)}, u32[]{:S(2)}, u32[]{:S(2)}) collective-permute-start(bf16[128,512]{1,0:T(8,128)(2,1)} %get-tuple-element.115.refs_4_), channel_id=1, source_target_pairs={{0,2},{1,3},{2,0},{3,1},{4,6},{5,7},{6,4},{7,5},{8,10},{9,11},{10,... | collective-permute-start | bytes 393224 | tf_op jit(solution)/shard_map/ppermute | solution.py:311
  6.6 3.7 %collective-permute-done.3.refs_5_ = bf16[128,512]{1,0:T(8,128)(2,1)S(1)} collective-permute-done((bf16[128,512]{1,0:T(8,128)(2,1)}, bf16[128,512]{1,0:T(8,128)(2,1)S(1)}, u32[]{:S(2)}, u32[]{:S(2)}) %collective-permute-start.3) | collective-permute-done | bytes 131104 | tf_op jit(solution)/shard_map/ppermute | solution.py:311
  12.4 4.1 %shard_map.174 = (bf16[1552,128]{1,0:T(8,128)(2,1)}, bf16[1552,128]{1,0:T(8,128)(2,1)}, bf16[1552,128]{1,0:T(8,128)(2,1)}, bf16[1552,128]{1,0:T(8,128)(2,1)}, bf...) custom-call(s32[3]{0:T(128)} %pad_add_fusion.place_ref.refs_0_, bf16[8,1024,128]{2,1,0:T(8,128)(2,1)} %in_hbm.3, ...), custom_call_target="tpu_custom_call" | custom-call | bytes 4194304 | tf_op jit(solution)/shard_map/pallas_call | solution.py:37
  16.7 3.0 %shard_map.173 = (bf16[1552,128]{1,0:T(8,128)(2,1)}, bf16[1552,128]{1,0:T(8,128)(2,1)}) custom-call(s32[3]{0:T(128)} %pad_add_fusion.place_ref.refs_0_, bf16[8,1024,128]{2,1,0:T(8,128)(2,1)} %in_hbm.3, bf16[9,128,512]{2,1,0:T(8,128)(2,1)} %out_hbm.5, f32[9,128]{1,0:T(8,128)} %bias_ref.5), custom_call_target="tpu_custom_call" | custom-call | bytes 4194304 | tf_op jit(solution)/shard_map/pallas_call | solution.py:37
  23.7 5.6 %collective-permute-done.6.refs_1_ = bf16[128,512]{1,0:T(8,128)(2,1)S(1)} collective-permute-done((bf16[128,512]{1,0:T(8,128)(2,1)S(1)}, bf16[128,512]{1,0:T(8,128)(2,1)S(1)}, u32[]{:S(2)}, u32[]{:S(2)}) %collective-permute-start.6) | collective-permute-done | bytes 131104 | tf_op jit(solution)/shard_map/ppermute | solution.py:314
  33.2 3.6 %collective-permute-start.8 = (bf16[128,512]{1,0:T(8,128)(2,1)S(1)}, bf16[128,512]{1,0:T(8,128)(2,1)S(1)}, u32[]{:S(2)}, u32[]{:S(2)}) collective-permute-start(bf16[128,512]{1,0:T(8,128)(2,1)S(1)} %shard_map.175.refs_0_.refs_9_.refs_17_), channel_id=1, source_target_pairs={{0,12},{4,0},{8,4},{12,8},{1,13},{5,1},{9,5},{13,9},{2,14},{6,2},{... | collective-permute-start | bytes 393224 | tf_op jit(solution)/shard_map/ppermute | solution.py:314
  39.3 4.5 %collective-permute-done.21.refs_1_ = s32[1,1152]{1,0:T(1,128)S(1)} collective-permute-done((s32[1,1152]{1,0:T(1,128)S(1)}, s32[1,1152]{1,0:T(1,128)S(1)}, u32[]{:S(2)}, u32[]{:S(2)}) %collective-permute-start.21) | collective-permute-done | bytes 4640 | tf_op jit(solution)/shard_map/ppermute | solution.py:314
  43.8 3.5 %collective-permute-start.22 = (s32[1,1152]{1,0:T(1,128)S(1)}, s32[1,1152]{1,0:T(1,128)S(1)}, u32[]{:S(2)}, u32[]{:S(2)}) collective-permute-start(s32[1,1152]{1,0:T(1,128)S(1)} %copy-done.23), channel_id=1, source_target_pairs={{0,8},{4,12},{8,0},{12,4},{1,9},{5,13},{9,1},{13,5},{2,10},{6,14},... | collective-permute-start | bytes 13832 | tf_op jit(solution)/shard_map/ppermute | solution.py:314
  49.3 3.2 %collective-permute-done.23.refs_3_ = s32[1,1152]{1,0:T(1,128)S(1)} collective-permute-done((s32[1,1152]{1,0:T(1,128)S(1)}, s32[1,1152]{1,0:T(1,128)S(1)}, u32[]{:S(2)}, u32[]{:S(2)}) %collective-permute-start.23) | collective-permute-done | bytes 4640 | tf_op jit(solution)/shard_map/ppermute | solution.py:314
  58.8 2.8 %collective-permute-done.11.refs_6_ = bf16[128,512]{1,0:T(8,128)(2,1)S(1)} collective-permute-done((bf16[128,512]{1,0:T(8,128)(2,1)S(1)}, bf16[128,512]{1,0:T(8,128)(2,1)S(1)}, u32[]{:S(2)}, u32[]{:S(2)}) %collective-permute-start.11) | collective-permute-done | bytes 131104 | tf_op jit(solution)/shard_map/ppermute | solution.py:311
  78.6 5.8 %collective-permute-done.30.refs_1_ = bf16[128,512]{1,0:T(8,128)(2,1)S(1)} collective-permute-done((bf16[128,512]{1,0:T(8,128)(2,1)S(1)}, bf16[128,512]{1,0:T(8,128)(2,1)S(1)}, u32[]{:S(2)}, u32[]{:S(2)}) %collective-permute-start.30) | collective-permute-done | bytes 131104 | tf_op jit(solution)/shard_map/ppermute | solution.py:314
  86.5 3.6 %collective-permute-done.32.refs_3_ = bf16[128,512]{1,0:T(8,128)(2,1)S(1)} collective-permute-done((bf16[128,512]{1,0:T(8,128)(2,1)S(1)}, bf16[128,512]{1,0:T(8,128)(2,1)S(1)}, u32[]{:S(2)}, u32[]{:S(2)}) %collective-permute-start.32) | collective-permute-done | bytes 131104 | tf_op jit(solution)/shard_map/ppermute | solution.py:314
  90.7 3.8 %collective-permute-done.31.refs_2_ = bf16[128,512]{1,0:T(8,128)(2,1)S(1)} collective-permute-done((bf16[128,512]{1,0:T(8,128)(2,1)S(1)}, bf16[128,512]{1,0:T(8,128)(2,1)S(1)}, u32[]{:S(2)}, u32[]{:S(2)}) %collective-permute-start.31) | collective-permute-done | bytes 131104 | tf_op jit(solution)/shard_map/ppermute | solution.py:314
  97.1 3.6 %collective-permute-done.35.refs_6_ = bf16[128,512]{1,0:T(8,128)(2,1)S(1)} collective-permute-done((bf16[128,512]{1,0:T(8,128)(2,1)S(1)}, bf16[128,512]{1,0:T(8,128)(2,1)S(1)}, u32[]{:S(2)}, u32[]{:S(2)}) %collective-permute-start.35) | collective-permute-done | bytes 131104 | tf_op jit(solution)/shard_map/ppermute | solution.py:311
  108.9 2.9 %shard_map.180.refs_9_.refs_0_.refs_17_ = bf16[128,512]{1,0:T(8,128)(2,1)S(1)} custom-call(bf16[128,512]{1,0:T(8,128)(2,1)S(1)} %shard_map.178.refs_9_.refs_0_.refs_17_, bf16[128,512]{1,0:T(8,128)(2,1)S(1)} %collective-permute-done.30.refs_1_, bf16[128,512]{1,0:T(8,128)(2,1)S(1)} %collective-permute-done.31.refs_2_, ...), custom_call_target="tpu_custom_call" | custom-call | flops 1879048192 | bytes 4194304 | tf_op jit(solution)/shard_map/pallas_call | solution.py:37
  113.0 4.7 %collective-permute-done.66.refs_3_ = bf16[1552,128]{1,0:T(8,128)(2,1)S(1)} collective-permute-done((bf16[1552,128]{1,0:T(8,128)(2,1)S(1)}, bf16[1552,128]{1,0:T(8,128)(2,1)S(1)}, u32[]{:S(2)}, u32[]{:S(2)}) %collective-permute-start.66) | collective-permute-done | bytes 397344 | tf_op jit(solution)/shard_map/ppermute | solution.py:311
  133.1 3.3 %collective-permute-done.56.refs_6_ = bf16[128,512]{1,0:T(8,128)(2,1)S(1)} collective-permute-done((bf16[128,512]{1,0:T(8,128)(2,1)S(1)}, bf16[128,512]{1,0:T(8,128)(2,1)S(1)}, u32[]{:S(2)}, u32[]{:S(2)}) %collective-permute-start.56) | collective-permute-done | bytes 131104 | tf_op jit(solution)/shard_map/ppermute | solution.py:311
  145.0 2.8 %shard_map.182.refs_0_ = bf16[128,512]{1,0:T(8,128)(2,1)S(1)} custom-call(bf16[128,512]{1,0:T(8,128)(2,1)S(1)} %shard_map.180.refs_9_.refs_0_.refs_17_, bf16[128,512]{1,0:T(8,128)(2,1)S(1)} %collective-permute-done.51.refs_1_, bf16[128,512]{1,0:T(8,128)(2,1)S(1)} %collective-permute-done.52.refs_2_, bf16[128,512]{1,0:T(8,128)(2,1)S(1)} %collective-permute-done.53.refs_3_, ...), custom_call_target="tpu_custom_call" | custom-call | flops 1879048192 | bytes 4194304 | tf_op jit(solution)/shard_map/pallas_call | solution.py:37
  148.3 5.0 %collective-permute-done.87.refs_3_ = bf16[1552,128]{1,0:T(8,128)(2,1)S(1)} collective-permute-done((bf16[1552,128]{1,0:T(8,128)(2,1)S(1)}, bf16[1552,128]{1,0:T(8,128)(2,1)S(1)}, u32[]{:S(2)}, u32[]{:S(2)}) %collective-permute-start.87) | collective-permute-done | bytes 397344 | tf_op jit(solution)/shard_map/ppermute | solution.py:311
  158.3 2.9 %collective-permute-done.74.refs_3_ = bf16[128,512]{1,0:T(8,128)(2,1)S(1)} collective-permute-done((bf16[128,512]{1,0:T(8,128)(2,1)S(1)}, bf16[128,512]{1,0:T(8,128)(2,1)S(1)}, u32[]{:S(2)}, u32[]{:S(2)}) %collective-permute-start.74) | collective-permute-done | bytes 131104 | tf_op jit(solution)/shard_map/ppermute | solution.py:314
  166.9 2.9 %collective-permute-done.77.refs_6_ = bf16[128,512]{1,0:T(8,128)(2,1)S(1)} collective-permute-done((bf16[128,512]{1,0:T(8,128)(2,1)S(1)}, bf16[128,512]{1,0:T(8,128)(2,1)S(1)}, u32[]{:S(2)}, u32[]{:S(2)}) %collective-permute-start.77) | collective-permute-done | bytes 131104 | tf_op jit(solution)/shard_map/ppermute | solution.py:311
  170.9 3.9 %collective-permute-done.78.refs_7_ = bf16[128,512]{1,0:T(8,128)(2,1)S(1)} collective-permute-done((bf16[128,512]{1,0:T(8,128)(2,1)S(1)}, bf16[128,512]{1,0:T(8,128)(2,1)S(1)}, u32[]{:S(2)}, u32[]{:S(2)}) %collective-permute-start.78) | collective-permute-done | bytes 131104 | tf_op jit(solution)/shard_map/ppermute | solution.py:311
  180.4 3.4 %shard_map.184 = f32[227,128]{1,0:T(8,128)} custom-call(bf16[128,512]{1,0:T(8,128)(2,1)S(1)} %shard_map.182.refs_0_, bf16[128,512]{1,0:T(8,128)(2,1)S(1)} %collective-permute-done.72.refs_1_, bf16[128,512]{1,0:T(8,128)(2,1)S(1)} %collective-permute-done.73.refs_2_, bf16[128,512]{1,0:T(8,128)(2,1)S(1)} %collective-permute-done.74.refs_3_, ...), custom_call_target="tpu_custom_call" | custom-call | flops 1409286144 | bytes 4194304 | tf_op jit(solution)/shard_map/pallas_call | solution.py:37
  (227 shorter events, 94.6 us)
Async XLA Ops:
  6.6 13.2 %collective-permute-start.4 = (bf16[128,512]{1,0:T(8,128)(2,1)}, bf16[128,512]{1,0:T(8,128)(2,1)S(1)}, u32[]{:S(2)}, u32[]{:S(2)}) collective-permute-start(bf16[128,512]{1,0:T(8,128)(2,1)} %get-tuple-element.115.refs_4_), channel_id=1, source_target_pairs={{0,1},{1,0},{2,3},{3,2},{4,5},{5,4},{6,7},{7,6},{8,9},{9,8},{10,11... | collective-permute-start | bytes 393224 | tf_op jit(solution)/shard_map/ppermute | solution.py:311
  10.3 9.5 %collective-permute-start.5 = (bf16[128,512]{1,0:T(8,128)(2,1)S(1)}, bf16[128,512]{1,0:T(8,128)(2,1)S(1)}, u32[]{:S(2)}, u32[]{:S(2)}) collective-permute-start(bf16[128,512]{1,0:T(8,128)(2,1)S(1)} %collective-permute-done.3.refs_5_), channel_id=1, source_target_pairs={{0,1},{1,0},{2,3},{3,2},{4,5},{5,4},{6,7},{7,6},{8,9},{9,8},{10,11... | collective-permute-start | bytes 393224 | tf_op jit(solution)/shard_map/ppermute | solution.py:311
  10.3 9.5 %collective-permute-start = (bf16[128,128]{1,0:T(8,128)(2,1)}, bf16[128,128]{1,0:T(8,128)(2,1)S(1)}, u32[]{:S(2)}, u32[]{:S(2)}) collective-permute-start(bf16[128,128]{1,0:T(8,128)(2,1)} %get-tuple-element.99), channel_id=1, source_target_pairs={{0,2},{1,3},{2,0},{3,1},{4,6},{5,7},{6,4},{7,5},{8,10},{9,11},{10,... | collective-permute-start | bytes 98312 | tf_op jit(solution)/shard_map/ppermute | solution.py:311
  19.8 11.6 %collective-permute-start.24 = (bf16[1552,128]{1,0:T(8,128)(2,1)}, bf16[1552,128]{1,0:T(8,128)(2,1)S(1)}, u32[]{:S(2)}, u32[]{:S(2)}) collective-permute-start(bf16[1552,128]{1,0:T(8,128)(2,1)} %get-tuple-element.133.refs_1_), channel_id=1, source_target_pairs={{0,2},{1,3},{2,0},{3,1},{4,6},{5,7},{6,4},{7,5},{8,10},{9,11},{10,... | collective-permute-start | bytes 1191944 | tf_op jit(solution)/shard_map/ppermute | solution.py:311
  31.4 24.6 %collective-permute-start.25 = (bf16[1552,128]{1,0:T(8,128)(2,1)S(1)}, bf16[1552,128]{1,0:T(8,128)(2,1)S(1)}, u32[]{:S(2)}, u32[]{:S(2)}) collective-permute-start(bf16[1552,128]{1,0:T(8,128)(2,1)S(1)} %collective-permute-done.24.refs_3_), channel_id=1, source_target_pairs={{0,16},{16,0},{1,17},{17,1},{2,18},{18,2},{3,19},{19,3},{4,20},{20... | collective-permute-start | bytes 1191944 | tf_op jit(solution)/shard_map/ppermute | solution.py:409
  33.2 19.3 %collective-permute-start.8 = (bf16[128,512]{1,0:T(8,128)(2,1)S(1)}, bf16[128,512]{1,0:T(8,128)(2,1)S(1)}, u32[]{:S(2)}, u32[]{:S(2)}) collective-permute-start(bf16[128,512]{1,0:T(8,128)(2,1)S(1)} %shard_map.175.refs_0_.refs_9_.refs_17_), channel_id=1, source_target_pairs={{0,12},{4,0},{8,4},{12,8},{1,13},{5,1},{9,5},{13,9},{2,14},{6,2},{... | collective-permute-start | bytes 393224 | tf_op jit(solution)/shard_map/ppermute | solution.py:314
  36.8 17.2 %collective-permute-start.7 = (bf16[128,512]{1,0:T(8,128)(2,1)S(1)}, bf16[128,512]{1,0:T(8,128)(2,1)S(1)}, u32[]{:S(2)}, u32[]{:S(2)}) collective-permute-start(bf16[128,512]{1,0:T(8,128)(2,1)S(1)} %shard_map.175.refs_0_.refs_9_.refs_17_), channel_id=1, source_target_pairs={{0,8},{4,12},{8,0},{12,4},{1,9},{5,13},{9,1},{13,5},{2,10},{6,14},... | collective-permute-start | bytes 393224 | tf_op jit(solution)/shard_map/ppermute | solution.py:314
  36.8 17.7 %collective-permute-start.9 = (bf16[128,512]{1,0:T(8,128)(2,1)S(1)}, bf16[128,512]{1,0:T(8,128)(2,1)S(1)}, u32[]{:S(2)}, u32[]{:S(2)}) collective-permute-start(bf16[128,512]{1,0:T(8,128)(2,1)S(1)} %shard_map.175.refs_0_.refs_9_.refs_17_), channel_id=1, source_target_pairs={{0,2},{1,3},{2,0},{3,1},{4,6},{5,7},{6,4},{7,5},{8,10},{9,11},{10,... | collective-permute-start | bytes 393224 | tf_op jit(solution)/shard_map/ppermute | solution.py:311
  54.5 9.5 %collective-permute-start.12 = (bf16[128,512]{1,0:T(8,128)(2,1)S(1)}, bf16[128,512]{1,0:T(8,128)(2,1)S(1)}, u32[]{:S(2)}, u32[]{:S(2)}) collective-permute-start(bf16[128,512]{1,0:T(8,128)(2,1)S(1)} %collective-permute-done.8.refs_3_), channel_id=1, source_target_pairs={{0,2},{1,3},{2,0},{3,1},{4,6},{5,7},{6,4},{7,5},{8,10},{9,11},{10,... | collective-permute-start | bytes 393224 | tf_op jit(solution)/shard_map/ppermute | solution.py:311
  56.0 12.8 %collective-permute-start.27 = (bf16[1552,128]{1,0:T(8,128)(2,1)}, bf16[1552,128]{1,0:T(8,128)(2,1)S(1)}, u32[]{:S(2)}, u32[]{:S(2)}) collective-permute-start(bf16[1552,128]{1,0:T(8,128)(2,1)} %get-tuple-element.134.refs_2_), channel_id=1, source_target_pairs={{0,1},{1,0},{2,3},{3,2},{4,5},{5,4},{6,7},{7,6},{8,9},{9,8},{10,11... | collective-permute-start | bytes 1191944 | tf_op jit(solution)/shard_map/ppermute | solution.py:311
  58.8 10.0 %collective-permute-start.26 = (bf16[1552,128]{1,0:T(8,128)(2,1)}, bf16[1552,128]{1,0:T(8,128)(2,1)S(1)}, u32[]{:S(2)}, u32[]{:S(2)}) collective-permute-start(bf16[1552,128]{1,0:T(8,128)(2,1)} %get-tuple-element.133.refs_1_), channel_id=1, source_target_pairs={{0,1},{1,0},{2,3},{3,2},{4,5},{5,4},{6,7},{7,6},{8,9},{9,8},{10,11... | collective-permute-start | bytes 1191944 | tf_op jit(solution)/shard_map/ppermute | solution.py:311
  67.3 11.3 %collective-permute-start.45 = (bf16[1552,128]{1,0:T(8,128)(2,1)S(1)}, bf16[1552,128]{1,0:T(8,128)(2,1)S(1)}, u32[]{:S(2)}, u32[]{:S(2)}) collective-permute-start(bf16[1552,128]{1,0:T(8,128)(2,1)S(1)} %copy-done.4), channel_id=1, source_target_pairs={{0,2},{1,3},{2,0},{3,1},{4,6},{5,7},{6,4},{7,5},{8,10},{9,11},{10,... | collective-permute-start | bytes 1191944 | tf_op jit(solution)/shard_map/ppermute | solution.py:311
  84.4 16.3 %collective-permute-start.46 = (bf16[1552,128]{1,0:T(8,128)(2,1)S(1)}, bf16[1552,128]{1,0:T(8,128)(2,1)S(1)}, u32[]{:S(2)}, u32[]{:S(2)}) collective-permute-start(bf16[1552,128]{1,0:T(8,128)(2,1)S(1)} %collective-permute-done.45.refs_3_), channel_id=1, source_target_pairs={{0,16},{16,0},{1,17},{17,1},{2,18},{18,2},{3,19},{19,3},{4,20},{20... | collective-permute-start | bytes 1191944 | tf_op jit(solution)/shard_map/ppermute | solution.py:409
  86.0 9.1 %collective-permute-start.33 = (bf16[128,512]{1,0:T(8,128)(2,1)S(1)}, bf16[128,512]{1,0:T(8,128)(2,1)S(1)}, u32[]{:S(2)}, u32[]{:S(2)}) collective-permute-start(bf16[128,512]{1,0:T(8,128)(2,1)S(1)} %shard_map.178.refs_9_.refs_0_.refs_17_), channel_id=1, source_target_pairs={{0,2},{1,3},{2,0},{3,1},{4,6},{5,7},{6,4},{7,5},{8,10},{9,11},{10,... | collective-permute-start | bytes 393224 | tf_op jit(solution)/shard_map/ppermute | solution.py:311
  86.5 10.1 %collective-permute-start.37 = (bf16[128,512]{1,0:T(8,128)(2,1)S(1)}, bf16[128,512]{1,0:T(8,128)(2,1)S(1)}, u32[]{:S(2)}, u32[]{:S(2)}) collective-permute-start(bf16[128,512]{1,0:T(8,128)(2,1)S(1)} %shard_map.178.refs_9_.refs_0_.refs_17_), channel_id=1, source_target_pairs={{0,1},{1,0},{2,3},{3,2},{4,5},{5,4},{6,7},{7,6},{8,9},{9,8},{10,11... | collective-permute-start | bytes 393224 | tf_op jit(solution)/shard_map/ppermute | solution.py:311
  96.6 9.3 %collective-permute-start.48 = (bf16[1552,128]{1,0:T(8,128)(2,1)S(1)}, bf16[1552,128]{1,0:T(8,128)(2,1)S(1)}, u32[]{:S(2)}, u32[]{:S(2)}) collective-permute-start(bf16[1552,128]{1,0:T(8,128)(2,1)S(1)} %copy-done.5), channel_id=1, source_target_pairs={{0,1},{1,0},{2,3},{3,2},{4,5},{5,4},{6,7},{7,6},{8,9},{9,8},{10,11... | collective-permute-start | bytes 1191944 | tf_op jit(solution)/shard_map/ppermute | solution.py:311
  106.4 11.3 %collective-permute-start.66 = (bf16[1552,128]{1,0:T(8,128)(2,1)S(1)}, bf16[1552,128]{1,0:T(8,128)(2,1)S(1)}, u32[]{:S(2)}, u32[]{:S(2)}) collective-permute-start(bf16[1552,128]{1,0:T(8,128)(2,1)S(1)} %copy-done.2), channel_id=1, source_target_pairs={{0,2},{1,3},{2,0},{3,1},{4,6},{5,7},{6,4},{7,5},{8,10},{9,11},{10,... | collective-permute-start | bytes 1191944 | tf_op jit(solution)/shard_map/ppermute | solution.py:311
  119.3 17.0 %collective-permute-start.67 = (bf16[1552,128]{1,0:T(8,128)(2,1)S(1)}, bf16[1552,128]{1,0:T(8,128)(2,1)S(1)}, u32[]{:S(2)}, u32[]{:S(2)}) collective-permute-start(bf16[1552,128]{1,0:T(8,128)(2,1)S(1)} %collective-permute-done.66.refs_3_), channel_id=1, source_target_pairs={{0,16},{16,0},{1,17},{17,1},{2,18},{18,2},{3,19},{19,3},{4,20},{20... | collective-permute-start | bytes 1191944 | tf_op jit(solution)/shard_map/ppermute | solution.py:409
  142.0 11.3 %collective-permute-start.87 = (bf16[1552,128]{1,0:T(8,128)(2,1)S(1)}, bf16[1552,128]{1,0:T(8,128)(2,1)S(1)}, u32[]{:S(2)}, u32[]{:S(2)}) collective-permute-start(bf16[1552,128]{1,0:T(8,128)(2,1)S(1)} %copy-done), channel_id=1, source_target_pairs={{0,2},{1,3},{2,0},{3,1},{4,6},{5,7},{6,4},{7,5},{8,10},{9,11},{10,... | collective-permute-start | bytes 1191944 | tf_op jit(solution)/shard_map/ppermute | solution.py:311
  155.0 10.9 %collective-permute-start.88 = (bf16[1552,128]{1,0:T(8,128)(2,1)S(1)}, bf16[1552,128]{1,0:T(8,128)(2,1)S(1)}, u32[]{:S(2)}, u32[]{:S(2)}) collective-permute-start(bf16[1552,128]{1,0:T(8,128)(2,1)S(1)} %collective-permute-done.87.refs_3_), channel_id=1, source_target_pairs={{0,16},{16,0},{1,17},{17,1},{2,18},{18,2},{3,19},{19,3},{4,20},{20... | collective-permute-start | bytes 1191944 | tf_op jit(solution)/shard_map/ppermute | solution.py:409
  165.9 11.8 %collective-permute-start.91 = (bf16[1552,128]{1,0:T(8,128)(2,1)S(1)}, bf16[1552,128]{1,0:T(8,128)(2,1)S(1)}, u32[]{:S(2)}, u32[]{:S(2)}) collective-permute-start(bf16[1552,128]{1,0:T(8,128)(2,1)S(1)} %collective-permute-done.87.refs_3_), channel_id=1, source_target_pairs={{0,1},{1,0},{2,3},{3,2},{4,5},{5,4},{6,7},{7,6},{8,9},{9,8},{10,11... | collective-permute-start | bytes 1191944 | tf_op jit(solution)/shard_map/ppermute | solution.py:311
  165.9 12.1 %collective-permute-start.90 = (bf16[1552,128]{1,0:T(8,128)(2,1)S(1)}, bf16[1552,128]{1,0:T(8,128)(2,1)S(1)}, u32[]{:S(2)}, u32[]{:S(2)}) collective-permute-start(bf16[1552,128]{1,0:T(8,128)(2,1)S(1)} %copy-done.1), channel_id=1, source_target_pairs={{0,1},{1,0},{2,3},{3,2},{4,5},{5,4},{6,7},{7,6},{8,9},{9,8},{10,11... | collective-permute-start | bytes 1191944 | tf_op jit(solution)/shard_map/ppermute | solution.py:311
  166.4 11.8 %collective-permute-start.89 = (bf16[1552,128]{1,0:T(8,128)(2,1)S(1)}, bf16[1552,128]{1,0:T(8,128)(2,1)S(1)}, u32[]{:S(2)}, u32[]{:S(2)}) collective-permute-start(bf16[1552,128]{1,0:T(8,128)(2,1)S(1)} %copy-done), channel_id=1, source_target_pairs={{0,1},{1,0},{2,3},{3,2},{4,5},{5,4},{6,7},{7,6},{8,9},{9,8},{10,11... | collective-permute-start | bytes 1191944 | tf_op jit(solution)/shard_map/ppermute | solution.py:311
  166.5 12.0 %collective-permute-start.92 = (bf16[1552,128]{1,0:T(8,128)(2,1)S(1)}, bf16[1552,128]{1,0:T(8,128)(2,1)S(1)}, u32[]{:S(2)}, u32[]{:S(2)}) collective-permute-start(bf16[1552,128]{1,0:T(8,128)(2,1)S(1)} %collective-permute-done.88.refs_4_), channel_id=1, source_target_pairs={{0,1},{1,0},{2,3},{3,2},{4,5},{5,4},{6,7},{7,6},{8,9},{9,8},{10,11... | collective-permute-start | bytes 1191944 | tf_op jit(solution)/shard_map/ppermute | solution.py:311
  (94 other events, 1099.7 us)

commit v8 on v7

--- a/solution.py
+++ b/solution.py
@@ -90,18 +90,19 @@
     out[...] = layer_norm(dot(hidden, weights), gain[row, :], shift[row, :]).astype(BF16)
 
 
-def pack(first_id, place_ref, in_hbm, out_hbm, bias_ref, *refs):
-    outs = refs[:-2]
-    terms, sem = refs[-2:]
+def pack(place_ref, in_hbm, out_ref, bias_ref, packed, *refs):
+    crossing, sem = refs[:-1], refs[-1]
     part = place_ref[2]
     inner, width = in_hbm.shape[1:]
-    latent = out_hbm.shape[2]
+    latent = out_ref.shape[2]
+    targets = []
     pairs = []
-    for i, out in enumerate(outs):
-        section_id = first_id + (i - i % 2) + (part if i % 2 == 0 else 1 - part)
-        pairs.append((in_hbm.at[section_id], out.at[pl.ds(0, inner)]))
-        for b in range(0, latent, width):
-            pairs.append((out_hbm.at[section_id, :, pl.ds(b, width)], out.at[pl.ds(inner + b, width)]))
+    for i in range(packed.shape[0]):
+        section_id = (i - i % 2) + (part if i % 2 == 0 else 1 - part)
+        targets.append((section_id, [packed.at[i]] + ([crossing[i // 2]] if i % 2 == 0 else [])))
+        pairs += [(in_hbm.at[section_id], out.at[pl.ds(0, inner)]) for out in targets[-1][1]]
+    copies = started(pairs, sem)
+    for section_id, outs in targets:
         rest = bias_ref[pl.ds(section_id, 1), :]
         index = lax.broadcasted_iota(jnp.int32, (BIAS_ROWS, width), 0)
         value = jnp.zeros((BIAS_ROWS, width), F32)
@@ -109,9 +110,12 @@
             head = rest.astype(BF16).astype(F32)
             value = jnp.where(index == term, head, value)
             rest = rest - head
-        terms[i] = value.astype(BF16)
-        pairs.append((terms.at[i], out.at[pl.ds(inner + latent, BIAS_ROWS)]))
-    wait_all(started(pairs, sem))
+        second = out_ref[section_id]
+        for out in outs:
+            out[pl.ds(inner + latent, BIAS_ROWS), :] = value.astype(BF16)
+            for b in range(0, latent, width):
+                out[pl.ds(inner + b, width), :] = second[:, b : b + width]
+    wait_all(copies)
 
 
 def route(bits, direct, bands, caps, counts, edges, place_ref, *refs):
@@ -164,17 +168,22 @@
     mesh_out[...] = (mesh + turned[:, 2:3] * pos_w[2:3, :]).astype(BF16)
 
 
-def stage(places, last, *refs):
-    place_ref = refs[0]
-    pieces = refs[1 : 1 + len(places)]
-    own_ref, *rest = refs[1 + len(places) :]
-    if last:
-        w_send, w_out, w_agg, w_out2, recv_pre, node_pre = rest
-    else:
-        recv_col, w_send, w_out, w_agg, w_out2, recv_pre, node_pre = rest
+def stage(group_id, last, *refs):
+    place_ref, mine_hbm, other_hbm, *across, own_ref = refs[:8]
+    rest = refs[8:]
+    if not last:
+        recv_col, *rest = rest
+    w_send, w_out, w_agg, w_out2, recv_pre, node_pre, mine, other, sem = rest
+    chosen = pl.ds(2 * group_id, 2)
+    copies = started([(mine_hbm.at[chosen], mine), (other_hbm.at[chosen], other)], sem)
+    x_first, y_second, cx_first, cy_second = across
+    kinds = (
+        [mine.at[0], x_first, other.at[0], cx_first],
+        [mine.at[1], y_second, other.at[1], cy_second],
+    )
     own = own_ref[...]
     rows, latent = own.shape
-    width = pieces[0].shape[1]
+    width = mine.shape[2]
     edges = recv_pre.shape[0]
     if last:
         degree = edges // rows
@@ -196,15 +205,10 @@
             for b in range(0, latent, width):
                 out[columns, pl.ds(b, width)] = ref[pl.ds(2 * latent + b, width), :]
 
+    wait_all(copies)
+
     def emit(edge_kind):
-        ordered = [
-            [ref for _, ref in sorted(
-                    ((slot, ref) for (kind, slot), ref in zip(places, pieces) if kind == wanted),
-                    key=lambda pair: pair[0],
-                )]
-            for wanted in (edge_kind, 1 - edge_kind)
-        ]
-        first, second = ordered
+        first, second = kinds[edge_kind], kinds[1 - edge_kind]
         fill(w_send, w_out, 0, first)
         fill(w_agg, w_out2, latent, second)
         weights = jnp.concatenate([ref[pl.ds(latent, latent), :] for ref in first], axis=1)
@@ -333,6 +337,8 @@
 
     caps = [take.shape[2] for take in (g2m_take, m2m_take, m2g_take)]
     direct = direct and all(cap % 128 == 0 for cap in caps)
+    names = [v[None, :] for v in (g2m_from, m2m_from, m2g_from, g2m_to, m2m_to)]
+    names, x_grid, place = lax.optimization_barrier((names, x_grid, place))
     hidden = kernel_call(
         functools.partial(embed_hidden, order, embed_id),
         [jax.ShapeDtypeStruct((width, latent), BF16)]
@@ -351,19 +357,18 @@
     rows = hidden[1 + quarters :]
     hidden = [hidden[1]] + [swap(h, other) for h, other in zip(hidden[2:], order[1:])]
 
-    def packs(first_id, sections):
-        shape = jax.ShapeDtypeStruct((3 * latent + BIAS_ROWS, width), BF16)
-        return kernel_call(
-            functools.partial(pack, first_id),
-            [shape] * sections,
-            (place, pair_in, pair_out, hidden_bias),
-            (scalar, hbm, hbm, vmem),
-            scratch=(
-                pltpu.VMEM((sections, BIAS_ROWS, width), BF16),
-                pltpu.SemaphoreType.DMA((sections * (2 + latent // width),)),
-            ),
-            vmem=GRANT,
-        )
+    sections = embed_id
+    piece = (3 * latent + BIAS_ROWS, width)
+    packed, *crossing = kernel_call(
+        pack,
+        [jax.ShapeDtypeStruct((sections, *piece), BF16)]
+        + [jax.ShapeDtypeStruct(piece, BF16)] * (sections // 2),
+        (place, pair_in, pair_out, hidden_bias),
+        (scalar, hbm, vmem, vmem),
+        scratch=(pltpu.SemaphoreType.DMA((sections + sections // 2,)),),
+        vmem=20 << 20,
+    )
+    swapped = swap(packed, bits[1])
 
     if direct:
         tables = [rows[0]] + [shift(row, step) for step, row in enumerate(rows[1:], 1)]
@@ -378,13 +383,6 @@
     columns = [jax.ShapeDtypeStruct((n, 1), jnp.int32) for n in edges + edges[:2]]
     lines = [jax.ShapeDtypeStruct((1, n), jnp.int32) for n in edges[:2]]
     shape = jax.ShapeDtypeStruct((mesh_rows, latent), BF16)
-    names = [v[None, :] for v in (g2m_from, m2m_from, m2g_from, g2m_to, m2m_to)]
-    packed = packs(0, 2)
-    later = packs(2, embed_id - 2)
-    hidden, out_pieces, names, packed, later = lax.optimization_barrier(
-        (hidden, out_pieces, names, packed, later)
-    )
-    packed = packed + later
     routed = kernel_call(
         functools.partial(route, bits, direct, bands, caps, (grid_rows, mesh_rows, mesh_rows), edges),
         [*columns, *lines, shape],
@@ -400,35 +398,30 @@
         (vmem,) * (2 * quarters + 2),
     )
 
-    def group(section_id, after, table):
-        first, second = packed[section_id : section_id + 2]
+    def cross(group_id, after):
+        first = crossing[group_id]
         if after is not None:
             first, _ = lax.optimization_barrier((first, after))
-        across = swap(first, bits[0])
-        across, _ = lax.optimization_barrier((across, table[1]))
-        over = lax.ppermute(across, "parts", [(0, 1), (1, 0)])
-        found = [((0, 0), first), ((1, 0), second), ((0, 1), across), ((1, 1), over)]
-        for i, bit in enumerate(bits[1:]):
-            other = [((kind, slot + (2 << i)), piece) for (kind, slot), piece in found]
-            for place_of, piece in other:
-                piece, _ = lax.optimization_barrier((piece, table[bands - 1 if direct else 1]))
-                found.append((place_of, swap(piece, bit)))
-        return found
-
-    def run(section_id, table, after, ids, own_latent, column, extra, last=False):
+        return swap(first, bits[0])
+
+    def share(first, after):
+        if after is not None:
+            first, _ = lax.optimization_barrier((first, after))
+        second = lax.ppermute(first, "parts", [(0, 1), (1, 0)])
+        return [first, second, swap(first, bits[1]), swap(second, bits[1])]
+
+    def run(section_id, table, across, ids, own_latent, column, extra, last=False):
         rows = sum(part.shape[0] for part in table)
         edges = ids.shape[0]
-        weights = group(section_id, after, table)
-        places = [p for p, _ in weights]
-        weights = [piece for _, piece in weights]
         square = jax.ShapeDtypeStruct((latent, latent), BF16)
         columns = () if last else (column,)
         staged = kernel_call(
-            functools.partial(stage, places, last),
+            functools.partial(stage, section_id // 2, last),
             [square] * 4
             + [jax.ShapeDtypeStruct((n, latent), F32) for n in (edges, own_latent.shape[0])],
-            (place, *weights, own_latent, *columns),
-            (scalar,) + (vmem,) * (len(weights) + 1 + len(columns)),
+            (place, packed, swapped, *across, own_latent, *columns),
+            (scalar, hbm, hbm) + (vmem,) * (5 + len(columns)),
+            scratch=[pltpu.VMEM((2, *piece), BF16)] * 2 + [pltpu.SemaphoreType.DMA((2,))],
             flops=4 * edges * latent * latent,
             vmem=20 << 20,
         )
@@ -447,13 +440,17 @@
     def held(table):
         return table[2 * bands - 1] if direct else table[-1]
 
+    across = share(cross(0, None), None)
     table = everyone(grid)
-    mesh = run(0, table, None, ids_g, mesh, col_g, row_g)
+    later = cross(1, grid)
+    mesh = run(0, table, across, ids_g, mesh, col_g, row_g)
     for layer_id in range(LAYERS):
-        after = held(table)
+        across = share(later, held(table))
         table = everyone(mesh)
-        mesh = run(2 + 2 * layer_id, table, after, ids_m, mesh, col_m, row_m)
-    return run(2 * LAYERS + 2, everyone(mesh), held(table), ids_d, grid, None, head.T, True).T
+        later = cross(2 + layer_id, mesh)
+        mesh = run(2 + 2 * layer_id, table, across, ids_m, mesh, col_m, row_m)
+    across = share(later, held(table))
+    return run(2 * LAYERS + 2, everyone(mesh), across, ids_d, grid, None, head.T, True).T
 
 
 def solution(mesh):

time: 184 us -> 191 us (1.038)
  local copies, waits for them, and re-layouts: 2.12 us -> 9.35 us
  starting transfers between devices: 59.3 us -> 64 us
  waiting for transfers between devices: 91.1 us -> 88.5 us
  Pallas kernels: 29.9 us -> 27.6 us
    ppermute x15, waiting for transfers between devices: 41.4 us -> 34.6 us  [shift(): lax.ppermute(value, 'band', [(b, (b + step) % bands) for b in range(bands)])]
    unnamed x50 -> x42, local copies, waits for them, and re-layouts: 2.12 us -> 8.64 us
    ppermute x15, starting transfers between devices: 18.7 us -> 24.9 us  [shift(): lax.ppermute(value, 'band', [(b, (b + step) % bands) for b in range(bands)])]
    ppermute x4, waiting for transfers between devices: 0.01 us -> 3.85 us  [share(): second = lax.ppermute(first, 'parts', [(0, 1), (1, 0)])]
    ppermute x74 -> x67, starting transfers between devices: 36.4 us -> 33.9 us  [swap(): return lax.ppermute(value, 'feat', [(f, f ^ bit) for f in range(quarters)])]
    pallas_call x13 -> x12, Pallas kernels: 29.9 us -> 27.6 us  [kernel_call(): pl.pallas_call(body, out_shape=out_shape, in_specs=[pl.BlockSpec(memory_s...]
    ppermute x74 -> x67, waiting for transfers between devices: 49.7 us -> 50.1 us  [swap(): return lax.ppermute(value, 'feat', [(f, f ^ bit) for f in range(quarters)])]
  transfers between devices with their start and end apart: 93 -> 86, of which waited for: 36 -> 31; matrix products, arithmetic and copies ran while one was open for 0% -> 0% of each run, Pallas kernels for 13% -> 12%
where the time goes in v8:
time: 191 us; the launch traced here: 190 us
  waiting for transfers between devices  88.5 us (46%)
  starting transfers between devices  64 us (34%)
  Pallas kernels  27.6 us (14%)
  local copies, waits for them, and re-layouts  9.35 us (5%)
    ppermute x67, waiting for transfers between devices, swap(): return lax.ppermute(value, 'feat', [(f, f ^ bit) for f in range(quarters)])  50.1 us
    ppermute x15, waiting for transfers between devices, shift(): lax.ppermute(value, 'band', [(b, (b + step) % bands) for b in range(bands)])  34.6 us
    ppermute x67, starting transfers between devices, swap(): return lax.ppermute(value, 'feat', [(f, f ^ bit) for f in range(quarters)])  33.9 us
    pallas_call x12, Pallas kernels, kernel_call(): pl.pallas_call(body, out_shape=out_shape, in_specs=[pl.BlockSpec(memory_s...  27.6 us
    ppermute x15, starting transfers between devices, shift(): lax.ppermute(value, 'band', [(b, (b + step) % bands) for b in range(bands)])  24.9 us
    unnamed x42, local copies, waits for them, and re-layouts  8.64 us
    ppermute x4, starting transfers between devices, share(): second = lax.ppermute(first, 'parts', [(0, 1), (1, 0)])  5.23 us
    ppermute x4, waiting for transfers between devices, share(): second = lax.ppermute(first, 'parts', [(0, 1), (1, 0)])  3.85 us
  transfers between devices with their start and end apart: 86, of which 31 were waited for; matrix products, arithmetic and copies ran while one was open for 0% of the time, Pallas kernels for 12%

profile of v8, /device:TPU:0, one launch (start us, length us, event | category | flops | bytes accessed | tf_op | source)
XLA Modules:
  0.0 189.9 jit_solution(12925513276532555428)
XLA Ops:
  7.5 2.9 %shard_map.172 = (bf16[128,512]{1,0:T(8,128)(2,1)}, bf16[128,128]{1,0:T(8,128)(2,1)}, bf16[128,128]{1,0:T(8,128)(2,1)}, bf16[128,128]{1,0:T(8,128)(2,1)}, bf16[1...) custom-call(s32[3]{0:T(128)} %copy-done.8, ...), custom_call_target="tpu_custom_call" | custom-call | bytes 4194304 | tf_op jit(solution)/shard_map/pallas_call | solution.py:37
  13.3 4.3 %collective-permute-done.3.refs_5_ = bf16[128,512]{1,0:T(8,128)(2,1)S(1)} collective-permute-done((bf16[128,512]{1,0:T(8,128)(2,1)}, bf16[128,512]{1,0:T(8,128)(2,1)S(1)}, u32[]{:S(2)}, u32[]{:S(2)}) %collective-permute-start.3) | collective-permute-done | bytes 131104 | tf_op jit(solution)/shard_map/ppermute | solution.py:315
  19.5 7.1 %collective-permute-done.refs_1_ = bf16[128,128]{1,0:T(8,128)(2,1)S(1)} collective-permute-done((bf16[128,128]{1,0:T(8,128)(2,1)}, bf16[128,128]{1,0:T(8,128)(2,1)S(1)}, u32[]{:S(2)}, u32[]{:S(2)}) %collective-permute-start) | collective-permute-done | bytes 32800 | tf_op jit(solution)/shard_map/ppermute | solution.py:315
  35.5 2.6 %collective-permute-start.7 = (bf16[128,512]{1,0:T(8,128)(2,1)S(1)}, bf16[128,512]{1,0:T(8,128)(2,1)S(1)}, u32[]{:S(2)}, u32[]{:S(2)}) collective-permute-start(bf16[128,512]{1,0:T(8,128)(2,1)S(1)} %shard_map.173.refs_0_.refs_7_.refs_17_), channel_id=1, source_target_pairs={{0,8},{4,12},{8,0},{12,4},{1,9},{5,13},{9,1},{13,5},{2,10},{6,14},... | collective-permute-start | bytes 393224 | tf_op jit(solution)/shard_map/ppermute | solution.py:318
  38.2 6.2 %collective-permute-done.21.refs_1_ = s32[1,1152]{1,0:T(1,128)S(1)} collective-permute-done((s32[1,1152]{1,0:T(1,128)}, s32[1,1152]{1,0:T(1,128)S(1)}, u32[]{:S(2)}, u32[]{:S(2)}) %collective-permute-start.21) | collective-permute-done | bytes 4640 | tf_op jit(solution)/shard_map/ppermute | solution.py:318
  44.4 3.4 %collective-permute-start.22 = (s32[1,1152]{1,0:T(1,128)}, s32[1,1152]{1,0:T(1,128)S(1)}, u32[]{:S(2)}, u32[]{:S(2)}) collective-permute-start(s32[1,1152]{1,0:T(1,128)} %get-tuple-element.73), channel_id=1, source_target_pairs={{0,8},{4,12},{8,0},{12,4},{1,9},{5,13},{9,1},{13,5},{2,10},{6,14},... | collective-permute-start | bytes 13832 | tf_op jit(solution)/shard_map/ppermute | solution.py:318
  50.0 3.4 %collective-permute-done.23.refs_3_ = s32[1,1152]{1,0:T(1,128)S(1)} collective-permute-done((s32[1,1152]{1,0:T(1,128)}, s32[1,1152]{1,0:T(1,128)S(1)}, u32[]{:S(2)}, u32[]{:S(2)}) %collective-permute-start.23) | collective-permute-done | bytes 4640 | tf_op jit(solution)/shard_map/ppermute | solution.py:318
  59.9 5.9 %collective-permute-done.9.refs_4_ = bf16[128,512]{1,0:T(8,128)(2,1)S(1)} collective-permute-done((bf16[128,512]{1,0:T(8,128)(2,1)S(1)}, bf16[128,512]{1,0:T(8,128)(2,1)S(1)}, u32[]{:S(2)}, u32[]{:S(2)}) %collective-permute-start.9) | collective-permute-done | bytes 131104 | tf_op jit(solution)/shard_map/ppermute | solution.py:315
  67.8 3.5 %collective-permute-done.12.refs_7_ = bf16[128,512]{1,0:T(8,128)(2,1)S(1)} collective-permute-done((bf16[128,512]{1,0:T(8,128)(2,1)S(1)}, bf16[128,512]{1,0:T(8,128)(2,1)S(1)}, u32[]{:S(2)}, u32[]{:S(2)}) %collective-permute-start.12) | collective-permute-done | bytes 131104 | tf_op jit(solution)/shard_map/ppermute | solution.py:315
  80.6 3.8 %collective-permute-done.45.refs_4_ = bf16[1552,128]{1,0:T(8,128)(2,1)S(1)} collective-permute-done((bf16[1552,128]{1,0:T(8,128)(2,1)S(1)}, bf16[1552,128]{1,0:T(8,128)(2,1)S(1)}, u32[]{:S(2)}, u32[]{:S(2)}) %collective-permute-start.45) | collective-permute-done | bytes 397344 | tf_op jit(solution)/shard_map/ppermute | solution.py:410
  102.3 4.2 %collective-permute-done.30.refs_2_ = bf16[128,512]{1,0:T(8,128)(2,1)S(1)} collective-permute-done((bf16[128,512]{1,0:T(8,128)(2,1)S(1)}, bf16[128,512]{1,0:T(8,128)(2,1)S(1)}, u32[]{:S(2)}, u32[]{:S(2)}) %collective-permute-start.30) | collective-permute-done | bytes 131104 | tf_op jit(solution)/shard_map/ppermute | solution.py:318
  109.2 3.8 %collective-permute-done.34.refs_6_ = bf16[128,512]{1,0:T(8,128)(2,1)S(1)} collective-permute-done((bf16[128,512]{1,0:T(8,128)(2,1)S(1)}, bf16[128,512]{1,0:T(8,128)(2,1)S(1)}, u32[]{:S(2)}, u32[]{:S(2)}) %collective-permute-start.34) | collective-permute-done | bytes 131104 | tf_op jit(solution)/shard_map/ppermute | solution.py:315
  116.8 2.8 %shard_map.178 = (bf16[512,512]{1,0:T(8,128)(2,1)S(1)}, bf16[512,512]{1,0:T(8,128)(2,1)S(1)}, bf16[512,512]{1,0:T(8,128)(2,1)S(1)}, bf16[512,512]{1,0:T(8,128)(2...) custom-call(s32[3]{0:T(128)S(1)} %copy-done.10, bf16[8,1552,128]{2,1,0:T(8,128)(2,1)S(1)} %get-tuple-element.82.refs_1_, ...), custom_call_target="tpu_custom_call" | custom-call | flops 536870912 | bytes 4194304 | tf_op jit(solution)/shard_map/pallas_call | solution.py:37
  119.7 2.9 %shard_map.179.refs_7_.refs_0_.refs_17_ = bf16[128,512]{1,0:T(8,128)(2,1)S(1)} custom-call(bf16[128,512]{1,0:T(8,128)(2,1)S(1)} %shard_map.177.refs_7_.refs_0_.refs_17_, bf16[128,512]{1,0:T(8,128)(2,1)S(1)} %collective-permute-done.29.refs_1_, bf16[128,512]{1,0:T(8,128)(2,1)S(1)} %collective-permute-done.30.refs_2_, ...), custom_call_target="tpu_custom_call" | custom-call | flops 1879048192 | bytes 4194304 | tf_op jit(solution)/shard_map/pallas_call | solution.py:37
  129.6 3.8 %collective-permute-done.48.refs_1_ = bf16[128,512]{1,0:T(8,128)(2,1)S(1)} collective-permute-done((bf16[128,512]{1,0:T(8,128)(2,1)S(1)}, bf16[128,512]{1,0:T(8,128)(2,1)S(1)}, u32[]{:S(2)}, u32[]{:S(2)}) %collective-permute-start.48) | collective-permute-done | bytes 131104 | tf_op jit(solution)/shard_map/ppermute | solution.py:318
  135.9 4.7 %collective-permute-done.49.refs_2_ = bf16[128,512]{1,0:T(8,128)(2,1)S(1)} collective-permute-done((bf16[128,512]{1,0:T(8,128)(2,1)S(1)}, bf16[128,512]{1,0:T(8,128)(2,1)S(1)}, u32[]{:S(2)}, u32[]{:S(2)}) %collective-permute-start.49) | collective-permute-done | bytes 131104 | tf_op jit(solution)/shard_map/ppermute | solution.py:318
  143.7 3.7 %collective-permute-done.52.refs_5_ = bf16[128,512]{1,0:T(8,128)(2,1)S(1)} collective-permute-done((bf16[128,512]{1,0:T(8,128)(2,1)S(1)}, bf16[128,512]{1,0:T(8,128)(2,1)S(1)}, u32[]{:S(2)}, u32[]{:S(2)}) %collective-permute-start.52) | collective-permute-done | bytes 131104 | tf_op jit(solution)/shard_map/ppermute | solution.py:315
  152.8 2.7 %shard_map.180 = (bf16[512,512]{1,0:T(8,128)(2,1)S(1)}, bf16[512,512]{1,0:T(8,128)(2,1)S(1)}, bf16[512,512]{1,0:T(8,128)(2,1)S(1)}, bf16[512,512]{1,0:T(8,128)(2...) custom-call(s32[3]{0:T(128)S(1)} %copy-done.10, bf16[8,1552,128]{2,1,0:T(8,128)(2,1)S(1)} %get-tuple-element.82.refs_1_, ...), custom_call_target="tpu_custom_call" | custom-call | flops 536870912 | bytes 4194304 | tf_op jit(solution)/shard_map/pallas_call | solution.py:37
  155.9 2.8 %shard_map.181.refs_0_ = bf16[128,512]{1,0:T(8,128)(2,1)S(1)} custom-call(bf16[128,512]{1,0:T(8,128)(2,1)S(1)} %shard_map.179.refs_7_.refs_0_.refs_17_, bf16[128,512]{1,0:T(8,128)(2,1)S(1)} %collective-permute-done.48.refs_1_, bf16[128,512]{1,0:T(8,128)(2,1)S(1)} %collective-permute-done.49.refs_2_, bf16[128,512]{1,0:T(8,128)(2,1)S(1)} %collective-permute-done.50.refs_3_, ...), custom_call_target="tpu_custom_call" | custom-call | flops 1879048192 | bytes 4194304 | tf_op jit(solution)/shard_map/pallas_call | solution.py:37
  164.3 2.7 %collective-permute-done.67.refs_1_ = bf16[128,512]{1,0:T(8,128)(2,1)S(1)} collective-permute-done((bf16[128,512]{1,0:T(8,128)(2,1)S(1)}, bf16[128,512]{1,0:T(8,128)(2,1)S(1)}, u32[]{:S(2)}, u32[]{:S(2)}) %collective-permute-start.67) | collective-permute-done | bytes 131104 | tf_op jit(solution)/shard_map/ppermute | solution.py:318
  167.1 4.8 %collective-permute-done.68.refs_2_ = bf16[128,512]{1,0:T(8,128)(2,1)S(1)} collective-permute-done((bf16[128,512]{1,0:T(8,128)(2,1)S(1)}, bf16[128,512]{1,0:T(8,128)(2,1)S(1)}, u32[]{:S(2)}, u32[]{:S(2)}) %collective-permute-start.68) | collective-permute-done | bytes 131104 | tf_op jit(solution)/shard_map/ppermute | solution.py:318
  175.5 2.8 %collective-permute-done.71.refs_5_ = bf16[128,512]{1,0:T(8,128)(2,1)S(1)} collective-permute-done((bf16[128,512]{1,0:T(8,128)(2,1)S(1)}, bf16[128,512]{1,0:T(8,128)(2,1)S(1)}, u32[]{:S(2)}, u32[]{:S(2)}) %collective-permute-start.71) | collective-permute-done | bytes 131104 | tf_op jit(solution)/shard_map/ppermute | solution.py:315
  178.2 2.8 %collective-permute-done.72.refs_6_ = bf16[128,512]{1,0:T(8,128)(2,1)S(1)} collective-permute-done((bf16[128,512]{1,0:T(8,128)(2,1)S(1)}, bf16[128,512]{1,0:T(8,128)(2,1)S(1)}, u32[]{:S(2)}, u32[]{:S(2)}) %collective-permute-start.72) | collective-permute-done | bytes 131104 | tf_op jit(solution)/shard_map/ppermute | solution.py:315
  186.5 3.3 %shard_map.183 = f32[227,128]{1,0:T(8,128)} custom-call(bf16[128,512]{1,0:T(8,128)(2,1)S(1)} %shard_map.181.refs_0_, bf16[128,512]{1,0:T(8,128)(2,1)S(1)} %collective-permute-done.67.refs_1_, bf16[128,512]{1,0:T(8,128)(2,1)S(1)} %collective-permute-done.68.refs_2_, bf16[128,512]{1,0:T(8,128)(2,1)S(1)} %collective-permute-done.69.refs_3_, ...), custom_call_target="tpu_custom_call" | custom-call | flops 1409286144 | bytes 4194304 | tf_op jit(solution)/shard_map/pallas_call | solution.py:37
  (204 shorter events, 98.6 us)
Async XLA Ops:
  7.0 78.1 %collective-permute-start.24 = (bf16[8,1552,128]{2,1,0:T(8,128)(2,1)S(1)}, bf16[8,1552,128]{2,1,0:T(8,128)(2,1)}, u32[]{:S(2)}, u32[]{:S(2)}) collective-permute-start(bf16[8,1552,128]{2,1,0:T(8,128)(2,1)S(1)} %get-tuple-element.82.refs_1_), channel_id=1, source_target_pairs={{0,1},{1,0},{2,3},{3,2},{4,5},{5,4},{6,7},{7,6},{8,9},{9,8},{10,11... | collective-permute-start | bytes 9535496 | tf_op jit(solution)/shard_map/ppermute | solution.py:315
  12.9 44.8 %collective-permute-start.25 = (bf16[1552,128]{1,0:T(8,128)(2,1)}, bf16[1552,128]{1,0:T(8,128)(2,1)S(1)}, u32[]{:S(2)}, u32[]{:S(2)}) collective-permute-start(bf16[1552,128]{1,0:T(8,128)(2,1)} %copy-done.20), channel_id=1, source_target_pairs={{0,2},{1,3},{2,0},{3,1},{4,6},{5,7},{6,4},{7,5},{8,10},{9,11},{10,... | collective-permute-start | bytes 1191944 | tf_op jit(solution)/shard_map/ppermute | solution.py:315
  13.0 18.5 %collective-permute-start.4 = (bf16[128,512]{1,0:T(8,128)(2,1)}, bf16[128,512]{1,0:T(8,128)(2,1)S(1)}, u32[]{:S(2)}, u32[]{:S(2)}) collective-permute-start(bf16[128,512]{1,0:T(8,128)(2,1)} %get-tuple-element.70.refs_4_), channel_id=1, source_target_pairs={{0,1},{1,0},{2,3},{3,2},{4,5},{5,4},{6,7},{7,6},{8,9},{9,8},{10,11... | collective-permute-start | bytes 393224 | tf_op jit(solution)/shard_map/ppermute | solution.py:315
  17.5 14.0 %collective-permute-start.5 = (bf16[128,512]{1,0:T(8,128)(2,1)S(1)}, bf16[128,512]{1,0:T(8,128)(2,1)S(1)}, u32[]{:S(2)}, u32[]{:S(2)}) collective-permute-start(bf16[128,512]{1,0:T(8,128)(2,1)S(1)} %collective-permute-done.3.refs_5_), channel_id=1, source_target_pairs={{0,1},{1,0},{2,3},{3,2},{4,5},{5,4},{6,7},{7,6},{8,9},{9,8},{10,11... | collective-permute-start | bytes 393224 | tf_op jit(solution)/shard_map/ppermute | solution.py:315
  33.6 21.3 %collective-permute-start.6 = (bf16[128,512]{1,0:T(8,128)(2,1)S(1)}, bf16[128,512]{1,0:T(8,128)(2,1)S(1)}, u32[]{:S(2)}, u32[]{:S(2)}) collective-permute-start(bf16[128,512]{1,0:T(8,128)(2,1)S(1)} %shard_map.173.refs_0_.refs_7_.refs_17_), channel_id=1, source_target_pairs={{0,4},{4,8},{8,12},{12,0},{1,5},{5,9},{9,13},{13,1},{2,6},{6,10},{... | collective-permute-start | bytes 393224 | tf_op jit(solution)/shard_map/ppermute | solution.py:318
  35.5 21.7 %collective-permute-start.7 = (bf16[128,512]{1,0:T(8,128)(2,1)S(1)}, bf16[128,512]{1,0:T(8,128)(2,1)S(1)}, u32[]{:S(2)}, u32[]{:S(2)}) collective-permute-start(bf16[128,512]{1,0:T(8,128)(2,1)S(1)} %shard_map.173.refs_0_.refs_7_.refs_17_), channel_id=1, source_target_pairs={{0,8},{4,12},{8,0},{12,4},{1,9},{5,13},{9,1},{13,5},{2,10},{6,14},... | collective-permute-start | bytes 393224 | tf_op jit(solution)/shard_map/ppermute | solution.py:318
  53.4 19.4 %collective-permute-start.44 = (bf16[1552,128]{1,0:T(8,128)(2,1)}, bf16[1552,128]{1,0:T(8,128)(2,1)S(1)}, u32[]{:S(2)}, u32[]{:S(2)}) collective-permute-start(bf16[1552,128]{1,0:T(8,128)(2,1)} %copy-done.19), channel_id=1, source_target_pairs={{0,2},{1,3},{2,0},{3,1},{4,6},{5,7},{6,4},{7,5},{8,10},{9,11},{10,... | collective-permute-start | bytes 1191944 | tf_op jit(solution)/shard_map/ppermute | solution.py:315
  57.7 19.1 %collective-permute-start.26 = (bf16[1552,128]{1,0:T(8,128)(2,1)S(1)}, bf16[1552,128]{1,0:T(8,128)(2,1)S(1)}, u32[]{:S(2)}, u32[]{:S(2)}) collective-permute-start(bf16[1552,128]{1,0:T(8,128)(2,1)S(1)} %collective-permute-done.25.refs_3_), channel_id=1, source_target_pairs={{0,16},{16,0},{1,17},{17,1},{2,18},{18,2},{3,19},{19,3},{4,20},{20... | collective-permute-start | bytes 1191944 | tf_op jit(solution)/shard_map/ppermute | solution.py:410
  72.9 11.6 %collective-permute-start.45 = (bf16[1552,128]{1,0:T(8,128)(2,1)S(1)}, bf16[1552,128]{1,0:T(8,128)(2,1)S(1)}, u32[]{:S(2)}, u32[]{:S(2)}) collective-permute-start(bf16[1552,128]{1,0:T(8,128)(2,1)S(1)} %collective-permute-done.44.refs_3_), channel_id=1, source_target_pairs={{0,16},{16,0},{1,17},{17,1},{2,18},{18,2},{3,19},{19,3},{4,20},{20... | collective-permute-start | bytes 1191944 | tf_op jit(solution)/shard_map/ppermute | solution.py:410
  80.3 18.8 %collective-permute-start.46 = (bf16[1552,128]{1,0:T(8,128)(2,1)S(1)}, bf16[1552,128]{1,0:T(8,128)(2,1)S(1)}, u32[]{:S(2)}, u32[]{:S(2)}) collective-permute-start(bf16[1552,128]{1,0:T(8,128)(2,1)S(1)} %collective-permute-done.44.refs_3_), channel_id=1, source_target_pairs={{0,1},{1,0},{2,3},{3,2},{4,5},{5,4},{6,7},{7,6},{8,9},{9,8},{10,11... | collective-permute-start | bytes 1191944 | tf_op jit(solution)/shard_map/ppermute | solution.py:315
  84.5 15.1 %collective-permute-start.47 = (bf16[1552,128]{1,0:T(8,128)(2,1)S(1)}, bf16[1552,128]{1,0:T(8,128)(2,1)S(1)}, u32[]{:S(2)}, u32[]{:S(2)}) collective-permute-start(bf16[1552,128]{1,0:T(8,128)(2,1)S(1)} %collective-permute-done.45.refs_4_), channel_id=1, source_target_pairs={{0,1},{1,0},{2,3},{3,2},{4,5},{5,4},{6,7},{7,6},{8,9},{9,8},{10,11... | collective-permute-start | bytes 1191944 | tf_op jit(solution)/shard_map/ppermute | solution.py:315
  95.1 11.5 %collective-permute-start.30 = (bf16[128,512]{1,0:T(8,128)(2,1)S(1)}, bf16[128,512]{1,0:T(8,128)(2,1)S(1)}, u32[]{:S(2)}, u32[]{:S(2)}) collective-permute-start(bf16[128,512]{1,0:T(8,128)(2,1)S(1)} %shard_map.177.refs_7_.refs_0_.refs_17_), channel_id=1, source_target_pairs={{0,8},{4,12},{8,0},{12,4},{1,9},{5,13},{9,1},{13,5},{2,10},{6,14},... | collective-permute-start | bytes 393224 | tf_op jit(solution)/shard_map/ppermute | solution.py:318
  96.8 10.3 %collective-permute-start.31 = (bf16[128,512]{1,0:T(8,128)(2,1)S(1)}, bf16[128,512]{1,0:T(8,128)(2,1)S(1)}, u32[]{:S(2)}, u32[]{:S(2)}) collective-permute-start(bf16[128,512]{1,0:T(8,128)(2,1)S(1)} %shard_map.177.refs_7_.refs_0_.refs_17_), channel_id=1, source_target_pairs={{0,12},{4,0},{8,4},{12,8},{1,13},{5,1},{9,5},{13,9},{2,14},{6,2},{... | collective-permute-start | bytes 393224 | tf_op jit(solution)/shard_map/ppermute | solution.py:318
  113.0 10.3 %collective-permute-start.63 = (bf16[1552,128]{1,0:T(8,128)(2,1)S(1)}, bf16[1552,128]{1,0:T(8,128)(2,1)S(1)}, u32[]{:S(2)}, u32[]{:S(2)}) collective-permute-start(bf16[1552,128]{1,0:T(8,128)(2,1)S(1)} %get-tuple-element.105), channel_id=1, source_target_pairs={{0,2},{1,3},{2,0},{3,1},{4,6},{5,7},{6,4},{7,5},{8,10},{9,11},{10,... | collective-permute-start | bytes 1191944 | tf_op jit(solution)/shard_map/ppermute | solution.py:315
  122.6 20.1 %collective-permute-start.82 = (bf16[1552,128]{1,0:T(8,128)(2,1)S(1)}, bf16[1552,128]{1,0:T(8,128)(2,1)S(1)}, u32[]{:S(2)}, u32[]{:S(2)}) collective-permute-start(bf16[1552,128]{1,0:T(8,128)(2,1)S(1)} %get-tuple-element.115), channel_id=1, source_target_pairs={{0,2},{1,3},{2,0},{3,1},{4,6},{5,7},{6,4},{7,5},{8,10},{9,11},{10,... | collective-permute-start | bytes 1191944 | tf_op jit(solution)/shard_map/ppermute | solution.py:315
  123.2 19.9 %collective-permute-start.64 = (bf16[1552,128]{1,0:T(8,128)(2,1)S(1)}, bf16[1552,128]{1,0:T(8,128)(2,1)S(1)}, u32[]{:S(2)}, u32[]{:S(2)}) collective-permute-start(bf16[1552,128]{1,0:T(8,128)(2,1)S(1)} %collective-permute-done.63.refs_3_), channel_id=1, source_target_pairs={{0,16},{16,0},{1,17},{17,1},{2,18},{18,2},{3,19},{19,3},{4,20},{20... | collective-permute-start | bytes 1191944 | tf_op jit(solution)/shard_map/ppermute | solution.py:410
  129.0 11.6 %collective-permute-start.49 = (bf16[128,512]{1,0:T(8,128)(2,1)S(1)}, bf16[128,512]{1,0:T(8,128)(2,1)S(1)}, u32[]{:S(2)}, u32[]{:S(2)}) collective-permute-start(bf16[128,512]{1,0:T(8,128)(2,1)S(1)} %shard_map.179.refs_7_.refs_0_.refs_17_), channel_id=1, source_target_pairs={{0,8},{4,12},{8,0},{12,4},{1,9},{5,13},{9,1},{13,5},{2,10},{6,14},... | collective-permute-start | bytes 393224 | tf_op jit(solution)/shard_map/ppermute | solution.py:318
  140.6 11.6 %collective-permute-start.65 = (bf16[1552,128]{1,0:T(8,128)(2,1)S(1)}, bf16[1552,128]{1,0:T(8,128)(2,1)S(1)}, u32[]{:S(2)}, u32[]{:S(2)}) collective-permute-start(bf16[1552,128]{1,0:T(8,128)(2,1)S(1)} %collective-permute-done.63.refs_3_), channel_id=1, source_target_pairs={{0,1},{1,0},{2,3},{3,2},{4,5},{5,4},{6,7},{7,6},{8,9},{9,8},{10,11... | collective-permute-start | bytes 1191944 | tf_op jit(solution)/shard_map/ppermute | solution.py:315
  143.1 12.3 %collective-permute-start.83 = (bf16[1552,128]{1,0:T(8,128)(2,1)S(1)}, bf16[1552,128]{1,0:T(8,128)(2,1)S(1)}, u32[]{:S(2)}, u32[]{:S(2)}) collective-permute-start(bf16[1552,128]{1,0:T(8,128)(2,1)S(1)} %collective-permute-done.82.refs_3_), channel_id=1, source_target_pairs={{0,16},{16,0},{1,17},{17,1},{2,18},{18,2},{3,19},{19,3},{4,20},{20... | collective-permute-start | bytes 1191944 | tf_op jit(solution)/shard_map/ppermute | solution.py:410
  152.6 10.1 %collective-permute-start.84 = (bf16[1552,128]{1,0:T(8,128)(2,1)S(1)}, bf16[1552,128]{1,0:T(8,128)(2,1)S(1)}, u32[]{:S(2)}, u32[]{:S(2)}) collective-permute-start(bf16[1552,128]{1,0:T(8,128)(2,1)S(1)} %collective-permute-done.82.refs_3_), channel_id=1, source_target_pairs={{0,1},{1,0},{2,3},{3,2},{4,5},{5,4},{6,7},{7,6},{8,9},{9,8},{10,11... | collective-permute-start | bytes 1191944 | tf_op jit(solution)/shard_map/ppermute | solution.py:315
  155.4 28.0 %collective-permute-start.85 = (bf16[1552,128]{1,0:T(8,128)(2,1)S(1)}, bf16[1552,128]{1,0:T(8,128)(2,1)S(1)}, u32[]{:S(2)}, u32[]{:S(2)}) collective-permute-start(bf16[1552,128]{1,0:T(8,128)(2,1)S(1)} %collective-permute-done.83.refs_4_), channel_id=1, source_target_pairs={{0,1},{1,0},{2,3},{3,2},{4,5},{5,4},{6,7},{7,6},{8,9},{9,8},{10,11... | collective-permute-start | bytes 1191944 | tf_op jit(solution)/shard_map/ppermute | solution.py:315
  160.2 11.6 %collective-permute-start.68 = (bf16[128,512]{1,0:T(8,128)(2,1)S(1)}, bf16[128,512]{1,0:T(8,128)(2,1)S(1)}, u32[]{:S(2)}, u32[]{:S(2)}) collective-permute-start(bf16[128,512]{1,0:T(8,128)(2,1)S(1)} %shard_map.181.refs_0_), channel_id=1, source_target_pairs={{0,8},{4,12},{8,0},{12,4},{1,9},{5,13},{9,1},{13,5},{2,10},{6,14},... | collective-permute-start | bytes 393224 | tf_op jit(solution)/shard_map/ppermute | solution.py:318
  161.1 12.3 %collective-permute-start.69 = (bf16[128,512]{1,0:T(8,128)(2,1)S(1)}, bf16[128,512]{1,0:T(8,128)(2,1)S(1)}, u32[]{:S(2)}, u32[]{:S(2)}) collective-permute-start(bf16[128,512]{1,0:T(8,128)(2,1)S(1)} %shard_map.181.refs_0_), channel_id=1, source_target_pairs={{0,12},{4,0},{8,4},{12,8},{1,13},{5,1},{9,5},{13,9},{2,14},{6,2},{... | collective-permute-start | bytes 393224 | tf_op jit(solution)/shard_map/ppermute | solution.py:318
  162.7 11.2 %collective-permute-start.70 = (bf16[128,512]{1,0:T(8,128)(2,1)S(1)}, bf16[128,512]{1,0:T(8,128)(2,1)S(1)}, u32[]{:S(2)}, u32[]{:S(2)}) collective-permute-start(bf16[128,512]{1,0:T(8,128)(2,1)S(1)} %shard_map.181.refs_0_), channel_id=1, source_target_pairs={{0,2},{1,3},{2,0},{3,1},{4,6},{5,7},{6,4},{7,5},{8,10},{9,11},{10,... | collective-permute-start | bytes 393224 | tf_op jit(solution)/shard_map/ppermute | solution.py:315
  (83 other events, 973.1 us)

commit v9 on v8

--- a/solution.py
+++ b/solution.py
@@ -57,37 +57,48 @@
         copy.wait()
 
 
-def embed_hidden(order, section_id, place_ref, x_hbm, w_hbm, out_hbm, bias_ref, take_g, take_m, take_d, *refs):
-    out_w = refs[0]
-    outs = refs[1 : 1 + len(order)]
+def embed_hidden(order, section_id, place_ref, x_hbm, w_hbm, out_hbm, bias_ref, own_out, *refs):
+    sends = refs[:-3]
     x_ref, w_ref, sem = refs[-3:]
-    bands = take_g.shape[1]
-    for step, out in enumerate(refs[1 + len(order) : -3]):
-        target = place_ref[1] + step
-        target = jnp.where(target >= bands, target - bands, target)
-        begin = 0
-        for take in (take_g, take_m, take_d):
-            out[:, begin : begin + take.shape[2]] = take[0, pl.ds(target, 1), :]
-            begin += take.shape[2]
-    copies = started([(x_hbm, x_ref), (w_hbm, w_ref), (out_hbm.at[section_id], out_w)], sem)
-    wait_all(copies)
+    latent = out_hbm.shape[2]
+    width = w_ref.shape[1]
+    rows = own_out.shape[0]
+    pairs = [(x_hbm, x_ref), (w_hbm, w_ref)]
+    for out in sends:
+        for b in range(0, latent, width):
+            pairs.append((out_hbm.at[section_id, :, pl.ds(b, width)], out.at[pl.ds(b, width)]))
+    copies = started(pairs, sem)
+    wait_all(copies[:2])
     me = place_ref[0]
     bias = bias_ref[section_id : section_id + 1, :]
-    rows = outs[0].shape[0]
-    for other, out in zip(order, outs):
-        begin = pl.multiple_of((me ^ other) * rows, rows)
+    first, second = sends
+    _, across, core, diagonal = order
+    for other, out, begin in (
+        (across, first, latent + rows),
+        (diagonal, first, latent),
+        (core, second, latent),
+        (0, own_out, 0),
+    ):
+        source = pl.multiple_of((me ^ other) * rows, rows)
         product = lax.dot_general(
-            x_ref[:, pl.ds(begin, rows)], w_ref[...], (((0,), (0,)), ((), ())), preferred_element_type=F32
+            x_ref[:, pl.ds(source, rows)], w_ref[...], (((0,), (0,)), ((), ())), preferred_element_type=F32
         )
-        out[...] = silu(product + bias).astype(BF16)
-
-
-def embed_finish(section_id, count, *refs):
-    hidden = jnp.concatenate([r[...] for r in refs[:count]], axis=1)
-    weights = jnp.concatenate([r[...] for r in refs[count : 2 * count]], axis=0)
-    gain, shift, out = refs[2 * count :]
+        out[pl.ds(begin, rows), :] = silu(product + bias).astype(BF16)
+    wait_all(copies[2:])
+
+
+def embed_finish(section_id, own_ref, out_ref, across, core, diagonal, gain, shift, out):
+    rows, latent = out.shape
+    width = own_ref.shape[1]
+    hidden = [own_ref[...], across[pl.ds(latent + rows, rows), :]]
+    hidden += [ref[pl.ds(latent, rows), :] for ref in (core, diagonal)]
+    weights = [
+        jnp.concatenate([ref[pl.ds(b, width), :] for b in range(0, latent, width)], axis=1)
+        for ref in (out_ref, across, core, diagonal)
+    ]
+    product = dot(jnp.concatenate(hidden, axis=1), jnp.concatenate(weights, axis=0))
     row = slice(section_id, section_id + 1)
-    out[...] = layer_norm(dot(hidden, weights), gain[row, :], shift[row, :]).astype(BF16)
+    out[...] = layer_norm(product, gain[row, :], shift[row, :]).astype(BF16)
 
 
 def pack(place_ref, in_hbm, out_ref, bias_ref, packed, *refs):
@@ -134,7 +145,7 @@
         total = jnp.zeros((16, size), F32)
         for s in range(bands):
             if direct:
-                value = tables[s][:, begin : begin + padded]
+                value = tables[s][pl.ds(band, 1), begin : begin + padded]
                 source = jnp.where(band >= s, band - s, band - s + bands)
             else:
                 value = tables[0][s : s + 1, begin : begin + padded]
@@ -323,55 +334,22 @@
             parts = parts + [swap(part, bit) for part in parts]
         return parts
 
-    def everyone(rows):
+    def spread(rows):
         if direct:
             parts = [rows] + [shift(rows, step) for step in range(1, bands)]
-            for bit in bits:
-                parts = parts + [swap(part, bit) for part in parts]
-            return parts
-        parts = [rows]
-        for bit in bits[:-1]:
-            parts = parts + [swap(part, bit) for part in parts]
-        parts = [lax.all_gather(part, "band", axis=0, tiled=True) for part in parts]
-        return parts + [swap(part, bits[-1]) for part in parts]
+            return parts + [swap(part, bits[0]) for part in parts]
+        parts = [rows, swap(rows, bits[0])]
+        return [lax.all_gather(part, "band", axis=0, tiled=True) for part in parts]
+
+    def complete(parts, staged):
+        last, _ = lax.optimization_barrier((parts[-1], staged))
+        return parts + [swap(part, bits[1]) for part in parts[:-1] + [last]]
 
     caps = [take.shape[2] for take in (g2m_take, m2m_take, m2g_take)]
     direct = direct and all(cap % 128 == 0 for cap in caps)
-    names = [v[None, :] for v in (g2m_from, m2m_from, m2g_from, g2m_to, m2m_to)]
-    names, x_grid, place = lax.optimization_barrier((names, x_grid, place))
-    hidden = kernel_call(
-        functools.partial(embed_hidden, order, embed_id),
-        [jax.ShapeDtypeStruct((width, latent), BF16)]
-        + [jax.ShapeDtypeStruct((grid_rows, width), BF16)] * quarters
-        + [jax.ShapeDtypeStruct((1, sum(caps)), jnp.int32)] * (bands if direct else 0),
-        (place, x_grid.T, embed_in, pair_out, hidden_bias, g2m_take, m2m_take, m2g_take),
-        (scalar, hbm, hbm, hbm, vmem, vmem, vmem, vmem),
-        scratch=(
-            pltpu.VMEM(x_grid.shape[::-1], BF16),
-            pltpu.VMEM(embed_in.shape, BF16),
-            pltpu.SemaphoreType.DMA((3,)),
-        ),
-        vmem=GRANT,
-    )
-    out_pieces = pieces(hidden[0])
-    rows = hidden[1 + quarters :]
-    hidden = [hidden[1]] + [swap(h, other) for h, other in zip(hidden[2:], order[1:])]
-
-    sections = embed_id
-    piece = (3 * latent + BIAS_ROWS, width)
-    packed, *crossing = kernel_call(
-        pack,
-        [jax.ShapeDtypeStruct((sections, *piece), BF16)]
-        + [jax.ShapeDtypeStruct(piece, BF16)] * (sections // 2),
-        (place, pair_in, pair_out, hidden_bias),
-        (scalar, hbm, vmem, vmem),
-        scratch=(pltpu.SemaphoreType.DMA((sections + sections // 2,)),),
-        vmem=20 << 20,
-    )
-    swapped = swap(packed, bits[1])
-
     if direct:
-        tables = [rows[0]] + [shift(row, step) for step, row in enumerate(rows[1:], 1)]
+        whole = jnp.concatenate([g2m_take[0], m2m_take[0], m2g_take[0]], axis=1)
+        tables = [whole] + [shift(whole, step) for step in range(1, bands)]
     else:
         takes = [jnp.pad(t[0], ((0, 0), (0, -t.shape[2] % 128))) for t in (g2m_take, m2m_take, m2g_take)]
         tables = [
@@ -379,10 +357,46 @@
                 jnp.concatenate(takes, axis=1), "band", split_axis=0, concat_axis=0, tiled=True
             )
         ]
-    edges = [names.shape[0] // quarters for names in (g2m_from, m2m_from, m2g_from)]
+    names = [v[None, :] for v in (g2m_from, m2m_from, m2g_from, g2m_to, m2m_to)]
+    names, place = lax.optimization_barrier((names, place))
+    hidden, *sends = kernel_call(
+        functools.partial(embed_hidden, order, embed_id),
+        [jax.ShapeDtypeStruct((n, width), BF16) for n in (grid_rows, latent + 2 * grid_rows, latent + grid_rows)],
+        (place, x_grid.T, embed_in, pair_out, hidden_bias),
+        (scalar, hbm, hbm, hbm, vmem),
+        scratch=(
+            pltpu.VMEM(x_grid.shape[::-1], BF16),
+            pltpu.VMEM(embed_in.shape, BF16),
+            pltpu.SemaphoreType.DMA((2 + 2 * latent // width,)),
+        ),
+        vmem=GRANT,
+    )
+    met = swap(sends[0], bits[0])
+    received = [met, swap(sends[1], bits[1]), swap(met, bits[1])]
+    place_after, _ = lax.optimization_barrier((place, hidden))
+
+    sections = embed_id
+    piece = (3 * latent + BIAS_ROWS, width)
+    packed, *crossing = kernel_call(
+        pack,
+        [jax.ShapeDtypeStruct((sections, *piece), BF16)]
+        + [jax.ShapeDtypeStruct(piece, BF16)] * (sections // 2),
+        (place_after, pair_in, pair_out, hidden_bias),
+        (scalar, hbm, vmem, vmem),
+        scratch=(pltpu.SemaphoreType.DMA((sections + sections // 2,)),),
+        vmem=20 << 20,
+    )
+    edges = [v.shape[0] // quarters for v in (g2m_from, m2m_from, m2g_from)]
     columns = [jax.ShapeDtypeStruct((n, 1), jnp.int32) for n in edges + edges[:2]]
     lines = [jax.ShapeDtypeStruct((1, n), jnp.int32) for n in edges[:2]]
     shape = jax.ShapeDtypeStruct((mesh_rows, latent), BF16)
+    received, tables = lax.optimization_barrier((received, tables))
+    grid = kernel_call(
+        functools.partial(embed_finish, embed_id),
+        jax.ShapeDtypeStruct((grid_rows, latent), BF16),
+        (hidden, sends[0], *received, norm_gain, norm_shift),
+        (vmem,) * 7,
+    )
     routed = kernel_call(
         functools.partial(route, bits, direct, bands, caps, (grid_rows, mesh_rows, mesh_rows), edges),
         [*columns, *lines, shape],
@@ -391,12 +405,7 @@
         vmem=24 << 20,
     )
     ids_g, ids_m, ids_d, col_g, col_m, row_g, row_m, mesh = routed
-    grid = kernel_call(
-        functools.partial(embed_finish, embed_id, quarters),
-        jax.ShapeDtypeStruct((grid_rows, latent), BF16),
-        (*hidden, *out_pieces, norm_gain, norm_shift),
-        (vmem,) * (2 * quarters + 2),
-    )
+    swapped = swap(lax.optimization_barrier((packed, grid))[0], bits[1])
 
     def cross(group_id, after):
         first = crossing[group_id]
@@ -410,8 +419,7 @@
         second = lax.ppermute(first, "parts", [(0, 1), (1, 0)])
         return [first, second, swap(first, bits[1]), swap(second, bits[1])]
 
-    def run(section_id, table, across, ids, own_latent, column, extra, last=False):
-        rows = sum(part.shape[0] for part in table)
+    def run(section_id, parts, across, ids, own_latent, column, extra, last=False):
         edges = ids.shape[0]
         square = jax.ShapeDtypeStruct((latent, latent), BF16)
         columns = () if last else (column,)
@@ -425,6 +433,8 @@
             flops=4 * edges * latent * latent,
             vmem=20 << 20,
         )
+        table = complete(parts, staged)
+        rows = sum(part.shape[0] for part in table)
         out_shape = jax.ShapeDtypeStruct(own_latent.shape, BF16)
         if last:
             out_shape = jax.ShapeDtypeStruct((head.shape[1], own_latent.shape[0]), F32)
@@ -437,20 +447,17 @@
             vmem=(20 << 20) + rows * latent * 2,
         )
 
-    def held(table):
-        return table[2 * bands - 1] if direct else table[-1]
-
-    across = share(cross(0, None), None)
-    table = everyone(grid)
-    later = cross(1, grid)
-    mesh = run(0, table, across, ids_g, mesh, col_g, row_g)
+    across = share(cross(0, met), None)
+    parts = spread(grid)
+    later = cross(1, parts[bands + 1] if direct else grid)
+    mesh = run(0, parts, across, ids_g, mesh, col_g, row_g)
     for layer_id in range(LAYERS):
-        across = share(later, held(table))
-        table = everyone(mesh)
+        across = share(later, parts[-1])
+        parts = spread(mesh)
         later = cross(2 + layer_id, mesh)
-        mesh = run(2 + 2 * layer_id, table, across, ids_m, mesh, col_m, row_m)
-    across = share(later, held(table))
-    return run(2 * LAYERS + 2, everyone(mesh), across, ids_d, grid, None, head.T, True).T
+        mesh = run(2 + 2 * layer_id, parts, across, ids_m, mesh, col_m, row_m)
+    across = share(later, parts[-1])
+    return run(2 * LAYERS + 2, spread(mesh), across, ids_d, grid, None, head.T, True).T
 
 
 def solution(mesh):

time: 191 us -> 166 us (0.87)
  starting transfers between devices: 64 us -> 54.5 us
  waiting for transfers between devices: 88.5 us -> 79.3 us
  local copies, waits for them, and re-layouts: 9.35 us -> 4.96 us
  Pallas kernels: 27.6 us -> 24.7 us
    ppermute x67 -> x64, waiting for transfers between devices: 50.1 us -> 36.3 us  [swap(): return lax.ppermute(value, 'feat', [(f, f ^ bit) for f in range(quarters)])]
    ppermute x15, waiting for transfers between devices: 34.6 us -> 42.4 us  [shift(): lax.ppermute(value, 'band', [(b, (b + step) % bands) for b in range(bands)])]
    ppermute x15, starting transfers between devices: 24.9 us -> 18.5 us  [shift(): lax.ppermute(value, 'band', [(b, (b + step) % bands) for b in range(bands)])]
    unnamed x42 -> x32, local copies, waits for them, and re-layouts: 8.64 us -> 4.21 us
    ppermute x67 -> x64, starting transfers between devices: 33.9 us -> 30.4 us  [swap(): return lax.ppermute(value, 'feat', [(f, f ^ bit) for f in range(quarters)])]
    ppermute x4, waiting for transfers between devices: 3.85 us -> 0.6 us  [share(): second = lax.ppermute(first, 'parts', [(0, 1), (1, 0)])]
    pallas_call x12, Pallas kernels: 27.6 us -> 24.7 us  [kernel_call(): pl.pallas_call(body, out_shape=out_shape, in_specs=[pl.BlockSpec(memory_s...]
  transfers between devices with their start and end apart: 86 -> 83, of which waited for: 31 -> 34; matrix products, arithmetic and copies ran while one was open for 0% -> 0% of each run, Pallas kernels for 12% -> 11%
where the time goes in v9:
time: 166 us; the launch traced here: 165 us
  waiting for transfers between devices  79.3 us (48%)
  starting transfers between devices  54.5 us (33%)
  Pallas kernels  24.7 us (15%)
  local copies, waits for them, and re-layouts  4.96 us (3%)
    ppermute x15, waiting for transfers between devices, shift(): lax.ppermute(value, 'band', [(b, (b + step) % bands) for b in range(bands)])  42.4 us
    ppermute x64, waiting for transfers between devices, swap(): return lax.ppermute(value, 'feat', [(f, f ^ bit) for f in range(quarters)])  36.3 us
    ppermute x64, starting transfers between devices, swap(): return lax.ppermute(value, 'feat', [(f, f ^ bit) for f in range(quarters)])  30.4 us
    pallas_call x12, Pallas kernels, kernel_call(): pl.pallas_call(body, out_shape=out_shape, in_specs=[pl.BlockSpec(memory_s...  24.7 us
    ppermute x15, starting transfers between devices, shift(): lax.ppermute(value, 'band', [(b, (b + step) % bands) for b in range(bands)])  18.5 us
    ppermute x4, starting transfers between devices, share(): second = lax.ppermute(first, 'parts', [(0, 1), (1, 0)])  5.7 us
    unnamed x32, local copies, waits for them, and re-layouts  4.21 us
  transfers between devices with their start and end apart: 83, of which 34 were waited for; matrix products, arithmetic and copies ran while one was open for 0% of the time, Pallas kernels for 11%

profile of v9, /device:TPU:0, one launch (start us, length us, event | category | flops | bytes accessed | tf_op | source)
XLA Modules:
  0.0 165.2 jit_solution(8274723817266867533)
XLA Ops:
  1.4 3.0 %shard_map.172 = (bf16[128,128]{1,0:T(8,128)(2,1)}, bf16[768,128]{1,0:T(8,128)(2,1)}, bf16[640,128]{1,0:T(8,128)(2,1)}) custom-call(s32[3]{0:T(128)} %pad_add_fusion.1.place_ref.refs_0_, bf16[474,512]{1,0:T(8,128)(2,1)} %bitcast.18, bf16[474,128]{1,0:T(8,128)(2,1)} %w_hbm.1, bf16[9,128,512]{2,1,0:T(8,128)(2,1)} %out_ref.1, f32[9,128]{1,0:T(8,128)} %bias_ref.3), custom_call_target="tpu_custom_call" | custom-call | bytes 4194304 | tf_op jit(solution)/shard_map/pallas_call | solution.py:37
  4.4 3.0 %collective-permute-start = (bf16[768,128]{1,0:T(8,128)(2,1)}, bf16[768,128]{1,0:T(8,128)(2,1)S(1)}, u32[]{:S(2)}, u32[]{:S(2)}) collective-permute-start(bf16[768,128]{1,0:T(8,128)(2,1)} %get-tuple-element.73.out_ref), channel_id=1, source_target_pairs={{0,2},{1,3},{2,0},{3,1},{4,6},{5,7},{6,4},{7,5},{8,10},{9,11},{10,... | collective-permute-start | bytes 589832 | tf_op jit(solution)/shard_map/ppermute | solution.py:326
  7.4 5.1 %collective-permute-done.across = bf16[768,128]{1,0:T(8,128)(2,1)S(1)} collective-permute-done((bf16[768,128]{1,0:T(8,128)(2,1)}, bf16[768,128]{1,0:T(8,128)(2,1)S(1)}, u32[]{:S(2)}, u32[]{:S(2)}) %collective-permute-start) | collective-permute-done | bytes 196640 | tf_op jit(solution)/shard_map/ppermute | solution.py:326
  15.1 2.6 %collective-permute-start.4 = (s32[4,1152]{1,0:T(4,128)S(1)}, s32[4,1152]{1,0:T(4,128)S(1)}, u32[]{:S(2)}, u32[]{:S(2)}) collective-permute-start(s32[4,1152]{1,0:T(4,128)S(1)} %pad_add_fusion.refs_0_), channel_id=1, source_target_pairs={{0,8},{4,12},{8,0},{12,4},{1,9},{5,13},{9,1},{13,5},{2,10},{6,14},... | collective-permute-start | bytes 55304 | tf_op jit(solution)/shard_map/ppermute | solution.py:329
  27.1 6.7 %collective-permute-done.6.refs_1_ = bf16[128,512]{1,0:T(8,128)(2,1)S(1)} collective-permute-done((bf16[128,512]{1,0:T(8,128)(2,1)S(1)}, bf16[128,512]{1,0:T(8,128)(2,1)S(1)}, u32[]{:S(2)}, u32[]{:S(2)}) %collective-permute-start.6) | collective-permute-done | bytes 131104 | tf_op jit(solution)/shard_map/ppermute | solution.py:329
  34.3 2.6 %collective-permute-done.21.refs_3_ = bf16[1552,128]{1,0:T(8,128)(2,1)S(1)} collective-permute-done((bf16[1552,128]{1,0:T(8,128)(2,1)S(1)}, bf16[1552,128]{1,0:T(8,128)(2,1)S(1)}, u32[]{:S(2)}, u32[]{:S(2)}) %collective-permute-start.21) | collective-permute-done | bytes 397344 | tf_op jit(solution)/shard_map/ppermute | solution.py:326
  42.9 3.5 %collective-permute-done.8.refs_3_ = bf16[128,512]{1,0:T(8,128)(2,1)S(1)} collective-permute-done((bf16[128,512]{1,0:T(8,128)(2,1)S(1)}, bf16[128,512]{1,0:T(8,128)(2,1)S(1)}, u32[]{:S(2)}, u32[]{:S(2)}) %collective-permute-start.8) | collective-permute-done | bytes 131104 | tf_op jit(solution)/shard_map/ppermute | solution.py:329
  46.9 4.4 %collective-permute-done.7.refs_2_ = bf16[128,512]{1,0:T(8,128)(2,1)S(1)} collective-permute-done((bf16[128,512]{1,0:T(8,128)(2,1)S(1)}, bf16[128,512]{1,0:T(8,128)(2,1)S(1)}, u32[]{:S(2)}, u32[]{:S(2)}) %collective-permute-start.7) | collective-permute-done | bytes 131104 | tf_op jit(solution)/shard_map/ppermute | solution.py:329
  53.8 2.4 %collective-permute-done.9.refs_4_ = bf16[128,512]{1,0:T(8,128)(2,1)S(1)} collective-permute-done((bf16[128,512]{1,0:T(8,128)(2,1)S(1)}, bf16[128,512]{1,0:T(8,128)(2,1)S(1)}, u32[]{:S(2)}, u32[]{:S(2)}) %collective-permute-start.9) | collective-permute-done | bytes 131104 | tf_op jit(solution)/shard_map/ppermute | solution.py:326
  58.7 4.1 %collective-permute-done.11.refs_6_ = bf16[128,512]{1,0:T(8,128)(2,1)S(1)} collective-permute-done((bf16[128,512]{1,0:T(8,128)(2,1)S(1)}, bf16[128,512]{1,0:T(8,128)(2,1)S(1)}, u32[]{:S(2)}, u32[]{:S(2)}) %collective-permute-start.11) | collective-permute-done | bytes 131104 | tf_op jit(solution)/shard_map/ppermute | solution.py:326
  71.0 2.1 %shard_map.177.refs_7_.refs_0_.refs_17_ = bf16[128,512]{1,0:T(8,128)(2,1)S(1)} custom-call(bf16[128,512]{1,0:T(8,128)(2,1)S(1)} %shard_map.173.refs_0_.refs_7_.refs_17_, bf16[128,512]{1,0:T(8,128)(2,1)S(1)} %collective-permute-done.6.refs_1_, bf16[128,512]{1,0:T(8,128)(2,1)S(1)} %collective-permute-done.7.refs_2_, ...), custom_call_target="tpu_custom_call" | custom-call | flops 939524096 | bytes 4194304 | tf_op jit(solution)/shard_map/pallas_call | solution.py:37
  73.1 2.5 %collective-permute-start.59 = (bf16[1552,128]{1,0:T(8,128)(2,1)S(1)}, bf16[1552,128]{1,0:T(8,128)(2,1)S(1)}, u32[]{:S(2)}, u32[]{:S(2)}) collective-permute-start(bf16[1552,128]{1,0:T(8,128)(2,1)S(1)} %get-tuple-element.117), channel_id=1, source_target_pairs={{0,2},{1,3},{2,0},{3,1},{4,6},{5,7},{6,4},{7,5},{8,10},{9,11},{10,... | collective-permute-start | bytes 1191944 | tf_op jit(solution)/shard_map/ppermute | solution.py:326
  76.4 3.1 %collective-permute-start.28 = (bf16[128,512]{1,0:T(8,128)(2,1)S(1)}, bf16[128,512]{1,0:T(8,128)(2,1)S(1)}, u32[]{:S(2)}, u32[]{:S(2)}) collective-permute-start(bf16[128,512]{1,0:T(8,128)(2,1)S(1)} %shard_map.177.refs_7_.refs_0_.refs_17_), channel_id=1, source_target_pairs={{0,12},{4,0},{8,4},{12,8},{1,13},{5,1},{9,5},{13,9},{2,14},{6,2},{... | collective-permute-start | bytes 393224 | tf_op jit(solution)/shard_map/ppermute | solution.py:329
  79.7 4.2 %collective-permute-done.26.refs_1_ = bf16[128,512]{1,0:T(8,128)(2,1)S(1)} collective-permute-done((bf16[128,512]{1,0:T(8,128)(2,1)S(1)}, bf16[128,512]{1,0:T(8,128)(2,1)S(1)}, u32[]{:S(2)}, u32[]{:S(2)}) %collective-permute-start.26) | collective-permute-done | bytes 131104 | tf_op jit(solution)/shard_map/ppermute | solution.py:329
  86.1 3.5 %collective-permute-done.27.refs_2_ = bf16[128,512]{1,0:T(8,128)(2,1)S(1)} collective-permute-done((bf16[128,512]{1,0:T(8,128)(2,1)S(1)}, bf16[128,512]{1,0:T(8,128)(2,1)S(1)}, u32[]{:S(2)}, u32[]{:S(2)}) %collective-permute-start.27) | collective-permute-done | bytes 131104 | tf_op jit(solution)/shard_map/ppermute | solution.py:329
  100.1 2.9 %shard_map.179.refs_7_.refs_0_.refs_17_ = bf16[128,512]{1,0:T(8,128)(2,1)S(1)} custom-call(bf16[128,512]{1,0:T(8,128)(2,1)S(1)} %shard_map.177.refs_7_.refs_0_.refs_17_, bf16[128,512]{1,0:T(8,128)(2,1)S(1)} %collective-permute-done.26.refs_1_, bf16[128,512]{1,0:T(8,128)(2,1)S(1)} %collective-permute-done.27.refs_2_, ...), custom_call_target="tpu_custom_call" | custom-call | flops 1879048192 | bytes 4194304 | tf_op jit(solution)/shard_map/pallas_call | solution.py:37
  106.7 5.7 %collective-permute-done.47.refs_3_ = bf16[128,512]{1,0:T(8,128)(2,1)S(1)} collective-permute-done((bf16[128,512]{1,0:T(8,128)(2,1)S(1)}, bf16[128,512]{1,0:T(8,128)(2,1)S(1)}, u32[]{:S(2)}, u32[]{:S(2)}) %collective-permute-start.47) | collective-permute-done | bytes 131104 | tf_op jit(solution)/shard_map/ppermute | solution.py:329
  113.9 3.6 %collective-permute-done.51.refs_7_ = bf16[128,512]{1,0:T(8,128)(2,1)S(1)} collective-permute-done((bf16[128,512]{1,0:T(8,128)(2,1)S(1)}, bf16[128,512]{1,0:T(8,128)(2,1)S(1)}, u32[]{:S(2)}, u32[]{:S(2)}) %collective-permute-start.51) | collective-permute-done | bytes 131104 | tf_op jit(solution)/shard_map/ppermute | solution.py:326
  118.4 3.7 %collective-permute-done.46.refs_2_ = bf16[128,512]{1,0:T(8,128)(2,1)S(1)} collective-permute-done((bf16[128,512]{1,0:T(8,128)(2,1)S(1)}, bf16[128,512]{1,0:T(8,128)(2,1)S(1)}, u32[]{:S(2)}, u32[]{:S(2)}) %collective-permute-start.46) | collective-permute-done | bytes 131104 | tf_op jit(solution)/shard_map/ppermute | solution.py:329
  125.2 4.4 %collective-permute-done.49.refs_5_ = bf16[128,512]{1,0:T(8,128)(2,1)S(1)} collective-permute-done((bf16[128,512]{1,0:T(8,128)(2,1)S(1)}, bf16[128,512]{1,0:T(8,128)(2,1)S(1)}, u32[]{:S(2)}, u32[]{:S(2)}) %collective-permute-start.49) | collective-permute-done | bytes 131104 | tf_op jit(solution)/shard_map/ppermute | solution.py:326
  135.8 2.8 %shard_map.181.refs_0_ = bf16[128,512]{1,0:T(8,128)(2,1)S(1)} custom-call(bf16[128,512]{1,0:T(8,128)(2,1)S(1)} %shard_map.179.refs_7_.refs_0_.refs_17_, bf16[128,512]{1,0:T(8,128)(2,1)S(1)} %collective-permute-done.45.refs_1_, bf16[128,512]{1,0:T(8,128)(2,1)S(1)} %collective-permute-done.46.refs_2_, bf16[128,512]{1,0:T(8,128)(2,1)S(1)} %collective-permute-done.47.refs_3_, ...), custom_call_target="tpu_custom_call" | custom-call | flops 1879048192 | bytes 4194304 | tf_op jit(solution)/shard_map/pallas_call | solution.py:37
  142.1 5.3 %collective-permute-done.66.refs_3_ = bf16[128,512]{1,0:T(8,128)(2,1)S(1)} collective-permute-done((bf16[128,512]{1,0:T(8,128)(2,1)S(1)}, bf16[128,512]{1,0:T(8,128)(2,1)S(1)}, u32[]{:S(2)}, u32[]{:S(2)}) %collective-permute-start.66) | collective-permute-done | bytes 131104 | tf_op jit(solution)/shard_map/ppermute | solution.py:329
  149.0 3.7 %collective-permute-done.65.refs_2_ = bf16[128,512]{1,0:T(8,128)(2,1)S(1)} collective-permute-done((bf16[128,512]{1,0:T(8,128)(2,1)S(1)}, bf16[128,512]{1,0:T(8,128)(2,1)S(1)}, u32[]{:S(2)}, u32[]{:S(2)}) %collective-permute-start.65) | collective-permute-done | bytes 131104 | tf_op jit(solution)/shard_map/ppermute | solution.py:329
  161.9 3.3 %shard_map.183 = f32[227,128]{1,0:T(8,128)} custom-call(bf16[128,512]{1,0:T(8,128)(2,1)S(1)} %shard_map.181.refs_0_, bf16[128,512]{1,0:T(8,128)(2,1)S(1)} %collective-permute-done.64.refs_1_, bf16[128,512]{1,0:T(8,128)(2,1)S(1)} %collective-permute-done.65.refs_2_, bf16[128,512]{1,0:T(8,128)(2,1)S(1)} %collective-permute-done.66.refs_3_, ...), custom_call_target="tpu_custom_call" | custom-call | flops 1409286144 | bytes 4194304 | tf_op jit(solution)/shard_map/pallas_call | solution.py:37
  (189 shorter events, 76.5 us)
Async XLA Ops:
  7.4 16.9 %collective-permute-start.1 = (bf16[640,128]{1,0:T(8,128)(2,1)}, bf16[640,128]{1,0:T(8,128)(2,1)S(1)}, u32[]{:S(2)}, u32[]{:S(2)}) collective-permute-start(bf16[640,128]{1,0:T(8,128)(2,1)} %get-tuple-element.74), channel_id=1, source_target_pairs={{0,1},{1,0},{2,3},{3,2},{4,5},{5,4},{6,7},{7,6},{8,9},{9,8},{10,11... | collective-permute-start | bytes 491528 | tf_op jit(solution)/shard_map/ppermute | solution.py:326
  12.5 11.8 %collective-permute-start.2 = (bf16[768,128]{1,0:T(8,128)(2,1)S(1)}, bf16[768,128]{1,0:T(8,128)(2,1)S(1)}, u32[]{:S(2)}, u32[]{:S(2)}) collective-permute-start(bf16[768,128]{1,0:T(8,128)(2,1)S(1)} %collective-permute-done.across), channel_id=1, source_target_pairs={{0,1},{1,0},{2,3},{3,2},{4,5},{5,4},{6,7},{7,6},{8,9},{9,8},{10,11... | collective-permute-start | bytes 589832 | tf_op jit(solution)/shard_map/ppermute | solution.py:326
  13.3 11.0 %collective-permute-start.3 = (s32[4,1152]{1,0:T(4,128)S(1)}, s32[4,1152]{1,0:T(4,128)S(1)}, u32[]{:S(2)}, u32[]{:S(2)}) collective-permute-start(s32[4,1152]{1,0:T(4,128)S(1)} %pad_add_fusion.refs_0_), channel_id=1, source_target_pairs={{0,4},{4,8},{8,12},{12,0},{1,5},{5,9},{9,13},{13,1},{2,6},{6,10},{... | collective-permute-start | bytes 55304 | tf_op jit(solution)/shard_map/ppermute | solution.py:329
  24.8 40.6 %collective-permute-start.20 = (bf16[8,1552,128]{2,1,0:T(8,128)(2,1)S(1)}, bf16[8,1552,128]{2,1,0:T(8,128)(2,1)S(1)}, u32[]{:S(2)}, u32[]{:S(2)}) collective-permute-start(bf16[8,1552,128]{2,1,0:T(8,128)(2,1)S(1)} %get-tuple-element.80.refs_1_), channel_id=1, source_target_pairs={{0,1},{1,0},{2,3},{3,2},{4,5},{5,4},{6,7},{7,6},{8,9},{9,8},{10,11... | collective-permute-start | bytes 9535496 | tf_op jit(solution)/shard_map/ppermute | solution.py:326
  24.9 12.1 %collective-permute-start.21 = (bf16[1552,128]{1,0:T(8,128)(2,1)S(1)}, bf16[1552,128]{1,0:T(8,128)(2,1)S(1)}, u32[]{:S(2)}, u32[]{:S(2)}) collective-permute-start(bf16[1552,128]{1,0:T(8,128)(2,1)S(1)} %get-tuple-element.82), channel_id=1, source_target_pairs={{0,2},{1,3},{2,0},{3,1},{4,6},{5,7},{6,4},{7,5},{8,10},{9,11},{10,... | collective-permute-start | bytes 1191944 | tf_op jit(solution)/shard_map/ppermute | solution.py:326
  37.0 16.3 %collective-permute-start.22 = (bf16[1552,128]{1,0:T(8,128)(2,1)S(1)}, bf16[1552,128]{1,0:T(8,128)(2,1)S(1)}, u32[]{:S(2)}, u32[]{:S(2)}) collective-permute-start(bf16[1552,128]{1,0:T(8,128)(2,1)S(1)} %collective-permute-done.21.refs_3_), channel_id=1, source_target_pairs={{0,16},{16,0},{1,17},{17,1},{2,18},{18,2},{3,19},{19,3},{4,20},{20... | collective-permute-start | bytes 1191944 | tf_op jit(solution)/shard_map/ppermute | solution.py:419
  39.3 14.5 %collective-permute-start.40 = (bf16[1552,128]{1,0:T(8,128)(2,1)S(1)}, bf16[1552,128]{1,0:T(8,128)(2,1)S(1)}, u32[]{:S(2)}, u32[]{:S(2)}) collective-permute-start(bf16[1552,128]{1,0:T(8,128)(2,1)S(1)} %get-tuple-element.104), channel_id=1, source_target_pairs={{0,2},{1,3},{2,0},{3,1},{4,6},{5,7},{6,4},{7,5},{8,10},{9,11},{10,... | collective-permute-start | bytes 1191944 | tf_op jit(solution)/shard_map/ppermute | solution.py:326
  41.3 10.1 %collective-permute-start.7 = (bf16[128,512]{1,0:T(8,128)(2,1)S(1)}, bf16[128,512]{1,0:T(8,128)(2,1)S(1)}, u32[]{:S(2)}, u32[]{:S(2)}) collective-permute-start(bf16[128,512]{1,0:T(8,128)(2,1)S(1)} %shard_map.173.refs_0_.refs_7_.refs_17_), channel_id=1, source_target_pairs={{0,8},{4,12},{8,0},{12,4},{1,9},{5,13},{9,1},{13,5},{2,10},{6,14},... | collective-permute-start | bytes 393224 | tf_op jit(solution)/shard_map/ppermute | solution.py:329
  53.3 11.0 %collective-permute-start.23 = (bf16[1552,128]{1,0:T(8,128)(2,1)S(1)}, bf16[1552,128]{1,0:T(8,128)(2,1)S(1)}, u32[]{:S(2)}, u32[]{:S(2)}) collective-permute-start(bf16[1552,128]{1,0:T(8,128)(2,1)S(1)} %collective-permute-done.21.refs_3_), channel_id=1, source_target_pairs={{0,1},{1,0},{2,3},{3,2},{4,5},{5,4},{6,7},{7,6},{8,9},{9,8},{10,11... | collective-permute-start | bytes 1191944 | tf_op jit(solution)/shard_map/ppermute | solution.py:326
  53.3 11.4 %collective-permute-start.24 = (bf16[1552,128]{1,0:T(8,128)(2,1)S(1)}, bf16[1552,128]{1,0:T(8,128)(2,1)S(1)}, u32[]{:S(2)}, u32[]{:S(2)}) collective-permute-start(bf16[1552,128]{1,0:T(8,128)(2,1)S(1)} %collective-permute-done.22.refs_4_), channel_id=1, source_target_pairs={{0,1},{1,0},{2,3},{3,2},{4,5},{5,4},{6,7},{7,6},{8,9},{9,8},{10,11... | collective-permute-start | bytes 1191944 | tf_op jit(solution)/shard_map/ppermute | solution.py:326
  65.4 14.1 %collective-permute-start.42 = (bf16[1552,128]{1,0:T(8,128)(2,1)S(1)}, bf16[1552,128]{1,0:T(8,128)(2,1)S(1)}, u32[]{:S(2)}, u32[]{:S(2)}) collective-permute-start(bf16[1552,128]{1,0:T(8,128)(2,1)S(1)} %collective-permute-done.40.refs_3_), channel_id=1, source_target_pairs={{0,1},{1,0},{2,3},{3,2},{4,5},{5,4},{6,7},{7,6},{8,9},{9,8},{10,11... | collective-permute-start | bytes 1191944 | tf_op jit(solution)/shard_map/ppermute | solution.py:326
  65.4 14.1 %collective-permute-start.43 = (bf16[1552,128]{1,0:T(8,128)(2,1)S(1)}, bf16[1552,128]{1,0:T(8,128)(2,1)S(1)}, u32[]{:S(2)}, u32[]{:S(2)}) collective-permute-start(bf16[1552,128]{1,0:T(8,128)(2,1)S(1)} %collective-permute-done.41.refs_4_), channel_id=1, source_target_pairs={{0,1},{1,0},{2,3},{3,2},{4,5},{5,4},{6,7},{7,6},{8,9},{9,8},{10,11... | collective-permute-start | bytes 1191944 | tf_op jit(solution)/shard_map/ppermute | solution.py:326
  73.1 24.9 %collective-permute-start.59 = (bf16[1552,128]{1,0:T(8,128)(2,1)S(1)}, bf16[1552,128]{1,0:T(8,128)(2,1)S(1)}, u32[]{:S(2)}, u32[]{:S(2)}) collective-permute-start(bf16[1552,128]{1,0:T(8,128)(2,1)S(1)} %get-tuple-element.117), channel_id=1, source_target_pairs={{0,2},{1,3},{2,0},{3,1},{4,6},{5,7},{6,4},{7,5},{8,10},{9,11},{10,... | collective-permute-start | bytes 1191944 | tf_op jit(solution)/shard_map/ppermute | solution.py:326
  79.5 10.1 %collective-permute-start.27 = (bf16[128,512]{1,0:T(8,128)(2,1)S(1)}, bf16[128,512]{1,0:T(8,128)(2,1)S(1)}, u32[]{:S(2)}, u32[]{:S(2)}) collective-permute-start(bf16[128,512]{1,0:T(8,128)(2,1)S(1)} %shard_map.177.refs_7_.refs_0_.refs_17_), channel_id=1, source_target_pairs={{0,8},{4,12},{8,0},{12,4},{1,9},{5,13},{9,1},{13,5},{2,10},{6,14},... | collective-permute-start | bytes 393224 | tf_op jit(solution)/shard_map/ppermute | solution.py:329
  79.5 11.8 %collective-permute-start.29 = (bf16[128,512]{1,0:T(8,128)(2,1)S(1)}, bf16[128,512]{1,0:T(8,128)(2,1)S(1)}, u32[]{:S(2)}, u32[]{:S(2)}) collective-permute-start(bf16[128,512]{1,0:T(8,128)(2,1)S(1)} %shard_map.177.refs_7_.refs_0_.refs_17_), channel_id=1, source_target_pairs={{0,2},{1,3},{2,0},{3,1},{4,6},{5,7},{6,4},{7,5},{8,10},{9,11},{10,... | collective-permute-start | bytes 393224 | tf_op jit(solution)/shard_map/ppermute | solution.py:326
  98.5 14.0 %collective-permute-start.60 = (bf16[1552,128]{1,0:T(8,128)(2,1)S(1)}, bf16[1552,128]{1,0:T(8,128)(2,1)S(1)}, u32[]{:S(2)}, u32[]{:S(2)}) collective-permute-start(bf16[1552,128]{1,0:T(8,128)(2,1)S(1)} %collective-permute-done.59.refs_3_), channel_id=1, source_target_pairs={{0,16},{16,0},{1,17},{17,1},{2,18},{18,2},{3,19},{19,3},{4,20},{20... | collective-permute-start | bytes 1191944 | tf_op jit(solution)/shard_map/ppermute | solution.py:419
  103.0 15.5 %collective-permute-start.78 = (bf16[1552,128]{1,0:T(8,128)(2,1)S(1)}, bf16[1552,128]{1,0:T(8,128)(2,1)S(1)}, u32[]{:S(2)}, u32[]{:S(2)}) collective-permute-start(bf16[1552,128]{1,0:T(8,128)(2,1)S(1)} %get-tuple-element.127), channel_id=1, source_target_pairs={{0,2},{1,3},{2,0},{3,1},{4,6},{5,7},{6,4},{7,5},{8,10},{9,11},{10,... | collective-permute-start | bytes 1191944 | tf_op jit(solution)/shard_map/ppermute | solution.py:326
  106.7 24.5 %collective-permute-start.61 = (bf16[1552,128]{1,0:T(8,128)(2,1)S(1)}, bf16[1552,128]{1,0:T(8,128)(2,1)S(1)}, u32[]{:S(2)}, u32[]{:S(2)}) collective-permute-start(bf16[1552,128]{1,0:T(8,128)(2,1)S(1)} %collective-permute-done.59.refs_3_), channel_id=1, source_target_pairs={{0,1},{1,0},{2,3},{3,2},{4,5},{5,4},{6,7},{7,6},{8,9},{9,8},{10,11... | collective-permute-start | bytes 1191944 | tf_op jit(solution)/shard_map/ppermute | solution.py:326
  112.5 19.2 %collective-permute-start.62 = (bf16[1552,128]{1,0:T(8,128)(2,1)S(1)}, bf16[1552,128]{1,0:T(8,128)(2,1)S(1)}, u32[]{:S(2)}, u32[]{:S(2)}) collective-permute-start(bf16[1552,128]{1,0:T(8,128)(2,1)S(1)} %collective-permute-done.60.refs_4_), channel_id=1, source_target_pairs={{0,1},{1,0},{2,3},{3,2},{4,5},{5,4},{6,7},{7,6},{8,9},{9,8},{10,11... | collective-permute-start | bytes 1191944 | tf_op jit(solution)/shard_map/ppermute | solution.py:326
  112.5 9.6 %collective-permute-start.46 = (bf16[128,512]{1,0:T(8,128)(2,1)S(1)}, bf16[128,512]{1,0:T(8,128)(2,1)S(1)}, u32[]{:S(2)}, u32[]{:S(2)}) collective-permute-start(bf16[128,512]{1,0:T(8,128)(2,1)S(1)} %shard_map.179.refs_7_.refs_0_.refs_17_), channel_id=1, source_target_pairs={{0,8},{4,12},{8,0},{12,4},{1,9},{5,13},{9,1},{13,5},{2,10},{6,14},... | collective-permute-start | bytes 393224 | tf_op jit(solution)/shard_map/ppermute | solution.py:329
  122.1 12.7 %collective-permute-start.79 = (bf16[1552,128]{1,0:T(8,128)(2,1)S(1)}, bf16[1552,128]{1,0:T(8,128)(2,1)S(1)}, u32[]{:S(2)}, u32[]{:S(2)}) collective-permute-start(bf16[1552,128]{1,0:T(8,128)(2,1)S(1)} %collective-permute-done.78.refs_3_), channel_id=1, source_target_pairs={{0,16},{16,0},{1,17},{17,1},{2,18},{18,2},{3,19},{19,3},{4,20},{20... | collective-permute-start | bytes 1191944 | tf_op jit(solution)/shard_map/ppermute | solution.py:419
  134.8 19.9 %collective-permute-start.81 = (bf16[1552,128]{1,0:T(8,128)(2,1)S(1)}, bf16[1552,128]{1,0:T(8,128)(2,1)S(1)}, u32[]{:S(2)}, u32[]{:S(2)}) collective-permute-start(bf16[1552,128]{1,0:T(8,128)(2,1)S(1)} %collective-permute-done.79.refs_4_), channel_id=1, source_target_pairs={{0,1},{1,0},{2,3},{3,2},{4,5},{5,4},{6,7},{7,6},{8,9},{9,8},{10,11... | collective-permute-start | bytes 1191944 | tf_op jit(solution)/shard_map/ppermute | solution.py:326
  140.7 12.0 %collective-permute-start.65 = (bf16[128,512]{1,0:T(8,128)(2,1)S(1)}, bf16[128,512]{1,0:T(8,128)(2,1)S(1)}, u32[]{:S(2)}, u32[]{:S(2)}) collective-permute-start(bf16[128,512]{1,0:T(8,128)(2,1)S(1)} %shard_map.181.refs_0_), channel_id=1, source_target_pairs={{0,8},{4,12},{8,0},{12,4},{1,9},{5,13},{9,1},{13,5},{2,10},{6,14},... | collective-permute-start | bytes 393224 | tf_op jit(solution)/shard_map/ppermute | solution.py:329
  141.3 12.6 %collective-permute-start.67 = (bf16[128,512]{1,0:T(8,128)(2,1)S(1)}, bf16[128,512]{1,0:T(8,128)(2,1)S(1)}, u32[]{:S(2)}, u32[]{:S(2)}) collective-permute-start(bf16[128,512]{1,0:T(8,128)(2,1)S(1)} %shard_map.181.refs_0_), channel_id=1, source_target_pairs={{0,2},{1,3},{2,0},{3,1},{4,6},{5,7},{6,4},{7,5},{8,10},{9,11},{10,... | collective-permute-start | bytes 393224 | tf_op jit(solution)/shard_map/ppermute | solution.py:326
  (75 other events, 852.3 us)

commit v10 on v9

--- a/solution.py
+++ b/solution.py
@@ -101,16 +101,22 @@
     out[...] = layer_norm(product, gain[row, :], shift[row, :]).astype(BF16)
 
 
-def pack(place_ref, in_hbm, out_ref, bias_ref, packed, *refs):
-    crossing, sem = refs[:-1], refs[-1]
+def pack(place_ref, in_hbm, out_ref, bias_ref, *refs):
+    groups = (len(refs) - 2) // 2
+    packed, bundle, crossing, sem = refs[:groups], refs[groups], refs[groups + 1 : -1], refs[-1]
     part = place_ref[2]
     inner, width = in_hbm.shape[1:]
     latent = out_ref.shape[2]
     targets = []
     pairs = []
-    for i in range(packed.shape[0]):
+    for i in range(2 * groups):
         section_id = (i - i % 2) + (part if i % 2 == 0 else 1 - part)
-        targets.append((section_id, [packed.at[i]] + ([crossing[i // 2]] if i % 2 == 0 else [])))
+        outs = [packed[i // 2].at[i % 2]]
+        if i % 2 == 0:
+            outs.append(crossing[i // 2])
+        if i > 1:
+            outs.append(bundle.at[i - 2])
+        targets.append((section_id, outs))
         pairs += [(in_hbm.at[section_id], out.at[pl.ds(0, inner)]) for out in targets[-1][1]]
     copies = started(pairs, sem)
     for section_id, outs in targets:
@@ -179,14 +185,13 @@
     mesh_out[...] = (mesh + turned[:, 2:3] * pos_w[2:3, :]).astype(BF16)
 
 
-def stage(group_id, last, *refs):
-    place_ref, mine_hbm, other_hbm, *across, own_ref = refs[:8]
+def stage(begin, last, *refs):
+    place_ref, mine, other_hbm, *across, own_ref = refs[:8]
     rest = refs[8:]
     if not last:
         recv_col, *rest = rest
-    w_send, w_out, w_agg, w_out2, recv_pre, node_pre, mine, other, sem = rest
-    chosen = pl.ds(2 * group_id, 2)
-    copies = started([(mine_hbm.at[chosen], mine), (other_hbm.at[chosen], other)], sem)
+    w_send, w_out, w_agg, w_out2, recv_pre, node_pre, other, sem = rest
+    copies = started([(other_hbm.at[pl.ds(begin, 2)], other)], sem)
     x_first, y_second, cx_first, cy_second = across
     kinds = (
         [mine.at[0], x_first, other.at[0], cx_first],
@@ -232,20 +237,27 @@
     pl.when(part == 1)(functools.partial(emit, 1))
 
 
-def phase(section_id, tables, last, *refs):
+def stack(*refs):
+    begin = 0
+    for ref in refs[:-1]:
+        refs[-1][pl.ds(begin, ref.shape[0]), :] = ref[...]
+        begin += ref.shape[0]
+
+
+def phase(section_id, tables, segments, last, *refs):
     table_refs = refs[:tables]
     ids, own_ref, w_send, w_out, w_agg, w_out2, recv_pre, node_pre, gain, shift, extra, out = refs[tables:]
     rows, latent = own_ref.shape
     edges = ids.shape[0]
     chunks = [[]]
     held = 0
-    for ref in table_refs:
-        size = min(ref.shape[0], CHUNK)
-        for begin in range(0, ref.shape[0], size):
+    for which, first, count in segments:
+        size = min(count, CHUNK)
+        for begin in range(first, first + count, size):
             if held + size > CHUNK:
                 chunks.append([])
                 held = 0
-            chunks[-1].append(ref[pl.ds(begin, size), :])
+            chunks[-1].append(table_refs[which][pl.ds(begin, size), :])
             held += size
     preact = recv_pre[...]
     sent = None
@@ -334,16 +346,36 @@
             parts = parts + [swap(part, bit) for part in parts]
         return parts
 
-    def spread(rows):
+    def spread(rows, opening, second, next_id):
         if direct:
-            parts = [rows] + [shift(rows, step) for step in range(1, bands)]
-            return parts + [swap(part, bits[0]) for part in parts]
+            near = [rows] + [shift(rows, step) for step in range(1, bands)]
+            far = [opening]
+            following = cross(next_id, far[0]) if 2 * next_id < sections else None
+            far.append(swap(near[1], bits[0]))
+            late, _ = lax.optimization_barrier((near[2:], (second, following)))
+            return near + far + [swap(part, bits[0]) for part in late], following
         parts = [rows, swap(rows, bits[0])]
-        return [lax.all_gather(part, "band", axis=0, tiled=True) for part in parts]
+        following = cross(next_id, rows) if 2 * next_id < sections else None
+        return [lax.all_gather(part, "band", axis=0, tiled=True) for part in parts], following
+
+    def stacked(parts):
+        rows = sum(part.shape[0] for part in parts)
+        return kernel_call(
+            stack,
+            jax.ShapeDtypeStruct((rows, latent), BF16),
+            parts,
+            (vmem,) * len(parts),
+            vmem=8 << 20,
+        )
 
     def complete(parts, staged):
-        last, _ = lax.optimization_barrier((parts[-1], staged))
-        return parts + [swap(part, bits[1]) for part in parts[:-1] + [last]]
+        if not direct:
+            table = parts + [swap(part, bits[1]) for part in parts]
+            return table, [(i, 0, part.shape[0]) for i, part in enumerate(table)]
+        near, far = parts[:bands], parts[bands:]
+        far, _ = lax.optimization_barrier((far, staged))
+        table = parts + [swap(stacked(near), bits[1]), swap(stacked(far), bits[1])]
+        return table, [(i, 0, part.shape[0]) for i, part in enumerate(table)]
 
     caps = [take.shape[2] for take in (g2m_take, m2m_take, m2g_take)]
     direct = direct and all(cap % 128 == 0 for cap in caps)
@@ -374,23 +406,39 @@
     met = swap(sends[0], bits[0])
     received = [met, swap(sends[1], bits[1]), swap(met, bits[1])]
     place_after, _ = lax.optimization_barrier((place, hidden))
+    nearby = received[1]
 
     sections = embed_id
     piece = (3 * latent + BIAS_ROWS, width)
-    packed, *crossing = kernel_call(
+    packed = kernel_call(
         pack,
-        [jax.ShapeDtypeStruct((sections, *piece), BF16)]
+        [jax.ShapeDtypeStruct((2, *piece), BF16)] * (sections // 2)
+        + [jax.ShapeDtypeStruct((sections - 2, *piece), BF16)]
         + [jax.ShapeDtypeStruct(piece, BF16)] * (sections // 2),
         (place_after, pair_in, pair_out, hidden_bias),
         (scalar, hbm, vmem, vmem),
-        scratch=(pltpu.SemaphoreType.DMA((sections + sections // 2,)),),
-        vmem=20 << 20,
+        scratch=(pltpu.SemaphoreType.DMA((2 * sections - 2 + sections // 2,)),),
+        vmem=GRANT,
     )
     edges = [v.shape[0] // quarters for v in (g2m_from, m2m_from, m2g_from)]
     columns = [jax.ShapeDtypeStruct((n, 1), jnp.int32) for n in edges + edges[:2]]
     lines = [jax.ShapeDtypeStruct((1, n), jnp.int32) for n in edges[:2]]
     shape = jax.ShapeDtypeStruct((mesh_rows, latent), BF16)
-    received, tables = lax.optimization_barrier((received, tables))
+    bundle = packed[sections // 2]
+    crossing = packed[sections // 2 + 1 :]
+
+    def held(value, after):
+        return lax.optimization_barrier((value, after))[0]
+
+    def cross(group_id, after):
+        first = crossing[group_id]
+        if after is not None:
+            first, _ = lax.optimization_barrier((first, after))
+        return swap(first, bits[0])
+
+    first = cross(0, nearby)
+    swapped = swap(held(packed[0], met), bits[1])
+    received, tables, first, swapped = lax.optimization_barrier((received, tables, first, swapped))
     grid = kernel_call(
         functools.partial(embed_finish, embed_id),
         jax.ShapeDtypeStruct((grid_rows, latent), BF16),
@@ -405,41 +453,35 @@
         vmem=24 << 20,
     )
     ids_g, ids_m, ids_d, col_g, col_m, row_g, row_m, mesh = routed
-    swapped = swap(lax.optimization_barrier((packed, grid))[0], bits[1])
-
-    def cross(group_id, after):
-        first = crossing[group_id]
-        if after is not None:
-            first, _ = lax.optimization_barrier((first, after))
-        return swap(first, bits[0])
-
-    def share(first, after):
-        if after is not None:
-            first, _ = lax.optimization_barrier((first, after))
-        second = lax.ppermute(first, "parts", [(0, 1), (1, 0)])
+    def over(first, after):
+        first, _ = lax.optimization_barrier((first, after))
+        return lax.ppermute(first, "parts", [(0, 1), (1, 0)])
+
+    def share(first, second, after):
+        first, second, _ = lax.optimization_barrier((first, second, after))
         return [first, second, swap(first, bits[1]), swap(second, bits[1])]
 
-    def run(section_id, parts, across, ids, own_latent, column, extra, last=False):
+    def run(section_id, parts, swapped, across, ids, own_latent, column, extra, last=False):
         edges = ids.shape[0]
         square = jax.ShapeDtypeStruct((latent, latent), BF16)
         columns = () if last else (column,)
         staged = kernel_call(
-            functools.partial(stage, section_id // 2, last),
+            functools.partial(stage, max(section_id - 2, 0), last),
             [square] * 4
             + [jax.ShapeDtypeStruct((n, latent), F32) for n in (edges, own_latent.shape[0])],
-            (place, packed, swapped, *across, own_latent, *columns),
-            (scalar, hbm, hbm) + (vmem,) * (5 + len(columns)),
-            scratch=[pltpu.VMEM((2, *piece), BF16)] * 2 + [pltpu.SemaphoreType.DMA((2,))],
+            (place, packed[section_id // 2], swapped, *across, own_latent, *columns),
+            (scalar, vmem, hbm) + (vmem,) * (5 + len(columns)),
+            scratch=(pltpu.VMEM((2, *piece), BF16), pltpu.SemaphoreType.DMA((1,))),
             flops=4 * edges * latent * latent,
             vmem=20 << 20,
         )
-        table = complete(parts, staged)
+        table, segments = complete(parts, staged)
         rows = sum(part.shape[0] for part in table)
         out_shape = jax.ShapeDtypeStruct(own_latent.shape, BF16)
         if last:
             out_shape = jax.ShapeDtypeStruct((head.shape[1], own_latent.shape[0]), F32)
         return kernel_call(
-            functools.partial(phase, section_id, len(table), last),
+            functools.partial(phase, section_id, len(table), segments, last),
             out_shape,
             (*table, ids, own_latent, *staged, norm_gain, norm_shift, extra),
             (vmem,) * (len(table) + 11),
@@ -447,17 +489,22 @@
             vmem=(20 << 20) + rows * latent * 2,
         )
 
-    across = share(cross(0, met), None)
-    parts = spread(grid)
-    later = cross(1, parts[bands + 1] if direct else grid)
-    mesh = run(0, parts, across, ids_g, mesh, col_g, row_g)
+    def window(group_id, rows, first):
+        opening = swap(rows, bits[0]) if direct else rows
+        second = over(first, rows)
+        parts, following = spread(rows, opening, second, group_id + 1)
+        near = tuple(parts[: len(parts) // 2])
+        after = near if following is not None else (near, opening)
+        return parts, share(first, second, after), following
+
+    parts, across, first = window(0, grid, first)
+    bundled = swap(held(bundle, parts[len(parts) // 2]), bits[1])
+    mesh = run(0, parts, swapped, across, ids_g, mesh, col_g, row_g)
     for layer_id in range(LAYERS):
-        across = share(later, parts[-1])
-        parts = spread(mesh)
-        later = cross(2 + layer_id, mesh)
-        mesh = run(2 + 2 * layer_id, parts, across, ids_m, mesh, col_m, row_m)
-    across = share(later, parts[-1])
-    return run(2 * LAYERS + 2, spread(mesh), across, ids_d, grid, None, head.T, True).T
+        parts, across, first = window(1 + layer_id, mesh, first)
+        mesh = run(2 + 2 * layer_id, parts, bundled, across, ids_m, mesh, col_m, row_m)
+    parts, across, _ = window(LAYERS + 1, mesh, first)
+    return run(2 * LAYERS + 2, parts, bundled, across, ids_d, grid, None, head.T, True).T
 
 
 def solution(mesh):

time: 166 us -> 161 us (0.970)
  waiting for transfers between devices: 79.3 us -> 70.2 us
  Pallas kernels: 24.7 us -> 30 us
  local copies, waits for them, and re-layouts: 4.96 us -> 0.81 us
  starting transfers between devices: 54.5 us -> 57.9 us
    ppermute x15, waiting for transfers between devices: 42.4 us -> 30 us  [shift(): lax.ppermute(value, 'band', [(b, (b + step) % bands) for b in range(bands)])]
    ppermute x15, starting transfers between devices: 18.5 us -> 28.5 us  [shift(): lax.ppermute(value, 'band', [(b, (b + step) % bands) for b in range(bands)])]
    ppermute x64 -> x41, starting transfers between devices: 30.4 us -> 24.3 us  [swap(): return lax.ppermute(value, 'feat', [(f, f ^ bit) for f in range(quarters)])]
    pallas_call x12 -> x20, Pallas kernels: 24.7 us -> 30 us  [kernel_call(): pl.pallas_call(body, out_shape=out_shape, in_specs=[pl.BlockSpec(memory_s...]
    unnamed x32 -> x44, local copies, waits for them, and re-layouts: 4.21 us -> 0.11 us
    ppermute x64 -> x41, waiting for transfers between devices: 36.3 us -> 40.2 us  [swap(): return lax.ppermute(value, 'feat', [(f, f ^ bit) for f in range(quarters)])]
  transfers between devices with their start and end apart: 83 -> 60, of which waited for: 34 -> 34; matrix products, arithmetic and copies ran while one was open for 0% -> 0% of each run, Pallas kernels for 11% -> 11%
where the time goes in v10:
time: 161 us; the launch traced here: 160 us
  waiting for transfers between devices  70.2 us (44%)
  starting transfers between devices  57.9 us (36%)
  Pallas kernels  30 us (19%)
    ppermute x41, waiting for transfers between devices, swap(): return lax.ppermute(value, 'feat', [(f, f ^ bit) for f in range(quarters)])  40.2 us
    ppermute x15, waiting for transfers between devices, shift(): lax.ppermute(value, 'band', [(b, (b + step) % bands) for b in range(bands)])  30 us
    pallas_call x20, Pallas kernels, kernel_call(): pl.pallas_call(body, out_shape=out_shape, in_specs=[pl.BlockSpec(memory_s...  30 us
    ppermute x15, starting transfers between devices, shift(): lax.ppermute(value, 'band', [(b, (b + step) % bands) for b in range(bands)])  28.5 us
    ppermute x41, starting transfers between devices, swap(): return lax.ppermute(value, 'feat', [(f, f ^ bit) for f in range(quarters)])  24.3 us
    ppermute x4, starting transfers between devices, over(): return lax.ppermute(first, 'parts', [(0, 1), (1, 0)])  5.11 us
  transfers between devices with their start and end apart: 60, of which 34 were waited for; matrix products, arithmetic and copies ran while one was open for 0% of the time, Pallas kernels for 11%

profile of v10, /device:TPU:0, one launch (start us, length us, event | category | flops | bytes accessed | tf_op | source)
XLA Modules:
  0.0 160.1 jit_solution(3187562065624399695)
XLA Ops:
  1.3 3.0 %shard_map.172 = (bf16[128,128]{1,0:T(8,128)(2,1)}, bf16[768,128]{1,0:T(8,128)(2,1)}, bf16[640,128]{1,0:T(8,128)(2,1)}) custom-call(s32[3]{0:T(128)} %pad_add_fusion.1.place_ref.refs_0_, bf16[474,512]{1,0:T(8,128)(2,1)} %bitcast.18, bf16[474,128]{1,0:T(8,128)(2,1)} %w_hbm.1, bf16[9,128,512]{2,1,0:T(8,128)(2,1)} %out_ref.1, f32[9,128]{1,0:T(8,128)} %bias_ref.3), custom_call_target="tpu_custom_call" | custom-call | bytes 4194304 | tf_op jit(solution)/shard_map/pallas_call | solution.py:37
  4.5 3.0 %collective-permute-start = (bf16[768,128]{1,0:T(8,128)(2,1)}, bf16[768,128]{1,0:T(8,128)(2,1)S(1)}, u32[]{:S(2)}, u32[]{:S(2)}) collective-permute-start(bf16[768,128]{1,0:T(8,128)(2,1)} %get-tuple-element.109.out_ref), channel_id=1, source_target_pairs={{0,2},{1,3},{2,0},{3,1},{4,6},{5,7},{6,4},{7,5},{8,10},{9,11},{10,... | collective-permute-start | bytes 589832 | tf_op jit(solution)/shard_map/ppermute | solution.py:338
  7.5 6.8 %shard_map.173 = (bf16[2,1552,128]{2,1,0:T(8,128)(2,1)}, bf16[2,1552,128]{2,1,0:T(8,128)(2,1)}, bf16[2,1552,128]{2,1,0:T(8,128)(2,1)}, bf16[2,1552,128]{2,1,0:T(...) custom-call(s32[3]{0:T(128)} %pad_add_fusion.1.place_ref.refs_0_, ...), custom_call_target="tpu_custom_call" | custom-call | bytes 4194304 | tf_op jit(solution)/shard_map/pallas_call | solution.py:37
  17.0 2.0 %collective-permute-start.3 = (s32[4,1152]{1,0:T(4,128)S(1)}, s32[4,1152]{1,0:T(4,128)S(1)}, u32[]{:S(2)}, u32[]{:S(2)}) collective-permute-start(s32[4,1152]{1,0:T(4,128)S(1)} %pad_add_fusion.refs_0_), channel_id=1, source_target_pairs={{0,4},{4,8},{8,12},{12,0},{1,5},{5,9},{9,13},{13,1},{2,6},{6,10},{... | collective-permute-start | bytes 55304 | tf_op jit(solution)/shard_map/ppermute | solution.py:341
  19.1 2.6 %collective-permute-start.4 = (s32[4,1152]{1,0:T(4,128)S(1)}, s32[4,1152]{1,0:T(4,128)S(1)}, u32[]{:S(2)}, u32[]{:S(2)}) collective-permute-start(s32[4,1152]{1,0:T(4,128)S(1)} %pad_add_fusion.refs_0_), channel_id=1, source_target_pairs={{0,8},{4,12},{8,0},{12,4},{1,9},{5,13},{9,1},{13,5},{2,10},{6,14},... | collective-permute-start | bytes 55304 | tf_op jit(solution)/shard_map/ppermute | solution.py:341
  30.7 3.1 %collective-permute-done.11.refs_0_.refs_4_ = bf16[128,512]{1,0:T(8,128)(2,1)S(1)} collective-permute-done((bf16[128,512]{1,0:T(8,128)(2,1)S(1)}, bf16[128,512]{1,0:T(8,128)(2,1)S(1)}, u32[]{:S(2)}, u32[]{:S(2)}) %collective-permute-start.11) | collective-permute-done | bytes 131104 | tf_op jit(solution)/shard_map/ppermute | solution.py:338
  33.8 3.6 %collective-permute-start.10 = (bf16[128,512]{1,0:T(8,128)(2,1)S(1)}, bf16[128,512]{1,0:T(8,128)(2,1)S(1)}, u32[]{:S(2)}, u32[]{:S(2)}) collective-permute-start(bf16[128,512]{1,0:T(8,128)(2,1)S(1)} %shard_map.174.refs_0_.refs_7_.refs_11_), channel_id=1, source_target_pairs={{0,12},{4,0},{8,4},{12,8},{1,13},{5,1},{9,5},{13,9},{2,14},{6,2},{... | collective-permute-start | bytes 393224 | tf_op jit(solution)/shard_map/ppermute | solution.py:341
  38.4 2.8 %collective-permute-done.10.refs_3_ = bf16[128,512]{1,0:T(8,128)(2,1)S(1)} collective-permute-done((bf16[128,512]{1,0:T(8,128)(2,1)S(1)}, bf16[128,512]{1,0:T(8,128)(2,1)S(1)}, u32[]{:S(2)}, u32[]{:S(2)}) %collective-permute-start.10) | collective-permute-done | bytes 131104 | tf_op jit(solution)/shard_map/ppermute | solution.py:341
  41.8 3.8 %collective-permute-done.8.refs_1_ = bf16[128,512]{1,0:T(8,128)(2,1)S(1)} collective-permute-done((bf16[128,512]{1,0:T(8,128)(2,1)S(1)}, bf16[128,512]{1,0:T(8,128)(2,1)S(1)}, u32[]{:S(2)}, u32[]{:S(2)}) %collective-permute-start.8) | collective-permute-done | bytes 131104 | tf_op jit(solution)/shard_map/ppermute | solution.py:341
  45.6 3.9 %collective-permute-done.9.refs_2_ = bf16[128,512]{1,0:T(8,128)(2,1)S(1)} collective-permute-done((bf16[128,512]{1,0:T(8,128)(2,1)S(1)}, bf16[128,512]{1,0:T(8,128)(2,1)S(1)}, u32[]{:S(2)}, u32[]{:S(2)}) %collective-permute-start.9) | collective-permute-done | bytes 131104 | tf_op jit(solution)/shard_map/ppermute | solution.py:341
  63.1 2.1 %shard_map.179.refs_0_.refs_7_.refs_11_ = bf16[128,512]{1,0:T(8,128)(2,1)S(1)} custom-call(bf16[128,512]{1,0:T(8,128)(2,1)S(1)} %shard_map.174.refs_0_.refs_7_.refs_11_, bf16[128,512]{1,0:T(8,128)(2,1)S(1)} %collective-permute-done.8.refs_1_, bf16[128,512]{1,0:T(8,128)(2,1)S(1)} %collective-permute-done.9.refs_2_, ...), custom_call_target="tpu_custom_call" | custom-call | flops 939524096 | bytes 4194304 | tf_op jit(solution)/shard_map/pallas_call | solution.py:37
  67.2 4.0 %collective-permute-start.22 = (bf16[128,512]{1,0:T(8,128)(2,1)S(1)}, bf16[128,512]{1,0:T(8,128)(2,1)S(1)}, u32[]{:S(2)}, u32[]{:S(2)}) collective-permute-start(bf16[128,512]{1,0:T(8,128)(2,1)S(1)} %shard_map.179.refs_0_.refs_7_.refs_11_), channel_id=1, source_target_pairs={{0,8},{4,12},{8,0},{12,4},{1,9},{5,13},{9,1},{13,5},{2,10},{6,14},... | collective-permute-start | bytes 393224 | tf_op jit(solution)/shard_map/ppermute | solution.py:341
  71.9 3.5 %collective-permute-start.23 = (bf16[128,512]{1,0:T(8,128)(2,1)S(1)}, bf16[128,512]{1,0:T(8,128)(2,1)S(1)}, u32[]{:S(2)}, u32[]{:S(2)}) collective-permute-start(bf16[128,512]{1,0:T(8,128)(2,1)S(1)} %shard_map.179.refs_0_.refs_7_.refs_11_), channel_id=1, source_target_pairs={{0,12},{4,0},{8,4},{12,8},{1,13},{5,1},{9,5},{13,9},{2,14},{6,2},{... | collective-permute-start | bytes 393224 | tf_op jit(solution)/shard_map/ppermute | solution.py:341
  77.0 2.6 %collective-permute-done.22.refs_2_ = bf16[128,512]{1,0:T(8,128)(2,1)S(1)} collective-permute-done((bf16[128,512]{1,0:T(8,128)(2,1)S(1)}, bf16[128,512]{1,0:T(8,128)(2,1)S(1)}, u32[]{:S(2)}, u32[]{:S(2)}) %collective-permute-start.22) | collective-permute-done | bytes 131104 | tf_op jit(solution)/shard_map/ppermute | solution.py:341
  81.7 5.6 %collective-permute-done.27.refs_3_ = bf16[1552,128]{1,0:T(8,128)(2,1)S(1)} collective-permute-done((bf16[1552,128]{1,0:T(8,128)(2,1)S(1)}, bf16[1552,128]{1,0:T(8,128)(2,1)S(1)}, u32[]{:S(2)}, u32[]{:S(2)}) %collective-permute-start.27) | collective-permute-done | bytes 397344 | tf_op jit(solution)/shard_map/ppermute | solution.py:338
  95.7 2.8 %shard_map.183.refs_0_.refs_7_.refs_11_ = bf16[128,512]{1,0:T(8,128)(2,1)S(1)} custom-call(bf16[128,512]{1,0:T(8,128)(2,1)S(1)} %shard_map.179.refs_0_.refs_7_.refs_11_, bf16[128,512]{1,0:T(8,128)(2,1)S(1)} %collective-permute-done.21.refs_1_, bf16[128,512]{1,0:T(8,128)(2,1)S(1)} %collective-permute-done.22.refs_2_, ...), custom_call_target="tpu_custom_call" | custom-call | flops 1879048192 | bytes 4194304 | tf_op jit(solution)/shard_map/pallas_call | solution.py:37
  105.2 3.0 %collective-permute-done.35.refs_1_ = bf16[128,512]{1,0:T(8,128)(2,1)S(1)} collective-permute-done((bf16[128,512]{1,0:T(8,128)(2,1)S(1)}, bf16[128,512]{1,0:T(8,128)(2,1)S(1)}, u32[]{:S(2)}, u32[]{:S(2)}) %collective-permute-start.35) | collective-permute-done | bytes 131104 | tf_op jit(solution)/shard_map/ppermute | solution.py:341
  108.2 4.2 %collective-permute-done.36.refs_2_ = bf16[128,512]{1,0:T(8,128)(2,1)S(1)} collective-permute-done((bf16[128,512]{1,0:T(8,128)(2,1)S(1)}, bf16[128,512]{1,0:T(8,128)(2,1)S(1)}, u32[]{:S(2)}, u32[]{:S(2)}) %collective-permute-start.36) | collective-permute-done | bytes 131104 | tf_op jit(solution)/shard_map/ppermute | solution.py:341
  119.3 2.8 %collective-permute-done.42.refs_2_.refs_6_ = bf16[128,512]{1,0:T(8,128)(2,1)S(1)} collective-permute-done((bf16[128,512]{1,0:T(8,128)(2,1)S(1)}, bf16[128,512]{1,0:T(8,128)(2,1)S(1)}, u32[]{:S(2)}, u32[]{:S(2)}) %collective-permute-start.42) | collective-permute-done | bytes 131104 | tf_op jit(solution)/shard_map/ppermute | solution.py:338
  126.0 2.8 %shard_map.187.refs_0_ = bf16[128,512]{1,0:T(8,128)(2,1)S(1)} custom-call(bf16[128,512]{1,0:T(8,128)(2,1)S(1)} %shard_map.183.refs_0_.refs_7_.refs_11_, bf16[128,512]{1,0:T(8,128)(2,1)S(1)} %collective-permute-done.35.refs_1_, bf16[128,512]{1,0:T(8,128)(2,1)S(1)} %collective-permute-done.36.refs_2_, bf16[128,512]{1,0:T(8,128)(2,1)S(1)} %collective-permute-done.37.refs_3_, ...), custom_call_target="tpu_custom_call" | custom-call | flops 1879048192 | bytes 4194304 | tf_op jit(solution)/shard_map/pallas_call | solution.py:37
  130.3 3.2 %collective-permute-start.48 = (bf16[128,512]{1,0:T(8,128)(2,1)S(1)}, bf16[128,512]{1,0:T(8,128)(2,1)S(1)}, u32[]{:S(2)}, u32[]{:S(2)}) collective-permute-start(bf16[128,512]{1,0:T(8,128)(2,1)S(1)} %shard_map.187.refs_0_), channel_id=1, source_target_pairs={{0,4},{4,8},{8,12},{12,0},{1,5},{5,9},{9,13},{13,1},{2,6},{6,10},{... | collective-permute-start | bytes 393224 | tf_op jit(solution)/shard_map/ppermute | solution.py:341
  138.5 4.5 %collective-permute-done.49.refs_2_ = bf16[128,512]{1,0:T(8,128)(2,1)S(1)} collective-permute-done((bf16[128,512]{1,0:T(8,128)(2,1)S(1)}, bf16[128,512]{1,0:T(8,128)(2,1)S(1)}, u32[]{:S(2)}, u32[]{:S(2)}) %collective-permute-start.49) | collective-permute-done | bytes 131104 | tf_op jit(solution)/shard_map/ppermute | solution.py:341
  150.0 2.8 %collective-permute-done.54.refs_2_.refs_6_ = bf16[128,512]{1,0:T(8,128)(2,1)S(1)} collective-permute-done((bf16[128,512]{1,0:T(8,128)(2,1)S(1)}, bf16[128,512]{1,0:T(8,128)(2,1)S(1)}, u32[]{:S(2)}, u32[]{:S(2)}) %collective-permute-start.54) | collective-permute-done | bytes 131104 | tf_op jit(solution)/shard_map/ppermute | solution.py:338
  156.7 3.3 %shard_map.191 = f32[227,128]{1,0:T(8,128)} custom-call(bf16[128,512]{1,0:T(8,128)(2,1)S(1)} %shard_map.187.refs_0_, bf16[128,512]{1,0:T(8,128)(2,1)S(1)} %collective-permute-done.48.refs_1_, bf16[128,512]{1,0:T(8,128)(2,1)S(1)} %collective-permute-done.49.refs_2_, bf16[128,512]{1,0:T(8,128)(2,1)S(1)} %collective-permute-done.50.refs_3_, ...), custom_call_target="tpu_custom_call" | custom-call | flops 1409286144 | bytes 4194304 | tf_op jit(solution)/shard_map/pallas_call | solution.py:37
  (163 shorter events, 77.3 us)
Async XLA Ops:
  4.5 9.8 %collective-permute-start = (bf16[768,128]{1,0:T(8,128)(2,1)}, bf16[768,128]{1,0:T(8,128)(2,1)S(1)}, u32[]{:S(2)}, u32[]{:S(2)}) collective-permute-start(bf16[768,128]{1,0:T(8,128)(2,1)} %get-tuple-element.109.out_ref), channel_id=1, source_target_pairs={{0,2},{1,3},{2,0},{3,1},{4,6},{5,7},{6,4},{7,5},{8,10},{9,11},{10,... | collective-permute-start | bytes 589832 | tf_op jit(solution)/shard_map/ppermute | solution.py:338
  14.3 14.0 %collective-permute-start.7 = (bf16[2,1552,128]{2,1,0:T(8,128)(2,1)}, bf16[2,1552,128]{2,1,0:T(8,128)(2,1)S(1)}, u32[]{:S(2)}, u32[]{:S(2)}) collective-permute-start(bf16[2,1552,128]{2,1,0:T(8,128)(2,1)} %get-tuple-element.115.refs_1_), channel_id=1, source_target_pairs={{0,1},{1,0},{2,3},{3,2},{4,5},{5,4},{6,7},{7,6},{8,9},{9,8},{10,11... | collective-permute-start | bytes 2383880 | tf_op jit(solution)/shard_map/ppermute | solution.py:338
  16.9 11.5 %collective-permute-start.6 = (bf16[1552,128]{1,0:T(8,128)(2,1)}, bf16[1552,128]{1,0:T(8,128)(2,1)S(1)}, u32[]{:S(2)}, u32[]{:S(2)}) collective-permute-start(bf16[1552,128]{1,0:T(8,128)(2,1)} %get-tuple-element.113), channel_id=1, source_target_pairs={{0,2},{1,3},{2,0},{3,1},{4,6},{5,7},{6,4},{7,5},{8,10},{9,11},{10,... | collective-permute-start | bytes 1191944 | tf_op jit(solution)/shard_map/ppermute | solution.py:338
  17.0 9.6 %collective-permute-start.2 = (bf16[768,128]{1,0:T(8,128)(2,1)S(1)}, bf16[768,128]{1,0:T(8,128)(2,1)S(1)}, u32[]{:S(2)}, u32[]{:S(2)}) collective-permute-start(bf16[768,128]{1,0:T(8,128)(2,1)S(1)} %collective-permute-done.across), channel_id=1, source_target_pairs={{0,1},{1,0},{2,3},{3,2},{4,5},{5,4},{6,7},{7,6},{8,9},{9,8},{10,11... | collective-permute-start | bytes 589832 | tf_op jit(solution)/shard_map/ppermute | solution.py:338
  29.1 20.4 %collective-permute-start.13 = (bf16[1552,128]{1,0:T(8,128)(2,1)S(1)}, bf16[1552,128]{1,0:T(8,128)(2,1)S(1)}, u32[]{:S(2)}, u32[]{:S(2)}) collective-permute-start(bf16[1552,128]{1,0:T(8,128)(2,1)S(1)} %collective-permute-done.6.refs_3_), channel_id=1, source_target_pairs={{0,16},{16,0},{1,17},{17,1},{2,18},{18,2},{3,19},{19,3},{4,20},{20... | collective-permute-start | bytes 1191944 | tf_op jit(solution)/shard_map/ppermute | solution.py:458
  33.8 55.7 %collective-permute-start.31 = (bf16[6,1552,128]{2,1,0:T(8,128)(2,1)}, bf16[6,1552,128]{2,1,0:T(8,128)(2,1)S(1)}, u32[]{:S(2)}, u32[]{:S(2)}) collective-permute-start(bf16[6,1552,128]{2,1,0:T(8,128)(2,1)} %get-tuple-element.158), channel_id=1, source_target_pairs={{0,1},{1,0},{2,3},{3,2},{4,5},{5,4},{6,7},{7,6},{8,9},{9,8},{10,11... | collective-permute-start | bytes 7151624 | tf_op jit(solution)/shard_map/ppermute | solution.py:338
  37.4 12.1 %collective-permute-start.9 = (bf16[128,512]{1,0:T(8,128)(2,1)S(1)}, bf16[128,512]{1,0:T(8,128)(2,1)S(1)}, u32[]{:S(2)}, u32[]{:S(2)}) collective-permute-start(bf16[128,512]{1,0:T(8,128)(2,1)S(1)} %shard_map.174.refs_0_.refs_7_.refs_11_), channel_id=1, source_target_pairs={{0,8},{4,12},{8,0},{12,4},{1,9},{5,13},{9,1},{13,5},{2,10},{6,14},... | collective-permute-start | bytes 393224 | tf_op jit(solution)/shard_map/ppermute | solution.py:341
  41.3 10.7 %collective-permute-start.14 = (bf16[1552,128]{1,0:T(8,128)(2,1)}, bf16[1552,128]{1,0:T(8,128)(2,1)S(1)}, u32[]{:S(2)}, u32[]{:S(2)}) collective-permute-start(bf16[1552,128]{1,0:T(8,128)(2,1)} %get-tuple-element.122), channel_id=1, source_target_pairs={{0,2},{1,3},{2,0},{3,1},{4,6},{5,7},{6,4},{7,5},{8,10},{9,11},{10,... | collective-permute-start | bytes 1191944 | tf_op jit(solution)/shard_map/ppermute | solution.py:338
  52.5 8.6 %collective-permute-start.16 = (bf16[128,512]{1,0:T(8,128)(2,1)S(1)}, bf16[128,512]{1,0:T(8,128)(2,1)S(1)}, u32[]{:S(2)}, u32[]{:S(2)}) collective-permute-start(bf16[128,512]{1,0:T(8,128)(2,1)S(1)} %collective-permute-done.10.refs_3_), channel_id=1, source_target_pairs={{0,2},{1,3},{2,0},{3,1},{4,6},{5,7},{6,4},{7,5},{8,10},{9,11},{10,... | collective-permute-start | bytes 393224 | tf_op jit(solution)/shard_map/ppermute | solution.py:338
  65.2 14.8 %collective-permute-start.26 = (bf16[1552,128]{1,0:T(8,128)(2,1)S(1)}, bf16[1552,128]{1,0:T(8,128)(2,1)S(1)}, u32[]{:S(2)}, u32[]{:S(2)}) collective-permute-start(bf16[1552,128]{1,0:T(8,128)(2,1)S(1)} %collective-permute-done.14.refs_3_), channel_id=1, source_target_pairs={{0,16},{16,0},{1,17},{17,1},{2,18},{18,2},{3,19},{19,3},{4,20},{20... | collective-permute-start | bytes 1191944 | tf_op jit(solution)/shard_map/ppermute | solution.py:458
  67.1 8.4 %collective-permute-start.21 = (bf16[128,512]{1,0:T(8,128)(2,1)S(1)}, bf16[128,512]{1,0:T(8,128)(2,1)S(1)}, u32[]{:S(2)}, u32[]{:S(2)}) collective-permute-start(bf16[128,512]{1,0:T(8,128)(2,1)S(1)} %shard_map.179.refs_0_.refs_7_.refs_11_), channel_id=1, source_target_pairs={{0,4},{4,8},{8,12},{12,0},{1,5},{5,9},{9,13},{13,1},{2,6},{6,10},{... | collective-permute-start | bytes 393224 | tf_op jit(solution)/shard_map/ppermute | solution.py:341
  67.2 12.4 %collective-permute-start.22 = (bf16[128,512]{1,0:T(8,128)(2,1)S(1)}, bf16[128,512]{1,0:T(8,128)(2,1)S(1)}, u32[]{:S(2)}, u32[]{:S(2)}) collective-permute-start(bf16[128,512]{1,0:T(8,128)(2,1)S(1)} %shard_map.179.refs_0_.refs_7_.refs_11_), channel_id=1, source_target_pairs={{0,8},{4,12},{8,0},{12,4},{1,9},{5,13},{9,1},{13,5},{2,10},{6,14},... | collective-permute-start | bytes 393224 | tf_op jit(solution)/shard_map/ppermute | solution.py:341
  75.5 11.8 %collective-permute-start.27 = (bf16[1552,128]{1,0:T(8,128)(2,1)S(1)}, bf16[1552,128]{1,0:T(8,128)(2,1)S(1)}, u32[]{:S(2)}, u32[]{:S(2)}) collective-permute-start(bf16[1552,128]{1,0:T(8,128)(2,1)S(1)} %copy-done.20), channel_id=1, source_target_pairs={{0,2},{1,3},{2,0},{3,1},{4,6},{5,7},{6,4},{7,5},{8,10},{9,11},{10,... | collective-permute-start | bytes 1191944 | tf_op jit(solution)/shard_map/ppermute | solution.py:338
  80.0 9.4 %collective-permute-start.33 = (bf16[1552,128]{1,0:T(8,128)(2,1)S(1)}, bf16[1552,128]{1,0:T(8,128)(2,1)S(1)}, u32[]{:S(2)}, u32[]{:S(2)}) collective-permute-start(bf16[1552,128]{1,0:T(8,128)(2,1)S(1)} %collective-permute-done.26.refs_4_), channel_id=1, source_target_pairs={{0,1},{1,0},{2,3},{3,2},{4,5},{5,4},{6,7},{7,6},{8,9},{9,8},{10,11... | collective-permute-start | bytes 1191944 | tf_op jit(solution)/shard_map/ppermute | solution.py:338
  80.5 10.8 %collective-permute-start.25 = (bf16[128,512]{1,0:T(8,128)(2,1)S(1)}, bf16[128,512]{1,0:T(8,128)(2,1)S(1)}, u32[]{:S(2)}, u32[]{:S(2)}) collective-permute-start(bf16[128,512]{1,0:T(8,128)(2,1)S(1)} %collective-permute-done.21.refs_1_), channel_id=1, source_target_pairs={{0,2},{1,3},{2,0},{3,1},{4,6},{5,7},{6,4},{7,5},{8,10},{9,11},{10,... | collective-permute-start | bytes 393224 | tf_op jit(solution)/shard_map/ppermute | solution.py:338
  98.5 13.9 %collective-permute-start.40 = (bf16[1552,128]{1,0:T(8,128)(2,1)S(1)}, bf16[1552,128]{1,0:T(8,128)(2,1)S(1)}, u32[]{:S(2)}, u32[]{:S(2)}) collective-permute-start(bf16[1552,128]{1,0:T(8,128)(2,1)S(1)} %collective-permute-done.27.refs_3_), channel_id=1, source_target_pairs={{0,16},{16,0},{1,17},{17,1},{2,18},{18,2},{3,19},{19,3},{4,20},{20... | collective-permute-start | bytes 1191944 | tf_op jit(solution)/shard_map/ppermute | solution.py:458
  101.6 10.8 %collective-permute-start.36 = (bf16[128,512]{1,0:T(8,128)(2,1)S(1)}, bf16[128,512]{1,0:T(8,128)(2,1)S(1)}, u32[]{:S(2)}, u32[]{:S(2)}) collective-permute-start(bf16[128,512]{1,0:T(8,128)(2,1)S(1)} %shard_map.183.refs_0_.refs_7_.refs_11_), channel_id=1, source_target_pairs={{0,8},{4,12},{8,0},{12,4},{1,9},{5,13},{9,1},{13,5},{2,10},{6,14},... | collective-permute-start | bytes 393224 | tf_op jit(solution)/shard_map/ppermute | solution.py:341
  103.2 9.2 %collective-permute-start.37 = (bf16[128,512]{1,0:T(8,128)(2,1)S(1)}, bf16[128,512]{1,0:T(8,128)(2,1)S(1)}, u32[]{:S(2)}, u32[]{:S(2)}) collective-permute-start(bf16[128,512]{1,0:T(8,128)(2,1)S(1)} %shard_map.183.refs_0_.refs_7_.refs_11_), channel_id=1, source_target_pairs={{0,12},{4,0},{8,4},{12,8},{1,13},{5,1},{9,5},{13,9},{2,14},{6,2},{... | collective-permute-start | bytes 393224 | tf_op jit(solution)/shard_map/ppermute | solution.py:341
  104.5 10.1 %collective-permute-start.41 = (bf16[1552,128]{1,0:T(8,128)(2,1)S(1)}, bf16[1552,128]{1,0:T(8,128)(2,1)S(1)}, u32[]{:S(2)}, u32[]{:S(2)}) collective-permute-start(bf16[1552,128]{1,0:T(8,128)(2,1)S(1)} %copy-done.19), channel_id=1, source_target_pairs={{0,2},{1,3},{2,0},{3,1},{4,6},{5,7},{6,4},{7,5},{8,10},{9,11},{10,... | collective-permute-start | bytes 1191944 | tf_op jit(solution)/shard_map/ppermute | solution.py:338
  115.3 8.7 %collective-permute-start.43 = (bf16[128,512]{1,0:T(8,128)(2,1)S(1)}, bf16[128,512]{1,0:T(8,128)(2,1)S(1)}, u32[]{:S(2)}, u32[]{:S(2)}) collective-permute-start(bf16[128,512]{1,0:T(8,128)(2,1)S(1)} %collective-permute-done.37.refs_3_), channel_id=1, source_target_pairs={{0,2},{1,3},{2,0},{3,1},{4,6},{5,7},{6,4},{7,5},{8,10},{9,11},{10,... | collective-permute-start | bytes 393224 | tf_op jit(solution)/shard_map/ppermute | solution.py:338
  128.9 14.2 %collective-permute-start.53 = (bf16[1552,128]{1,0:T(8,128)(2,1)S(1)}, bf16[1552,128]{1,0:T(8,128)(2,1)S(1)}, u32[]{:S(2)}, u32[]{:S(2)}) collective-permute-start(bf16[1552,128]{1,0:T(8,128)(2,1)S(1)} %collective-permute-done.41.refs_3_), channel_id=1, source_target_pairs={{0,16},{16,0},{1,17},{17,1},{2,18},{18,2},{3,19},{19,3},{4,20},{20... | collective-permute-start | bytes 1191944 | tf_op jit(solution)/shard_map/ppermute | solution.py:458
  133.5 9.5 %collective-permute-start.49 = (bf16[128,512]{1,0:T(8,128)(2,1)S(1)}, bf16[128,512]{1,0:T(8,128)(2,1)S(1)}, u32[]{:S(2)}, u32[]{:S(2)}) collective-permute-start(bf16[128,512]{1,0:T(8,128)(2,1)S(1)} %shard_map.187.refs_0_), channel_id=1, source_target_pairs={{0,8},{4,12},{8,0},{12,4},{1,9},{5,13},{9,1},{13,5},{2,10},{6,14},... | collective-permute-start | bytes 393224 | tf_op jit(solution)/shard_map/ppermute | solution.py:341
  134.0 9.0 %collective-permute-start.50 = (bf16[128,512]{1,0:T(8,128)(2,1)S(1)}, bf16[128,512]{1,0:T(8,128)(2,1)S(1)}, u32[]{:S(2)}, u32[]{:S(2)}) collective-permute-start(bf16[128,512]{1,0:T(8,128)(2,1)S(1)} %shard_map.187.refs_0_), channel_id=1, source_target_pairs={{0,12},{4,0},{8,4},{12,8},{1,13},{5,1},{9,5},{13,9},{2,14},{6,2},{... | collective-permute-start | bytes 393224 | tf_op jit(solution)/shard_map/ppermute | solution.py:341
  145.7 9.1 %collective-permute-start.55 = (bf16[128,512]{1,0:T(8,128)(2,1)S(1)}, bf16[128,512]{1,0:T(8,128)(2,1)S(1)}, u32[]{:S(2)}, u32[]{:S(2)}) collective-permute-start(bf16[128,512]{1,0:T(8,128)(2,1)S(1)} %collective-permute-done.50.refs_3_), channel_id=1, source_target_pairs={{0,2},{1,3},{2,0},{3,1},{4,6},{5,7},{6,4},{7,5},{8,10},{9,11},{10,... | collective-permute-start | bytes 393224 | tf_op jit(solution)/shard_map/ppermute | solution.py:338
  (58 other events, 849.5 us)

commit v11 on v10

--- a/solution.py
+++ b/solution.py
@@ -102,20 +102,15 @@
 
 
 def pack(place_ref, in_hbm, out_ref, bias_ref, *refs):
-    groups = (len(refs) - 2) // 2
-    packed, bundle, crossing, sem = refs[:groups], refs[groups], refs[groups + 1 : -1], refs[-1]
+    packed, *crossing, sem = refs
     part = place_ref[2]
     inner, width = in_hbm.shape[1:]
     latent = out_ref.shape[2]
     targets = []
     pairs = []
-    for i in range(2 * groups):
+    for i in range(packed.shape[0]):
         section_id = (i - i % 2) + (part if i % 2 == 0 else 1 - part)
-        outs = [packed[i // 2].at[i % 2]]
-        if i % 2 == 0:
-            outs.append(crossing[i // 2])
-        if i > 1:
-            outs.append(bundle.at[i - 2])
+        outs = [packed.at[i]] + ([crossing[i // 2]] if i % 2 == 0 else [])
         targets.append((section_id, outs))
         pairs += [(in_hbm.at[section_id], out.at[pl.ds(0, inner)]) for out in targets[-1][1]]
     copies = started(pairs, sem)
@@ -186,12 +181,12 @@
 
 
 def stage(begin, last, *refs):
-    place_ref, mine, other_hbm, *across, own_ref = refs[:8]
+    place_ref, mine_hbm, other_hbm, *across, own_ref = refs[:8]
     rest = refs[8:]
     if not last:
         recv_col, *rest = rest
-    w_send, w_out, w_agg, w_out2, recv_pre, node_pre, other, sem = rest
-    copies = started([(other_hbm.at[pl.ds(begin, 2)], other)], sem)
+    w_send, w_out, w_agg, w_out2, recv_pre, node_pre, mine, other, sem = rest
+    copies = started([(ref.at[pl.ds(begin, 2)], out) for ref, out in ((mine_hbm, mine), (other_hbm, other))], sem)
     x_first, y_second, cx_first, cy_second = across
     kinds = (
         [mine.at[0], x_first, other.at[0], cx_first],
@@ -379,18 +374,12 @@
 
     caps = [take.shape[2] for take in (g2m_take, m2m_take, m2g_take)]
     direct = direct and all(cap % 128 == 0 for cap in caps)
-    if direct:
-        whole = jnp.concatenate([g2m_take[0], m2m_take[0], m2g_take[0]], axis=1)
-        tables = [whole] + [shift(whole, step) for step in range(1, bands)]
-    else:
-        takes = [jnp.pad(t[0], ((0, 0), (0, -t.shape[2] % 128))) for t in (g2m_take, m2m_take, m2g_take)]
-        tables = [
-            lax.all_to_all(
-                jnp.concatenate(takes, axis=1), "band", split_axis=0, concat_axis=0, tiled=True
-            )
-        ]
+    takes = [take[0] for take in (g2m_take, m2m_take, m2g_take)]
+    if not direct:
+        takes = [jnp.pad(take, ((0, 0), (0, -take.shape[1] % 128))) for take in takes]
+    whole = jnp.concatenate(takes, axis=1)
     names = [v[None, :] for v in (g2m_from, m2m_from, m2g_from, g2m_to, m2m_to)]
-    names, place = lax.optimization_barrier((names, place))
+    names, whole, place = lax.optimization_barrier((names, whole, place))
     hidden, *sends = kernel_call(
         functools.partial(embed_hidden, order, embed_id),
         [jax.ShapeDtypeStruct((n, width), BF16) for n in (grid_rows, latent + 2 * grid_rows, latent + grid_rows)],
@@ -405,27 +394,24 @@
     )
     met = swap(sends[0], bits[0])
     received = [met, swap(sends[1], bits[1]), swap(met, bits[1])]
-    place_after, _ = lax.optimization_barrier((place, hidden))
+    place_after, _ = lax.optimization_barrier((place, received[1]))
     nearby = received[1]
 
     sections = embed_id
     piece = (3 * latent + BIAS_ROWS, width)
-    packed = kernel_call(
+    packed, *crossing = kernel_call(
         pack,
-        [jax.ShapeDtypeStruct((2, *piece), BF16)] * (sections // 2)
-        + [jax.ShapeDtypeStruct((sections - 2, *piece), BF16)]
+        [jax.ShapeDtypeStruct((sections, *piece), BF16)]
         + [jax.ShapeDtypeStruct(piece, BF16)] * (sections // 2),
         (place_after, pair_in, pair_out, hidden_bias),
         (scalar, hbm, vmem, vmem),
-        scratch=(pltpu.SemaphoreType.DMA((2 * sections - 2 + sections // 2,)),),
+        scratch=(pltpu.SemaphoreType.DMA((sections + sections // 2,)),),
         vmem=GRANT,
     )
     edges = [v.shape[0] // quarters for v in (g2m_from, m2m_from, m2g_from)]
     columns = [jax.ShapeDtypeStruct((n, 1), jnp.int32) for n in edges + edges[:2]]
     lines = [jax.ShapeDtypeStruct((1, n), jnp.int32) for n in edges[:2]]
     shape = jax.ShapeDtypeStruct((mesh_rows, latent), BF16)
-    bundle = packed[sections // 2]
-    crossing = packed[sections // 2 + 1 :]
 
     def held(value, after):
         return lax.optimization_barrier((value, after))[0]
@@ -437,22 +423,14 @@
         return swap(first, bits[0])
 
     first = cross(0, nearby)
-    swapped = swap(held(packed[0], met), bits[1])
-    received, tables, first, swapped = lax.optimization_barrier((received, tables, first, swapped))
+    swapped = swap(held(packed, met), bits[1])
+    received, first = lax.optimization_barrier((received, first))
     grid = kernel_call(
         functools.partial(embed_finish, embed_id),
         jax.ShapeDtypeStruct((grid_rows, latent), BF16),
         (hidden, sends[0], *received, norm_gain, norm_shift),
         (vmem,) * 7,
     )
-    routed = kernel_call(
-        functools.partial(route, bits, direct, bands, caps, (grid_rows, mesh_rows, mesh_rows), edges),
-        [*columns, *lines, shape],
-        (place, *tables, *names, mesh_pos, pos_weight),
-        (scalar,) + (vmem,) * (len(tables) + 7),
-        vmem=24 << 20,
-    )
-    ids_g, ids_m, ids_d, col_g, col_m, row_g, row_m, mesh = routed
     def over(first, after):
         first, _ = lax.optimization_barrier((first, after))
         return lax.ppermute(first, "parts", [(0, 1), (1, 0)])
@@ -466,12 +444,12 @@
         square = jax.ShapeDtypeStruct((latent, latent), BF16)
         columns = () if last else (column,)
         staged = kernel_call(
-            functools.partial(stage, max(section_id - 2, 0), last),
+            functools.partial(stage, section_id, last),
             [square] * 4
             + [jax.ShapeDtypeStruct((n, latent), F32) for n in (edges, own_latent.shape[0])],
-            (place, packed[section_id // 2], swapped, *across, own_latent, *columns),
-            (scalar, vmem, hbm) + (vmem,) * (5 + len(columns)),
-            scratch=(pltpu.VMEM((2, *piece), BF16), pltpu.SemaphoreType.DMA((1,))),
+            (place, packed, swapped, *across, own_latent, *columns),
+            (scalar, hbm, hbm) + (vmem,) * (5 + len(columns)),
+            scratch=[pltpu.VMEM((2, *piece), BF16)] * 2 + [pltpu.SemaphoreType.DMA((2,))],
             flops=4 * edges * latent * latent,
             vmem=20 << 20,
         )
@@ -498,13 +476,25 @@
         return parts, share(first, second, after), following
 
     parts, across, first = window(0, grid, first)
-    bundled = swap(held(bundle, parts[len(parts) // 2]), bits[1])
+    if direct:
+        whole = held(whole, tuple(parts[:bands]))
+        tables = [whole] + [shift(whole, step) for step in range(1, bands)]
+    else:
+        tables = [lax.all_to_all(whole, "band", split_axis=0, concat_axis=0, tiled=True)]
+    routed = kernel_call(
+        functools.partial(route, bits, direct, bands, caps, (grid_rows, mesh_rows, mesh_rows), edges),
+        [*columns, *lines, shape],
+        (place, *tables, *names, mesh_pos, pos_weight),
+        (scalar,) + (vmem,) * (len(tables) + 7),
+        vmem=24 << 20,
+    )
+    ids_g, ids_m, ids_d, col_g, col_m, row_g, row_m, mesh = routed
     mesh = run(0, parts, swapped, across, ids_g, mesh, col_g, row_g)
     for layer_id in range(LAYERS):
         parts, across, first = window(1 + layer_id, mesh, first)
-        mesh = run(2 + 2 * layer_id, parts, bundled, across, ids_m, mesh, col_m, row_m)
+        mesh = run(2 + 2 * layer_id, parts, swapped, across, ids_m, mesh, col_m, row_m)
     parts, across, _ = window(LAYERS + 1, mesh, first)
-    return run(2 * LAYERS + 2, parts, bundled, across, ids_d, grid, None, head.T, True).T
+    return run(2 * LAYERS + 2, parts, swapped, across, ids_d, grid, None, head.T, True).T
 
 
 def solution(mesh):

time: 161 us -> 161 us (level)
  waiting for transfers between devices: 70.2 us -> 65.2 us
  starting transfers between devices: 57.9 us -> 61.2 us
  local copies, waits for them, and re-layouts: 0.81 us -> 2.67 us
    ppermute x41 -> x40, starting transfers between devices: 24.3 us -> 28 us  [swap(): return lax.ppermute(value, 'feat', [(f, f ^ bit) for f in range(quarters)])]
    ppermute x15, waiting for transfers between devices: 30 us -> 26.5 us  [shift(): lax.ppermute(value, 'band', [(b, (b + step) % bands) for b in range(bands)])]
    unnamed x44 -> x32, local copies, waits for them, and re-layouts: 0.11 us -> 1.96 us
    ppermute x41 -> x40, waiting for transfers between devices: 40.2 us -> 38.7 us  [swap(): return lax.ppermute(value, 'feat', [(f, f ^ bit) for f in range(quarters)])]
  transfers between devices with their start and end apart: 60 -> 59, of which waited for: 34 -> 29; matrix products, arithmetic and copies ran while one was open for 0% -> 0% of each run, Pallas kernels for 11% -> 9%
where the time goes in v11:
time: 161 us; the launch traced here: 160 us
  waiting for transfers between devices  65.2 us (40%)
  starting transfers between devices  61.2 us (38%)
  Pallas kernels  29.1 us (18%)
  local copies, waits for them, and re-layouts  2.67 us (2%)
    ppermute x40, waiting for transfers between devices, swap(): return lax.ppermute(value, 'feat', [(f, f ^ bit) for f in range(quarters)])  38.7 us
    pallas_call x20, Pallas kernels, kernel_call(): pl.pallas_call(body, out_shape=out_shape, in_specs=[pl.BlockSpec(memory_s...  29.1 us
    ppermute x15, starting transfers between devices, shift(): lax.ppermute(value, 'band', [(b, (b + step) % bands) for b in range(bands)])  28.8 us
    ppermute x40, starting transfers between devices, swap(): return lax.ppermute(value, 'feat', [(f, f ^ bit) for f in range(quarters)])  28 us
    ppermute x15, waiting for transfers between devices, shift(): lax.ppermute(value, 'band', [(b, (b + step) % bands) for b in range(bands)])  26.5 us
    ppermute x4, starting transfers between devices, over(): return lax.ppermute(first, 'parts', [(0, 1), (1, 0)])  4.3 us
  transfers between devices with their start and end apart: 59, of which 29 were waited for; matrix products, arithmetic and copies ran while one was open for 0% of the time, Pallas kernels for 9%

profile of v11, /device:TPU:0, one launch (start us, length us, event | category | flops | bytes accessed | tf_op | source)
XLA Modules:
  0.0 159.9 jit_solution(16682942649904989767)
XLA Ops:
  2.1 3.0 %shard_map.172 = (bf16[128,128]{1,0:T(8,128)(2,1)}, bf16[768,128]{1,0:T(8,128)(2,1)}, bf16[640,128]{1,0:T(8,128)(2,1)}) custom-call(s32[3]{0:T(128)} %pad_add_fusion.1.place_ref.refs_0_, bf16[474,512]{1,0:T(8,128)(2,1)} %bitcast.18, bf16[474,128]{1,0:T(8,128)(2,1)} %w_hbm.1, bf16[9,128,512]{2,1,0:T(8,128)(2,1)} %out_ref.1, f32[9,128]{1,0:T(8,128)} %bias_ref.3), custom_call_target="tpu_custom_call" | custom-call | bytes 4194304 | tf_op jit(solution)/shard_map/pallas_call | solution.py:37
  5.1 3.0 %collective-permute-start = (bf16[768,128]{1,0:T(8,128)(2,1)}, bf16[768,128]{1,0:T(8,128)(2,1)S(1)}, u32[]{:S(2)}, u32[]{:S(2)}) collective-permute-start(bf16[768,128]{1,0:T(8,128)(2,1)} %get-tuple-element.101.out_ref), channel_id=1, source_target_pairs={{0,2},{1,3},{2,0},{3,1},{4,6},{5,7},{6,4},{7,5},{8,10},{9,11},{10,... | collective-permute-start | bytes 589832 | tf_op jit(solution)/shard_map/ppermute | solution.py:333
  9.8 5.6 %shard_map.173 = (bf16[8,1552,128]{2,1,0:T(8,128)(2,1)}, bf16[1552,128]{1,0:T(8,128)(2,1)}, bf16[1552,128]{1,0:T(8,128)(2,1)}, bf16[1552,128]{1,0:T(8,128)(2,1)}, bf16[1552,128]{1,0:T(8,128)(2,1)}) custom-call(s32[3]{0:T(128)} %pad_add_fusion.1.place_ref.refs_0_, bf16[8,1024,128]{2,1,0:T(8,128)(2,1)} %in_hbm.1, bf16[9,128,512]{2,1,0:T(8,128)(2,1)} %out_ref.1, ...), custom_call_target="tpu_custom_call" | custom-call | bytes 4194304 | tf_op jit(solution)/shard_map/pallas_call | solution.py:37
  15.9 4.7 %collective-permute-done.2.diagonal = bf16[768,128]{1,0:T(8,128)(2,1)S(1)} collective-permute-done((bf16[768,128]{1,0:T(8,128)(2,1)S(1)}, bf16[768,128]{1,0:T(8,128)(2,1)S(1)}, u32[]{:S(2)}, u32[]{:S(2)}) %collective-permute-start.2) | collective-permute-done | bytes 196640 | tf_op jit(solution)/shard_map/ppermute | solution.py:333
  20.6 6.6 %collective-permute-done.3.refs_3_ = bf16[1552,128]{1,0:T(8,128)(2,1)S(1)} collective-permute-done((bf16[1552,128]{1,0:T(8,128)(2,1)}, bf16[1552,128]{1,0:T(8,128)(2,1)S(1)}, u32[]{:S(2)}, u32[]{:S(2)}) %collective-permute-start.3) | collective-permute-done | bytes 397344 | tf_op jit(solution)/shard_map/ppermute | solution.py:333
  31.3 2.6 %collective-permute-start.5 = (bf16[128,512]{1,0:T(8,128)(2,1)S(1)}, bf16[128,512]{1,0:T(8,128)(2,1)S(1)}, u32[]{:S(2)}, u32[]{:S(2)}) collective-permute-start(bf16[128,512]{1,0:T(8,128)(2,1)S(1)} %shard_map.174.refs_0_.refs_7_.refs_11_), channel_id=1, source_target_pairs={{0,8},{4,12},{8,0},{12,4},{1,9},{5,13},{9,1},{13,5},{2,10},{6,14},... | collective-permute-start | bytes 393224 | tf_op jit(solution)/shard_map/ppermute | solution.py:336
  34.2 3.6 %collective-permute-start.6 = (bf16[128,512]{1,0:T(8,128)(2,1)S(1)}, bf16[128,512]{1,0:T(8,128)(2,1)S(1)}, u32[]{:S(2)}, u32[]{:S(2)}) collective-permute-start(bf16[128,512]{1,0:T(8,128)(2,1)S(1)} %shard_map.174.refs_0_.refs_7_.refs_11_), channel_id=1, source_target_pairs={{0,12},{4,0},{8,4},{12,8},{1,13},{5,1},{9,5},{13,9},{2,14},{6,2},{... | collective-permute-start | bytes 393224 | tf_op jit(solution)/shard_map/ppermute | solution.py:336
  39.5 2.1 %collective-permute-done.5.refs_2_ = bf16[128,512]{1,0:T(8,128)(2,1)S(1)} collective-permute-done((bf16[128,512]{1,0:T(8,128)(2,1)S(1)}, bf16[128,512]{1,0:T(8,128)(2,1)S(1)}, u32[]{:S(2)}, u32[]{:S(2)}) %collective-permute-start.5) | collective-permute-done | bytes 131104 | tf_op jit(solution)/shard_map/ppermute | solution.py:336
  42.6 2.9 %collective-permute-start.17 = (s32[4,1152]{1,0:T(4,128)S(1)}, s32[4,1152]{1,0:T(4,128)S(1)}, u32[]{:S(2)}, u32[]{:S(2)}) collective-permute-start(s32[4,1152]{1,0:T(4,128)S(1)} %pad_add_fusion.refs_0_), channel_id=1, source_target_pairs={{0,4},{4,8},{8,12},{12,0},{1,5},{5,9},{9,13},{13,1},{2,6},{6,10},{... | collective-permute-start | bytes 55304 | tf_op jit(solution)/shard_map/ppermute | solution.py:336
  45.5 2.8 %collective-permute-done.17.refs_1_ = s32[4,1152]{1,0:T(4,128)S(1)} collective-permute-done((s32[4,1152]{1,0:T(4,128)S(1)}, s32[4,1152]{1,0:T(4,128)S(1)}, u32[]{:S(2)}, u32[]{:S(2)}) %collective-permute-start.17) | collective-permute-done | bytes 18464 | tf_op jit(solution)/shard_map/ppermute | solution.py:336
  64.0 2.1 %shard_map.179.refs_0_.refs_7_.refs_11_ = bf16[128,512]{1,0:T(8,128)(2,1)S(1)} custom-call(bf16[128,512]{1,0:T(8,128)(2,1)S(1)} %shard_map.174.refs_0_.refs_7_.refs_11_, bf16[128,512]{1,0:T(8,128)(2,1)S(1)} %collective-permute-done.4.refs_1_, bf16[128,512]{1,0:T(8,128)(2,1)S(1)} %collective-permute-done.5.refs_2_, ...), custom_call_target="tpu_custom_call" | custom-call | flops 939524096 | bytes 4194304 | tf_op jit(solution)/shard_map/pallas_call | solution.py:37
  69.3 2.2 %collective-permute-start.22 = (bf16[128,512]{1,0:T(8,128)(2,1)S(1)}, bf16[128,512]{1,0:T(8,128)(2,1)S(1)}, u32[]{:S(2)}, u32[]{:S(2)}) collective-permute-start(bf16[128,512]{1,0:T(8,128)(2,1)S(1)} %shard_map.179.refs_0_.refs_7_.refs_11_), channel_id=1, source_target_pairs={{0,8},{4,12},{8,0},{12,4},{1,9},{5,13},{9,1},{13,5},{2,10},{6,14},... | collective-permute-start | bytes 393224 | tf_op jit(solution)/shard_map/ppermute | solution.py:336
  73.6 3.0 %collective-permute-done.21.refs_1_ = bf16[128,512]{1,0:T(8,128)(2,1)S(1)} collective-permute-done((bf16[128,512]{1,0:T(8,128)(2,1)S(1)}, bf16[128,512]{1,0:T(8,128)(2,1)S(1)}, u32[]{:S(2)}, u32[]{:S(2)}) %collective-permute-start.21) | collective-permute-done | bytes 131104 | tf_op jit(solution)/shard_map/ppermute | solution.py:336
  76.6 4.2 %collective-permute-done.22.refs_2_ = bf16[128,512]{1,0:T(8,128)(2,1)S(1)} collective-permute-done((bf16[128,512]{1,0:T(8,128)(2,1)S(1)}, bf16[128,512]{1,0:T(8,128)(2,1)S(1)}, u32[]{:S(2)}, u32[]{:S(2)}) %collective-permute-start.22) | collective-permute-done | bytes 131104 | tf_op jit(solution)/shard_map/ppermute | solution.py:336
  87.7 2.8 %collective-permute-done.28.refs_2_.refs_6_ = bf16[128,512]{1,0:T(8,128)(2,1)S(1)} collective-permute-done((bf16[128,512]{1,0:T(8,128)(2,1)S(1)}, bf16[128,512]{1,0:T(8,128)(2,1)S(1)}, u32[]{:S(2)}, u32[]{:S(2)}) %collective-permute-start.28) | collective-permute-done | bytes 131104 | tf_op jit(solution)/shard_map/ppermute | solution.py:333
  94.4 2.8 %shard_map.183.refs_0_.refs_7_.refs_11_ = bf16[128,512]{1,0:T(8,128)(2,1)S(1)} custom-call(bf16[128,512]{1,0:T(8,128)(2,1)S(1)} %shard_map.179.refs_0_.refs_7_.refs_11_, bf16[128,512]{1,0:T(8,128)(2,1)S(1)} %collective-permute-done.21.refs_1_, bf16[128,512]{1,0:T(8,128)(2,1)S(1)} %collective-permute-done.22.refs_2_, ...), custom_call_target="tpu_custom_call" | custom-call | flops 1879048192 | bytes 4194304 | tf_op jit(solution)/shard_map/pallas_call | solution.py:37
  99.4 3.1 %collective-permute-start.34 = (bf16[128,512]{1,0:T(8,128)(2,1)S(1)}, bf16[128,512]{1,0:T(8,128)(2,1)S(1)}, u32[]{:S(2)}, u32[]{:S(2)}) collective-permute-start(bf16[128,512]{1,0:T(8,128)(2,1)S(1)} %shard_map.183.refs_0_.refs_7_.refs_11_), channel_id=1, source_target_pairs={{0,4},{4,8},{8,12},{12,0},{1,5},{5,9},{9,13},{13,1},{2,6},{6,10},{... | collective-permute-start | bytes 393224 | tf_op jit(solution)/shard_map/ppermute | solution.py:336
  107.4 4.4 %collective-permute-done.35.refs_2_ = bf16[128,512]{1,0:T(8,128)(2,1)S(1)} collective-permute-done((bf16[128,512]{1,0:T(8,128)(2,1)S(1)}, bf16[128,512]{1,0:T(8,128)(2,1)S(1)}, u32[]{:S(2)}, u32[]{:S(2)}) %collective-permute-start.35) | collective-permute-done | bytes 131104 | tf_op jit(solution)/shard_map/ppermute | solution.py:336
  119.0 2.5 %collective-permute-done.41.refs_2_.refs_6_ = bf16[128,512]{1,0:T(8,128)(2,1)S(1)} collective-permute-done((bf16[128,512]{1,0:T(8,128)(2,1)S(1)}, bf16[128,512]{1,0:T(8,128)(2,1)S(1)}, u32[]{:S(2)}, u32[]{:S(2)}) %collective-permute-start.41) | collective-permute-done | bytes 131104 | tf_op jit(solution)/shard_map/ppermute | solution.py:333
  125.5 2.8 %shard_map.187.refs_0_ = bf16[128,512]{1,0:T(8,128)(2,1)S(1)} custom-call(bf16[128,512]{1,0:T(8,128)(2,1)S(1)} %shard_map.183.refs_0_.refs_7_.refs_11_, bf16[128,512]{1,0:T(8,128)(2,1)S(1)} %collective-permute-done.34.refs_1_, bf16[128,512]{1,0:T(8,128)(2,1)S(1)} %collective-permute-done.35.refs_2_, bf16[128,512]{1,0:T(8,128)(2,1)S(1)} %collective-permute-done.36.refs_3_, ...), custom_call_target="tpu_custom_call" | custom-call | flops 1879048192 | bytes 4194304 | tf_op jit(solution)/shard_map/pallas_call | solution.py:37
  129.0 3.2 %collective-permute-start.47 = (bf16[128,512]{1,0:T(8,128)(2,1)S(1)}, bf16[128,512]{1,0:T(8,128)(2,1)S(1)}, u32[]{:S(2)}, u32[]{:S(2)}) collective-permute-start(bf16[128,512]{1,0:T(8,128)(2,1)S(1)} %shard_map.187.refs_0_), channel_id=1, source_target_pairs={{0,4},{4,8},{8,12},{12,0},{1,5},{5,9},{9,13},{13,1},{2,6},{6,10},{... | collective-permute-start | bytes 393224 | tf_op jit(solution)/shard_map/ppermute | solution.py:336
  138.0 4.8 %collective-permute-done.48.refs_2_ = bf16[128,512]{1,0:T(8,128)(2,1)S(1)} collective-permute-done((bf16[128,512]{1,0:T(8,128)(2,1)S(1)}, bf16[128,512]{1,0:T(8,128)(2,1)S(1)}, u32[]{:S(2)}, u32[]{:S(2)}) %collective-permute-start.48) | collective-permute-done | bytes 131104 | tf_op jit(solution)/shard_map/ppermute | solution.py:336
  149.8 2.8 %collective-permute-done.53.refs_2_.refs_6_ = bf16[128,512]{1,0:T(8,128)(2,1)S(1)} collective-permute-done((bf16[128,512]{1,0:T(8,128)(2,1)S(1)}, bf16[128,512]{1,0:T(8,128)(2,1)S(1)}, u32[]{:S(2)}, u32[]{:S(2)}) %collective-permute-start.53) | collective-permute-done | bytes 131104 | tf_op jit(solution)/shard_map/ppermute | solution.py:333
  156.6 3.3 %shard_map.191 = f32[227,128]{1,0:T(8,128)} custom-call(bf16[128,512]{1,0:T(8,128)(2,1)S(1)} %shard_map.187.refs_0_, bf16[128,512]{1,0:T(8,128)(2,1)S(1)} %collective-permute-done.47.refs_1_, bf16[128,512]{1,0:T(8,128)(2,1)S(1)} %collective-permute-done.48.refs_2_, bf16[128,512]{1,0:T(8,128)(2,1)S(1)} %collective-permute-done.49.refs_3_, ...), custom_call_target="tpu_custom_call" | custom-call | flops 1409286144 | bytes 4194304 | tf_op jit(solution)/shard_map/pallas_call | solution.py:37
  (149 shorter events, 78.2 us)
Async XLA Ops:
  5.1 10.2 %collective-permute-start = (bf16[768,128]{1,0:T(8,128)(2,1)}, bf16[768,128]{1,0:T(8,128)(2,1)S(1)}, u32[]{:S(2)}, u32[]{:S(2)}) collective-permute-start(bf16[768,128]{1,0:T(8,128)(2,1)} %get-tuple-element.101.out_ref), channel_id=1, source_target_pairs={{0,2},{1,3},{2,0},{3,1},{4,6},{5,7},{6,4},{7,5},{8,10},{9,11},{10,... | collective-permute-start | bytes 589832 | tf_op jit(solution)/shard_map/ppermute | solution.py:333
  15.4 42.8 %collective-permute-start.14 = (bf16[8,1552,128]{2,1,0:T(8,128)(2,1)}, bf16[8,1552,128]{2,1,0:T(8,128)(2,1)S(1)}, u32[]{:S(2)}, u32[]{:S(2)}) collective-permute-start(bf16[8,1552,128]{2,1,0:T(8,128)(2,1)} %get-tuple-element.116.refs_1_), channel_id=1, source_target_pairs={{0,1},{1,0},{2,3},{3,2},{4,5},{5,4},{6,7},{7,6},{8,9},{9,8},{10,11... | collective-permute-start | bytes 9535496 | tf_op jit(solution)/shard_map/ppermute | solution.py:333
  15.6 11.7 %collective-permute-start.3 = (bf16[1552,128]{1,0:T(8,128)(2,1)}, bf16[1552,128]{1,0:T(8,128)(2,1)S(1)}, u32[]{:S(2)}, u32[]{:S(2)}) collective-permute-start(bf16[1552,128]{1,0:T(8,128)(2,1)} %get-tuple-element.105), channel_id=1, source_target_pairs={{0,2},{1,3},{2,0},{3,1},{4,6},{5,7},{6,4},{7,5},{8,10},{9,11},{10,... | collective-permute-start | bytes 1191944 | tf_op jit(solution)/shard_map/ppermute | solution.py:333
  27.7 14.4 %collective-permute-start.9 = (bf16[1552,128]{1,0:T(8,128)(2,1)S(1)}, bf16[1552,128]{1,0:T(8,128)(2,1)S(1)}, u32[]{:S(2)}, u32[]{:S(2)}) collective-permute-start(bf16[1552,128]{1,0:T(8,128)(2,1)S(1)} %collective-permute-done.3.refs_3_), channel_id=1, source_target_pairs={{0,16},{16,0},{1,17},{17,1},{2,18},{18,2},{3,19},{19,3},{4,20},{20... | collective-permute-start | bytes 1191944 | tf_op jit(solution)/shard_map/ppermute | solution.py:436
  31.3 10.4 %collective-permute-start.5 = (bf16[128,512]{1,0:T(8,128)(2,1)S(1)}, bf16[128,512]{1,0:T(8,128)(2,1)S(1)}, u32[]{:S(2)}, u32[]{:S(2)}) collective-permute-start(bf16[128,512]{1,0:T(8,128)(2,1)S(1)} %shard_map.174.refs_0_.refs_7_.refs_11_), channel_id=1, source_target_pairs={{0,8},{4,12},{8,0},{12,4},{1,9},{5,13},{9,1},{13,5},{2,10},{6,14},... | collective-permute-start | bytes 393224 | tf_op jit(solution)/shard_map/ppermute | solution.py:336
  37.8 11.8 %collective-permute-start.10 = (bf16[1552,128]{1,0:T(8,128)(2,1)}, bf16[1552,128]{1,0:T(8,128)(2,1)S(1)}, u32[]{:S(2)}, u32[]{:S(2)}) collective-permute-start(bf16[1552,128]{1,0:T(8,128)(2,1)} %get-tuple-element.112), channel_id=1, source_target_pairs={{0,2},{1,3},{2,0},{3,1},{4,6},{5,7},{6,4},{7,5},{8,10},{9,11},{10,... | collective-permute-start | bytes 1191944 | tf_op jit(solution)/shard_map/ppermute | solution.py:333
  42.1 12.9 %collective-permute-start.15 = (bf16[1552,128]{1,0:T(8,128)(2,1)S(1)}, bf16[1552,128]{1,0:T(8,128)(2,1)S(1)}, u32[]{:S(2)}, u32[]{:S(2)}) collective-permute-start(bf16[1552,128]{1,0:T(8,128)(2,1)S(1)} %collective-permute-done.3.refs_3_), channel_id=1, source_target_pairs={{0,1},{1,0},{2,3},{3,2},{4,5},{5,4},{6,7},{7,6},{8,9},{9,8},{10,11... | collective-permute-start | bytes 1191944 | tf_op jit(solution)/shard_map/ppermute | solution.py:333
  42.1 15.9 %collective-permute-start.16 = (bf16[1552,128]{1,0:T(8,128)(2,1)S(1)}, bf16[1552,128]{1,0:T(8,128)(2,1)S(1)}, u32[]{:S(2)}, u32[]{:S(2)}) collective-permute-start(bf16[1552,128]{1,0:T(8,128)(2,1)S(1)} %collective-permute-done.9.refs_4_), channel_id=1, source_target_pairs={{0,1},{1,0},{2,3},{3,2},{4,5},{5,4},{6,7},{7,6},{8,9},{9,8},{10,11... | collective-permute-start | bytes 1191944 | tf_op jit(solution)/shard_map/ppermute | solution.py:333
  52.9 8.8 %collective-permute-start.8 = (bf16[128,512]{1,0:T(8,128)(2,1)S(1)}, bf16[128,512]{1,0:T(8,128)(2,1)S(1)}, u32[]{:S(2)}, u32[]{:S(2)}) collective-permute-start(bf16[128,512]{1,0:T(8,128)(2,1)S(1)} %collective-permute-done.4.refs_1_), channel_id=1, source_target_pairs={{0,2},{1,3},{2,0},{3,1},{4,6},{5,7},{6,4},{7,5},{8,10},{9,11},{10,... | collective-permute-start | bytes 393224 | tf_op jit(solution)/shard_map/ppermute | solution.py:333
  66.1 14.7 %collective-permute-start.26 = (bf16[1552,128]{1,0:T(8,128)(2,1)S(1)}, bf16[1552,128]{1,0:T(8,128)(2,1)S(1)}, u32[]{:S(2)}, u32[]{:S(2)}) collective-permute-start(bf16[1552,128]{1,0:T(8,128)(2,1)S(1)} %collective-permute-done.10.refs_3_), channel_id=1, source_target_pairs={{0,16},{16,0},{1,17},{17,1},{2,18},{18,2},{3,19},{19,3},{4,20},{20... | collective-permute-start | bytes 1191944 | tf_op jit(solution)/shard_map/ppermute | solution.py:436
  68.3 8.3 %collective-permute-start.21 = (bf16[128,512]{1,0:T(8,128)(2,1)S(1)}, bf16[128,512]{1,0:T(8,128)(2,1)S(1)}, u32[]{:S(2)}, u32[]{:S(2)}) collective-permute-start(bf16[128,512]{1,0:T(8,128)(2,1)S(1)} %shard_map.179.refs_0_.refs_7_.refs_11_), channel_id=1, source_target_pairs={{0,4},{4,8},{8,12},{12,0},{1,5},{5,9},{9,13},{13,1},{2,6},{6,10},{... | collective-permute-start | bytes 393224 | tf_op jit(solution)/shard_map/ppermute | solution.py:336
  69.3 11.5 %collective-permute-start.22 = (bf16[128,512]{1,0:T(8,128)(2,1)S(1)}, bf16[128,512]{1,0:T(8,128)(2,1)S(1)}, u32[]{:S(2)}, u32[]{:S(2)}) collective-permute-start(bf16[128,512]{1,0:T(8,128)(2,1)S(1)} %shard_map.179.refs_0_.refs_7_.refs_11_), channel_id=1, source_target_pairs={{0,8},{4,12},{8,0},{12,4},{1,9},{5,13},{9,1},{13,5},{2,10},{6,14},... | collective-permute-start | bytes 393224 | tf_op jit(solution)/shard_map/ppermute | solution.py:336
  71.6 9.2 %collective-permute-start.23 = (bf16[128,512]{1,0:T(8,128)(2,1)S(1)}, bf16[128,512]{1,0:T(8,128)(2,1)S(1)}, u32[]{:S(2)}, u32[]{:S(2)}) collective-permute-start(bf16[128,512]{1,0:T(8,128)(2,1)S(1)} %shard_map.179.refs_0_.refs_7_.refs_11_), channel_id=1, source_target_pairs={{0,12},{4,0},{8,4},{12,8},{1,13},{5,1},{9,5},{13,9},{2,14},{6,2},{... | collective-permute-start | bytes 393224 | tf_op jit(solution)/shard_map/ppermute | solution.py:336
  72.2 10.2 %collective-permute-start.27 = (bf16[1552,128]{1,0:T(8,128)(2,1)S(1)}, bf16[1552,128]{1,0:T(8,128)(2,1)S(1)}, u32[]{:S(2)}, u32[]{:S(2)}) collective-permute-start(bf16[1552,128]{1,0:T(8,128)(2,1)S(1)} %copy-done.15), channel_id=1, source_target_pairs={{0,2},{1,3},{2,0},{3,1},{4,6},{5,7},{6,4},{7,5},{8,10},{9,11},{10,... | collective-permute-start | bytes 1191944 | tf_op jit(solution)/shard_map/ppermute | solution.py:333
  83.6 8.8 %collective-permute-start.29 = (bf16[128,512]{1,0:T(8,128)(2,1)S(1)}, bf16[128,512]{1,0:T(8,128)(2,1)S(1)}, u32[]{:S(2)}, u32[]{:S(2)}) collective-permute-start(bf16[128,512]{1,0:T(8,128)(2,1)S(1)} %collective-permute-done.23.refs_3_), channel_id=1, source_target_pairs={{0,2},{1,3},{2,0},{3,1},{4,6},{5,7},{6,4},{7,5},{8,10},{9,11},{10,... | collective-permute-start | bytes 393224 | tf_op jit(solution)/shard_map/ppermute | solution.py:333
  97.3 14.6 %collective-permute-start.39 = (bf16[1552,128]{1,0:T(8,128)(2,1)S(1)}, bf16[1552,128]{1,0:T(8,128)(2,1)S(1)}, u32[]{:S(2)}, u32[]{:S(2)}) collective-permute-start(bf16[1552,128]{1,0:T(8,128)(2,1)S(1)} %collective-permute-done.27.refs_3_), channel_id=1, source_target_pairs={{0,16},{16,0},{1,17},{17,1},{2,18},{18,2},{3,19},{19,3},{4,20},{20... | collective-permute-start | bytes 1191944 | tf_op jit(solution)/shard_map/ppermute | solution.py:436
  102.5 9.4 %collective-permute-start.35 = (bf16[128,512]{1,0:T(8,128)(2,1)S(1)}, bf16[128,512]{1,0:T(8,128)(2,1)S(1)}, u32[]{:S(2)}, u32[]{:S(2)}) collective-permute-start(bf16[128,512]{1,0:T(8,128)(2,1)S(1)} %shard_map.183.refs_0_.refs_7_.refs_11_), channel_id=1, source_target_pairs={{0,8},{4,12},{8,0},{12,4},{1,9},{5,13},{9,1},{13,5},{2,10},{6,14},... | collective-permute-start | bytes 393224 | tf_op jit(solution)/shard_map/ppermute | solution.py:336
  103.0 8.9 %collective-permute-start.36 = (bf16[128,512]{1,0:T(8,128)(2,1)S(1)}, bf16[128,512]{1,0:T(8,128)(2,1)S(1)}, u32[]{:S(2)}, u32[]{:S(2)}) collective-permute-start(bf16[128,512]{1,0:T(8,128)(2,1)S(1)} %shard_map.183.refs_0_.refs_7_.refs_11_), channel_id=1, source_target_pairs={{0,12},{4,0},{8,4},{12,8},{1,13},{5,1},{9,5},{13,9},{2,14},{6,2},{... | collective-permute-start | bytes 393224 | tf_op jit(solution)/shard_map/ppermute | solution.py:336
  104.8 10.1 %collective-permute-start.40 = (bf16[1552,128]{1,0:T(8,128)(2,1)S(1)}, bf16[1552,128]{1,0:T(8,128)(2,1)S(1)}, u32[]{:S(2)}, u32[]{:S(2)}) collective-permute-start(bf16[1552,128]{1,0:T(8,128)(2,1)S(1)} %copy-done.14), channel_id=1, source_target_pairs={{0,2},{1,3},{2,0},{3,1},{4,6},{5,7},{6,4},{7,5},{8,10},{9,11},{10,... | collective-permute-start | bytes 1191944 | tf_op jit(solution)/shard_map/ppermute | solution.py:333
  128.3 14.5 %collective-permute-start.52 = (bf16[1552,128]{1,0:T(8,128)(2,1)S(1)}, bf16[1552,128]{1,0:T(8,128)(2,1)S(1)}, u32[]{:S(2)}, u32[]{:S(2)}) collective-permute-start(bf16[1552,128]{1,0:T(8,128)(2,1)S(1)} %collective-permute-done.40.refs_3_), channel_id=1, source_target_pairs={{0,16},{16,0},{1,17},{17,1},{2,18},{18,2},{3,19},{19,3},{4,20},{20... | collective-permute-start | bytes 1191944 | tf_op jit(solution)/shard_map/ppermute | solution.py:436
  129.0 9.0 %collective-permute-start.47 = (bf16[128,512]{1,0:T(8,128)(2,1)S(1)}, bf16[128,512]{1,0:T(8,128)(2,1)S(1)}, u32[]{:S(2)}, u32[]{:S(2)}) collective-permute-start(bf16[128,512]{1,0:T(8,128)(2,1)S(1)} %shard_map.187.refs_0_), channel_id=1, source_target_pairs={{0,4},{4,8},{8,12},{12,0},{1,5},{5,9},{9,13},{13,1},{2,6},{6,10},{... | collective-permute-start | bytes 393224 | tf_op jit(solution)/shard_map/ppermute | solution.py:336
  132.2 10.6 %collective-permute-start.48 = (bf16[128,512]{1,0:T(8,128)(2,1)S(1)}, bf16[128,512]{1,0:T(8,128)(2,1)S(1)}, u32[]{:S(2)}, u32[]{:S(2)}) collective-permute-start(bf16[128,512]{1,0:T(8,128)(2,1)S(1)} %shard_map.187.refs_0_), channel_id=1, source_target_pairs={{0,8},{4,12},{8,0},{12,4},{1,9},{5,13},{9,1},{13,5},{2,10},{6,14},... | collective-permute-start | bytes 393224 | tf_op jit(solution)/shard_map/ppermute | solution.py:336
  134.2 8.7 %collective-permute-start.49 = (bf16[128,512]{1,0:T(8,128)(2,1)S(1)}, bf16[128,512]{1,0:T(8,128)(2,1)S(1)}, u32[]{:S(2)}, u32[]{:S(2)}) collective-permute-start(bf16[128,512]{1,0:T(8,128)(2,1)S(1)} %shard_map.187.refs_0_), channel_id=1, source_target_pairs={{0,12},{4,0},{8,4},{12,8},{1,13},{5,1},{9,5},{13,9},{2,14},{6,2},{... | collective-permute-start | bytes 393224 | tf_op jit(solution)/shard_map/ppermute | solution.py:336
  145.5 9.1 %collective-permute-start.54 = (bf16[128,512]{1,0:T(8,128)(2,1)S(1)}, bf16[128,512]{1,0:T(8,128)(2,1)S(1)}, u32[]{:S(2)}, u32[]{:S(2)}) collective-permute-start(bf16[128,512]{1,0:T(8,128)(2,1)S(1)} %collective-permute-done.49.refs_3_), channel_id=1, source_target_pairs={{0,2},{1,3},{2,0},{3,1},{4,6},{5,7},{6,4},{7,5},{8,10},{9,11},{10,... | collective-permute-start | bytes 393224 | tf_op jit(solution)/shard_map/ppermute | solution.py:333
  (51 other events, 727.4 us)

commit v12 on v11

--- a/solution.py
+++ b/solution.py
@@ -423,8 +423,7 @@
         return swap(first, bits[0])
 
     first = cross(0, nearby)
-    swapped = swap(held(packed, met), bits[1])
-    received, first = lax.optimization_barrier((received, first))
+    received, _ = lax.optimization_barrier((received, place_after))
     grid = kernel_call(
         functools.partial(embed_finish, embed_id),
         jax.ShapeDtypeStruct((grid_rows, latent), BF16),
@@ -434,6 +433,8 @@
     def over(first, after):
         first, _ = lax.optimization_barrier((first, after))
         return lax.ppermute(first, "parts", [(0, 1), (1, 0)])
+
+    swapped = swap(held(packed, grid), bits[1])
 
     def share(first, second, after):
         first, second, _ = lax.optimization_barrier((first, second, after))
@@ -469,8 +470,10 @@
 
     def window(group_id, rows, first):
         opening = swap(rows, bits[0]) if direct else rows
-        second = over(first, rows)
+        second = over(first, rows) if group_id > 0 else None
         parts, following = spread(rows, opening, second, group_id + 1)
+        if second is None:
+            second = over(first, tuple(parts[: len(parts) // 2]))
         near = tuple(parts[: len(parts) // 2])
         after = near if following is not None else (near, opening)
         return parts, share(first, second, after), following

time: 161 us -> 167 us (1.037)
  waiting for transfers between devices: 65.2 us -> 73.8 us
  starting transfers between devices: 61.2 us -> 58.4 us
    ppermute x15, waiting for transfers between devices: 26.5 us -> 31.4 us  [shift(): lax.ppermute(value, 'band', [(b, (b + step) % bands) for b in range(bands)])]
    ppermute x4, waiting for transfers between devices: 0.01 us -> 4.03 us  [over(): return lax.ppermute(first, 'parts', [(0, 1), (1, 0)])]
    ppermute x40, starting transfers between devices: 28 us -> 25.1 us  [swap(): return lax.ppermute(value, 'feat', [(f, f ^ bit) for f in range(quarters)])]
  transfers between devices with their start and end apart: 59 -> 59, of which waited for: 29 -> 31; matrix products, arithmetic and copies ran while one was open for 0% -> 0% of each run, Pallas kernels for 9% -> 9%
where the time goes in v12:
time: 167 us; the launch traced here: 166 us
  waiting for transfers between devices  73.8 us (44%)
  starting transfers between devices  58.4 us (35%)
  Pallas kernels  29.1 us (17%)
  local copies, waits for them, and re-layouts  2.67 us (2%)
    ppermute x40, waiting for transfers between devices, swap(): return lax.ppermute(value, 'feat', [(f, f ^ bit) for f in range(quarters)])  38.3 us
    ppermute x15, waiting for transfers between devices, shift(): lax.ppermute(value, 'band', [(b, (b + step) % bands) for b in range(bands)])  31.4 us
    pallas_call x20, Pallas kernels, kernel_call(): pl.pallas_call(body, out_shape=out_shape, in_specs=[pl.BlockSpec(memory_s...  29.1 us
    ppermute x15, starting transfers between devices, shift(): lax.ppermute(value, 'band', [(b, (b + step) % bands) for b in range(bands)])  28.2 us
    ppermute x40, starting transfers between devices, swap(): return lax.ppermute(value, 'feat', [(f, f ^ bit) for f in range(quarters)])  25.1 us
    ppermute x4, starting transfers between devices, over(): return lax.ppermute(first, 'parts', [(0, 1), (1, 0)])  5.08 us
    ppermute x4, waiting for transfers between devices, over(): return lax.ppermute(first, 'parts', [(0, 1), (1, 0)])  4.03 us
  transfers between devices with their start and end apart: 59, of which 31 were waited for; matrix products, arithmetic and copies ran while one was open for 0% of the time, Pallas kernels for 9%

profile of v12, /device:TPU:0, one launch (start us, length us, event | category | flops | bytes accessed | tf_op | source)
XLA Modules:
  0.0 165.7 jit_solution(2189138615464427615)
XLA Ops:
  2.1 3.0 %shard_map.172 = (bf16[128,128]{1,0:T(8,128)(2,1)}, bf16[768,128]{1,0:T(8,128)(2,1)}, bf16[640,128]{1,0:T(8,128)(2,1)}) custom-call(s32[3]{0:T(128)} %pad_add_fusion.1.place_ref.refs_0_, bf16[474,512]{1,0:T(8,128)(2,1)} %bitcast.18, bf16[474,128]{1,0:T(8,128)(2,1)} %w_hbm.1, bf16[9,128,512]{2,1,0:T(8,128)(2,1)} %out_ref.1, f32[9,128]{1,0:T(8,128)} %bias_ref.3), custom_call_target="tpu_custom_call" | custom-call | bytes 4194304 | tf_op jit(solution)/shard_map/pallas_call | solution.py:37
  5.1 3.0 %collective-permute-start = (bf16[768,128]{1,0:T(8,128)(2,1)}, bf16[768,128]{1,0:T(8,128)(2,1)S(1)}, u32[]{:S(2)}, u32[]{:S(2)}) collective-permute-start(bf16[768,128]{1,0:T(8,128)(2,1)} %get-tuple-element.100.out_ref), channel_id=1, source_target_pairs={{0,2},{1,3},{2,0},{3,1},{4,6},{5,7},{6,4},{7,5},{8,10},{9,11},{10,... | collective-permute-start | bytes 589832 | tf_op jit(solution)/shard_map/ppermute | solution.py:333
  8.2 5.1 %collective-permute-done.across = bf16[768,128]{1,0:T(8,128)(2,1)S(1)} collective-permute-done((bf16[768,128]{1,0:T(8,128)(2,1)}, bf16[768,128]{1,0:T(8,128)(2,1)S(1)}, u32[]{:S(2)}, u32[]{:S(2)}) %collective-permute-start) | collective-permute-done | bytes 196640 | tf_op jit(solution)/shard_map/ppermute | solution.py:333
  15.1 5.6 %shard_map.174 = (bf16[8,1552,128]{2,1,0:T(8,128)(2,1)}, bf16[1552,128]{1,0:T(8,128)(2,1)}, bf16[1552,128]{1,0:T(8,128)(2,1)}, bf16[1552,128]{1,0:T(8,128)(2,1)}, bf16[1552,128]{1,0:T(8,128)(2,1)}) custom-call(s32[3]{0:T(128)} %pad_add_fusion.1.place_ref.refs_0_, bf16[8,1024,128]{2,1,0:T(8,128)(2,1)} %in_hbm.1, bf16[9,128,512]{2,1,0:T(8,128)(2,1)} %out_ref.1, ...), custom_call_target="tpu_custom_call" | custom-call | bytes 4194304 | tf_op jit(solution)/shard_map/pallas_call | solution.py:37
  24.8 2.6 %collective-permute-start.4 = (bf16[128,512]{1,0:T(8,128)(2,1)S(1)}, bf16[128,512]{1,0:T(8,128)(2,1)S(1)}, u32[]{:S(2)}, u32[]{:S(2)}) collective-permute-start(bf16[128,512]{1,0:T(8,128)(2,1)S(1)} %shard_map.173.refs_0_.refs_7_.refs_11_), channel_id=1, source_target_pairs={{0,8},{4,12},{8,0},{12,4},{1,9},{5,13},{9,1},{13,5},{2,10},{6,14},... | collective-permute-start | bytes 393224 | tf_op jit(solution)/shard_map/ppermute | solution.py:336
  28.8 2.7 %collective-permute-done.3.refs_1_ = bf16[128,512]{1,0:T(8,128)(2,1)S(1)} collective-permute-done((bf16[128,512]{1,0:T(8,128)(2,1)S(1)}, bf16[128,512]{1,0:T(8,128)(2,1)S(1)}, u32[]{:S(2)}, u32[]{:S(2)}) %collective-permute-start.3) | collective-permute-done | bytes 131104 | tf_op jit(solution)/shard_map/ppermute | solution.py:336
  31.5 4.7 %collective-permute-done.4.refs_2_ = bf16[128,512]{1,0:T(8,128)(2,1)S(1)} collective-permute-done((bf16[128,512]{1,0:T(8,128)(2,1)S(1)}, bf16[128,512]{1,0:T(8,128)(2,1)S(1)}, u32[]{:S(2)}, u32[]{:S(2)}) %collective-permute-start.4) | collective-permute-done | bytes 131104 | tf_op jit(solution)/shard_map/ppermute | solution.py:336
  38.2 4.5 %collective-permute-done.6.refs_0_.refs_4_ = bf16[128,512]{1,0:T(8,128)(2,1)S(1)} collective-permute-done((bf16[128,512]{1,0:T(8,128)(2,1)S(1)}, bf16[128,512]{1,0:T(8,128)(2,1)S(1)}, u32[]{:S(2)}, u32[]{:S(2)}) %collective-permute-start.6) | collective-permute-done | bytes 131104 | tf_op jit(solution)/shard_map/ppermute | solution.py:333
  43.2 4.0 %collective-permute-done.14.refs_4_ = bf16[1552,128]{1,0:T(8,128)(2,1)S(1)} collective-permute-done((bf16[1552,128]{1,0:T(8,128)(2,1)S(1)}, bf16[1552,128]{1,0:T(8,128)(2,1)S(1)}, u32[]{:S(2)}, u32[]{:S(2)}) %collective-permute-start.14) | collective-permute-done | bytes 397344 | tf_op jit(solution)/shard_map/ppermute | solution.py:435
  47.8 3.4 %collective-permute-start.17 = (s32[4,1152]{1,0:T(4,128)S(1)}, s32[4,1152]{1,0:T(4,128)S(1)}, u32[]{:S(2)}, u32[]{:S(2)}) collective-permute-start(s32[4,1152]{1,0:T(4,128)S(1)} %pad_add_fusion.refs_0_), channel_id=1, source_target_pairs={{0,4},{4,8},{8,12},{12,0},{1,5},{5,9},{9,13},{13,1},{2,6},{6,10},{... | collective-permute-start | bytes 55304 | tf_op jit(solution)/shard_map/ppermute | solution.py:336
  54.3 2.9 %collective-permute-start.19 = (s32[4,1152]{1,0:T(4,128)S(1)}, s32[4,1152]{1,0:T(4,128)S(1)}, u32[]{:S(2)}, u32[]{:S(2)}) collective-permute-start(s32[4,1152]{1,0:T(4,128)S(1)} %pad_add_fusion.refs_0_), channel_id=1, source_target_pairs={{0,12},{4,0},{8,4},{12,8},{1,13},{5,1},{9,5},{13,9},{2,14},{6,2},{... | collective-permute-start | bytes 55304 | tf_op jit(solution)/shard_map/ppermute | solution.py:336
  78.8 2.5 %collective-permute-done.21.refs_1_ = bf16[128,512]{1,0:T(8,128)(2,1)S(1)} collective-permute-done((bf16[128,512]{1,0:T(8,128)(2,1)S(1)}, bf16[128,512]{1,0:T(8,128)(2,1)S(1)}, u32[]{:S(2)}, u32[]{:S(2)}) %collective-permute-start.21) | collective-permute-done | bytes 131104 | tf_op jit(solution)/shard_map/ppermute | solution.py:336
  81.4 4.4 %collective-permute-done.22.refs_2_ = bf16[128,512]{1,0:T(8,128)(2,1)S(1)} collective-permute-done((bf16[128,512]{1,0:T(8,128)(2,1)S(1)}, bf16[128,512]{1,0:T(8,128)(2,1)S(1)}, u32[]{:S(2)}, u32[]{:S(2)}) %collective-permute-start.22) | collective-permute-done | bytes 131104 | tf_op jit(solution)/shard_map/ppermute | solution.py:336
  92.7 2.8 %collective-permute-done.28.refs_2_.refs_6_ = bf16[128,512]{1,0:T(8,128)(2,1)S(1)} collective-permute-done((bf16[128,512]{1,0:T(8,128)(2,1)S(1)}, bf16[128,512]{1,0:T(8,128)(2,1)S(1)}, u32[]{:S(2)}, u32[]{:S(2)}) %collective-permute-start.28) | collective-permute-done | bytes 131104 | tf_op jit(solution)/shard_map/ppermute | solution.py:333
  99.4 2.8 %shard_map.183.refs_0_.refs_7_.refs_11_ = bf16[128,512]{1,0:T(8,128)(2,1)S(1)} custom-call(bf16[128,512]{1,0:T(8,128)(2,1)S(1)} %shard_map.179.refs_0_.refs_7_.refs_11_, bf16[128,512]{1,0:T(8,128)(2,1)S(1)} %collective-permute-done.21.refs_1_, bf16[128,512]{1,0:T(8,128)(2,1)S(1)} %collective-permute-done.22.refs_2_, ...), custom_call_target="tpu_custom_call" | custom-call | flops 1879048192 | bytes 4194304 | tf_op jit(solution)/shard_map/pallas_call | solution.py:37
  104.2 3.2 %collective-permute-start.34 = (bf16[128,512]{1,0:T(8,128)(2,1)S(1)}, bf16[128,512]{1,0:T(8,128)(2,1)S(1)}, u32[]{:S(2)}, u32[]{:S(2)}) collective-permute-start(bf16[128,512]{1,0:T(8,128)(2,1)S(1)} %shard_map.183.refs_0_.refs_7_.refs_11_), channel_id=1, source_target_pairs={{0,4},{4,8},{8,12},{12,0},{1,5},{5,9},{9,13},{13,1},{2,6},{6,10},{... | collective-permute-start | bytes 393224 | tf_op jit(solution)/shard_map/ppermute | solution.py:336
  112.3 4.5 %collective-permute-done.35.refs_2_ = bf16[128,512]{1,0:T(8,128)(2,1)S(1)} collective-permute-done((bf16[128,512]{1,0:T(8,128)(2,1)S(1)}, bf16[128,512]{1,0:T(8,128)(2,1)S(1)}, u32[]{:S(2)}, u32[]{:S(2)}) %collective-permute-start.35) | collective-permute-done | bytes 131104 | tf_op jit(solution)/shard_map/ppermute | solution.py:336
  124.0 2.4 %collective-permute-done.41.refs_2_.refs_6_ = bf16[128,512]{1,0:T(8,128)(2,1)S(1)} collective-permute-done((bf16[128,512]{1,0:T(8,128)(2,1)S(1)}, bf16[128,512]{1,0:T(8,128)(2,1)S(1)}, u32[]{:S(2)}, u32[]{:S(2)}) %collective-permute-start.41) | collective-permute-done | bytes 131104 | tf_op jit(solution)/shard_map/ppermute | solution.py:333
  130.4 2.8 %shard_map.187.refs_0_ = bf16[128,512]{1,0:T(8,128)(2,1)S(1)} custom-call(bf16[128,512]{1,0:T(8,128)(2,1)S(1)} %shard_map.183.refs_0_.refs_7_.refs_11_, bf16[128,512]{1,0:T(8,128)(2,1)S(1)} %collective-permute-done.34.refs_1_, bf16[128,512]{1,0:T(8,128)(2,1)S(1)} %collective-permute-done.35.refs_2_, bf16[128,512]{1,0:T(8,128)(2,1)S(1)} %collective-permute-done.36.refs_3_, ...), custom_call_target="tpu_custom_call" | custom-call | flops 1879048192 | bytes 4194304 | tf_op jit(solution)/shard_map/pallas_call | solution.py:37
  134.7 3.2 %collective-permute-start.47 = (bf16[128,512]{1,0:T(8,128)(2,1)S(1)}, bf16[128,512]{1,0:T(8,128)(2,1)S(1)}, u32[]{:S(2)}, u32[]{:S(2)}) collective-permute-start(bf16[128,512]{1,0:T(8,128)(2,1)S(1)} %shard_map.187.refs_0_), channel_id=1, source_target_pairs={{0,4},{4,8},{8,12},{12,0},{1,5},{5,9},{9,13},{13,1},{2,6},{6,10},{... | collective-permute-start | bytes 393224 | tf_op jit(solution)/shard_map/ppermute | solution.py:336
  141.0 2.9 %collective-permute-done.47.refs_1_ = bf16[128,512]{1,0:T(8,128)(2,1)S(1)} collective-permute-done((bf16[128,512]{1,0:T(8,128)(2,1)S(1)}, bf16[128,512]{1,0:T(8,128)(2,1)S(1)}, u32[]{:S(2)}, u32[]{:S(2)}) %collective-permute-start.47) | collective-permute-done | bytes 131104 | tf_op jit(solution)/shard_map/ppermute | solution.py:336
  143.9 4.8 %collective-permute-done.48.refs_2_ = bf16[128,512]{1,0:T(8,128)(2,1)S(1)} collective-permute-done((bf16[128,512]{1,0:T(8,128)(2,1)S(1)}, bf16[128,512]{1,0:T(8,128)(2,1)S(1)}, u32[]{:S(2)}, u32[]{:S(2)}) %collective-permute-start.48) | collective-permute-done | bytes 131104 | tf_op jit(solution)/shard_map/ppermute | solution.py:336
  155.6 2.8 %collective-permute-done.53.refs_2_.refs_6_ = bf16[128,512]{1,0:T(8,128)(2,1)S(1)} collective-permute-done((bf16[128,512]{1,0:T(8,128)(2,1)S(1)}, bf16[128,512]{1,0:T(8,128)(2,1)S(1)}, u32[]{:S(2)}, u32[]{:S(2)}) %collective-permute-start.53) | collective-permute-done | bytes 131104 | tf_op jit(solution)/shard_map/ppermute | solution.py:333
  162.4 3.3 %shard_map.191 = f32[227,128]{1,0:T(8,128)} custom-call(bf16[128,512]{1,0:T(8,128)(2,1)S(1)} %shard_map.187.refs_0_, bf16[128,512]{1,0:T(8,128)(2,1)S(1)} %collective-permute-done.47.refs_1_, bf16[128,512]{1,0:T(8,128)(2,1)S(1)} %collective-permute-done.48.refs_2_, bf16[128,512]{1,0:T(8,128)(2,1)S(1)} %collective-permute-done.49.refs_3_, ...), custom_call_target="tpu_custom_call" | custom-call | flops 1409286144 | bytes 4194304 | tf_op jit(solution)/shard_map/pallas_call | solution.py:37
  (149 shorter events, 81.1 us)
Async XLA Ops:
  21.2 41.2 %collective-permute-start.12 = (bf16[8,1552,128]{2,1,0:T(8,128)(2,1)}, bf16[8,1552,128]{2,1,0:T(8,128)(2,1)S(1)}, u32[]{:S(2)}, u32[]{:S(2)}) collective-permute-start(bf16[8,1552,128]{2,1,0:T(8,128)(2,1)} %get-tuple-element.111.refs_1_), channel_id=1, source_target_pairs={{0,1},{1,0},{2,3},{3,2},{4,5},{5,4},{6,7},{7,6},{8,9},{9,8},{10,11... | collective-permute-start | bytes 9535496 | tf_op jit(solution)/shard_map/ppermute | solution.py:333
  21.5 14.7 %collective-permute-start.13 = (bf16[1552,128]{1,0:T(8,128)(2,1)}, bf16[1552,128]{1,0:T(8,128)(2,1)S(1)}, u32[]{:S(2)}, u32[]{:S(2)}) collective-permute-start(bf16[1552,128]{1,0:T(8,128)(2,1)} %get-tuple-element.113), channel_id=1, source_target_pairs={{0,2},{1,3},{2,0},{3,1},{4,6},{5,7},{6,4},{7,5},{8,10},{9,11},{10,... | collective-permute-start | bytes 1191944 | tf_op jit(solution)/shard_map/ppermute | solution.py:333
  24.8 11.4 %collective-permute-start.4 = (bf16[128,512]{1,0:T(8,128)(2,1)S(1)}, bf16[128,512]{1,0:T(8,128)(2,1)S(1)}, u32[]{:S(2)}, u32[]{:S(2)}) collective-permute-start(bf16[128,512]{1,0:T(8,128)(2,1)S(1)} %shard_map.173.refs_0_.refs_7_.refs_11_), channel_id=1, source_target_pairs={{0,8},{4,12},{8,0},{12,4},{1,9},{5,13},{9,1},{13,5},{2,10},{6,14},... | collective-permute-start | bytes 393224 | tf_op jit(solution)/shard_map/ppermute | solution.py:336
  27.4 8.8 %collective-permute-start.5 = (bf16[128,512]{1,0:T(8,128)(2,1)S(1)}, bf16[128,512]{1,0:T(8,128)(2,1)S(1)}, u32[]{:S(2)}, u32[]{:S(2)}) collective-permute-start(bf16[128,512]{1,0:T(8,128)(2,1)S(1)} %shard_map.173.refs_0_.refs_7_.refs_11_), channel_id=1, source_target_pairs={{0,12},{4,0},{8,4},{12,8},{1,13},{5,1},{9,5},{13,9},{2,14},{6,2},{... | collective-permute-start | bytes 393224 | tf_op jit(solution)/shard_map/ppermute | solution.py:336
  36.2 11.0 %collective-permute-start.14 = (bf16[1552,128]{1,0:T(8,128)(2,1)S(1)}, bf16[1552,128]{1,0:T(8,128)(2,1)S(1)}, u32[]{:S(2)}, u32[]{:S(2)}) collective-permute-start(bf16[1552,128]{1,0:T(8,128)(2,1)S(1)} %collective-permute-done.13.refs_3_), channel_id=1, source_target_pairs={{0,16},{16,0},{1,17},{17,1},{2,18},{18,2},{3,19},{19,3},{4,20},{20... | collective-permute-start | bytes 1191944 | tf_op jit(solution)/shard_map/ppermute | solution.py:435
  42.7 11.6 %collective-permute-start.8 = (bf16[1552,128]{1,0:T(8,128)(2,1)}, bf16[1552,128]{1,0:T(8,128)(2,1)S(1)}, u32[]{:S(2)}, u32[]{:S(2)}) collective-permute-start(bf16[1552,128]{1,0:T(8,128)(2,1)} %get-tuple-element.107), channel_id=1, source_target_pairs={{0,2},{1,3},{2,0},{3,1},{4,6},{5,7},{6,4},{7,5},{8,10},{9,11},{10,... | collective-permute-start | bytes 1191944 | tf_op jit(solution)/shard_map/ppermute | solution.py:333
  47.2 12.8 %collective-permute-start.15 = (bf16[1552,128]{1,0:T(8,128)(2,1)S(1)}, bf16[1552,128]{1,0:T(8,128)(2,1)S(1)}, u32[]{:S(2)}, u32[]{:S(2)}) collective-permute-start(bf16[1552,128]{1,0:T(8,128)(2,1)S(1)} %collective-permute-done.13.refs_3_), channel_id=1, source_target_pairs={{0,1},{1,0},{2,3},{3,2},{4,5},{5,4},{6,7},{7,6},{8,9},{9,8},{10,11... | collective-permute-start | bytes 1191944 | tf_op jit(solution)/shard_map/ppermute | solution.py:333
  47.2 15.1 %collective-permute-start.16 = (bf16[1552,128]{1,0:T(8,128)(2,1)S(1)}, bf16[1552,128]{1,0:T(8,128)(2,1)S(1)}, u32[]{:S(2)}, u32[]{:S(2)}) collective-permute-start(bf16[1552,128]{1,0:T(8,128)(2,1)S(1)} %collective-permute-done.14.refs_4_), channel_id=1, source_target_pairs={{0,1},{1,0},{2,3},{3,2},{4,5},{5,4},{6,7},{7,6},{8,9},{9,8},{10,11... | collective-permute-start | bytes 1191944 | tf_op jit(solution)/shard_map/ppermute | solution.py:333
  71.0 14.8 %collective-permute-start.26 = (bf16[1552,128]{1,0:T(8,128)(2,1)S(1)}, bf16[1552,128]{1,0:T(8,128)(2,1)S(1)}, u32[]{:S(2)}, u32[]{:S(2)}) collective-permute-start(bf16[1552,128]{1,0:T(8,128)(2,1)S(1)} %collective-permute-done.8.refs_3_), channel_id=1, source_target_pairs={{0,16},{16,0},{1,17},{17,1},{2,18},{18,2},{3,19},{19,3},{4,20},{20... | collective-permute-start | bytes 1191944 | tf_op jit(solution)/shard_map/ppermute | solution.py:435
  74.7 11.1 %collective-permute-start.22 = (bf16[128,512]{1,0:T(8,128)(2,1)S(1)}, bf16[128,512]{1,0:T(8,128)(2,1)S(1)}, u32[]{:S(2)}, u32[]{:S(2)}) collective-permute-start(bf16[128,512]{1,0:T(8,128)(2,1)S(1)} %shard_map.179.refs_0_.refs_7_.refs_11_), channel_id=1, source_target_pairs={{0,8},{4,12},{8,0},{12,4},{1,9},{5,13},{9,1},{13,5},{2,10},{6,14},... | collective-permute-start | bytes 393224 | tf_op jit(solution)/shard_map/ppermute | solution.py:336
  77.0 8.8 %collective-permute-start.23 = (bf16[128,512]{1,0:T(8,128)(2,1)S(1)}, bf16[128,512]{1,0:T(8,128)(2,1)S(1)}, u32[]{:S(2)}, u32[]{:S(2)}) collective-permute-start(bf16[128,512]{1,0:T(8,128)(2,1)S(1)} %shard_map.179.refs_0_.refs_7_.refs_11_), channel_id=1, source_target_pairs={{0,12},{4,0},{8,4},{12,8},{1,13},{5,1},{9,5},{13,9},{2,14},{6,2},{... | collective-permute-start | bytes 393224 | tf_op jit(solution)/shard_map/ppermute | solution.py:336
  77.7 10.1 %collective-permute-start.27 = (bf16[1552,128]{1,0:T(8,128)(2,1)S(1)}, bf16[1552,128]{1,0:T(8,128)(2,1)S(1)}, u32[]{:S(2)}, u32[]{:S(2)}) collective-permute-start(bf16[1552,128]{1,0:T(8,128)(2,1)S(1)} %copy-done.15), channel_id=1, source_target_pairs={{0,2},{1,3},{2,0},{3,1},{4,6},{5,7},{6,4},{7,5},{8,10},{9,11},{10,... | collective-permute-start | bytes 1191944 | tf_op jit(solution)/shard_map/ppermute | solution.py:333
  88.9 8.5 %collective-permute-start.29 = (bf16[128,512]{1,0:T(8,128)(2,1)S(1)}, bf16[128,512]{1,0:T(8,128)(2,1)S(1)}, u32[]{:S(2)}, u32[]{:S(2)}) collective-permute-start(bf16[128,512]{1,0:T(8,128)(2,1)S(1)} %collective-permute-done.23.refs_3_), channel_id=1, source_target_pairs={{0,2},{1,3},{2,0},{3,1},{4,6},{5,7},{6,4},{7,5},{8,10},{9,11},{10,... | collective-permute-start | bytes 393224 | tf_op jit(solution)/shard_map/ppermute | solution.py:333
  102.3 14.5 %collective-permute-start.39 = (bf16[1552,128]{1,0:T(8,128)(2,1)S(1)}, bf16[1552,128]{1,0:T(8,128)(2,1)S(1)}, u32[]{:S(2)}, u32[]{:S(2)}) collective-permute-start(bf16[1552,128]{1,0:T(8,128)(2,1)S(1)} %collective-permute-done.27.refs_3_), channel_id=1, source_target_pairs={{0,16},{16,0},{1,17},{17,1},{2,18},{18,2},{3,19},{19,3},{4,20},{20... | collective-permute-start | bytes 1191944 | tf_op jit(solution)/shard_map/ppermute | solution.py:435
  107.5 9.3 %collective-permute-start.35 = (bf16[128,512]{1,0:T(8,128)(2,1)S(1)}, bf16[128,512]{1,0:T(8,128)(2,1)S(1)}, u32[]{:S(2)}, u32[]{:S(2)}) collective-permute-start(bf16[128,512]{1,0:T(8,128)(2,1)S(1)} %shard_map.183.refs_0_.refs_7_.refs_11_), channel_id=1, source_target_pairs={{0,8},{4,12},{8,0},{12,4},{1,9},{5,13},{9,1},{13,5},{2,10},{6,14},... | collective-permute-start | bytes 393224 | tf_op jit(solution)/shard_map/ppermute | solution.py:336
  107.9 8.8 %collective-permute-start.36 = (bf16[128,512]{1,0:T(8,128)(2,1)S(1)}, bf16[128,512]{1,0:T(8,128)(2,1)S(1)}, u32[]{:S(2)}, u32[]{:S(2)}) collective-permute-start(bf16[128,512]{1,0:T(8,128)(2,1)S(1)} %shard_map.183.refs_0_.refs_7_.refs_11_), channel_id=1, source_target_pairs={{0,12},{4,0},{8,4},{12,8},{1,13},{5,1},{9,5},{13,9},{2,14},{6,2},{... | collective-permute-start | bytes 393224 | tf_op jit(solution)/shard_map/ppermute | solution.py:336
  109.8 10.1 %collective-permute-start.40 = (bf16[1552,128]{1,0:T(8,128)(2,1)S(1)}, bf16[1552,128]{1,0:T(8,128)(2,1)S(1)}, u32[]{:S(2)}, u32[]{:S(2)}) collective-permute-start(bf16[1552,128]{1,0:T(8,128)(2,1)S(1)} %copy-done.14), channel_id=1, source_target_pairs={{0,2},{1,3},{2,0},{3,1},{4,6},{5,7},{6,4},{7,5},{8,10},{9,11},{10,... | collective-permute-start | bytes 1191944 | tf_op jit(solution)/shard_map/ppermute | solution.py:333
  133.2 15.5 %collective-permute-start.52 = (bf16[1552,128]{1,0:T(8,128)(2,1)S(1)}, bf16[1552,128]{1,0:T(8,128)(2,1)S(1)}, u32[]{:S(2)}, u32[]{:S(2)}) collective-permute-start(bf16[1552,128]{1,0:T(8,128)(2,1)S(1)} %collective-permute-done.40.refs_3_), channel_id=1, source_target_pairs={{0,16},{16,0},{1,17},{17,1},{2,18},{18,2},{3,19},{19,3},{4,20},{20... | collective-permute-start | bytes 1191944 | tf_op jit(solution)/shard_map/ppermute | solution.py:435
  134.7 9.1 %collective-permute-start.47 = (bf16[128,512]{1,0:T(8,128)(2,1)S(1)}, bf16[128,512]{1,0:T(8,128)(2,1)S(1)}, u32[]{:S(2)}, u32[]{:S(2)}) collective-permute-start(bf16[128,512]{1,0:T(8,128)(2,1)S(1)} %shard_map.187.refs_0_), channel_id=1, source_target_pairs={{0,4},{4,8},{8,12},{12,0},{1,5},{5,9},{9,13},{13,1},{2,6},{6,10},{... | collective-permute-start | bytes 393224 | tf_op jit(solution)/shard_map/ppermute | solution.py:336
  137.9 10.8 %collective-permute-start.48 = (bf16[128,512]{1,0:T(8,128)(2,1)S(1)}, bf16[128,512]{1,0:T(8,128)(2,1)S(1)}, u32[]{:S(2)}, u32[]{:S(2)}) collective-permute-start(bf16[128,512]{1,0:T(8,128)(2,1)S(1)} %shard_map.187.refs_0_), channel_id=1, source_target_pairs={{0,8},{4,12},{8,0},{12,4},{1,9},{5,13},{9,1},{13,5},{2,10},{6,14},... | collective-permute-start | bytes 393224 | tf_op jit(solution)/shard_map/ppermute | solution.py:336
  140.0 8.7 %collective-permute-start.49 = (bf16[128,512]{1,0:T(8,128)(2,1)S(1)}, bf16[128,512]{1,0:T(8,128)(2,1)S(1)}, u32[]{:S(2)}, u32[]{:S(2)}) collective-permute-start(bf16[128,512]{1,0:T(8,128)(2,1)S(1)} %shard_map.187.refs_0_), channel_id=1, source_target_pairs={{0,12},{4,0},{8,4},{12,8},{1,13},{5,1},{9,5},{13,9},{2,14},{6,2},{... | collective-permute-start | bytes 393224 | tf_op jit(solution)/shard_map/ppermute | solution.py:336
  150.0 8.5 %collective-permute-start.53 = (bf16[128,512]{1,0:T(8,128)(2,1)S(1)}, bf16[128,512]{1,0:T(8,128)(2,1)S(1)}, u32[]{:S(2)}, u32[]{:S(2)}) collective-permute-start(bf16[128,512]{1,0:T(8,128)(2,1)S(1)} %collective-permute-done.48.refs_2_), channel_id=1, source_target_pairs={{0,2},{1,3},{2,0},{3,1},{4,6},{5,7},{6,4},{7,5},{8,10},{9,11},{10,... | collective-permute-start | bytes 393224 | tf_op jit(solution)/shard_map/ppermute | solution.py:333
  151.3 9.1 %collective-permute-start.54 = (bf16[128,512]{1,0:T(8,128)(2,1)S(1)}, bf16[128,512]{1,0:T(8,128)(2,1)S(1)}, u32[]{:S(2)}, u32[]{:S(2)}) collective-permute-start(bf16[128,512]{1,0:T(8,128)(2,1)S(1)} %collective-permute-done.49.refs_3_), channel_id=1, source_target_pairs={{0,2},{1,3},{2,0},{3,1},{4,6},{5,7},{6,4},{7,5},{8,10},{9,11},{10,... | collective-permute-start | bytes 393224 | tf_op jit(solution)/shard_map/ppermute | solution.py:333
  152.0 8.4 %collective-permute-start.55 = (bf16[512,512]{1,0:T(8,128)(2,1)S(1)}, bf16[512,512]{1,0:T(8,128)(2,1)S(1)}, u32[]{:S(2)}, u32[]{:S(2)}) collective-permute-start(bf16[512,512]{1,0:T(8,128)(2,1)S(1)} %shard_map.188), channel_id=1, source_target_pairs={{0,1},{1,0},{2,3},{3,2},{4,5},{5,4},{6,7},{7,6},{8,9},{9,8},{10,11... | collective-permute-start | bytes 1572872 | tf_op jit(solution)/shard_map/ppermute | solution.py:333
  (51 other events, 736.9 us)
